TPU v7x, 256 devices: a whole 4x4x8 slice. The times are simulated.
256 devices in a mesh: layer: 2 (over core), rows: 128 (over y, x, z).
Axes of the slice: x: 4, y: 4, z: 8, core: 2. Of those that a mesh axis runs over, the one named last changes fastest.
Arguments:
- frames: bfloat16 [3, 256, 256, 256], P(None, 'rows'), may hold values from -6 to 6
- initial_state: bfloat16 [2, 256, 256, 256], P('layer', 'rows'), may hold values from -3 to 3
- w_gates: bfloat16 [2, 3, 3, 512, 512], P('layer'), may hold values from -0.25 to 0.25
- w_cand: bfloat16 [2, 3, 3, 512, 256], P('layer'), may hold values from -0.125 to 0.125
- biases: float32 [2, 768], P('layer'), may hold values from -4 to 4
Outputs:
- hidden_frames: bfloat16 [2, 3, 256, 256, 256], P('layer', None, 'rows')
All inputs are finite; a program needn't handle non-finite values.
Results may differ from a plain program's by a relative error of at most 0.0048.
Values may be sent and summed in bfloat16 or wider, within the bound.
No kernel may reach another device: no remote copies, remote signals or barrier semaphores. Data moves between devices by JAX's collectives and lax.ppermute only.
A program may use at most 64 MiB of HBM per device.

v0:
```python
import jax
import jax.numpy as jnp
from jax import lax
from jax.sharding import PartitionSpec as P


def with_halo(block, sides, width):
    for axis, dim in sides:
        count = lax.axis_size(axis)
        forward = [(i, i + 1) for i in range(count - 1)]
        backward = [(target, source) for source, target in forward]
        low = lax.ppermute(
            lax.slice_in_dim(block, block.shape[dim] - width, None, axis=dim), axis, forward
        )
        high = lax.ppermute(lax.slice_in_dim(block, 0, width, axis=dim), axis, backward)
        block = jnp.concatenate([low, block, high], axis=dim)
    return block


def shifted(block, axis, distance):
    devices = range(lax.axis_size(axis))
    route = [(i - distance, i) for i in devices if i - distance in devices]
    return lax.ppermute(block, axis, route)


def convolve(padded, weight):
    out_rows = padded.shape[0] - 2
    out_cols = padded.shape[1] - 2
    pieces = [
        padded[row_off : row_off + out_rows, col_off : col_off + out_cols]
        for row_off in range(3)
        for col_off in range(3)
    ]
    stacked = jnp.concatenate(pieces, axis=-1).reshape(out_rows * out_cols, -1)
    weight_flat = weight.reshape(-1, weight.shape[-1])
    return jnp.dot(stacked, weight_flat, preferred_element_type=jnp.float32).reshape(
        out_rows, out_cols, -1
    )


def pad_cols(field, width):
    return jnp.pad(field, ((0, 0), (width, width), (0, 0)))


def gru_step(inputs, hidden, gate_weight, cand_weight, bias_row, widen_one, widen_reset):
    channels = hidden.shape[-1]
    joined = jnp.concatenate([inputs, hidden], -1)
    hidden_f = hidden.astype(jnp.float32)
    padded = widen_one(joined)
    gate_all = jax.nn.sigmoid(convolve(padded, gate_weight) + bias_row[: 2 * channels])
    update = gate_all[..., :channels]
    reset_state = (gate_all[..., channels:] * hidden_f).astype(jnp.bfloat16)
    reset_wide = widen_reset(reset_state)
    cand_in = jnp.concatenate([padded[..., :channels], reset_wide], -1)
    candidate = jnp.tanh(convolve(cand_in, cand_weight) + bias_row[2 * channels :])
    return ((1.0 - update) * hidden_f + update * candidate).astype(jnp.bfloat16)


def shards(frames, initial_state, w_gates, w_cand, biases):
    frame_count = frames.shape[0]

    def strip_one(field):
        return pad_cols(with_halo(field, (("rows", 0),), 1), 1)

    def strip_reset(field):
        return pad_cols(with_halo(field, (("rows", 0),), 1), 1)

    section_index = lax.axis_index("layer")
    gate_weight = w_gates[0]
    cand_weight = w_cand[0]
    bias_row = biases[0]
    hidden = initial_state[0]
    produced = jnp.zeros((frame_count,) + hidden.shape, jnp.bfloat16)
    passed = jnp.zeros_like(hidden)
    for step_index in range(frame_count + 1):
        if step_index > 0:
            received = shifted(passed, "layer", 1)
        else:
            received = jnp.zeros_like(hidden)
        own_frame = frames[min(step_index, frame_count - 1)]
        inputs = jnp.where(section_index == 0, own_frame, received)
        fresh_state = gru_step(
            inputs, hidden, gate_weight, cand_weight, bias_row, strip_one, strip_reset
        )
        active = jnp.logical_or(
            jnp.logical_and(section_index == 0, step_index < frame_count),
            jnp.logical_and(section_index == 1, step_index >= 1),
        )
        hidden = jnp.where(active, fresh_state, hidden)
        slot_index = jnp.clip(step_index - section_index, 0, frame_count - 1)
        current = lax.dynamic_index_in_dim(produced, slot_index, 0, keepdims=False)
        produced = lax.dynamic_update_index_in_dim(
            produced, jnp.where(active, fresh_state, current), slot_index, 0
        )
        passed = fresh_state
    return produced[None]


def solution(mesh):
    placed = (
        P(None, "rows", None, None),
        P("layer", "rows", None, None),
        P("layer", None, None, None, None),
        P("layer", None, None, None, None),
        P("layer", None),
    )
    return jax.shard_map(
        shards,
        mesh=mesh,
        in_specs=placed,
        out_specs=P("layer", None, "rows", None, None),
        check_vma=False,
    )
```

profile of v0, /device:TPU:25, one launch (start us, length us, event | category | flops | bytes accessed | tf_op | source)
XLA Modules:
  0.0 166.6 jit_solution(3018877560106625188)
XLA Ops:
  0.0 1.1 select_bitcast_fusion
  1.2 1.2 fusion.123
  2.3 3.7 %collective-permute-start = (bf16[1,256,512]{2,1,0:T(8,128)(2,1)S(1)}, bf16[1,256,512]{2,1,0:T(8,128)(2,1)S(1)}, u32[]{:S(2)}, u32[]{:S(2)}) collective-permute-start(bf16[1,256,512]{2,1,0:T(8,128)(2,1)S(1)} %get-tuple-element.11), channel_id=1, source_target_pairs={{0,1},{1,2},{2,3},{3,4},{4,5},{5,6},{6,7},{7,8},{8,9},{9,10},{10,1... | collective-permute-start | bytes 786440 | tf_op jit(solution)/shard_map/ppermute | solution.py:12
  6.0 8.2 %collective-permute-start.1 = (bf16[1,256,512]{2,1,0:T(8,128)(2,1)S(1)}, bf16[1,256,512]{2,1,0:T(8,128)(2,1)S(1)}, u32[]{:S(2)}, u32[]{:S(2)}) collective-permute-start(bf16[1,256,512]{2,1,0:T(8,128)(2,1)S(1)} %get-tuple-element.12), channel_id=1, source_target_pairs={{1,0},{2,1},{3,2},{4,3},{5,4},{6,5},{7,6},{8,7},{9,8},{10,9},{11,1... | collective-permute-start | bytes 786440 | tf_op jit(solution)/shard_map/ppermute | solution.py:15
  14.3 0.7 slice.347
  15.0 3.4 %collective-permute-done = bf16[1,256,512]{2,1,0:T(8,128)(2,1)S(1)} collective-permute-done((bf16[1,256,512]{2,1,0:T(8,128)(2,1)S(1)}, bf16[1,256,512]{2,1,0:T(8,128)(2,1)S(1)}, u32[]{:S(2)}, u32[]{:S(2)}) %collective-permute-start) | collective-permute-done | bytes 262176 | tf_op jit(solution)/shard_map/ppermute | solution.py:12
  18.4 0.9 collective-permute-done.1
  19.2 1.2 select_maximum_fusion.9
  21.2 0.4 slice-done.1
  21.6 2.7 %fusion.10 = f32[2,256,512]{2,1,0:T(8,128)S(1)} fusion(bf16[2,256,4608]{2,1,0:T(8,128)(2,1)S(1)} %slice_dynamic-update-slice_fusion.18, bf16[4608,512,1]{1,0,2:T(8,128)(2,1)S(1)} %bitcast.78, f32[512]{0:T(512)S(1)} %bitcast.68), kind=kOutput, calls=%fused_computation.82 | convolution fusion | flops 2416967680 | bytes 10487808 | tf_op jit(solution)/shard_map/dot_general | solution.py:36
  24.5 1.9 %collective-permute-start.2 = (bf16[1,256,256]{2,1,0:T(8,128)(2,1)S(1)}, bf16[1,256,256]{2,1,0:T(8,128)(2,1)S(1)}, u32[]{:S(2)}, u32[]{:S(2)}) collective-permute-start(bf16[1,256,256]{2,1,0:T(8,128)(2,1)S(1)} %get-tuple-element.19), channel_id=1, source_target_pairs={{0,1},{1,2},{2,3},{3,4},{4,5},{5,6},{6,7},{7,8},{8,9},{9,10},{10,1... | collective-permute-start | bytes 393224 | tf_op jit(solution)/shard_map/ppermute | solution.py:12
  26.4 8.3 %collective-permute-start.3 = (bf16[1,256,256]{2,1,0:T(8,128)(2,1)S(1)}, bf16[1,256,256]{2,1,0:T(8,128)(2,1)S(1)}, u32[]{:S(2)}, u32[]{:S(2)}) collective-permute-start(bf16[1,256,256]{2,1,0:T(8,128)(2,1)S(1)} %get-tuple-element.20), channel_id=1, source_target_pairs={{1,0},{2,1},{3,2},{4,3},{5,4},{6,5},{7,6},{8,7},{9,8},{10,9},{11,1... | collective-permute-start | bytes 393224 | tf_op jit(solution)/shard_map/ppermute | solution.py:15
  34.7 0.7 slice.362
  35.5 1.2 collective-permute-done.3
  37.7 1.4 broadcast_select_fusion.2
  39.2 1.3 collective-permute-start.4
  40.5 3.4 %collective-permute-done.4 = bf16[2,256,256]{2,1,0:T(8,128)(2,1)S(1)} collective-permute-done((bf16[2,256,256]{2,1,0:T(8,128)(2,1)S(1)}, bf16[2,256,256]{2,1,0:T(8,128)(2,1)S(1)}, u32[]{:S(2)}, u32[]{:S(2)}) %collective-permute-start.4) | collective-permute-done | bytes 262176 | tf_op jit(solution)/shard_map/ppermute | solution.py:23
  44.0 1.9 %collective-permute-start.5 = (bf16[1,256,512]{2,1,0:T(8,128)(2,1)S(1)}, bf16[1,256,512]{2,1,0:T(8,128)(2,1)S(1)}, u32[]{:S(2)}, u32[]{:S(2)}) collective-permute-start(bf16[1,256,512]{2,1,0:T(8,128)(2,1)S(1)} %get-tuple-element.9), channel_id=1, source_target_pairs={{0,1},{1,2},{2,3},{3,4},{4,5},{5,6},{6,7},{7,8},{8,9},{9,10},{10,1... | collective-permute-start | bytes 786440 | tf_op jit(solution)/shard_map/ppermute | solution.py:12
  45.9 8.3 %collective-permute-start.6 = (bf16[1,256,512]{2,1,0:T(8,128)(2,1)S(1)}, bf16[1,256,512]{2,1,0:T(8,128)(2,1)S(1)}, u32[]{:S(2)}, u32[]{:S(2)}) collective-permute-start(bf16[1,256,512]{2,1,0:T(8,128)(2,1)S(1)} %get-tuple-element.10), channel_id=1, source_target_pairs={{1,0},{2,1},{3,2},{4,3},{5,4},{6,5},{7,6},{8,7},{9,8},{10,9},{11,1... | collective-permute-start | bytes 786440 | tf_op jit(solution)/shard_map/ppermute | solution.py:15
  54.2 4.6 %collective-permute-done.5 = bf16[1,256,512]{2,1,0:T(8,128)(2,1)S(1)} collective-permute-done((bf16[1,256,512]{2,1,0:T(8,128)(2,1)S(1)}, bf16[1,256,512]{2,1,0:T(8,128)(2,1)S(1)}, u32[]{:S(2)}, u32[]{:S(2)}) %collective-permute-start.5) | collective-permute-done | bytes 262176 | tf_op jit(solution)/shard_map/ppermute | solution.py:12
  58.8 0.9 collective-permute-done.6
  60.7 2.7 %fusion.12 = f32[2,256,512]{2,1,0:T(8,128)S(1)} fusion(bf16[2,256,4608]{2,1,0:T(8,128)(2,1)S(1)} %slice_dynamic-update-slice_fusion.12, bf16[4608,512,1]{1,0,2:T(8,128)(2,1)S(1)} %bitcast.79, f32[512]{0:T(512)S(1)} %bitcast.69), kind=kOutput, calls=%fused_computation.84 | convolution fusion | flops 2416967680 | bytes 10487808 | tf_op jit(solution)/shard_map/dot_general | solution.py:36
  63.6 0.8 copy-done.7
  64.4 0.7 fusion.126
  65.1 1.9 %collective-permute-start.7 = (bf16[1,256,256]{2,1,0:T(8,128)(2,1)}, bf16[1,256,256]{2,1,0:T(8,128)(2,1)}, u32[]{:S(2)}, u32[]{:S(2)}) collective-permute-start(bf16[1,256,256]{2,1,0:T(8,128)(2,1)} %get-tuple-element.17), channel_id=1, source_target_pairs={{0,1},{1,2},{2,3},{3,4},{4,5},{5,6},{6,7},{7,8},{8,9},{9,10},{10,1... | collective-permute-start | bytes 393224 | tf_op jit(solution)/shard_map/ppermute | solution.py:12
  67.0 8.3 %collective-permute-start.8 = (bf16[1,256,256]{2,1,0:T(8,128)(2,1)}, bf16[1,256,256]{2,1,0:T(8,128)(2,1)}, u32[]{:S(2)}, u32[]{:S(2)}) collective-permute-start(bf16[1,256,256]{2,1,0:T(8,128)(2,1)} %get-tuple-element.18), channel_id=1, source_target_pairs={{1,0},{2,1},{3,2},{4,3},{5,4},{6,5},{7,6},{8,7},{9,8},{10,9},{11,1... | collective-permute-start | bytes 393224 | tf_op jit(solution)/shard_map/ppermute | solution.py:15
  75.4 1.2 collective-permute-done.7
  76.7 1.0 collective-permute-done.8
  77.6 1.2 select_maximum_fusion.15
  79.8 0.3 copy-done.5
  80.1 0.4 copy-done.12
  80.4 1.4 broadcast_select_fusion.1
  81.9 1.3 collective-permute-start.9
  83.2 2.8 %collective-permute-done.9 = bf16[2,256,256]{2,1,0:T(8,128)(2,1)S(1)} collective-permute-done((bf16[2,256,256]{2,1,0:T(8,128)(2,1)S(1)}, bf16[2,256,256]{2,1,0:T(8,128)(2,1)S(1)}, u32[]{:S(2)}, u32[]{:S(2)}) %collective-permute-start.9) | collective-permute-done | bytes 262176 | tf_op jit(solution)/shard_map/ppermute | solution.py:23
  86.0 1.1 bitcast_select_fusion.2
  87.2 2.1 %collective-permute-start.10 = (bf16[1,256,512]{2,1,0:T(8,128)(2,1)S(1)}, bf16[1,256,512]{2,1,0:T(8,128)(2,1)S(1)}, u32[]{:S(2)}, u32[]{:S(2)}) collective-permute-start(bf16[1,256,512]{2,1,0:T(8,128)(2,1)S(1)} %get-tuple-element.7), channel_id=1, source_target_pairs={{0,1},{1,2},{2,3},{3,4},{4,5},{5,6},{6,7},{7,8},{8,9},{9,10},{10,1... | collective-permute-start | bytes 786440 | tf_op jit(solution)/shard_map/ppermute | solution.py:12
  89.2 8.5 %collective-permute-start.11 = (bf16[1,256,512]{2,1,0:T(8,128)(2,1)S(1)}, bf16[1,256,512]{2,1,0:T(8,128)(2,1)S(1)}, u32[]{:S(2)}, u32[]{:S(2)}) collective-permute-start(bf16[1,256,512]{2,1,0:T(8,128)(2,1)S(1)} %get-tuple-element.8), channel_id=1, source_target_pairs={{1,0},{2,1},{3,2},{4,3},{5,4},{6,5},{7,6},{8,7},{9,8},{10,9},{11,1... | collective-permute-start | bytes 786440 | tf_op jit(solution)/shard_map/ppermute | solution.py:15
  97.7 4.4 %collective-permute-done.10 = bf16[1,256,512]{2,1,0:T(8,128)(2,1)S(1)} collective-permute-done((bf16[1,256,512]{2,1,0:T(8,128)(2,1)S(1)}, bf16[1,256,512]{2,1,0:T(8,128)(2,1)S(1)}, u32[]{:S(2)}, u32[]{:S(2)}) %collective-permute-start.10) | collective-permute-done | bytes 262176 | tf_op jit(solution)/shard_map/ppermute | solution.py:12
  102.1 0.9 collective-permute-done.11
  104.1 0.4 slice-done.3
  104.5 2.7 %fusion.14 = f32[2,256,512]{2,1,0:T(8,128)S(1)} fusion(bf16[2,256,4608]{2,1,0:T(8,128)(2,1)S(1)} %slice_dynamic-update-slice_fusion.6, bf16[4608,512,1]{1,0,2:T(8,128)(2,1)S(1)} %bitcast.82, f32[512]{0:T(512)S(1)} %bitcast.70), kind=kOutput, calls=%fused_computation.86 | convolution fusion | flops 2416967680 | bytes 10487808 | tf_op jit(solution)/shard_map/dot_general | solution.py:36
  107.4 0.9 copy-done.6
  108.2 0.7 fusion.125
  109.0 1.9 %collective-permute-start.12 = (bf16[1,256,256]{2,1,0:T(8,128)(2,1)}, bf16[1,256,256]{2,1,0:T(8,128)(2,1)}, u32[]{:S(2)}, u32[]{:S(2)}) collective-permute-start(bf16[1,256,256]{2,1,0:T(8,128)(2,1)} %get-tuple-element.15), channel_id=1, source_target_pairs={{0,1},{1,2},{2,3},{3,4},{4,5},{5,6},{6,7},{7,8},{8,9},{9,10},{10,1... | collective-permute-start | bytes 393224 | tf_op jit(solution)/shard_map/ppermute | solution.py:12
  110.9 8.3 %collective-permute-start.13 = (bf16[1,256,256]{2,1,0:T(8,128)(2,1)}, bf16[1,256,256]{2,1,0:T(8,128)(2,1)}, u32[]{:S(2)}, u32[]{:S(2)}) collective-permute-start(bf16[1,256,256]{2,1,0:T(8,128)(2,1)} %get-tuple-element.16), channel_id=1, source_target_pairs={{1,0},{2,1},{3,2},{4,3},{5,4},{6,5},{7,6},{8,7},{9,8},{10,9},{11,1... | collective-permute-start | bytes 393224 | tf_op jit(solution)/shard_map/ppermute | solution.py:15
  119.3 1.2 collective-permute-done.12
  120.5 1.0 collective-permute-done.13
  121.5 1.2 select_maximum_fusion.13
  123.9 0.4 copy-done.10
  124.3 1.4 broadcast_select_fusion
  125.7 1.3 collective-permute-start.14
  127.2 2.6 %collective-permute-done.14 = bf16[2,256,256]{2,1,0:T(8,128)(2,1)S(1)} collective-permute-done((bf16[2,256,256]{2,1,0:T(8,128)(2,1)S(1)}, bf16[2,256,256]{2,1,0:T(8,128)(2,1)S(1)}, u32[]{:S(2)}, u32[]{:S(2)}) %collective-permute-start.14) | collective-permute-done | bytes 262176 | tf_op jit(solution)/shard_map/ppermute | solution.py:23
  129.8 1.0 bitcast_select_fusion.1
  130.9 2.2 %collective-permute-start.15 = (bf16[1,256,512]{2,1,0:T(8,128)(2,1)S(1)}, bf16[1,256,512]{2,1,0:T(8,128)(2,1)S(1)}, u32[]{:S(2)}, u32[]{:S(2)}) collective-permute-start(bf16[1,256,512]{2,1,0:T(8,128)(2,1)S(1)} %get-tuple-element.5), channel_id=1, source_target_pairs={{0,1},{1,2},{2,3},{3,4},{4,5},{5,6},{6,7},{7,8},{8,9},{9,10},{10,1... | collective-permute-start | bytes 786440 | tf_op jit(solution)/shard_map/ppermute | solution.py:12
  133.0 8.3 %collective-permute-start.16 = (bf16[1,256,512]{2,1,0:T(8,128)(2,1)S(1)}, bf16[1,256,512]{2,1,0:T(8,128)(2,1)S(1)}, u32[]{:S(2)}, u32[]{:S(2)}) collective-permute-start(bf16[1,256,512]{2,1,0:T(8,128)(2,1)S(1)} %get-tuple-element.6), channel_id=1, source_target_pairs={{1,0},{2,1},{3,2},{4,3},{5,4},{6,5},{7,6},{8,7},{9,8},{10,9},{11,1... | collective-permute-start | bytes 786440 | tf_op jit(solution)/shard_map/ppermute | solution.py:15
  141.5 4.5 %collective-permute-done.15 = bf16[1,256,512]{2,1,0:T(8,128)(2,1)S(1)} collective-permute-done((bf16[1,256,512]{2,1,0:T(8,128)(2,1)S(1)}, bf16[1,256,512]{2,1,0:T(8,128)(2,1)S(1)}, u32[]{:S(2)}, u32[]{:S(2)}) %collective-permute-start.15) | collective-permute-done | bytes 262176 | tf_op jit(solution)/shard_map/ppermute | solution.py:12
  146.0 0.9 collective-permute-done.16
  147.9 0.4 slice-done.5
  148.3 2.7 %fusion.16 = f32[2,256,512]{2,1,0:T(8,128)S(1)} fusion(bf16[2,256,4608]{2,1,0:T(8,128)(2,1)S(1)} %slice_dynamic-update-slice_fusion, bf16[4608,512,1]{1,0,2:T(8,128)(2,1)S(1)} %bitcast.85, f32[512]{0:T(512)S(1)} %bitcast.71), kind=kOutput, calls=%fused_computation.88 | convolution fusion | flops 2416967680 | bytes 10487808 | tf_op jit(solution)/shard_map/dot_general | solution.py:36
  151.2 1.9 %collective-permute-start.17 = (bf16[1,256,256]{2,1,0:T(8,128)(2,1)S(1)}, bf16[1,256,256]{2,1,0:T(8,128)(2,1)S(1)}, u32[]{:S(2)}, u32[]{:S(2)}) collective-permute-start(bf16[1,256,256]{2,1,0:T(8,128)(2,1)S(1)} %get-tuple-element.13), channel_id=1, source_target_pairs={{0,1},{1,2},{2,3},{3,4},{4,5},{5,6},{6,7},{7,8},{8,9},{9,10},{10,1... | collective-permute-start | bytes 393224 | tf_op jit(solution)/shard_map/ppermute | solution.py:12
  153.1 8.3 %collective-permute-start.18 = (bf16[1,256,256]{2,1,0:T(8,128)(2,1)S(1)}, bf16[1,256,256]{2,1,0:T(8,128)(2,1)S(1)}, u32[]{:S(2)}, u32[]{:S(2)}) collective-permute-start(bf16[1,256,256]{2,1,0:T(8,128)(2,1)S(1)} %get-tuple-element.14), channel_id=1, source_target_pairs={{1,0},{2,1},{3,2},{4,3},{5,4},{6,5},{7,6},{8,7},{9,8},{10,9},{11,1... | collective-permute-start | bytes 393224 | tf_op jit(solution)/shard_map/ppermute | solution.py:15
  161.5 0.9 copy.77
  162.4 0.9 collective-permute-done.18
  164.4 2.1 %fusion.35 = bf16[1,3,2,256,256]{4,3,2,1,0:T(8,128)(2,1)} fusion(bf16[1,3,2,256,256]{4,3,2,1,0:T(8,128)(2,1)} %copy.77, s32[]{:T(128)S(6)} %min.16, bf16[2,256,4608]{2,1,0:T(8,128)(2,1)S(1)} %fusion.108, bf16[4608,256,1]{1,0,2:T(8,128)(2,1)S(1)} %bitcast.62, bf16[2,256,256]{2,1,0:T(8,128)(2,1)S(1)} %get-tuple-element.25, f32[2,256,512]{2,1,0:T(8,128)S(1)} %fusion.16, ...), kind=kOutput, calls=%fused_computation.111 | convolution fusion | flops 1209008128 | bytes 8389637 | tf_op jit(solution)/shard_map/dot_general | solution.py:36
  (144 shorter events, 8.4 us)
Async XLA Ops:
  0.0 37.7 %copy-start = (bf16[1,3,3,512,256]{4,3,2,1,0:T(8,128)(2,1)S(1)}, bf16[1,3,3,512,256]{4,3,2,1,0:T(8,128)(2,1)}, u32[]{:S(2)}) copy-start(bf16[1,3,3,512,256]{4,3,2,1,0:T(8,128)(2,1)} %param.8) | copy-start | bytes 7077892
  0.0 20.7 %copy-start.8 = (bf16[3,2,256,256]{3,2,1,0:T(8,128)(2,1)S(1)}, bf16[3,2,256,256]{3,2,1,0:T(8,128)(2,1)}, u32[]{:S(2)}) copy-start(bf16[3,2,256,256]{3,2,1,0:T(8,128)(2,1)} %param.5) | copy-start | bytes 2359300
  0.0 20.5 %copy-start.1 = (bf16[1,2,256,256]{3,2,1,0:T(8,128)(2,1)S(1)}, bf16[1,2,256,256]{3,2,1,0:T(8,128)(2,1)}, u32[]{:S(2)}) copy-start(bf16[1,2,256,256]{3,2,1,0:T(8,128)(2,1)} %param.6) | copy-start | bytes 786436
  1.2 20.0 %slice-start = ((s8[4718592]{0:T(1024)(128)(4,1)}), s8[4194304]{0:T(1024)(128)(4,1)S(1)}, s32[]{:S(2)}) async-start(s8[4718592]{0:T(1024)(128)(4,1)} %bitcast.76), calls=%async_computation | async-start | bytes 8388608
  2.3 16.0 %collective-permute-start = (bf16[1,256,512]{2,1,0:T(8,128)(2,1)S(1)}, bf16[1,256,512]{2,1,0:T(8,128)(2,1)S(1)}, u32[]{:S(2)}, u32[]{:S(2)}) collective-permute-start(bf16[1,256,512]{2,1,0:T(8,128)(2,1)S(1)} %get-tuple-element.11), channel_id=1, source_target_pairs={{0,1},{1,2},{2,3},{3,4},{4,5},{5,6},{6,7},{7,8},{8,9},{9,10},{10,1... | collective-permute-start | bytes 786440 | tf_op jit(solution)/shard_map/ppermute | solution.py:12
  6.0 13.2 %collective-permute-start.1 = (bf16[1,256,512]{2,1,0:T(8,128)(2,1)S(1)}, bf16[1,256,512]{2,1,0:T(8,128)(2,1)S(1)}, u32[]{:S(2)}, u32[]{:S(2)}) collective-permute-start(bf16[1,256,512]{2,1,0:T(8,128)(2,1)S(1)} %get-tuple-element.12), channel_id=1, source_target_pairs={{1,0},{2,1},{3,2},{4,3},{5,4},{6,5},{7,6},{8,7},{9,8},{10,9},{11,1... | collective-permute-start | bytes 786440 | tf_op jit(solution)/shard_map/ppermute | solution.py:15
  20.5 1.0 slice-start.1
  24.5 11.0 %collective-permute-start.2 = (bf16[1,256,256]{2,1,0:T(8,128)(2,1)S(1)}, bf16[1,256,256]{2,1,0:T(8,128)(2,1)S(1)}, u32[]{:S(2)}, u32[]{:S(2)}) collective-permute-start(bf16[1,256,256]{2,1,0:T(8,128)(2,1)S(1)} %get-tuple-element.19), channel_id=1, source_target_pairs={{0,1},{1,2},{2,3},{3,4},{4,5},{5,6},{6,7},{7,8},{8,9},{9,10},{10,1... | collective-permute-start | bytes 393224 | tf_op jit(solution)/shard_map/ppermute | solution.py:12
  26.4 10.3 %collective-permute-start.3 = (bf16[1,256,256]{2,1,0:T(8,128)(2,1)S(1)}, bf16[1,256,256]{2,1,0:T(8,128)(2,1)S(1)}, u32[]{:S(2)}, u32[]{:S(2)}) collective-permute-start(bf16[1,256,256]{2,1,0:T(8,128)(2,1)S(1)} %get-tuple-element.20), channel_id=1, source_target_pairs={{1,0},{2,1},{3,2},{4,3},{5,4},{6,5},{7,6},{8,7},{9,8},{10,9},{11,1... | collective-permute-start | bytes 393224 | tf_op jit(solution)/shard_map/ppermute | solution.py:15
  39.2 21.2 %copy-start.13 = (bf16[2,256,256]{2,1,0:T(8,128)(2,1)}, bf16[2,256,256]{2,1,0:T(8,128)(2,1)S(1)}, u32[]{:S(2)}) copy-start(bf16[2,256,256]{2,1,0:T(8,128)(2,1)S(1)} %get-tuple-element.22) | copy-start | bytes 786436
  39.2 24.3 %copy-start.4 = (bf16[2,256,256]{2,1,0:T(8,128)(2,1)}, bf16[2,256,256]{2,1,0:T(8,128)(2,1)S(1)}, u32[]{:S(2)}) copy-start(bf16[2,256,256]{2,1,0:T(8,128)(2,1)S(1)} %get-tuple-element.21) | copy-start | bytes 786436
  39.2 4.7 %collective-permute-start.4 = (bf16[2,256,256]{2,1,0:T(8,128)(2,1)S(1)}, bf16[2,256,256]{2,1,0:T(8,128)(2,1)S(1)}, u32[]{:S(2)}, u32[]{:S(2)}) collective-permute-start(bf16[2,256,256]{2,1,0:T(8,128)(2,1)S(1)} %get-tuple-element.22), channel_id=1, source_target_pairs={{0,128},{1,129},{2,130},{3,131},{4,132},{5,133},{6,134},{7,135},{8... | collective-permute-start | bytes 786440 | tf_op jit(solution)/shard_map/ppermute | solution.py:23
  44.0 14.8 %collective-permute-start.5 = (bf16[1,256,512]{2,1,0:T(8,128)(2,1)S(1)}, bf16[1,256,512]{2,1,0:T(8,128)(2,1)S(1)}, u32[]{:S(2)}, u32[]{:S(2)}) collective-permute-start(bf16[1,256,512]{2,1,0:T(8,128)(2,1)S(1)} %get-tuple-element.9), channel_id=1, source_target_pairs={{0,1},{1,2},{2,3},{3,4},{4,5},{5,6},{6,7},{7,8},{8,9},{9,10},{10,1... | collective-permute-start | bytes 786440 | tf_op jit(solution)/shard_map/ppermute | solution.py:12
  45.9 13.8 %collective-permute-start.6 = (bf16[1,256,512]{2,1,0:T(8,128)(2,1)S(1)}, bf16[1,256,512]{2,1,0:T(8,128)(2,1)S(1)}, u32[]{:S(2)}, u32[]{:S(2)}) collective-permute-start(bf16[1,256,512]{2,1,0:T(8,128)(2,1)S(1)} %get-tuple-element.10), channel_id=1, source_target_pairs={{1,0},{2,1},{3,2},{4,3},{5,4},{6,5},{7,6},{8,7},{9,8},{10,9},{11,1... | collective-permute-start | bytes 786440 | tf_op jit(solution)/shard_map/ppermute | solution.py:15
  63.5 1.7 copy-start.11
  63.6 0.8 copy-start.7
  65.1 11.5 %collective-permute-start.7 = (bf16[1,256,256]{2,1,0:T(8,128)(2,1)}, bf16[1,256,256]{2,1,0:T(8,128)(2,1)}, u32[]{:S(2)}, u32[]{:S(2)}) collective-permute-start(bf16[1,256,256]{2,1,0:T(8,128)(2,1)} %get-tuple-element.17), channel_id=1, source_target_pairs={{0,1},{1,2},{2,3},{3,4},{4,5},{5,6},{6,7},{7,8},{8,9},{9,10},{10,1... | collective-permute-start | bytes 393224 | tf_op jit(solution)/shard_map/ppermute | solution.py:12
  67.0 10.6 %collective-permute-start.8 = (bf16[1,256,256]{2,1,0:T(8,128)(2,1)}, bf16[1,256,256]{2,1,0:T(8,128)(2,1)}, u32[]{:S(2)}, u32[]{:S(2)}) collective-permute-start(bf16[1,256,256]{2,1,0:T(8,128)(2,1)} %get-tuple-element.18), channel_id=1, source_target_pairs={{1,0},{2,1},{3,2},{4,3},{5,4},{6,5},{7,6},{8,7},{9,8},{10,9},{11,1... | collective-permute-start | bytes 393224 | tf_op jit(solution)/shard_map/ppermute | solution.py:15
  79.1 1.0 copy-start.5
  79.1 1.3 copy-start.12
  81.9 21.8 %copy-start.15 = (bf16[2,256,256]{2,1,0:T(8,128)(2,1)}, bf16[2,256,256]{2,1,0:T(8,128)(2,1)S(1)}, u32[]{:S(2)}) copy-start(bf16[2,256,256]{2,1,0:T(8,128)(2,1)S(1)} %get-tuple-element.24) | copy-start | bytes 786436
  81.9 25.4 %copy-start.2 = (bf16[2,256,256]{2,1,0:T(8,128)(2,1)}, bf16[2,256,256]{2,1,0:T(8,128)(2,1)S(1)}, u32[]{:S(2)}) copy-start(bf16[2,256,256]{2,1,0:T(8,128)(2,1)S(1)} %get-tuple-element.23) | copy-start | bytes 786436
  81.9 4.1 %collective-permute-start.9 = (bf16[2,256,256]{2,1,0:T(8,128)(2,1)S(1)}, bf16[2,256,256]{2,1,0:T(8,128)(2,1)S(1)}, u32[]{:S(2)}, u32[]{:S(2)}) collective-permute-start(bf16[2,256,256]{2,1,0:T(8,128)(2,1)S(1)} %get-tuple-element.24), channel_id=1, source_target_pairs={{0,128},{1,129},{2,130},{3,131},{4,132},{5,133},{6,134},{7,135},{8... | collective-permute-start | bytes 786440 | tf_op jit(solution)/shard_map/ppermute | solution.py:23
  86.0 18.1 %slice-start.2 = ((s8[4718592]{0:T(1024)(128)(4,1)}), s8[4194304]{0:T(1024)(128)(4,1)S(1)}, s32[]{:S(2)}) async-start(s8[4718592]{0:T(1024)(128)(4,1)} %bitcast.80), calls=%async_computation.2 | async-start | bytes 8388608
  87.2 15.0 %collective-permute-start.10 = (bf16[1,256,512]{2,1,0:T(8,128)(2,1)S(1)}, bf16[1,256,512]{2,1,0:T(8,128)(2,1)S(1)}, u32[]{:S(2)}, u32[]{:S(2)}) collective-permute-start(bf16[1,256,512]{2,1,0:T(8,128)(2,1)S(1)} %get-tuple-element.7), channel_id=1, source_target_pairs={{0,1},{1,2},{2,3},{3,4},{4,5},{5,6},{6,7},{7,8},{8,9},{9,10},{10,1... | collective-permute-start | bytes 786440 | tf_op jit(solution)/shard_map/ppermute | solution.py:12
  89.2 13.8 %collective-permute-start.11 = (bf16[1,256,512]{2,1,0:T(8,128)(2,1)S(1)}, bf16[1,256,512]{2,1,0:T(8,128)(2,1)S(1)}, u32[]{:S(2)}, u32[]{:S(2)}) collective-permute-start(bf16[1,256,512]{2,1,0:T(8,128)(2,1)S(1)} %get-tuple-element.8), channel_id=1, source_target_pairs={{1,0},{2,1},{3,2},{4,3},{5,4},{6,5},{7,6},{8,7},{9,8},{10,9},{11,1... | collective-permute-start | bytes 786440 | tf_op jit(solution)/shard_map/ppermute | solution.py:15
  103.5 1.0 slice-start.3
  107.3 1.7 %copy-start.9 = (f32[2,256,512]{2,1,0:T(8,128)}, f32[2,256,512]{2,1,0:T(8,128)S(1)}, u32[]{:S(2)}) copy-start(f32[2,256,512]{2,1,0:T(8,128)S(1)} %fusion.14) | copy-start | bytes 3145732
  107.4 0.9 copy-start.6
  109.0 11.5 %collective-permute-start.12 = (bf16[1,256,256]{2,1,0:T(8,128)(2,1)}, bf16[1,256,256]{2,1,0:T(8,128)(2,1)}, u32[]{:S(2)}, u32[]{:S(2)}) collective-permute-start(bf16[1,256,256]{2,1,0:T(8,128)(2,1)} %get-tuple-element.15), channel_id=1, source_target_pairs={{0,1},{1,2},{2,3},{3,4},{4,5},{5,6},{6,7},{7,8},{8,9},{9,10},{10,1... | collective-permute-start | bytes 393224 | tf_op jit(solution)/shard_map/ppermute | solution.py:12
  110.9 10.6 %collective-permute-start.13 = (bf16[1,256,256]{2,1,0:T(8,128)(2,1)}, bf16[1,256,256]{2,1,0:T(8,128)(2,1)}, u32[]{:S(2)}, u32[]{:S(2)}) collective-permute-start(bf16[1,256,256]{2,1,0:T(8,128)(2,1)} %get-tuple-element.16), channel_id=1, source_target_pairs={{1,0},{2,1},{3,2},{4,3},{5,4},{6,5},{7,6},{8,7},{9,8},{10,9},{11,1... | collective-permute-start | bytes 393224 | tf_op jit(solution)/shard_map/ppermute | solution.py:15
  122.9 1.0 copy-start.3
  123.0 1.3 copy-start.10
  124.3 2.8 %copy-start.14 = (bf16[2,256,256]{2,1,0:T(8,128)(2,1)S(1)}, bf16[2,256,256]{2,1,0:T(8,128)(2,1)}, u32[]{:S(2)}) copy-start(bf16[2,256,256]{2,1,0:T(8,128)(2,1)} %copy-done.13) | copy-start | bytes 786436
  124.3 17.1 %copy-start.16 = (bf16[2,256,256]{2,1,0:T(8,128)(2,1)S(1)}, bf16[2,256,256]{2,1,0:T(8,128)(2,1)}, u32[]{:S(2)}) copy-start(bf16[2,256,256]{2,1,0:T(8,128)(2,1)} %copy-done.15) | copy-start | bytes 786436
  125.7 4.1 %collective-permute-start.14 = (bf16[2,256,256]{2,1,0:T(8,128)(2,1)S(1)}, bf16[2,256,256]{2,1,0:T(8,128)(2,1)S(1)}, u32[]{:S(2)}, u32[]{:S(2)}) collective-permute-start(bf16[2,256,256]{2,1,0:T(8,128)(2,1)S(1)} %get-tuple-element.26), channel_id=1, source_target_pairs={{0,128},{1,129},{2,130},{3,131},{4,132},{5,133},{6,134},{7,135},{8... | collective-permute-start | bytes 786440 | tf_op jit(solution)/shard_map/ppermute | solution.py:23
  130.8 17.1 %slice-start.4 = ((s8[4718592]{0:T(1024)(128)(4,1)}), s8[4194304]{0:T(1024)(128)(4,1)S(1)}, s32[]{:S(2)}) async-start(s8[4718592]{0:T(1024)(128)(4,1)} %bitcast.83), calls=%async_computation.4 | async-start | bytes 8388608
  130.9 15.1 %collective-permute-start.15 = (bf16[1,256,512]{2,1,0:T(8,128)(2,1)S(1)}, bf16[1,256,512]{2,1,0:T(8,128)(2,1)S(1)}, u32[]{:S(2)}, u32[]{:S(2)}) collective-permute-start(bf16[1,256,512]{2,1,0:T(8,128)(2,1)S(1)} %get-tuple-element.5), channel_id=1, source_target_pairs={{0,1},{1,2},{2,3},{3,4},{4,5},{5,6},{6,7},{7,8},{8,9},{9,10},{10,1... | collective-permute-start | bytes 786440 | tf_op jit(solution)/shard_map/ppermute | solution.py:12
  133.0 13.8 %collective-permute-start.16 = (bf16[1,256,512]{2,1,0:T(8,128)(2,1)S(1)}, bf16[1,256,512]{2,1,0:T(8,128)(2,1)S(1)}, u32[]{:S(2)}, u32[]{:S(2)}) collective-permute-start(bf16[1,256,512]{2,1,0:T(8,128)(2,1)S(1)} %get-tuple-element.6), channel_id=1, source_target_pairs={{1,0},{2,1},{3,2},{4,3},{5,4},{6,5},{7,6},{8,7},{9,8},{10,9},{11,1... | collective-permute-start | bytes 786440 | tf_op jit(solution)/shard_map/ppermute | solution.py:15
  147.3 1.0 slice-start.5
  151.2 11.3 %collective-permute-start.17 = (bf16[1,256,256]{2,1,0:T(8,128)(2,1)S(1)}, bf16[1,256,256]{2,1,0:T(8,128)(2,1)S(1)}, u32[]{:S(2)}, u32[]{:S(2)}) collective-permute-start(bf16[1,256,256]{2,1,0:T(8,128)(2,1)S(1)} %get-tuple-element.13), channel_id=1, source_target_pairs={{0,1},{1,2},{2,3},{3,4},{4,5},{5,6},{6,7},{7,8},{8,9},{9,10},{10,1... | collective-permute-start | bytes 393224 | tf_op jit(solution)/shard_map/ppermute | solution.py:12
  153.1 10.3 %collective-permute-start.18 = (bf16[1,256,256]{2,1,0:T(8,128)(2,1)S(1)}, bf16[1,256,256]{2,1,0:T(8,128)(2,1)S(1)}, u32[]{:S(2)}, u32[]{:S(2)}) collective-permute-start(bf16[1,256,256]{2,1,0:T(8,128)(2,1)S(1)} %get-tuple-element.14), channel_id=1, source_target_pairs={{1,0},{2,1},{3,2},{4,3},{5,4},{6,5},{7,6},{8,7},{9,8},{10,9},{11,1... | collective-permute-start | bytes 393224 | tf_op jit(solution)/shard_map/ppermute | solution.py:15
where the time goes:
time: 169 us; the launch traced here: 167 us
  starting transfers between devices  88 us (52%)
  waiting for transfers between devices  35.9 us (21%)
  matrix products  17.3 us (10%)
  other arithmetic  13.6 us (8%)
  local copies, waits for them, and re-layouts  10.5 us (6%)
    ppermute x8, starting transfers between devices, with_halo(): lax.ppermute(lax.slice_in_dim(block, 0, width, axis=dim), axis, backward)  66.6 us
    ppermute x8, waiting for transfers between devices, with_halo(): lax.ppermute(lax.slice_in_dim(block, block.shape[dim] - width, None, axis...  19.4 us
    ppermute x8, starting transfers between devices, with_halo(): lax.ppermute(lax.slice_in_dim(block, block.shape[dim] - width, None, axis...  17.5 us
    dot_general x8, matrix products, convolve(): jnp.dot(stacked, weight_flat, preferred_element_type=jnp.float32)  17.3 us
    ppermute x3, waiting for transfers between devices, shifted(): return lax.ppermute(block, axis, route)  8.86 us
    ppermute x8, waiting for transfers between devices, with_halo(): lax.ppermute(lax.slice_in_dim(block, 0, width, axis=dim), axis, backward)  7.72 us
    unnamed x74, local copies, waits for them, and re-layouts  6.86 us
    concatenate x8, other arithmetic, with_halo(): block = jnp.concatenate([low, block, high], axis=dim)  4.66 us
  transfers between devices with their start and end apart: 19, of which 17 were waited for; matrix products, arithmetic and copies ran while one was open for 2% of the time, Pallas kernels for 0%

commit v1 on v0

v1 whole, which is shorter than its diff:
```python
import functools

import jax
import jax.numpy as jnp
from jax import lax
from jax.experimental import pallas as pl
from jax.experimental.pallas import tpu as pltpu
from jax.sharding import PartitionSpec as P

VMEM_BYTES = 26 * 1024 * 1024


def widen(target, row, value):
    cols, channels = value.shape
    wide = value.astype(jnp.float32)
    position = lax.broadcasted_iota(jnp.int32, (cols, channels), 0)
    left = jnp.where(position == 0, 0.0, pltpu.roll(wide, 1, 0))
    right = jnp.where(position == cols - 1, 0.0, pltpu.roll(wide, cols - 1, 0))
    target[row, :, 0:channels] = left.astype(jnp.bfloat16)
    target[row, :, channels : 2 * channels] = value
    target[row, :, 2 * channels : 3 * channels] = right.astype(jnp.bfloat16)


def fill(target, own, first, second, odd):
    for row in range(2):
        widen(target, row, jnp.where(odd, first[row], second[row]))
        widen(target, row + 2, own[row])
        widen(target, row + 4, jnp.where(odd, second[row], first[row]))


def taps(source, start, rows, weight, lo, out_lo, channels):
    cols = source.shape[1]
    total = None
    for row_off in range(3):
        view = source[start + row_off : start + row_off + rows].reshape(rows * cols, 3 * channels)
        kernel = weight[row_off, :, lo : lo + channels, out_lo : out_lo + channels]
        part = jnp.dot(
            view, kernel.reshape(3 * channels, channels), preferred_element_type=jnp.float32
        )
        total = part if total is None else total + part
    return total


def step_kernel(
    lag, flags, own, first, second, x0, x0a, x0b, x1, x1h, wg, wc, bias, out,
    wide_h, wide_x, wide_r, pre_r, pre_u, pre_c,
):
    layer, odd = flags[0], flags[1] == 1
    cols, channels = own.shape[1:]
    if lag == 0:
        active = layer == 0
    elif lag == 3:
        active = layer == 1
    else:
        active = layer >= 0

    @pl.when(jnp.logical_not(active))
    def _():
        out[...] = own[...]

    @pl.when(active)
    def _():
        fill(wide_h, own, first, second, odd)
        pre_r[...] = taps(wide_h, 0, 4, wg, channels, channels, channels)
        pre_u[...] = taps(wide_h, 1, 2, wg, channels, 0, channels)

        if lag < 3:
            @pl.when(layer == 0)
            def _():
                fill(wide_x, x0, x0a, x0b, odd)

        if lag > 0:
            @pl.when(layer == 1)
            def _():
                fill(wide_x, x1, x1h.at[0:2], x1h.at[2:4], odd)

        pre_r[...] += taps(wide_x, 0, 4, wg, 0, channels, channels)
        pre_u[...] += taps(wide_x, 1, 2, wg, 0, 0, channels)
        pre_c[...] = taps(wide_x, 1, 2, wc, 0, 0, channels)
        for row in range(4):
            held = wide_h[row + 1, :, channels : 2 * channels].astype(jnp.float32)
            gate = jax.nn.sigmoid(
                pre_r[row * cols : (row + 1) * cols] + bias[:, channels : 2 * channels]
            )
            widen(wide_r, row, (gate * held).astype(jnp.bfloat16))
        pre_c[...] += taps(wide_r, 0, 2, wc, channels, 0, channels)
        for row in range(2):
            part = slice(row * cols, (row + 1) * cols)
            held = own[row].astype(jnp.float32)
            update = jax.nn.sigmoid(pre_u[part] + bias[:, 0:channels])
            candidate = jnp.tanh(pre_c[part] + bias[:, 2 * channels : 3 * channels])
            out[row] = ((1.0 - update) * held + update * candidate).astype(jnp.bfloat16)


def gru_step(lag, flags, own, first, second, x0, x0a, x0b, x1, x1h, wg, wc, bias):
    rows, cols, channels = own.shape
    wide = lambda n: pltpu.VMEM((n, cols, 3 * channels), jnp.bfloat16)
    pre = lambda n: pltpu.VMEM((n * cols, channels), jnp.float32)
    held = pl.BlockSpec(memory_space=pltpu.VMEM)
    return pl.pallas_call(
        functools.partial(step_kernel, lag),
        out_shape=jax.ShapeDtypeStruct(own.shape, own.dtype),
        in_specs=[pl.BlockSpec(memory_space=pltpu.SMEM)] + [held] * 11,
        out_specs=held,
        scratch_shapes=[wide(6), wide(6), wide(4), pre(4), pre(2), pre(2)],
        compiler_params=pltpu.CompilerParams(vmem_limit_bytes=VMEM_BYTES),
        cost_estimate=pl.CostEstimate(
            flops=2 * 8 * cols * channels * 9 * channels, bytes_accessed=8 << 20, transcendentals=0
        ),
    )(flags, own, first, second, x0, x0a, x0b, x1, x1h, wg, wc, bias)


def pairs(count, start, offset):
    found = []
    for low in range(start, count - 1, 2):
        found += [(offset + low, offset + low + 1), (offset + low + 1, offset + low)]
    return found


def swap(field, layers):
    count = lax.axis_size("rows")
    route = lambda start: [p for layer in layers for p in pairs(count, start, layer * count)]
    names = ("layer", "rows")
    return lax.ppermute(field, names, route(0)), lax.ppermute(field, names, route(1))


def shards(frames, initial_state, w_gates, w_cand, biases):
    layer = lax.axis_index("layer")
    strip = lax.axis_index("rows")
    flags = jnp.stack([layer, lax.rem(strip, 2)]).astype(jnp.int32)
    wg, wc = w_gates[0], w_cand[0]
    hidden = initial_state[0]
    up = [(0, 1)]
    down = [(1, 0)]

    first, second = swap(jnp.where(layer == 0, hidden, frames[0]), (0, 1))
    halo = lax.ppermute(jnp.concatenate([first, second]), "layer", down)
    later_a, later_b = swap(frames[1:3].reshape((4,) + hidden.shape[1:]), (1,))
    later = lax.ppermute(jnp.concatenate([later_a, later_b]), "layer", down)
    frame_halos = [
        (halo[0:2], halo[2:4]),
        (later[0:2], later[4:6]),
        (later[2:4], later[6:8]),
    ]
    x1 = hidden
    x1h = halo
    states = []
    for step in range(4):
        frame = min(step, 2)
        x0a, x0b = frame_halos[frame]
        hidden = gru_step(
            step, flags, hidden, first, second, frames[frame], x0a, x0b, x1, x1h, wg, wc, biases
        )
        states.append(hidden)
        if step < 3:
            x1 = lax.ppermute(hidden, "layer", up)
            first, second = swap(hidden, (0, 1))
            x1h = lax.ppermute(jnp.concatenate([first, second]), "layer", up)
    out = [
        jnp.where(layer == 0, states[0], states[1]),
        jnp.where(layer == 0, states[1], states[2]),
        states[3],
    ]
    return jnp.stack(out)[None]


def solution(mesh):
    placed = (
        P(None, "rows", None, None),
        P("layer", "rows", None, None),
        P("layer", None, None, None, None),
        P("layer", None, None, None, None),
        P("layer", None),
    )
    return jax.shard_map(
        shards,
        mesh=mesh,
        in_specs=placed,
        out_specs=P("layer", None, "rows", None, None),
        check_vma=False,
    )
```

time: 169 us -> 113 us (0.67); the launches traced: 167 us -> 112 us
  starting transfers between devices: 88 us -> 48.7 us
  Pallas kernels: 0 us -> 22 us
  matrix products: 17.3 us -> 0 us
  other arithmetic: 13.6 us -> 4.58 us
  local copies, waits for them, and re-layouts: 10.5 us -> 4.98 us
  waiting for transfers between devices: 35.9 us -> 31.8 us
    ppermute x19 -> x18, starting transfers between devices: 88 us -> 48.7 us  [the longest x5 31.3 us: swap(): lax.ppermute(field, names, route(1))]
    pallas_call x0 -> x4, Pallas kernels: none -> 22 us  [gru_step(): pl.pallas_call(functools.partial(step_kernel, lag), out_shape=jax.ShapeDt...]
    dot_general x8 -> x0, matrix products: 17.3 us -> none  [convolve(): jnp.dot(stacked, weight_flat, preferred_element_type=jnp.float32)]
    unnamed x74 -> x12, local copies, waits for them, and re-layouts: 6.86 us -> 1.68 us
    ppermute x19 -> x18, waiting for transfers between devices: 35.9 us -> 31.8 us  [the longest x5 22.1 us: swap(): lax.ppermute(field, names, route(1))]
    concatenate x16 -> x5, other arithmetic: 6.43 us -> 2.28 us  [the longest x1 1.29 us: shards(): later = lax.ppermute(jnp.concatenate([later_a, later_b]), 'layer', down)]
    unnamed x44 -> x0, other arithmetic: 3.32 us -> none
    select_n x4 -> x1, other arithmetic: 3.31 us -> 1.21 us  [shards(): first, second = swap(jnp.where(layer == 0, hidden, frames[0]), (0, 1))]
  transfers between devices with their start and end apart: 19 -> 18, of which waited for: 17 -> 8; matrix products, arithmetic and copies ran while one was open for 2% -> 5% of each run, Pallas kernels for 0% -> 1%
where the time goes in v1:
time: 113 us; the launch traced here: 112 us
  starting transfers between devices  48.7 us (43%)
  waiting for transfers between devices  31.8 us (28%)
  Pallas kernels  22 us (19%)
  local copies, waits for them, and re-layouts  4.98 us (4%)
  other arithmetic  4.58 us (4%)
    ppermute x5, starting transfers between devices, swap(): lax.ppermute(field, names, route(1))  31.3 us
    ppermute x5, waiting for transfers between devices, swap(): lax.ppermute(field, names, route(1))  22.1 us
    pallas_call x4, Pallas kernels, gru_step(): pl.pallas_call(functools.partial(step_kernel, lag), out_shape=jax.ShapeDt...  22 us
    ppermute x3, waiting for transfers between devices, shards(): x1 = lax.ppermute(hidden, 'layer', up)  9.21 us
    ppermute x1, starting transfers between devices, shards(): halo = lax.ppermute(jnp.concatenate([first, second]), 'layer', down)  4.13 us
    ppermute x5, starting transfers between devices, swap(): lax.ppermute(field, names, route(0))  4.11 us
    ppermute x3, starting transfers between devices, shards(): x1h = lax.ppermute(jnp.concatenate([first, second]), 'layer', up)  3.88 us
    ppermute x3, starting transfers between devices, shards(): x1 = lax.ppermute(hidden, 'layer', up)  3.88 us
  transfers between devices with their start and end apart: 18, of which 8 were waited for; matrix products, arithmetic and copies ran while one was open for 5% of the time, Pallas kernels for 1%

profile of v1, /device:TPU:25, one launch (start us, length us, event | category | flops | bytes accessed | tf_op | source)
XLA Modules:
  0.0 112.3 jit_solution(13013366674286754855)
XLA Ops:
  0.0 0.0 copy-start.2
  0.0 0.0 copy-start.1
  0.0 0.0 copy-start.5
  0.0 1.2 %broadcast_select_fusion = bf16[2,256,256]{2,1,0:T(8,128)(2,1)S(1)} fusion(pred[]{:T(512)S(6)} %eq.2, bf16[1,2,256,256]{3,2,1,0:T(8,128)(2,1)} %param.6, bf16[3,2,256,256]{3,2,1,0:T(8,128)(2,1)} %param.5), kind=kLoop, calls=%fused_computation.11 | loop fusion | flops 131072 | bytes 786433 | tf_op jit(solution)/shard_map/jit(_where)/select_n | solution.py:136
  1.2 1.7 %collective-permute-start = (bf16[2,256,256]{2,1,0:T(8,128)(2,1)S(1)}, bf16[2,256,256]{2,1,0:T(8,128)(2,1)S(1)}, u32[]{:S(2)}, u32[]{:S(2)}) collective-permute-start(bf16[2,256,256]{2,1,0:T(8,128)(2,1)S(1)} %broadcast_select_fusion), channel_id=1, source_target_pairs={{0,1},{1,0},{2,3},{3,2},{4,5},{5,4},{6,7},{7,6},{8,9},{9,8},{10,11... | collective-permute-start | bytes 786440 | tf_op jit(solution)/shard_map/ppermute | solution.py:124
  3.0 8.9 %collective-permute-start.1 = (bf16[2,256,256]{2,1,0:T(8,128)(2,1)S(1)}, bf16[2,256,256]{2,1,0:T(8,128)(2,1)S(1)}, u32[]{:S(2)}, u32[]{:S(2)}) collective-permute-start(bf16[2,256,256]{2,1,0:T(8,128)(2,1)S(1)} %broadcast_select_fusion), channel_id=1, source_target_pairs={{1,2},{2,1},{3,4},{4,3},{5,6},{6,5},{7,8},{8,7},{9,10},{10,9},{11,... | collective-permute-start | bytes 786440 | tf_op jit(solution)/shard_map/ppermute | solution.py:124
  11.9 1.9 %slice.36 = bf16[2,2,256,256]{3,2,1,0:T(8,128)(2,1)} slice(bf16[3,2,256,256]{3,2,1,0:T(8,128)(2,1)} %param.5), slice={[1:3], [0:2], [0:256], [0:256]} | slice | bytes 1048576 | tf_op jit(solution)/shard_map/slice | solution.py:138
  13.8 1.9 %collective-permute-start.6 = (bf16[4,256,256]{2,1,0:T(8,128)(2,1)}, bf16[4,256,256]{2,1,0:T(8,128)(2,1)}, u32[]{:S(2)}, u32[]{:S(2)}) collective-permute-start(bf16[4,256,256]{2,1,0:T(8,128)(2,1)} %bitcast.7), channel_id=1, source_target_pairs={{129,130},{130,129},{131,132},{132,131},{133,134},{134,133},{135,1... | collective-permute-start | bytes 1572872 | tf_op jit(solution)/shard_map/ppermute | solution.py:124
  15.7 1.9 %collective-permute-start.5 = (bf16[4,256,256]{2,1,0:T(8,128)(2,1)}, bf16[4,256,256]{2,1,0:T(8,128)(2,1)}, u32[]{:S(2)}, u32[]{:S(2)}) collective-permute-start(bf16[4,256,256]{2,1,0:T(8,128)(2,1)} %bitcast.7), channel_id=1, source_target_pairs={{128,129},{129,128},{130,131},{131,130},{132,133},{133,132},{134,1... | collective-permute-start | bytes 1572872 | tf_op jit(solution)/shard_map/ppermute | solution.py:124
  17.6 0.0 collective-permute-done.first
  17.6 0.0 collective-permute-done.1.second
  17.7 0.8 pad_maximum_fusion.1
  18.5 0.0 copy-start.3
  18.5 0.7 copy-done.3
  19.2 4.1 %collective-permute-start.2 = (bf16[4,256,256]{2,1,0:T(8,128)(2,1)}, bf16[4,256,256]{2,1,0:T(8,128)(2,1)S(1)}, u32[]{:S(2)}, u32[]{:S(2)}) collective-permute-start(bf16[4,256,256]{2,1,0:T(8,128)(2,1)} %pad_maximum_fusion.1), channel_id=1, source_target_pairs={{128,0},{129,1},{130,2},{131,3},{132,4},{133,5},{134,6},{135,7},{1... | collective-permute-start | bytes 1572872 | tf_op jit(solution)/shard_map/ppermute | solution.py:137
  23.4 0.0 copy-start
  23.4 0.1 pad_add_fusion.flags
  23.4 1.3 %slice_bitcast_fusion = (bf16[2,256,256]{2,1,0:T(8,128)(2,1)S(1)}, bf16[2,256,256]{2,1,0:T(8,128)(2,1)S(1)}, bf16[2,256,256]{2,1,0:T(8,128)(2,1)S(1)}) fusion(bf16[3,2,256,256]{3,2,1,0:T(8,128)(2,1)} %param.5), kind=kLoop, calls=%fused_computation.7 | loop fusion | bytes 1572864 | tf_op jit(solution)/shard_map/squeeze | solution.py:152
  24.8 3.5 %collective-permute-done.6 = bf16[4,256,256]{2,1,0:T(8,128)(2,1)} collective-permute-done((bf16[4,256,256]{2,1,0:T(8,128)(2,1)}, bf16[4,256,256]{2,1,0:T(8,128)(2,1)}, u32[]{:S(2)}, u32[]{:S(2)}) %collective-permute-start.6) | collective-permute-done | bytes 524320 | tf_op jit(solution)/shard_map/ppermute | solution.py:124
  28.2 0.0 collective-permute-done.5
  28.2 1.3 %pad_maximum_fusion = bf16[8,256,256]{2,1,0:T(8,128)(2,1)S(1)} fusion(bf16[4,256,256]{2,1,0:T(8,128)(2,1)} %collective-permute-done.6, bf16[4,256,256]{2,1,0:T(8,128)(2,1)} %collective-permute-done.5), kind=kLoop, calls=%fused_computation | loop fusion | flops 524288 | bytes 2097152 | tf_op jit(solution)/shard_map/concatenate | solution.py:139
  29.5 1.4 %collective-permute-start.7 = (bf16[8,256,256]{2,1,0:T(8,128)(2,1)S(1)}, bf16[8,256,256]{2,1,0:T(8,128)(2,1)S(1)}, u32[]{:S(2)}, u32[]{:S(2)}) collective-permute-start(bf16[8,256,256]{2,1,0:T(8,128)(2,1)S(1)} %pad_maximum_fusion), channel_id=1, source_target_pairs={{128,0},{129,1},{130,2},{131,3},{132,4},{133,5},{134,6},{135,7},{1... | collective-permute-start | bytes 3145736 | tf_op jit(solution)/shard_map/ppermute | solution.py:139
  30.9 0.0 collective-permute-done.2.x1h
  31.0 0.0 copy-done.2
  31.0 0.0 copy-done.1
  31.0 0.0 copy-done.5
  31.0 0.0 copy-done
  31.0 0.0 copy-start.4
  31.0 0.9 copy-done.4
  32.0 0.6 shard_map.55.own
  32.5 0.1 collective-permute-start.3
  32.6 5.3 %collective-permute-start.4 = (bf16[2,256,256]{2,1,0:T(8,128)(2,1)S(1)}, bf16[2,256,256]{2,1,0:T(8,128)(2,1)S(1)}, u32[]{:S(2)}, u32[]{:S(2)}) collective-permute-start(bf16[2,256,256]{2,1,0:T(8,128)(2,1)S(1)} %shard_map.55.own), channel_id=1, source_target_pairs={{1,2},{2,1},{3,4},{4,3},{5,6},{6,5},{7,8},{8,7},{9,10},{10,9},{11,... | collective-permute-start | bytes 786440 | tf_op jit(solution)/shard_map/ppermute | solution.py:124
  37.9 0.0 collective-permute-done.3.first
  37.9 6.0 %collective-permute-done.4.second = bf16[2,256,256]{2,1,0:T(8,128)(2,1)S(1)} collective-permute-done((bf16[2,256,256]{2,1,0:T(8,128)(2,1)S(1)}, bf16[2,256,256]{2,1,0:T(8,128)(2,1)S(1)}, u32[]{:S(2)}, u32[]{:S(2)}) %collective-permute-start.4) | collective-permute-done | bytes 262176 | tf_op jit(solution)/shard_map/ppermute | solution.py:124
  44.0 1.3 %collective-permute-start.9 = (bf16[4,256,256]{2,1,0:T(8,128)(2,1)S(1)}, bf16[4,256,256]{2,1,0:T(8,128)(2,1)S(1)}, u32[]{:S(2)}, u32[]{:S(2)}) collective-permute-start(bf16[4,256,256]{2,1,0:T(8,128)(2,1)S(1)} %pad_maximum_fusion.2), channel_id=1, source_target_pairs={{0,128},{1,129},{2,130},{3,131},{4,132},{5,133},{6,134},{7,135},{8... | collective-permute-start | bytes 1572872 | tf_op jit(solution)/shard_map/ppermute | solution.py:158
  45.3 1.3 %collective-permute-start.8 = (bf16[2,256,256]{2,1,0:T(8,128)(2,1)S(1)}, bf16[2,256,256]{2,1,0:T(8,128)(2,1)S(1)}, u32[]{:S(2)}, u32[]{:S(2)}) collective-permute-start(bf16[2,256,256]{2,1,0:T(8,128)(2,1)S(1)} %shard_map.55.own), channel_id=1, source_target_pairs={{0,128},{1,129},{2,130},{3,131},{4,132},{5,133},{6,134},{7,135},{8... | collective-permute-start | bytes 786440 | tf_op jit(solution)/shard_map/ppermute | solution.py:156
  46.6 0.0 collective-permute-done.7
  46.6 0.1 fusion
  46.7 5.0 %collective-permute-done.8.x1 = bf16[2,256,256]{2,1,0:T(8,128)(2,1)S(1)} collective-permute-done((bf16[2,256,256]{2,1,0:T(8,128)(2,1)S(1)}, bf16[2,256,256]{2,1,0:T(8,128)(2,1)S(1)}, u32[]{:S(2)}, u32[]{:S(2)}) %collective-permute-start.8) | collective-permute-done | bytes 262176 | tf_op jit(solution)/shard_map/ppermute | solution.py:156
  51.7 0.0 collective-permute-done.9.x1h
  51.7 7.2 %shard_map.56.own = bf16[2,256,256]{2,1,0:T(8,128)(2,1)S(1)} custom-call(s32[2]{0:T(128)S(1)} %pad_add_fusion.flags, bf16[2,256,256]{2,1,0:T(8,128)(2,1)S(1)} %shard_map.55.own, bf16[2,256,256]{2,1,0:T(8,128)(2,1)S(1)} %collective-permute-done.3.first, bf16[2,256,256]{2,1,0:T(8,128)(2,1)S(1)} %collective-permute-done.4.second, ...), custom_call_target="tpu_custom_call" | custom-call | flops 2415919104 | bytes 8388608 | tf_op jit(solution)/shard_map/pallas_call | solution.py:100
  58.9 0.3 collective-permute-start.10
  59.2 7.9 %collective-permute-start.11 = (bf16[2,256,256]{2,1,0:T(8,128)(2,1)S(1)}, bf16[2,256,256]{2,1,0:T(8,128)(2,1)S(1)}, u32[]{:S(2)}, u32[]{:S(2)}) collective-permute-start(bf16[2,256,256]{2,1,0:T(8,128)(2,1)S(1)} %shard_map.56.own), channel_id=1, source_target_pairs={{1,2},{2,1},{3,4},{4,3},{5,6},{6,5},{7,8},{8,7},{9,10},{10,9},{11,... | collective-permute-start | bytes 786440 | tf_op jit(solution)/shard_map/ppermute | solution.py:124
  67.1 0.0 collective-permute-done.10.first
  67.1 6.5 %collective-permute-done.11.second = bf16[2,256,256]{2,1,0:T(8,128)(2,1)S(1)} collective-permute-done((bf16[2,256,256]{2,1,0:T(8,128)(2,1)S(1)}, bf16[2,256,256]{2,1,0:T(8,128)(2,1)S(1)}, u32[]{:S(2)}, u32[]{:S(2)}) %collective-permute-start.11) | collective-permute-done | bytes 262176 | tf_op jit(solution)/shard_map/ppermute | solution.py:124
  73.6 1.3 %collective-permute-start.13 = (bf16[4,256,256]{2,1,0:T(8,128)(2,1)S(1)}, bf16[4,256,256]{2,1,0:T(8,128)(2,1)S(1)}, u32[]{:S(2)}, u32[]{:S(2)}) collective-permute-start(bf16[4,256,256]{2,1,0:T(8,128)(2,1)S(1)} %pad_maximum_fusion.3), channel_id=1, source_target_pairs={{0,128},{1,129},{2,130},{3,131},{4,132},{5,133},{6,134},{7,135},{8... | collective-permute-start | bytes 1572872 | tf_op jit(solution)/shard_map/ppermute | solution.py:158
  74.9 1.3 %collective-permute-start.12 = (bf16[2,256,256]{2,1,0:T(8,128)(2,1)S(1)}, bf16[2,256,256]{2,1,0:T(8,128)(2,1)S(1)}, u32[]{:S(2)}, u32[]{:S(2)}) collective-permute-start(bf16[2,256,256]{2,1,0:T(8,128)(2,1)S(1)} %shard_map.56.own), channel_id=1, source_target_pairs={{0,128},{1,129},{2,130},{3,131},{4,132},{5,133},{6,134},{7,135},{8... | collective-permute-start | bytes 786440 | tf_op jit(solution)/shard_map/ppermute | solution.py:156
  76.2 2.2 %collective-permute-done.12.x1 = bf16[2,256,256]{2,1,0:T(8,128)(2,1)S(1)} collective-permute-done((bf16[2,256,256]{2,1,0:T(8,128)(2,1)S(1)}, bf16[2,256,256]{2,1,0:T(8,128)(2,1)S(1)}, u32[]{:S(2)}, u32[]{:S(2)}) %collective-permute-start.12) | collective-permute-done | bytes 262176 | tf_op jit(solution)/shard_map/ppermute | solution.py:156
  78.4 0.0 collective-permute-done.13.x1h
  78.4 7.2 %shard_map.57.own = bf16[2,256,256]{2,1,0:T(8,128)(2,1)S(1)} custom-call(s32[2]{0:T(128)S(1)} %pad_add_fusion.flags, bf16[2,256,256]{2,1,0:T(8,128)(2,1)S(1)} %shard_map.56.own, bf16[2,256,256]{2,1,0:T(8,128)(2,1)S(1)} %collective-permute-done.10.first, bf16[2,256,256]{2,1,0:T(8,128)(2,1)S(1)} %collective-permute-done.11.second, ...), custom_call_target="tpu_custom_call" | custom-call | flops 2415919104 | bytes 8388608 | tf_op jit(solution)/shard_map/pallas_call | solution.py:100
  85.6 0.1 collective-permute-start.14
  85.8 7.4 %collective-permute-start.15 = (bf16[2,256,256]{2,1,0:T(8,128)(2,1)S(1)}, bf16[2,256,256]{2,1,0:T(8,128)(2,1)S(1)}, u32[]{:S(2)}, u32[]{:S(2)}) collective-permute-start(bf16[2,256,256]{2,1,0:T(8,128)(2,1)S(1)} %shard_map.57.own), channel_id=1, source_target_pairs={{1,2},{2,1},{3,4},{4,3},{5,6},{6,5},{7,8},{8,7},{9,10},{10,9},{11,... | collective-permute-start | bytes 786440 | tf_op jit(solution)/shard_map/ppermute | solution.py:124
  93.1 0.4 collective-permute-done.14.first
  93.5 6.1 %collective-permute-done.15.second = bf16[2,256,256]{2,1,0:T(8,128)(2,1)S(1)} collective-permute-done((bf16[2,256,256]{2,1,0:T(8,128)(2,1)S(1)}, bf16[2,256,256]{2,1,0:T(8,128)(2,1)S(1)}, u32[]{:S(2)}, u32[]{:S(2)}) %collective-permute-start.15) | collective-permute-done | bytes 262176 | tf_op jit(solution)/shard_map/ppermute | solution.py:124
  99.7 1.3 %collective-permute-start.17 = (bf16[4,256,256]{2,1,0:T(8,128)(2,1)S(1)}, bf16[4,256,256]{2,1,0:T(8,128)(2,1)S(1)}, u32[]{:S(2)}, u32[]{:S(2)}) collective-permute-start(bf16[4,256,256]{2,1,0:T(8,128)(2,1)S(1)} %pad_maximum_fusion.4), channel_id=1, source_target_pairs={{0,128},{1,129},{2,130},{3,131},{4,132},{5,133},{6,134},{7,135},{8... | collective-permute-start | bytes 1572872 | tf_op jit(solution)/shard_map/ppermute | solution.py:158
  101.0 1.3 %collective-permute-start.16 = (bf16[2,256,256]{2,1,0:T(8,128)(2,1)S(1)}, bf16[2,256,256]{2,1,0:T(8,128)(2,1)S(1)}, u32[]{:S(2)}, u32[]{:S(2)}) collective-permute-start(bf16[2,256,256]{2,1,0:T(8,128)(2,1)S(1)} %shard_map.57.own), channel_id=1, source_target_pairs={{0,128},{1,129},{2,130},{3,131},{4,132},{5,133},{6,134},{7,135},{8... | collective-permute-start | bytes 786440 | tf_op jit(solution)/shard_map/ppermute | solution.py:156
  102.3 2.1 %collective-permute-done.16.x1 = bf16[2,256,256]{2,1,0:T(8,128)(2,1)S(1)} collective-permute-done((bf16[2,256,256]{2,1,0:T(8,128)(2,1)S(1)}, bf16[2,256,256]{2,1,0:T(8,128)(2,1)S(1)}, u32[]{:S(2)}, u32[]{:S(2)}) %collective-permute-start.16) | collective-permute-done | bytes 262176 | tf_op jit(solution)/shard_map/ppermute | solution.py:156
  104.4 0.0 collective-permute-done.17.x1h
  104.4 6.9 %shard_map.58 = bf16[2,256,256]{2,1,0:T(8,128)(2,1)S(1)} custom-call(s32[2]{0:T(128)S(1)} %pad_add_fusion.flags, bf16[2,256,256]{2,1,0:T(8,128)(2,1)S(1)} %shard_map.57.own, bf16[2,256,256]{2,1,0:T(8,128)(2,1)S(1)} %collective-permute-done.14.first, bf16[2,256,256]{2,1,0:T(8,128)(2,1)S(1)} %collective-permute-done.15.second, ...), custom_call_target="tpu_custom_call" | custom-call | flops 2415919104 | bytes 8388608 | tf_op jit(solution)/shard_map/pallas_call | solution.py:100
  111.4 1.0 maximum_bitcast_fusion
  (5 shorter events, 0.2 us)
Async XLA Ops:
  0.0 31.0 %copy-start.2 = (bf16[1,2,256,256]{3,2,1,0:T(8,128)(2,1)S(1)}, bf16[1,2,256,256]{3,2,1,0:T(8,128)(2,1)}, u32[]{:S(2)}) copy-start(bf16[1,2,256,256]{3,2,1,0:T(8,128)(2,1)} %param.6) | copy-start | bytes 786436
  0.0 31.0 %copy-start.1 = (bf16[1,3,3,512,256]{4,3,2,1,0:T(8,128)(2,1)S(1)}, bf16[1,3,3,512,256]{4,3,2,1,0:T(8,128)(2,1)}, u32[]{:S(2)}) copy-start(bf16[1,3,3,512,256]{4,3,2,1,0:T(8,128)(2,1)} %param.8) | copy-start | bytes 7077892
  0.0 31.0 %copy-start.5 = (f32[1,768]{1,0:T(1,128)S(1)}, f32[1,768]{1,0:T(1,128)}, u32[]{:S(2)}) copy-start(f32[1,768]{1,0:T(1,128)} %bias.7) | copy-start | bytes 9220
  1.2 16.4 %collective-permute-start = (bf16[2,256,256]{2,1,0:T(8,128)(2,1)S(1)}, bf16[2,256,256]{2,1,0:T(8,128)(2,1)S(1)}, u32[]{:S(2)}, u32[]{:S(2)}) collective-permute-start(bf16[2,256,256]{2,1,0:T(8,128)(2,1)S(1)} %broadcast_select_fusion), channel_id=1, source_target_pairs={{0,1},{1,0},{2,3},{3,2},{4,5},{5,4},{6,7},{7,6},{8,9},{9,8},{10,11... | collective-permute-start | bytes 786440 | tf_op jit(solution)/shard_map/ppermute | solution.py:124
  3.0 14.7 %collective-permute-start.1 = (bf16[2,256,256]{2,1,0:T(8,128)(2,1)S(1)}, bf16[2,256,256]{2,1,0:T(8,128)(2,1)S(1)}, u32[]{:S(2)}, u32[]{:S(2)}) collective-permute-start(bf16[2,256,256]{2,1,0:T(8,128)(2,1)S(1)} %broadcast_select_fusion), channel_id=1, source_target_pairs={{1,2},{2,1},{3,4},{4,3},{5,6},{6,5},{7,8},{8,7},{9,10},{10,9},{11,... | collective-permute-start | bytes 786440 | tf_op jit(solution)/shard_map/ppermute | solution.py:124
  13.8 14.4 %collective-permute-start.6 = (bf16[4,256,256]{2,1,0:T(8,128)(2,1)}, bf16[4,256,256]{2,1,0:T(8,128)(2,1)}, u32[]{:S(2)}, u32[]{:S(2)}) collective-permute-start(bf16[4,256,256]{2,1,0:T(8,128)(2,1)} %bitcast.7), channel_id=1, source_target_pairs={{129,130},{130,129},{131,132},{132,131},{133,134},{134,133},{135,1... | collective-permute-start | bytes 1572872 | tf_op jit(solution)/shard_map/ppermute | solution.py:124
  15.7 12.5 %collective-permute-start.5 = (bf16[4,256,256]{2,1,0:T(8,128)(2,1)}, bf16[4,256,256]{2,1,0:T(8,128)(2,1)}, u32[]{:S(2)}, u32[]{:S(2)}) collective-permute-start(bf16[4,256,256]{2,1,0:T(8,128)(2,1)} %bitcast.7), channel_id=1, source_target_pairs={{128,129},{129,128},{130,131},{131,130},{132,133},{133,132},{134,1... | collective-permute-start | bytes 1572872 | tf_op jit(solution)/shard_map/ppermute | solution.py:124
  18.5 0.7 copy-start.3
  19.2 11.7 %collective-permute-start.2 = (bf16[4,256,256]{2,1,0:T(8,128)(2,1)}, bf16[4,256,256]{2,1,0:T(8,128)(2,1)S(1)}, u32[]{:S(2)}, u32[]{:S(2)}) collective-permute-start(bf16[4,256,256]{2,1,0:T(8,128)(2,1)} %pad_maximum_fusion.1), channel_id=1, source_target_pairs={{128,0},{129,1},{130,2},{131,3},{132,4},{133,5},{134,6},{135,7},{1... | collective-permute-start | bytes 1572872 | tf_op jit(solution)/shard_map/ppermute | solution.py:137
  23.4 7.6 %copy-start = (bf16[1,3,3,512,512]{4,3,2,1,0:T(8,128)(2,1)S(1)}, bf16[1,3,3,512,512]{4,3,2,1,0:T(8,128)(2,1)}, u32[]{:S(2)}) copy-start(bf16[1,3,3,512,512]{4,3,2,1,0:T(8,128)(2,1)} %param.7) | copy-start | bytes 14155780
  29.5 17.1 %collective-permute-start.7 = (bf16[8,256,256]{2,1,0:T(8,128)(2,1)S(1)}, bf16[8,256,256]{2,1,0:T(8,128)(2,1)S(1)}, u32[]{:S(2)}, u32[]{:S(2)}) collective-permute-start(bf16[8,256,256]{2,1,0:T(8,128)(2,1)S(1)} %pad_maximum_fusion), channel_id=1, source_target_pairs={{128,0},{129,1},{130,2},{131,3},{132,4},{133,5},{134,6},{135,7},{1... | collective-permute-start | bytes 3145736 | tf_op jit(solution)/shard_map/ppermute | solution.py:139
  31.0 1.0 copy-start.4
  32.5 5.4 %collective-permute-start.3 = (bf16[2,256,256]{2,1,0:T(8,128)(2,1)S(1)}, bf16[2,256,256]{2,1,0:T(8,128)(2,1)S(1)}, u32[]{:S(2)}, u32[]{:S(2)}) collective-permute-start(bf16[2,256,256]{2,1,0:T(8,128)(2,1)S(1)} %shard_map.55.own), channel_id=1, source_target_pairs={{0,1},{1,0},{2,3},{3,2},{4,5},{5,4},{6,7},{7,6},{8,9},{9,8},{10,11... | collective-permute-start | bytes 786440 | tf_op jit(solution)/shard_map/ppermute | solution.py:124
  32.6 11.3 %collective-permute-start.4 = (bf16[2,256,256]{2,1,0:T(8,128)(2,1)S(1)}, bf16[2,256,256]{2,1,0:T(8,128)(2,1)S(1)}, u32[]{:S(2)}, u32[]{:S(2)}) collective-permute-start(bf16[2,256,256]{2,1,0:T(8,128)(2,1)S(1)} %shard_map.55.own), channel_id=1, source_target_pairs={{1,2},{2,1},{3,4},{4,3},{5,6},{6,5},{7,8},{8,7},{9,10},{10,9},{11,... | collective-permute-start | bytes 786440 | tf_op jit(solution)/shard_map/ppermute | solution.py:124
  44.0 7.6 %collective-permute-start.9 = (bf16[4,256,256]{2,1,0:T(8,128)(2,1)S(1)}, bf16[4,256,256]{2,1,0:T(8,128)(2,1)S(1)}, u32[]{:S(2)}, u32[]{:S(2)}) collective-permute-start(bf16[4,256,256]{2,1,0:T(8,128)(2,1)S(1)} %pad_maximum_fusion.2), channel_id=1, source_target_pairs={{0,128},{1,129},{2,130},{3,131},{4,132},{5,133},{6,134},{7,135},{8... | collective-permute-start | bytes 1572872 | tf_op jit(solution)/shard_map/ppermute | solution.py:158
  45.3 6.3 %collective-permute-start.8 = (bf16[2,256,256]{2,1,0:T(8,128)(2,1)S(1)}, bf16[2,256,256]{2,1,0:T(8,128)(2,1)S(1)}, u32[]{:S(2)}, u32[]{:S(2)}) collective-permute-start(bf16[2,256,256]{2,1,0:T(8,128)(2,1)S(1)} %shard_map.55.own), channel_id=1, source_target_pairs={{0,128},{1,129},{2,130},{3,131},{4,132},{5,133},{6,134},{7,135},{8... | collective-permute-start | bytes 786440 | tf_op jit(solution)/shard_map/ppermute | solution.py:156
  58.9 8.2 %collective-permute-start.10 = (bf16[2,256,256]{2,1,0:T(8,128)(2,1)S(1)}, bf16[2,256,256]{2,1,0:T(8,128)(2,1)S(1)}, u32[]{:S(2)}, u32[]{:S(2)}) collective-permute-start(bf16[2,256,256]{2,1,0:T(8,128)(2,1)S(1)} %shard_map.56.own), channel_id=1, source_target_pairs={{0,1},{1,0},{2,3},{3,2},{4,5},{5,4},{6,7},{7,6},{8,9},{9,8},{10,11... | collective-permute-start | bytes 786440 | tf_op jit(solution)/shard_map/ppermute | solution.py:124
  59.2 14.4 %collective-permute-start.11 = (bf16[2,256,256]{2,1,0:T(8,128)(2,1)S(1)}, bf16[2,256,256]{2,1,0:T(8,128)(2,1)S(1)}, u32[]{:S(2)}, u32[]{:S(2)}) collective-permute-start(bf16[2,256,256]{2,1,0:T(8,128)(2,1)S(1)} %shard_map.56.own), channel_id=1, source_target_pairs={{1,2},{2,1},{3,4},{4,3},{5,6},{6,5},{7,8},{8,7},{9,10},{10,9},{11,... | collective-permute-start | bytes 786440 | tf_op jit(solution)/shard_map/ppermute | solution.py:124
  73.6 4.8 %collective-permute-start.13 = (bf16[4,256,256]{2,1,0:T(8,128)(2,1)S(1)}, bf16[4,256,256]{2,1,0:T(8,128)(2,1)S(1)}, u32[]{:S(2)}, u32[]{:S(2)}) collective-permute-start(bf16[4,256,256]{2,1,0:T(8,128)(2,1)S(1)} %pad_maximum_fusion.3), channel_id=1, source_target_pairs={{0,128},{1,129},{2,130},{3,131},{4,132},{5,133},{6,134},{7,135},{8... | collective-permute-start | bytes 1572872 | tf_op jit(solution)/shard_map/ppermute | solution.py:158
  74.9 3.5 %collective-permute-start.12 = (bf16[2,256,256]{2,1,0:T(8,128)(2,1)S(1)}, bf16[2,256,256]{2,1,0:T(8,128)(2,1)S(1)}, u32[]{:S(2)}, u32[]{:S(2)}) collective-permute-start(bf16[2,256,256]{2,1,0:T(8,128)(2,1)S(1)} %shard_map.56.own), channel_id=1, source_target_pairs={{0,128},{1,129},{2,130},{3,131},{4,132},{5,133},{6,134},{7,135},{8... | collective-permute-start | bytes 786440 | tf_op jit(solution)/shard_map/ppermute | solution.py:156
  85.6 7.9 %collective-permute-start.14 = (bf16[2,256,256]{2,1,0:T(8,128)(2,1)S(1)}, bf16[2,256,256]{2,1,0:T(8,128)(2,1)S(1)}, u32[]{:S(2)}, u32[]{:S(2)}) collective-permute-start(bf16[2,256,256]{2,1,0:T(8,128)(2,1)S(1)} %shard_map.57.own), channel_id=1, source_target_pairs={{0,1},{1,0},{2,3},{3,2},{4,5},{5,4},{6,7},{7,6},{8,9},{9,8},{10,11... | collective-permute-start | bytes 786440 | tf_op jit(solution)/shard_map/ppermute | solution.py:124
  85.8 13.9 %collective-permute-start.15 = (bf16[2,256,256]{2,1,0:T(8,128)(2,1)S(1)}, bf16[2,256,256]{2,1,0:T(8,128)(2,1)S(1)}, u32[]{:S(2)}, u32[]{:S(2)}) collective-permute-start(bf16[2,256,256]{2,1,0:T(8,128)(2,1)S(1)} %shard_map.57.own), channel_id=1, source_target_pairs={{1,2},{2,1},{3,4},{4,3},{5,6},{6,5},{7,8},{8,7},{9,10},{10,9},{11,... | collective-permute-start | bytes 786440 | tf_op jit(solution)/shard_map/ppermute | solution.py:124
  99.7 4.8 %collective-permute-start.17 = (bf16[4,256,256]{2,1,0:T(8,128)(2,1)S(1)}, bf16[4,256,256]{2,1,0:T(8,128)(2,1)S(1)}, u32[]{:S(2)}, u32[]{:S(2)}) collective-permute-start(bf16[4,256,256]{2,1,0:T(8,128)(2,1)S(1)} %pad_maximum_fusion.4), channel_id=1, source_target_pairs={{0,128},{1,129},{2,130},{3,131},{4,132},{5,133},{6,134},{7,135},{8... | collective-permute-start | bytes 1572872 | tf_op jit(solution)/shard_map/ppermute | solution.py:158
  101.0 3.5 %collective-permute-start.16 = (bf16[2,256,256]{2,1,0:T(8,128)(2,1)S(1)}, bf16[2,256,256]{2,1,0:T(8,128)(2,1)S(1)}, u32[]{:S(2)}, u32[]{:S(2)}) collective-permute-start(bf16[2,256,256]{2,1,0:T(8,128)(2,1)S(1)} %shard_map.57.own), channel_id=1, source_target_pairs={{0,128},{1,129},{2,130},{3,131},{4,132},{5,133},{6,134},{7,135},{8... | collective-permute-start | bytes 786440 | tf_op jit(solution)/shard_map/ppermute | solution.py:156

commit v2 on v1

v2 whole, which is shorter than its diff:
```python
import functools

import jax
import jax.numpy as jnp
from jax import lax
from jax.experimental import pallas as pl
from jax.experimental.pallas import tpu as pltpu
from jax.sharding import PartitionSpec as P

MIB = 1024 * 1024


def widen(target, row, value):
    cols, channels = value.shape
    wide = value.astype(jnp.float32)
    position = lax.broadcasted_iota(jnp.int32, (cols, channels), 0)
    left = jnp.where(position == 0, 0.0, pltpu.roll(wide, 1, 0))
    right = jnp.where(position == cols - 1, 0.0, pltpu.roll(wide, cols - 1, 0))
    target[row, :, 0:channels] = left.astype(jnp.bfloat16)
    target[row, :, channels : 2 * channels] = value
    target[row, :, 2 * channels : 3 * channels] = right.astype(jnp.bfloat16)


def halo_row(first, second, odd, row, base=0):
    one, other = first[base + row % 2], second[base + row % 2]
    return jnp.where(odd == (row < 2), one, other)


def fill(target, own, first, second, odd, own_base, halo_base):
    for row in range(2):
        widen(target, row, halo_row(first, second, odd, row, halo_base))
        widen(target, row + 2, own[own_base + row])
        widen(target, row + 4, halo_row(first, second, odd, row + 2, halo_base))


def taps(source, start, rows, weight, lo, out_lo, channels):
    cols = source.shape[1]
    total = None
    for row_off in range(3):
        view = source[start + row_off : start + row_off + rows].reshape(rows * cols, 3 * channels)
        kernel = weight[row_off, :, lo : lo + channels, out_lo : out_lo + channels]
        part = jnp.dot(
            view, kernel.reshape(3 * channels, channels), preferred_element_type=jnp.float32
        )
        total = part if total is None else total + part
    return total


def early_kernel(
    role, bases, of_state, flags, own, first, second, wg, wc, *rest
):
    pre_r, pre_u = rest[:2]
    channels = own.shape[-1]
    lo = channels if of_state else 0

    @pl.when(flags[0] == role)
    def _():
        wide = rest[-1]
        fill(wide, own, first, second, flags[1] == 1, *bases)
        pre_r[...] = taps(wide, 0, 4, wg, lo, channels, channels)
        pre_u[...] = taps(wide, 1, 2, wg, lo, 0, channels)
        if not of_state:
            rest[2][...] = taps(wide, 1, 2, wc, 0, 0, channels)


def late_kernel(role, bases, of_state, with_other, flags, state, source, pre, weights, rest):
    own, first, second = state
    wg, wc, bias = weights
    out, wide, wide_r, sum_c = rest[-4:]
    cols, channels = own.shape[1:]
    lo = channels if of_state else 0

    @pl.when(flags[0] == role)
    def _():
        odd = flags[1] == 1
        fill(wide, *source, odd, *bases)
        sum_r = pre[0][...] + taps(wide, 0, 4, wg, lo, channels, channels)
        for row in range(4):
            held = own[row - 1] if 0 < row < 3 else halo_row(first, second, odd, 1 if row == 0 else 2)
            gate = jax.nn.sigmoid(
                sum_r[row * cols : (row + 1) * cols] + bias[:, channels : 2 * channels]
            )
            widen(wide_r, row, (gate * held.astype(jnp.float32)).astype(jnp.bfloat16))
        sum_u = pre[1][...] + taps(wide, 1, 2, wg, lo, 0, channels)
        of_input = pre[2][...] if of_state else taps(wide, 1, 2, wc, 0, 0, channels)
        sum_c[...] = of_input + taps(wide_r, 0, 2, wc, channels, 0, channels)
        for row in range(2):
            part = slice(row * cols, (row + 1) * cols)
            held = own[row].astype(jnp.float32)
            update = jax.nn.sigmoid(sum_u[part] + bias[:, 0:channels])
            candidate = jnp.tanh(sum_c[part] + bias[:, 2 * channels : 3 * channels])
            out[row] = ((1.0 - update) * held + update * candidate).astype(jnp.bfloat16)

    if with_other:
        @pl.when(flags[0] != role)
        def _():
            out[...] = rest[0][...]


HELD = pl.BlockSpec(memory_space=pltpu.VMEM)
SCALARS = pl.BlockSpec(memory_space=pltpu.SMEM)


def cost(cols, channels):
    return pl.CostEstimate(
        flops=2 * 8 * cols * channels * 9 * channels, bytes_accessed=1 << 20, transcendentals=0
    )


def early(role, flags, source, wg, wc, bases=(0, 0), of_state=False):
    cols, channels = source[0].shape[1:]
    pre = lambda n: jax.ShapeDtypeStruct((n * cols, channels), jnp.float32)
    shapes = [pre(4), pre(2)] + ([] if of_state else [pre(2)])
    return pl.pallas_call(
        functools.partial(early_kernel, role, bases, of_state),
        out_shape=shapes,
        in_specs=[SCALARS] + [HELD] * 5,
        out_specs=[HELD] * len(shapes),
        scratch_shapes=[pltpu.VMEM((6, cols, 3 * channels), jnp.bfloat16)],
        compiler_params=pltpu.CompilerParams(vmem_limit_bytes=8 * MIB),
        cost_estimate=cost(cols, channels),
    )(flags, *source, wg, wc)


def late(role, flags, state, pre, wg, wc, bias, other=None, source=None, bases=(0, 0)):
    _, cols, channels = state[0].shape
    of_state = source is None
    operands = [*state, *([] if of_state else source), *pre, wg, wc, bias]
    if other is not None:
        operands.append(other)

    def kernel(scalars, *refs):
        held = refs[0:3]
        used = 3 if of_state else 6
        sums = refs[used : used + len(pre)]
        used += len(pre)
        late_kernel(
            role, bases, of_state, other is not None, scalars, held,
            held if of_state else refs[3:6], sums, refs[used : used + 3], refs[used + 3 :],
        )

    return pl.pallas_call(
        kernel,
        out_shape=jax.ShapeDtypeStruct((2, cols, channels), jnp.bfloat16),
        in_specs=[SCALARS] + [HELD] * len(operands),
        out_specs=HELD,
        scratch_shapes=[
            pltpu.VMEM((6, cols, 3 * channels), jnp.bfloat16),
            pltpu.VMEM((4, cols, 3 * channels), jnp.bfloat16),
            pltpu.VMEM((2 * cols, channels), jnp.float32),
        ],
        compiler_params=pltpu.CompilerParams(vmem_limit_bytes=12 * MIB),
        cost_estimate=cost(cols, channels),
    )(flags, *operands)


def swap(field, source, target):
    count = lax.axis_size("rows")

    def route(start):
        found = []
        for low in range(start, count - 1, 2):
            for here, there in ((low, low + 1), (low + 1, low)):
                found.append((source * count + here, target * count + there))
        return found

    names = ("layer", "rows")
    return lax.ppermute(field, names, route(0)), lax.ppermute(field, names, route(1))


def across(field, source):
    return lax.ppermute(field, "layer", [(source, 1 - source)])


def after(value, *others):
    return lax.optimization_barrier((value, *others))[0]


def shards(frames, initial_state, w_gates, w_cand, biases):
    layer = lax.axis_index("layer")
    strip = lax.axis_index("rows")
    flags = jnp.stack([layer, lax.rem(strip, 2)]).astype(jnp.int32)
    wg, wc = w_gates[0], w_cand[0]
    initial = initial_state[0]

    rows = frames.reshape((6,) + initial.shape[1:])
    halo0 = swap(initial, 0, 0)
    frame_halos = swap(rows[0:4], 1, 0)
    halo1 = swap(initial, 1, 1)
    last_halos = swap(rows[4:6], 1, 0)

    low, high = [], []
    state = (after(initial, *halo1), *halo0)
    pre = early(0, flags, state, wg, wc, of_state=True)
    low.append(late(0, flags, state, pre, wg, wc, biases, source=(rows, *frame_halos)))
    crossing = None
    hidden1 = initial
    for frame in range(3):
        below = across(low[frame], 0)
        below_halo = swap(low[frame], 0, 1)
        if frame < 2:
            halos, base = ((frame_halos, 2), (last_halos, 0))[frame]
            pre = early(
                0, flags, (after(rows, low[frame]), *halos), wg, wc, (2 * frame + 2, base)
            )
            halo0 = [across(h, 1) for h in below_halo]
            own = low[frame] if crossing is None else after(low[frame], *crossing)
            low.append(late(0, flags, (own, *halo0), pre, wg, wc, biases))
        if crossing is not None:
            halo1 = [across(h, 0) for h in crossing]
        if frame < 2:
            below = after(below, low[frame + 1])
        pre1 = early(1, flags, (below, *below_halo), wg, wc)
        hidden1 = late(
            1, flags, (hidden1, *halo1), pre1, wg, wc, biases, low[frame] if frame == 2 else None
        )
        high.append(hidden1)
        if frame < 2:
            crossing = swap(hidden1, 1, 0)
    out = jnp.zeros((3,) + initial.shape, initial.dtype)
    for frame in range(3):
        result = high[2] if frame == 2 else jnp.where(layer == 0, low[frame], high[frame])
        out = lax.dynamic_update_slice(out, result[None], (frame, 0, 0, 0))
    return out[None]


def solution(mesh):
    placed = (
        P(None, "rows", None, None),
        P("layer", "rows", None, None),
        P("layer", None, None, None, None),
        P("layer", None, None, None, None),
        P("layer", None),
    )
    return jax.shard_map(
        shards,
        mesh=mesh,
        in_specs=placed,
        out_specs=P("layer", None, "rows", None, None),
        check_vma=False,
    )
```

time: 113 us -> 142 us (1.26)
  local copies, waits for them, and re-layouts: 4.98 us -> 22 us
  starting transfers between devices: 48.7 us -> 60.7 us
  Pallas kernels: 22 us -> 28.8 us
  waiting for transfers between devices: 31.8 us -> 27.5 us
  other arithmetic: 4.58 us -> 1.13 us
    unnamed x12 -> x60, local copies, waits for them, and re-layouts: 1.68 us -> 19.3 us
    ppermute x5 -> x9, starting transfers between devices: 4.11 us -> 16.5 us  [swap(): lax.ppermute(field, names, route(0))]
    ppermute x8 -> x11, waiting for transfers between devices: 9.23 us -> 0.03 us  [across(): return lax.ppermute(field, 'layer', [(source, 1 - source)])]
    ppermute x5 -> x9, waiting for transfers between devices: 0.4 us -> 7.42 us  [swap(): lax.ppermute(field, names, route(0))]
    pallas_call x4 -> x12, Pallas kernels: 22 us -> 28.8 us  [the longest x6 16.4 us: late(): pl.pallas_call(kernel, out_shape=jax.ShapeDtypeStruct((2, cols, channels)...]
    ppermute x5 -> x9, starting transfers between devices: 31.3 us -> 27.4 us  [swap(): lax.ppermute(field, names, route(1))]
    ppermute x8 -> x11, starting transfers between devices: 13.2 us -> 16.8 us  [across(): return lax.ppermute(field, 'layer', [(source, 1 - source)])]
    concatenate x5 -> x0, other arithmetic: 2.28 us -> none  [the longest x1 1.29 us: shards(): later = lax.ppermute(jnp.concatenate([later_a, later_b]), 'layer', down)]
  transfers between devices with their start and end apart: 18 -> 29, of which waited for: 8 -> 5; matrix products, arithmetic and copies ran while one was open for 5% -> 2% of each run, Pallas kernels for 1% -> 13%
where the time goes in v2:
time: 142 us; the launch traced here: 141 us
  starting transfers between devices  60.7 us (43%)
  Pallas kernels  28.8 us (20%)
  waiting for transfers between devices  27.5 us (19%)
  local copies, waits for them, and re-layouts  22 us (15%)
    ppermute x9, starting transfers between devices, swap(): lax.ppermute(field, names, route(1))  27.4 us
    ppermute x9, waiting for transfers between devices, swap(): lax.ppermute(field, names, route(1))  20 us
    unnamed x60, local copies, waits for them, and re-layouts  19.3 us
    ppermute x11, starting transfers between devices, across(): return lax.ppermute(field, 'layer', [(source, 1 - source)])  16.8 us
    ppermute x9, starting transfers between devices, swap(): lax.ppermute(field, names, route(0))  16.5 us
    pallas_call x6, Pallas kernels, late(): pl.pallas_call(kernel, out_shape=jax.ShapeDtypeStruct((2, cols, channels)...  16.4 us
    pallas_call x6, Pallas kernels, early(): pl.pallas_call(functools.partial(early_kernel, role, bases, of_state), ou...  12.4 us
    ppermute x9, waiting for transfers between devices, swap(): lax.ppermute(field, names, route(0))  7.42 us
  transfers between devices with their start and end apart: 29, of which 5 were waited for; matrix products, arithmetic and copies ran while one was open for 2% of the time, Pallas kernels for 13%

profile of v2, /device:TPU:25, one launch (start us, length us, event | category | flops | bytes accessed | tf_op | source)
XLA Modules:
  0.0 140.7 jit_solution(3322845400795551114)
XLA Ops:
  0.0 3.5 %collective-permute-start = (bf16[2,256,256]{2,1,0:T(8,128)(2,1)}, bf16[2,256,256]{2,1,0:T(8,128)(2,1)S(1)}, u32[]{:S(2)}, u32[]{:S(2)}) collective-permute-start(bf16[2,256,256]{2,1,0:T(8,128)(2,1)} %bitcast.48), channel_id=1, source_target_pairs={{128,129},{129,128},{130,131},{131,130},{132,133},{133,132},{134,1... | collective-permute-start | bytes 786440 | tf_op jit(solution)/shard_map/ppermute | solution.py:168
  3.6 1.1 slice.12
  4.7 1.3 collective-permute-start.4
  6.1 7.5 %collective-permute-start.5 = (bf16[4,256,256]{2,1,0:T(8,128)(2,1)S(1)}, bf16[4,256,256]{2,1,0:T(8,128)(2,1)S(1)}, u32[]{:S(2)}, u32[]{:S(2)}) collective-permute-start(bf16[4,256,256]{2,1,0:T(8,128)(2,1)S(1)} %bitcast.56), channel_id=1, source_target_pairs={{129,2},{130,1},{131,4},{132,3},{133,6},{134,5},{135,8},{136,7},{1... | collective-permute-start | bytes 1572872 | tf_op jit(solution)/shard_map/ppermute | solution.py:168
  13.6 2.7 %collective-permute-start.1 = (bf16[2,256,256]{2,1,0:T(8,128)(2,1)}, bf16[2,256,256]{2,1,0:T(8,128)(2,1)S(1)}, u32[]{:S(2)}, u32[]{:S(2)}) collective-permute-start(bf16[2,256,256]{2,1,0:T(8,128)(2,1)} %bitcast.49), channel_id=1, source_target_pairs={{129,130},{130,129},{131,132},{132,131},{133,134},{134,133},{135,1... | collective-permute-start | bytes 786440 | tf_op jit(solution)/shard_map/ppermute | solution.py:168
  16.4 0.7 collective-permute-start.2
  17.1 0.7 collective-permute-start.3
  17.8 8.7 %collective-permute-done.1.refs_2_ = bf16[2,256,256]{2,1,0:T(8,128)(2,1)S(1)} collective-permute-done((bf16[2,256,256]{2,1,0:T(8,128)(2,1)}, bf16[2,256,256]{2,1,0:T(8,128)(2,1)S(1)}, u32[]{:S(2)}, u32[]{:S(2)}) %collective-permute-start.1) | collective-permute-done | bytes 262176 | tf_op jit(solution)/shard_map/ppermute | solution.py:168
  26.6 2.6 %copy-done = bf16[1,3,3,512,512]{4,3,2,1,0:T(8,128)(2,1)S(1)} copy-done((bf16[1,3,3,512,512]{4,3,2,1,0:T(8,128)(2,1)S(1)}, bf16[1,3,3,512,512]{4,3,2,1,0:T(8,128)(2,1)}, u32[]{:S(2)}) %copy-start) | copy-done | bytes 4718616
  29.2 1.7 %copy-done.3 = bf16[1,3,3,512,256]{4,3,2,1,0:T(8,128)(2,1)S(1)} copy-done((bf16[1,3,3,512,256]{4,3,2,1,0:T(8,128)(2,1)S(1)}, bf16[1,3,3,512,256]{4,3,2,1,0:T(8,128)(2,1)}, u32[]{:S(2)}) %copy-start.3) | copy-done | bytes 2359320
  30.9 0.9 copy-done.7
  31.8 0.5 shard_map.55
  32.4 0.8 copy-done.10
  33.2 0.8 copy-done.12
  34.6 1.0 copy-done.11
  35.6 1.0 copy-done.13
  36.7 0.9 copy-done.19
  37.6 0.9 copy-done.21
  38.6 0.5 shard_map.56.refs_0_
  39.1 1.4 %collective-permute-start.7 = (bf16[2,256,256]{2,1,0:T(8,128)(2,1)S(1)}, bf16[2,256,256]{2,1,0:T(8,128)(2,1)S(1)}, u32[]{:S(2)}, u32[]{:S(2)}) collective-permute-start(bf16[2,256,256]{2,1,0:T(8,128)(2,1)S(1)} %shard_map.56.refs_0_), channel_id=1, source_target_pairs={{0,129},{1,128},{2,131},{3,130},{4,133},{5,132},{6,135},{7,134},{8... | collective-permute-start | bytes 786440 | tf_op jit(solution)/shard_map/ppermute | solution.py:168
  40.6 1.3 collective-permute-start.9
  41.9 5.1 %collective-permute-done.7.first = bf16[2,256,256]{2,1,0:T(8,128)(2,1)S(1)} collective-permute-done((bf16[2,256,256]{2,1,0:T(8,128)(2,1)S(1)}, bf16[2,256,256]{2,1,0:T(8,128)(2,1)S(1)}, u32[]{:S(2)}, u32[]{:S(2)}) %collective-permute-start.7) | collective-permute-done | bytes 262176 | tf_op jit(solution)/shard_map/ppermute | solution.py:168
  47.0 3.7 %collective-permute-start.8 = (bf16[2,256,256]{2,1,0:T(8,128)(2,1)S(1)}, bf16[2,256,256]{2,1,0:T(8,128)(2,1)S(1)}, u32[]{:S(2)}, u32[]{:S(2)}) collective-permute-start(bf16[2,256,256]{2,1,0:T(8,128)(2,1)S(1)} %collective-permute-done.7.first), channel_id=1, source_target_pairs={{128,0},{129,1},{130,2},{131,3},{132,4},{133,5},{134,6},{135,7},{1... | collective-permute-start | bytes 786440 | tf_op jit(solution)/shard_map/ppermute | solution.py:172
  50.7 5.8 %collective-permute-done.9.second = bf16[2,256,256]{2,1,0:T(8,128)(2,1)S(1)} collective-permute-done((bf16[2,256,256]{2,1,0:T(8,128)(2,1)S(1)}, bf16[2,256,256]{2,1,0:T(8,128)(2,1)S(1)}, u32[]{:S(2)}, u32[]{:S(2)}) %collective-permute-start.9) | collective-permute-done | bytes 262176 | tf_op jit(solution)/shard_map/ppermute | solution.py:168
  56.5 1.3 collective-permute-start.10
  57.8 0.7 slice_bitcast_fusion
  58.5 1.3 collective-permute-start.20
  59.8 2.4 %collective-permute-start.21 = (bf16[2,256,256]{2,1,0:T(8,128)(2,1)}, bf16[2,256,256]{2,1,0:T(8,128)(2,1)}, u32[]{:S(2)}, u32[]{:S(2)}) collective-permute-start(bf16[2,256,256]{2,1,0:T(8,128)(2,1)} %slice_bitcast_fusion), channel_id=1, source_target_pairs={{129,2},{130,1},{131,4},{132,3},{133,6},{134,5},{135,8},{136,7},{1... | collective-permute-start | bytes 786440 | tf_op jit(solution)/shard_map/ppermute | solution.py:168
  62.2 1.3 collective-permute-start.6
  63.5 0.6 shard_map.57
  64.1 0.6 shard_map.58.refs_0_
  64.7 1.4 %collective-permute-start.16 = (bf16[2,256,256]{2,1,0:T(8,128)(2,1)S(1)}, bf16[2,256,256]{2,1,0:T(8,128)(2,1)}, u32[]{:S(2)}, u32[]{:S(2)}) collective-permute-start(bf16[2,256,256]{2,1,0:T(8,128)(2,1)S(1)} %shard_map.58.refs_0_), channel_id=1, source_target_pairs={{0,129},{1,128},{2,131},{3,130},{4,133},{5,132},{6,135},{7,134},{8... | collective-permute-start | bytes 786440 | tf_op jit(solution)/shard_map/ppermute | solution.py:168
  66.1 1.3 collective-permute-start.18
  67.4 3.4 %shard_map.59 = (f32[1024,256]{1,0:T(8,128)S(1)}, f32[512,256]{1,0:T(8,128)S(1)}, f32[512,256]{1,0:T(8,128)S(1)}) custom-call(s32[2]{0:T(128)S(1)} %pad_add_fusion.flags.scalars, bf16[2,256,256]{2,1,0:T(8,128)(2,1)S(1)} %collective-permute-done.6.own, bf16[2,256,256]{2,1,0:T(8,128)(2,1)S(1)} %collective-permute-done.7.first, ...), custom_call_target="tpu_custom_call" | custom-call | flops 2415919104 | bytes 1048576 | tf_op jit(solution)/shard_map/pallas_call | solution.py:114
  70.8 5.2 %shard_map.60.refs_0_ = bf16[2,256,256]{2,1,0:T(8,128)(2,1)} custom-call(s32[2]{0:T(128)S(1)} %pad_add_fusion.flags.scalars, bf16[2,256,256]{2,1,0:T(8,128)(2,1)S(1)} %bitcast.54, bf16[2,256,256]{2,1,0:T(8,128)(2,1)S(1)} %copy-done.15, bf16[2,256,256]{2,1,0:T(8,128)(2,1)S(1)} %copy-done.17, f32[1024,256]{1,0:T(8,128)S(1)} %get-tuple-element.36.refs_3_, ...), custom_call_target="tpu_custom_call" | custom-call | flops 2415919104 | bytes 1048576 | tf_op jit(solution)/shard_map/pallas_call | solution.py:142
  76.0 2.0 %collective-permute-start.11 = (bf16[2,256,256]{2,1,0:T(8,128)(2,1)}, bf16[2,256,256]{2,1,0:T(8,128)(2,1)}, u32[]{:S(2)}, u32[]{:S(2)}) collective-permute-start(bf16[2,256,256]{2,1,0:T(8,128)(2,1)} %shard_map.60.refs_0_), channel_id=1, source_target_pairs={{128,1},{129,0},{130,3},{131,2},{132,5},{133,4},{134,7},{135,6},{1... | collective-permute-start | bytes 786440 | tf_op jit(solution)/shard_map/ppermute | solution.py:168
  78.0 0.7 copy-done.23
  78.7 5.4 %collective-permute-start.13 = (bf16[2,256,256]{2,1,0:T(8,128)(2,1)}, bf16[2,256,256]{2,1,0:T(8,128)(2,1)}, u32[]{:S(2)}, u32[]{:S(2)}) collective-permute-start(bf16[2,256,256]{2,1,0:T(8,128)(2,1)} %shard_map.60.refs_0_), channel_id=1, source_target_pairs={{129,2},{130,1},{131,4},{132,3},{133,6},{134,5},{135,8},{136,7},{1... | collective-permute-start | bytes 786440 | tf_op jit(solution)/shard_map/ppermute | solution.py:168
  84.0 1.3 collective-permute-start.17
  85.3 1.3 collective-permute-start.19
  86.7 1.3 collective-permute-start.15
  88.0 2.3 %copy-done.1 = bf16[1,3,3,512,512]{4,3,2,1,0:T(8,128)(2,1)S(1)} copy-done((bf16[1,3,3,512,512]{4,3,2,1,0:T(8,128)(2,1)S(1)}, bf16[1,3,3,512,512]{4,3,2,1,0:T(8,128)(2,1)}, u32[]{:S(2)}) %copy-start.1) | copy-done | bytes 4718616
  90.3 1.1 copy-done.6
  91.4 0.9 copy-done.24
  92.4 1.1 shard_map.61
  93.5 1.4 %collective-permute-start.12 = (bf16[2,256,256]{2,1,0:T(8,128)(2,1)}, bf16[2,256,256]{2,1,0:T(8,128)(2,1)S(1)}, u32[]{:S(2)}, u32[]{:S(2)}) collective-permute-start(bf16[2,256,256]{2,1,0:T(8,128)(2,1)} %collective-permute-done.11), channel_id=1, source_target_pairs={{0,128},{1,129},{2,130},{3,131},{4,132},{5,133},{6,134},{7,135},{8... | collective-permute-start | bytes 786440 | tf_op jit(solution)/shard_map/ppermute | solution.py:172
  95.0 1.3 collective-permute-start.14
  96.3 2.3 %copy-done.2 = bf16[1,3,3,512,512]{4,3,2,1,0:T(8,128)(2,1)S(1)} copy-done((bf16[1,3,3,512,512]{4,3,2,1,0:T(8,128)(2,1)S(1)}, bf16[1,3,3,512,512]{4,3,2,1,0:T(8,128)(2,1)}, u32[]{:S(2)}) %copy-start.2) | copy-done | bytes 4718616
  98.6 0.5 shard_map.62.refs_9_
  99.7 3.6 %shard_map.63 = (f32[1024,256]{1,0:T(8,128)S(1)}, f32[512,256]{1,0:T(8,128)S(1)}, f32[512,256]{1,0:T(8,128)S(1)}) custom-call(s32[2]{0:T(128)S(1)} %pad_add_fusion.flags.scalars, bf16[2,256,256]{2,1,0:T(8,128)(2,1)S(1)} %collective-permute-done.15.own, bf16[2,256,256]{2,1,0:T(8,128)(2,1)} %collective-permute-done.16.first, ...), custom_call_target="tpu_custom_call" | custom-call | flops 2415919104 | bytes 1048576 | tf_op jit(solution)/shard_map/pallas_call | solution.py:114
  103.3 5.1 %shard_map.64.refs_0_ = bf16[2,256,256]{2,1,0:T(8,128)(2,1)S(1)} custom-call(s32[2]{0:T(128)S(1)} %pad_add_fusion.flags.scalars, bf16[2,256,256]{2,1,0:T(8,128)(2,1)} %shard_map.60.refs_0_, bf16[2,256,256]{2,1,0:T(8,128)(2,1)S(1)} %collective-permute-done.12.refs_1_, bf16[2,256,256]{2,1,0:T(8,128)(2,1)S(1)} %collective-permute-done.14.refs_2_, ...), custom_call_target="tpu_custom_call" | custom-call | flops 2415919104 | bytes 1048576 | tf_op jit(solution)/shard_map/pallas_call | solution.py:142
  108.5 3.6 %collective-permute-start.22 = (bf16[2,256,256]{2,1,0:T(8,128)(2,1)S(1)}, bf16[2,256,256]{2,1,0:T(8,128)(2,1)S(1)}, u32[]{:S(2)}, u32[]{:S(2)}) collective-permute-start(bf16[2,256,256]{2,1,0:T(8,128)(2,1)S(1)} %shard_map.64.refs_0_), channel_id=1, source_target_pairs={{128,1},{129,0},{130,3},{131,2},{132,5},{133,4},{134,7},{135,6},{1... | collective-permute-start | bytes 786440 | tf_op jit(solution)/shard_map/ppermute | solution.py:168
  112.0 4.8 %collective-permute-start.24 = (bf16[2,256,256]{2,1,0:T(8,128)(2,1)S(1)}, bf16[2,256,256]{2,1,0:T(8,128)(2,1)S(1)}, u32[]{:S(2)}, u32[]{:S(2)}) collective-permute-start(bf16[2,256,256]{2,1,0:T(8,128)(2,1)S(1)} %shard_map.64.refs_0_), channel_id=1, source_target_pairs={{129,2},{130,1},{131,4},{132,3},{133,6},{134,5},{135,8},{136,7},{1... | collective-permute-start | bytes 786440 | tf_op jit(solution)/shard_map/ppermute | solution.py:168
  116.9 1.0 select_bitcast_fusion
  117.9 1.3 collective-permute-start.26
  119.2 1.3 collective-permute-start.27
  120.5 1.3 collective-permute-start.28
  121.8 1.3 collective-permute-start.23
  123.1 1.3 collective-permute-start.25
  124.5 2.3 %collective-permute-done.27.first = bf16[2,256,256]{2,1,0:T(8,128)(2,1)S(1)} collective-permute-done((bf16[2,256,256]{2,1,0:T(8,128)(2,1)S(1)}, bf16[2,256,256]{2,1,0:T(8,128)(2,1)S(1)}, u32[]{:S(2)}, u32[]{:S(2)}) %collective-permute-start.27) | collective-permute-done | bytes 262176 | tf_op jit(solution)/shard_map/ppermute | solution.py:168
  126.9 5.5 %collective-permute-done.28.second = bf16[2,256,256]{2,1,0:T(8,128)(2,1)S(1)} collective-permute-done((bf16[2,256,256]{2,1,0:T(8,128)(2,1)S(1)}, bf16[2,256,256]{2,1,0:T(8,128)(2,1)S(1)}, u32[]{:S(2)}, u32[]{:S(2)}) %collective-permute-start.28) | collective-permute-done | bytes 262176 | tf_op jit(solution)/shard_map/ppermute | solution.py:168
  132.4 3.1 %shard_map.65 = (f32[1024,256]{1,0:T(8,128)S(1)}, f32[512,256]{1,0:T(8,128)S(1)}, f32[512,256]{1,0:T(8,128)S(1)}) custom-call(s32[2]{0:T(128)S(1)} %pad_add_fusion.flags.scalars, bf16[2,256,256]{2,1,0:T(8,128)(2,1)S(1)} %collective-permute-done.26.own, bf16[2,256,256]{2,1,0:T(8,128)(2,1)S(1)} %collective-permute-done.27.first, ...), custom_call_target="tpu_custom_call" | custom-call | flops 2415919104 | bytes 1048576 | tf_op jit(solution)/shard_map/pallas_call | solution.py:114
  135.5 4.5 %shard_map.66 = bf16[2,256,256]{2,1,0:T(8,128)(2,1)S(1)} custom-call(s32[2]{0:T(128)S(1)} %pad_add_fusion.flags.scalars, bf16[2,256,256]{2,1,0:T(8,128)(2,1)S(1)} %shard_map.64.refs_0_, bf16[2,256,256]{2,1,0:T(8,128)(2,1)S(1)} %collective-permute-done.23.refs_1_, bf16[2,256,256]{2,1,0:T(8,128)(2,1)S(1)} %collective-permute-done.25.refs_2_, ...), custom_call_target="tpu_custom_call" | custom-call | flops 2415919104 | bytes 1048576 | tf_op jit(solution)/shard_map/pallas_call | solution.py:142
  140.0 0.7 bitcast_dynamic-update-slice_fusion
  (75 shorter events, 1.4 us)
Async XLA Ops:
  0.0 17.0 %collective-permute-start = (bf16[2,256,256]{2,1,0:T(8,128)(2,1)}, bf16[2,256,256]{2,1,0:T(8,128)(2,1)S(1)}, u32[]{:S(2)}, u32[]{:S(2)}) collective-permute-start(bf16[2,256,256]{2,1,0:T(8,128)(2,1)} %bitcast.48), channel_id=1, source_target_pairs={{128,129},{129,128},{130,131},{131,130},{132,133},{133,132},{134,1... | collective-permute-start | bytes 786440 | tf_op jit(solution)/shard_map/ppermute | solution.py:168
  3.5 30.5 %slice-start = ((s8[4718592]{0:T(1024)(128)(4,1)}), s8[524288]{0:T(1024)(128)(4,1)S(1)}, s32[]{:S(2)}) async-start(s8[4718592]{0:T(1024)(128)(4,1)} %bitcast.18), calls=%async_computation | async-start | bytes 1048576
  3.6 30.5 %copy-start.8 = (bf16[1,2,256,256]{3,2,1,0:T(8,128)(2,1)S(1)}, bf16[1,2,256,256]{3,2,1,0:T(8,128)(2,1)}, u32[]{:S(2)}) copy-start(bf16[1,2,256,256]{3,2,1,0:T(8,128)(2,1)} %param.6) | copy-start | bytes 786436
  4.7 29.3 %copy-start.22 = (f32[1,768]{1,0:T(1,128)S(1)}, f32[1,768]{1,0:T(1,128)}, u32[]{:S(2)}) copy-start(f32[1,768]{1,0:T(1,128)} %refs_8_.9) | copy-start | bytes 9220
  4.7 27.7 %collective-permute-start.4 = (bf16[4,256,256]{2,1,0:T(8,128)(2,1)S(1)}, bf16[4,256,256]{2,1,0:T(8,128)(2,1)S(1)}, u32[]{:S(2)}, u32[]{:S(2)}) collective-permute-start(bf16[4,256,256]{2,1,0:T(8,128)(2,1)S(1)} %bitcast.55), channel_id=1, source_target_pairs={{128,1},{129,0},{130,3},{131,2},{132,5},{133,4},{134,7},{135,6},{1... | collective-permute-start | bytes 1572872 | tf_op jit(solution)/shard_map/ppermute | solution.py:168
  6.1 27.1 %collective-permute-start.5 = (bf16[4,256,256]{2,1,0:T(8,128)(2,1)S(1)}, bf16[4,256,256]{2,1,0:T(8,128)(2,1)S(1)}, u32[]{:S(2)}, u32[]{:S(2)}) collective-permute-start(bf16[4,256,256]{2,1,0:T(8,128)(2,1)S(1)} %bitcast.56), channel_id=1, source_target_pairs={{129,2},{130,1},{131,4},{132,3},{133,6},{134,5},{135,8},{136,7},{1... | collective-permute-start | bytes 1572872 | tf_op jit(solution)/shard_map/ppermute | solution.py:168
  13.6 12.9 %collective-permute-start.1 = (bf16[2,256,256]{2,1,0:T(8,128)(2,1)}, bf16[2,256,256]{2,1,0:T(8,128)(2,1)S(1)}, u32[]{:S(2)}, u32[]{:S(2)}) collective-permute-start(bf16[2,256,256]{2,1,0:T(8,128)(2,1)} %bitcast.49), channel_id=1, source_target_pairs={{129,130},{130,129},{131,132},{132,131},{133,134},{134,133},{135,1... | collective-permute-start | bytes 786440 | tf_op jit(solution)/shard_map/ppermute | solution.py:168
  16.4 10.2 %collective-permute-start.2 = (bf16[2,256,256]{2,1,0:T(8,128)(2,1)}, bf16[2,256,256]{2,1,0:T(8,128)(2,1)S(1)}, u32[]{:S(2)}, u32[]{:S(2)}) collective-permute-start(bf16[2,256,256]{2,1,0:T(8,128)(2,1)} %bitcast.50), channel_id=1, source_target_pairs={{0,1},{1,0},{2,3},{3,2},{4,5},{5,4},{6,7},{7,6},{8,9},{9,8},{10,11... | collective-permute-start | bytes 786440 | tf_op jit(solution)/shard_map/ppermute | solution.py:168
  17.0 17.0 %copy-start.14 = (bf16[2,256,256]{2,1,0:T(8,128)(2,1)}, bf16[2,256,256]{2,1,0:T(8,128)(2,1)S(1)}, u32[]{:S(2)}) copy-start(bf16[2,256,256]{2,1,0:T(8,128)(2,1)S(1)} %collective-permute-done.refs_1_) | copy-start | bytes 786436
  17.1 9.5 %collective-permute-start.3 = (bf16[2,256,256]{2,1,0:T(8,128)(2,1)}, bf16[2,256,256]{2,1,0:T(8,128)(2,1)S(1)}, u32[]{:S(2)}, u32[]{:S(2)}) collective-permute-start(bf16[2,256,256]{2,1,0:T(8,128)(2,1)} %bitcast.51), channel_id=1, source_target_pairs={{1,2},{2,1},{3,4},{4,3},{5,6},{6,5},{7,8},{8,7},{9,10},{10,9},{11,... | collective-permute-start | bytes 786440 | tf_op jit(solution)/shard_map/ppermute | solution.py:168
  26.6 7.4 %copy-start.16 = (bf16[2,256,256]{2,1,0:T(8,128)(2,1)}, bf16[2,256,256]{2,1,0:T(8,128)(2,1)S(1)}, u32[]{:S(2)}) copy-start(bf16[2,256,256]{2,1,0:T(8,128)(2,1)S(1)} %collective-permute-done.1.refs_2_) | copy-start | bytes 786436
  26.6 7.4 %copy-start.18 = (bf16[2,256,256]{2,1,0:T(8,128)(2,1)}, bf16[2,256,256]{2,1,0:T(8,128)(2,1)S(1)}, u32[]{:S(2)}) copy-start(bf16[2,256,256]{2,1,0:T(8,128)(2,1)S(1)} %collective-permute-done.2.first.refs_1_) | copy-start | bytes 786436
  26.6 7.4 %copy-start.20 = (bf16[2,256,256]{2,1,0:T(8,128)(2,1)}, bf16[2,256,256]{2,1,0:T(8,128)(2,1)S(1)}, u32[]{:S(2)}) copy-start(bf16[2,256,256]{2,1,0:T(8,128)(2,1)S(1)} %collective-permute-done.3.second.refs_2_) | copy-start | bytes 786436
  26.6 2.6 %copy-start = (bf16[1,3,3,512,512]{4,3,2,1,0:T(8,128)(2,1)S(1)}, bf16[1,3,3,512,512]{4,3,2,1,0:T(8,128)(2,1)}, u32[]{:S(2)}) copy-start(bf16[1,3,3,512,512]{4,3,2,1,0:T(8,128)(2,1)} %param.7) | copy-start | bytes 14155780
  29.2 1.7 %copy-start.3 = (bf16[1,3,3,512,256]{4,3,2,1,0:T(8,128)(2,1)S(1)}, bf16[1,3,3,512,256]{4,3,2,1,0:T(8,128)(2,1)}, u32[]{:S(2)}) copy-start(bf16[1,3,3,512,256]{4,3,2,1,0:T(8,128)(2,1)} %param.8) | copy-start | bytes 7077892
  30.9 0.9 copy-start.7
  31.8 2.5 %slice-start.1 = ((s8[4718592]{0:T(1024)(128)(4,1)}), s8[4194304]{0:T(1024)(128)(4,1)S(1)}, s32[]{:S(2)}) async-start(s8[4718592]{0:T(1024)(128)(4,1)} %bitcast.18), calls=%async_computation.1 | async-start | bytes 8388608
  31.8 2.8 %copy-start.5 = (bf16[3,2,256,256]{3,2,1,0:T(8,128)(2,1)S(1)}, bf16[3,2,256,256]{3,2,1,0:T(8,128)(2,1)}, u32[]{:S(2)}) copy-start(bf16[3,2,256,256]{3,2,1,0:T(8,128)(2,1)} %param.5) | copy-start | bytes 2359300
  32.4 0.8 copy-start.10
  33.2 0.8 copy-start.12
  34.6 1.0 copy-start.11
  35.6 1.0 copy-start.13
  36.7 0.9 copy-start.19
  37.6 0.9 copy-start.21
  38.6 24.9 %copy-start.4 = (bf16[1,3,3,512,256]{4,3,2,1,0:T(8,128)(2,1)S(1)}, bf16[1,3,3,512,256]{4,3,2,1,0:T(8,128)(2,1)}, u32[]{:S(2)}) copy-start(bf16[1,3,3,512,256]{4,3,2,1,0:T(8,128)(2,1)} %param.8) | copy-start | bytes 7077892
  39.1 7.8 %collective-permute-start.7 = (bf16[2,256,256]{2,1,0:T(8,128)(2,1)S(1)}, bf16[2,256,256]{2,1,0:T(8,128)(2,1)S(1)}, u32[]{:S(2)}, u32[]{:S(2)}) collective-permute-start(bf16[2,256,256]{2,1,0:T(8,128)(2,1)S(1)} %shard_map.56.refs_0_), channel_id=1, source_target_pairs={{0,129},{1,128},{2,131},{3,130},{4,133},{5,132},{6,135},{7,134},{8... | collective-permute-start | bytes 786440 | tf_op jit(solution)/shard_map/ppermute | solution.py:168
  40.6 15.9 %collective-permute-start.9 = (bf16[2,256,256]{2,1,0:T(8,128)(2,1)S(1)}, bf16[2,256,256]{2,1,0:T(8,128)(2,1)S(1)}, u32[]{:S(2)}, u32[]{:S(2)}) collective-permute-start(bf16[2,256,256]{2,1,0:T(8,128)(2,1)S(1)} %shard_map.56.refs_0_), channel_id=1, source_target_pairs={{1,130},{2,129},{3,132},{4,131},{5,134},{6,133},{7,136},{8,135},{9... | collective-permute-start | bytes 786440 | tf_op jit(solution)/shard_map/ppermute | solution.py:168
  47.0 17.1 %collective-permute-start.8 = (bf16[2,256,256]{2,1,0:T(8,128)(2,1)S(1)}, bf16[2,256,256]{2,1,0:T(8,128)(2,1)S(1)}, u32[]{:S(2)}, u32[]{:S(2)}) collective-permute-start(bf16[2,256,256]{2,1,0:T(8,128)(2,1)S(1)} %collective-permute-done.7.first), channel_id=1, source_target_pairs={{128,0},{129,1},{130,2},{131,3},{132,4},{133,5},{134,6},{135,7},{1... | collective-permute-start | bytes 786440 | tf_op jit(solution)/shard_map/ppermute | solution.py:172
  56.5 7.6 %collective-permute-start.10 = (bf16[2,256,256]{2,1,0:T(8,128)(2,1)S(1)}, bf16[2,256,256]{2,1,0:T(8,128)(2,1)S(1)}, u32[]{:S(2)}, u32[]{:S(2)}) collective-permute-start(bf16[2,256,256]{2,1,0:T(8,128)(2,1)S(1)} %collective-permute-done.9.second), channel_id=1, source_target_pairs={{128,0},{129,1},{130,2},{131,3},{132,4},{133,5},{134,6},{135,7},{1... | collective-permute-start | bytes 786440 | tf_op jit(solution)/shard_map/ppermute | solution.py:172
  58.5 19.5 %collective-permute-start.20 = (bf16[2,256,256]{2,1,0:T(8,128)(2,1)}, bf16[2,256,256]{2,1,0:T(8,128)(2,1)S(1)}, u32[]{:S(2)}, u32[]{:S(2)}) collective-permute-start(bf16[2,256,256]{2,1,0:T(8,128)(2,1)} %slice_bitcast_fusion), channel_id=1, source_target_pairs={{128,1},{129,0},{130,3},{131,2},{132,5},{133,4},{134,7},{135,6},{1... | collective-permute-start | bytes 786440 | tf_op jit(solution)/shard_map/ppermute | solution.py:168
  59.8 26.9 %collective-permute-start.21 = (bf16[2,256,256]{2,1,0:T(8,128)(2,1)}, bf16[2,256,256]{2,1,0:T(8,128)(2,1)}, u32[]{:S(2)}, u32[]{:S(2)}) collective-permute-start(bf16[2,256,256]{2,1,0:T(8,128)(2,1)} %slice_bitcast_fusion), channel_id=1, source_target_pairs={{129,2},{130,1},{131,4},{132,3},{133,6},{134,5},{135,8},{136,7},{1... | collective-permute-start | bytes 786440 | tf_op jit(solution)/shard_map/ppermute | solution.py:168
  62.2 5.2 %collective-permute-start.6 = (bf16[2,256,256]{2,1,0:T(8,128)(2,1)S(1)}, bf16[2,256,256]{2,1,0:T(8,128)(2,1)S(1)}, u32[]{:S(2)}, u32[]{:S(2)}) collective-permute-start(bf16[2,256,256]{2,1,0:T(8,128)(2,1)S(1)} %shard_map.56.refs_0_), channel_id=1, source_target_pairs={{0,128},{1,129},{2,130},{3,131},{4,132},{5,133},{6,134},{7,135},{8... | collective-permute-start | bytes 786440 | tf_op jit(solution)/shard_map/ppermute | solution.py:172
  64.6 6.1 %copy-start.9 = (bf16[1,2,256,256]{3,2,1,0:T(8,128)(2,1)S(1)}, bf16[1,2,256,256]{3,2,1,0:T(8,128)(2,1)}, u32[]{:S(2)}) copy-start(bf16[1,2,256,256]{3,2,1,0:T(8,128)(2,1)} %param.6) | copy-start | bytes 786436
  64.7 6.1 %copy-start.15 = (bf16[2,256,256]{2,1,0:T(8,128)(2,1)S(1)}, bf16[2,256,256]{2,1,0:T(8,128)(2,1)}, u32[]{:S(2)}) copy-start(bf16[2,256,256]{2,1,0:T(8,128)(2,1)} %copy-done.14) | copy-start | bytes 786436
  64.7 6.1 %copy-start.17 = (bf16[2,256,256]{2,1,0:T(8,128)(2,1)S(1)}, bf16[2,256,256]{2,1,0:T(8,128)(2,1)}, u32[]{:S(2)}) copy-start(bf16[2,256,256]{2,1,0:T(8,128)(2,1)} %copy-done.16) | copy-start | bytes 786436
  64.7 19.3 %collective-permute-start.16 = (bf16[2,256,256]{2,1,0:T(8,128)(2,1)S(1)}, bf16[2,256,256]{2,1,0:T(8,128)(2,1)}, u32[]{:S(2)}, u32[]{:S(2)}) collective-permute-start(bf16[2,256,256]{2,1,0:T(8,128)(2,1)S(1)} %shard_map.58.refs_0_), channel_id=1, source_target_pairs={{0,129},{1,128},{2,131},{3,130},{4,133},{5,132},{6,135},{7,134},{8... | collective-permute-start | bytes 786440 | tf_op jit(solution)/shard_map/ppermute | solution.py:168
  66.1 19.2 %collective-permute-start.18 = (bf16[2,256,256]{2,1,0:T(8,128)(2,1)S(1)}, bf16[2,256,256]{2,1,0:T(8,128)(2,1)}, u32[]{:S(2)}, u32[]{:S(2)}) collective-permute-start(bf16[2,256,256]{2,1,0:T(8,128)(2,1)S(1)} %shard_map.58.refs_0_), channel_id=1, source_target_pairs={{1,130},{2,129},{3,132},{4,131},{5,134},{6,133},{7,136},{8,135},{9... | collective-permute-start | bytes 786440 | tf_op jit(solution)/shard_map/ppermute | solution.py:168
  76.0 17.5 %collective-permute-start.11 = (bf16[2,256,256]{2,1,0:T(8,128)(2,1)}, bf16[2,256,256]{2,1,0:T(8,128)(2,1)}, u32[]{:S(2)}, u32[]{:S(2)}) collective-permute-start(bf16[2,256,256]{2,1,0:T(8,128)(2,1)} %shard_map.60.refs_0_), channel_id=1, source_target_pairs={{128,1},{129,0},{130,3},{131,2},{132,5},{133,4},{134,7},{135,6},{1... | collective-permute-start | bytes 786440 | tf_op jit(solution)/shard_map/ppermute | solution.py:168
  78.0 0.7 copy-start.23
  78.7 14.9 %collective-permute-start.13 = (bf16[2,256,256]{2,1,0:T(8,128)(2,1)}, bf16[2,256,256]{2,1,0:T(8,128)(2,1)}, u32[]{:S(2)}, u32[]{:S(2)}) collective-permute-start(bf16[2,256,256]{2,1,0:T(8,128)(2,1)} %shard_map.60.refs_0_), channel_id=1, source_target_pairs={{129,2},{130,1},{131,4},{132,3},{133,6},{134,5},{135,8},{136,7},{1... | collective-permute-start | bytes 786440 | tf_op jit(solution)/shard_map/ppermute | solution.py:168
  84.0 12.2 %collective-permute-start.17 = (bf16[2,256,256]{2,1,0:T(8,128)(2,1)}, bf16[2,256,256]{2,1,0:T(8,128)(2,1)S(1)}, u32[]{:S(2)}, u32[]{:S(2)}) collective-permute-start(bf16[2,256,256]{2,1,0:T(8,128)(2,1)} %collective-permute-done.16.first), channel_id=1, source_target_pairs={{128,0},{129,1},{130,2},{131,3},{132,4},{133,5},{134,6},{135,7},{1... | collective-permute-start | bytes 786440 | tf_op jit(solution)/shard_map/ppermute | solution.py:172
  85.3 10.9 %collective-permute-start.19 = (bf16[2,256,256]{2,1,0:T(8,128)(2,1)}, bf16[2,256,256]{2,1,0:T(8,128)(2,1)S(1)}, u32[]{:S(2)}, u32[]{:S(2)}) collective-permute-start(bf16[2,256,256]{2,1,0:T(8,128)(2,1)} %collective-permute-done.18.second), channel_id=1, source_target_pairs={{128,0},{129,1},{130,2},{131,3},{132,4},{133,5},{134,6},{135,7},{1... | collective-permute-start | bytes 786440 | tf_op jit(solution)/shard_map/ppermute | solution.py:172
  86.7 12.5 %collective-permute-start.15 = (bf16[2,256,256]{2,1,0:T(8,128)(2,1)S(1)}, bf16[2,256,256]{2,1,0:T(8,128)(2,1)S(1)}, u32[]{:S(2)}, u32[]{:S(2)}) collective-permute-start(bf16[2,256,256]{2,1,0:T(8,128)(2,1)S(1)} %shard_map.58.refs_0_), channel_id=1, source_target_pairs={{0,128},{1,129},{2,130},{3,131},{4,132},{5,133},{6,134},{7,135},{8... | collective-permute-start | bytes 786440 | tf_op jit(solution)/shard_map/ppermute | solution.py:172
  88.0 2.3 %copy-start.1 = (bf16[1,3,3,512,512]{4,3,2,1,0:T(8,128)(2,1)S(1)}, bf16[1,3,3,512,512]{4,3,2,1,0:T(8,128)(2,1)}, u32[]{:S(2)}) copy-start(bf16[1,3,3,512,512]{4,3,2,1,0:T(8,128)(2,1)} %param.7) | copy-start | bytes 14155780
  90.3 1.1 copy-start.6
  91.4 0.9 copy-start.24
  92.4 6.8 %slice-start.2 = ((s8[4718592]{0:T(1024)(128)(4,1)}), s8[4194304]{0:T(1024)(128)(4,1)S(1)}, s32[]{:S(2)}) async-start(s8[4718592]{0:T(1024)(128)(4,1)} %bitcast.27), calls=%async_computation.2 | async-start | bytes 8388608
  93.5 9.8 %collective-permute-start.12 = (bf16[2,256,256]{2,1,0:T(8,128)(2,1)}, bf16[2,256,256]{2,1,0:T(8,128)(2,1)S(1)}, u32[]{:S(2)}, u32[]{:S(2)}) collective-permute-start(bf16[2,256,256]{2,1,0:T(8,128)(2,1)} %collective-permute-done.11), channel_id=1, source_target_pairs={{0,128},{1,129},{2,130},{3,131},{4,132},{5,133},{6,134},{7,135},{8... | collective-permute-start | bytes 786440 | tf_op jit(solution)/shard_map/ppermute | solution.py:172
  95.0 8.4 %collective-permute-start.14 = (bf16[2,256,256]{2,1,0:T(8,128)(2,1)}, bf16[2,256,256]{2,1,0:T(8,128)(2,1)S(1)}, u32[]{:S(2)}, u32[]{:S(2)}) collective-permute-start(bf16[2,256,256]{2,1,0:T(8,128)(2,1)} %collective-permute-done.13), channel_id=1, source_target_pairs={{0,128},{1,129},{2,130},{3,131},{4,132},{5,133},{6,134},{7,135},{8... | collective-permute-start | bytes 786440 | tf_op jit(solution)/shard_map/ppermute | solution.py:172
  96.3 2.3 %copy-start.2 = (bf16[1,3,3,512,512]{4,3,2,1,0:T(8,128)(2,1)S(1)}, bf16[1,3,3,512,512]{4,3,2,1,0:T(8,128)(2,1)}, u32[]{:S(2)}) copy-start(bf16[1,3,3,512,512]{4,3,2,1,0:T(8,128)(2,1)} %param.7) | copy-start | bytes 14155780
  98.6 1.0 slice-start.3
  108.5 13.4 %collective-permute-start.22 = (bf16[2,256,256]{2,1,0:T(8,128)(2,1)S(1)}, bf16[2,256,256]{2,1,0:T(8,128)(2,1)S(1)}, u32[]{:S(2)}, u32[]{:S(2)}) collective-permute-start(bf16[2,256,256]{2,1,0:T(8,128)(2,1)S(1)} %shard_map.64.refs_0_), channel_id=1, source_target_pairs={{128,1},{129,0},{130,3},{131,2},{132,5},{133,4},{134,7},{135,6},{1... | collective-permute-start | bytes 786440 | tf_op jit(solution)/shard_map/ppermute | solution.py:168
  112.0 11.1 %collective-permute-start.24 = (bf16[2,256,256]{2,1,0:T(8,128)(2,1)S(1)}, bf16[2,256,256]{2,1,0:T(8,128)(2,1)S(1)}, u32[]{:S(2)}, u32[]{:S(2)}) collective-permute-start(bf16[2,256,256]{2,1,0:T(8,128)(2,1)S(1)} %shard_map.64.refs_0_), channel_id=1, source_target_pairs={{129,2},{130,1},{131,4},{132,3},{133,6},{134,5},{135,8},{136,7},{1... | collective-permute-start | bytes 786440 | tf_op jit(solution)/shard_map/ppermute | solution.py:168
  117.9 6.7 %collective-permute-start.26 = (bf16[2,256,256]{2,1,0:T(8,128)(2,1)S(1)}, bf16[2,256,256]{2,1,0:T(8,128)(2,1)S(1)}, u32[]{:S(2)}, u32[]{:S(2)}) collective-permute-start(bf16[2,256,256]{2,1,0:T(8,128)(2,1)S(1)} %shard_map.62.refs_9_), channel_id=1, source_target_pairs={{0,128},{1,129},{2,130},{3,131},{4,132},{5,133},{6,134},{7,135},{8... | collective-permute-start | bytes 786440 | tf_op jit(solution)/shard_map/ppermute | solution.py:172
  119.2 7.7 %collective-permute-start.27 = (bf16[2,256,256]{2,1,0:T(8,128)(2,1)S(1)}, bf16[2,256,256]{2,1,0:T(8,128)(2,1)S(1)}, u32[]{:S(2)}, u32[]{:S(2)}) collective-permute-start(bf16[2,256,256]{2,1,0:T(8,128)(2,1)S(1)} %shard_map.62.refs_9_), channel_id=1, source_target_pairs={{0,129},{1,128},{2,131},{3,130},{4,133},{5,132},{6,135},{7,134},{8... | collective-permute-start | bytes 786440 | tf_op jit(solution)/shard_map/ppermute | solution.py:168
  120.5 11.9 %collective-permute-start.28 = (bf16[2,256,256]{2,1,0:T(8,128)(2,1)S(1)}, bf16[2,256,256]{2,1,0:T(8,128)(2,1)S(1)}, u32[]{:S(2)}, u32[]{:S(2)}) collective-permute-start(bf16[2,256,256]{2,1,0:T(8,128)(2,1)S(1)} %shard_map.62.refs_9_), channel_id=1, source_target_pairs={{1,130},{2,129},{3,132},{4,131},{5,134},{6,133},{7,136},{8,135},{9... | collective-permute-start | bytes 786440 | tf_op jit(solution)/shard_map/ppermute | solution.py:168
  121.8 13.7 %collective-permute-start.23 = (bf16[2,256,256]{2,1,0:T(8,128)(2,1)S(1)}, bf16[2,256,256]{2,1,0:T(8,128)(2,1)S(1)}, u32[]{:S(2)}, u32[]{:S(2)}) collective-permute-start(bf16[2,256,256]{2,1,0:T(8,128)(2,1)S(1)} %collective-permute-done.22), channel_id=1, source_target_pairs={{0,128},{1,129},{2,130},{3,131},{4,132},{5,133},{6,134},{7,135},{8... | collective-permute-start | bytes 786440 | tf_op jit(solution)/shard_map/ppermute | solution.py:172
  123.1 12.4 %collective-permute-start.25 = (bf16[2,256,256]{2,1,0:T(8,128)(2,1)S(1)}, bf16[2,256,256]{2,1,0:T(8,128)(2,1)S(1)}, u32[]{:S(2)}, u32[]{:S(2)}) collective-permute-start(bf16[2,256,256]{2,1,0:T(8,128)(2,1)S(1)} %collective-permute-done.24), channel_id=1, source_target_pairs={{0,128},{1,129},{2,130},{3,131},{4,132},{5,133},{6,134},{7,135},{8... | collective-permute-start | bytes 786440 | tf_op jit(solution)/shard_map/ppermute | solution.py:172
  124.5 15.5 %copy-start.25 = (bf16[1,3,2,256,256]{4,3,2,1,0:T(8,128)(2,1)}, bf16[1,3,2,256,256]{4,3,2,1,0:T(8,128)(2,1)S(1)}, u32[]{:S(2)}) copy-start(bf16[1,3,2,256,256]{4,3,2,1,0:T(8,128)(2,1)S(1)} %bitcast_dynamic-update-slice_fusion.1) | copy-start | bytes 2359300

commit v3 on v1

v3 whole, which is shorter than its diff:
```python
import functools

import jax
import jax.numpy as jnp
from jax import lax
from jax.experimental import pallas as pl
from jax.experimental.pallas import tpu as pltpu
from jax.sharding import PartitionSpec as P

VMEM_BYTES = 16 * 1024 * 1024


def widen(target, row, value):
    cols, channels = value.shape
    wide = value.astype(jnp.float32)
    position = lax.broadcasted_iota(jnp.int32, (cols, channels), 0)
    left = jnp.where(position == 0, 0.0, pltpu.roll(wide, 1, 0))
    right = jnp.where(position == cols - 1, 0.0, pltpu.roll(wide, cols - 1, 0))
    target[row, :, 0:channels] = left.astype(jnp.bfloat16)
    target[row, :, channels : 2 * channels] = value
    target[row, :, 2 * channels : 3 * channels] = right.astype(jnp.bfloat16)


def halo_row(first, second, odd, row):
    one, other = first[row % 2], second[row % 2]
    return jnp.where(odd == (row < 2), one, other)


def fill(target, own, first, second, odd, base=0):
    for row in range(2):
        widen(target, row, halo_row(first, second, odd, row))
        widen(target, row + 2, own[base + row])
        widen(target, row + 4, halo_row(first, second, odd, row + 2))


def taps(source, start, rows, weight, lo, out_lo, channels):
    cols = source.shape[1]
    total = None
    for row_off in range(3):
        view = source[start + row_off : start + row_off + rows].reshape(rows * cols, 3 * channels)
        kernel = weight[row_off, :, lo : lo + channels, out_lo : out_lo + channels]
        part = jnp.dot(
            view, kernel.reshape(3 * channels, channels), preferred_element_type=jnp.float32
        )
        total = part if total is None else total + part
    return total


def active(lag, layer):
    return layer == 0 if lag == 0 else layer == 1 if lag == 3 else layer >= 0


def early_kernel(lag, flags, own, first, second, wg, pre_r, pre_u, wide):
    channels = own.shape[-1]

    @pl.when(active(lag, flags[0]))
    def _():
        fill(wide, own, first, second, flags[1] == 1)
        pre_r[...] = taps(wide, 0, 4, wg, channels, channels, channels)
        pre_u[...] = taps(wide, 1, 2, wg, channels, 0, channels)


def late_kernel(
    lag, flags, own, first, second, pre_r, pre_u, x0, x0a, x0b, x1, x1a, x1b, wg, wc, bias, out,
    wide, wide_r, sum_c,
):
    cols, channels = own.shape[1:]
    layer, odd = flags[0], flags[1] == 1

    @pl.when(active(lag, layer))
    def _():
        if lag < 3:
            @pl.when(layer == 0)
            def _():
                fill(wide, x0, x0a, x0b, odd, 2 * lag)

        if lag > 0:
            @pl.when(layer == 1)
            def _():
                fill(wide, x1, x1a, x1b, odd)

        sum_r = pre_r[...] + taps(wide, 0, 4, wg, 0, channels, channels)
        for row in range(4):
            held = own[row - 1] if 0 < row < 3 else halo_row(first, second, odd, 1 if row == 0 else 2)
            gate = jax.nn.sigmoid(
                sum_r[row * cols : (row + 1) * cols] + bias[:, channels : 2 * channels]
            )
            widen(wide_r, row, (gate * held.astype(jnp.float32)).astype(jnp.bfloat16))
        sum_u = pre_u[...] + taps(wide, 1, 2, wg, 0, 0, channels)
        of_input = taps(wide, 1, 2, wc, 0, 0, channels)
        sum_c[...] = of_input + taps(wide_r, 0, 2, wc, channels, 0, channels)
        for row in range(2):
            part = slice(row * cols, (row + 1) * cols)
            held = own[row].astype(jnp.float32)
            update = jax.nn.sigmoid(sum_u[part] + bias[:, 0:channels])
            candidate = jnp.tanh(sum_c[part] + bias[:, 2 * channels : 3 * channels])
            out[row] = ((1.0 - update) * held + update * candidate).astype(jnp.bfloat16)

    if lag in (0, 3):
        @pl.when(jnp.logical_not(active(lag, layer)))
        def _():
            out[...] = own[...]


HELD = pl.BlockSpec(memory_space=pltpu.VMEM)
SCALARS = pl.BlockSpec(memory_space=pltpu.SMEM)


def cost(cols, channels):
    return pl.CostEstimate(
        flops=2 * 8 * cols * channels * 9 * channels, bytes_accessed=1 << 20, transcendentals=0
    )


def early(lag, flags, state, wg):
    _, cols, channels = state[0].shape
    pre = lambda n: jax.ShapeDtypeStruct((n * cols, channels), jnp.float32)
    return pl.pallas_call(
        functools.partial(early_kernel, lag),
        out_shape=[pre(4), pre(2)],
        in_specs=[SCALARS] + [HELD] * 4,
        out_specs=[HELD] * 2,
        scratch_shapes=[pltpu.VMEM((6, cols, 3 * channels), jnp.bfloat16)],
        compiler_params=pltpu.CompilerParams(vmem_limit_bytes=VMEM_BYTES),
        cost_estimate=cost(cols, channels),
    )(flags, *state, wg)


def late(lag, flags, state, pre, x0, x1, wg, wc, bias):
    _, cols, channels = state[0].shape
    return pl.pallas_call(
        functools.partial(late_kernel, lag),
        out_shape=jax.ShapeDtypeStruct((2, cols, channels), jnp.bfloat16),
        in_specs=[SCALARS] + [HELD] * 14,
        out_specs=HELD,
        scratch_shapes=[
            pltpu.VMEM((6, cols, 3 * channels), jnp.bfloat16),
            pltpu.VMEM((4, cols, 3 * channels), jnp.bfloat16),
            pltpu.VMEM((2 * cols, channels), jnp.float32),
        ],
        compiler_params=pltpu.CompilerParams(vmem_limit_bytes=VMEM_BYTES),
        cost_estimate=cost(cols, channels),
    )(flags, *state, *pre, *x0, *x1, wg, wc, bias)


def pair_swap(field, start):
    count = lax.axis_size("rows")
    route = []
    for low in range(start, count - 1, 2):
        route += [(low, low + 1), (low + 1, low)]
    return lax.ppermute(field, "rows", route)


def gathered_swap(field, strip):
    count = lax.axis_size("rows")
    groups = [[0, count], [count - 1, 2 * count - 1]]
    for layer in range(2):
        groups += [[layer * count + low, layer * count + low + 1] for low in range(1, count - 1, 2)]
    both = lax.all_gather(field, ("layer", "rows"), axis_index_groups=groups)
    inner = jnp.logical_and(strip > 0, strip < count - 1)
    partner = jnp.where(lax.rem(strip, 2) == 1, both[1], both[0])
    return jnp.where(inner, partner, jnp.zeros_like(partner))


def across(field):
    return lax.ppermute(field, "layer", [(0, 1), (1, 0)])


def shards(frames, initial_state, w_gates, w_cand, biases):
    layer = lax.axis_index("layer")
    strip = lax.axis_index("rows")
    flags = jnp.stack([layer, lax.rem(strip, 2)]).astype(jnp.int32)
    wg, wc = w_gates[0], w_cand[0]
    hidden = initial_state[0]
    rows = frames.reshape((6,) + hidden.shape[1:])

    field = jnp.where(layer == 0, hidden, frames[0])
    first, second = pair_swap(field, 0), pair_swap(field, 1)
    field = jnp.where(layer == 0, frames[1], frames[2])
    late_first, late_second = pair_swap(field, 0), pair_swap(field, 1)
    halos = [
        (across(first), across(second)),
        (late_first, late_second),
        (across(late_first), across(late_second)),
    ]
    below = (hidden, first, second)
    states = []
    for step in range(4):
        state = (hidden, first, second)
        pre = early(step, flags, state, wg)
        own_halos = halos[min(step, 2)]
        hidden = late(step, flags, state, pre, (rows, *own_halos), below, wg, wc, biases)
        states.append(hidden)
        if step < 3:
            first = pair_swap(hidden, 0)
            own_below = across(hidden)
            second = gathered_swap(hidden, strip)
            below = (own_below, across(first), across(second))
    out = jnp.stack(
        [
            jnp.where(layer == 0, states[0], states[1]),
            jnp.where(layer == 0, states[1], states[2]),
            jnp.zeros_like(hidden),
        ]
    )
    return lax.dynamic_update_slice(out, states[3][None], (2, 0, 0, 0))[None]


def solution(mesh):
    placed = (
        P(None, "rows", None, None),
        P("layer", "rows", None, None),
        P("layer", None, None, None, None),
        P("layer", None, None, None, None),
        P("layer", None),
    )
    return jax.shard_map(
        shards,
        mesh=mesh,
        in_specs=placed,
        out_specs=P("layer", None, "rows", None, None),
        check_vma=False,
    )
```

time: 113 us -> 104 us (0.920)
  blocking collectives: 0 us -> 36.8 us
  waiting for transfers between devices: 31.8 us -> 5.95 us
  starting transfers between devices: 48.7 us -> 28.2 us
  Pallas kernels: 22 us -> 23.5 us
  other arithmetic: 4.58 us -> 3.33 us
    all_gather x0 -> x3, blocking collectives: none -> 36.8 us  [gathered_swap(): both = lax.all_gather(field, ('layer', 'rows'), axis_index_groups=groups)]
    ppermute x18 -> x20, waiting for transfers between devices: 31.8 us -> 5.95 us  [the longest x7 5.91 us: pair_swap(): return lax.ppermute(field, 'rows', route)]
    ppermute x18 -> x20, starting transfers between devices: 48.7 us -> 28.2 us  [the longest x7 14.3 us: pair_swap(): return lax.ppermute(field, 'rows', route)]
    unnamed x12 -> x14, local copies, waits for them, and re-layouts: 1.68 us -> 4.37 us
    concatenate x5 -> x0, other arithmetic: 2.28 us -> none  [the longest x1 1.29 us: shards(): later = lax.ppermute(jnp.concatenate([later_a, later_b]), 'layer', down)]
    slice x3 -> x0, local copies, waits for them, and re-layouts: 2 us -> none  [the longest x1 1.89 us: shards(): later_a, later_b = swap(frames[1:3].reshape((4,) + hidden.shape[1:]), (1,))]
    pallas_call x4 -> x8, Pallas kernels: 22 us -> 23.5 us  [the longest x4 15.1 us: late(): pl.pallas_call(functools.partial(late_kernel, lag), out_shape=jax.ShapeDt...]
    squeeze x1 -> x0, local copies, waits for them, and re-layouts: 1.31 us -> none  [shards(): frames[frame]]
  transfers between devices with their start and end apart: 18 -> 20, of which waited for: 8 -> 1; matrix products, arithmetic and copies ran while one was open for 5% -> 2% of each run, Pallas kernels for 1% -> 13%
where the time goes in v3:
time: 104 us; the launch traced here: 103 us
  blocking collectives  36.8 us (35%)
  starting transfers between devices  28.2 us (27%)
  Pallas kernels  23.5 us (23%)
  waiting for transfers between devices  5.95 us (6%)
  local copies, waits for them, and re-layouts  5.17 us (5%)
  other arithmetic  3.33 us (3%)
    all_gather x3, blocking collectives, gathered_swap(): both = lax.all_gather(field, ('layer', 'rows'), axis_index_groups=groups)  36.8 us
    pallas_call x4, Pallas kernels, late(): pl.pallas_call(functools.partial(late_kernel, lag), out_shape=jax.ShapeDt...  15.1 us
    ppermute x7, starting transfers between devices, pair_swap(): return lax.ppermute(field, 'rows', route)  14.3 us
    ppermute x13, starting transfers between devices, across(): return lax.ppermute(field, 'layer', [(0, 1), (1, 0)])  13.9 us
    pallas_call x4, Pallas kernels, early(): pl.pallas_call(functools.partial(early_kernel, lag), out_shape=[pre(4), p...  8.38 us
    ppermute x7, waiting for transfers between devices, pair_swap(): return lax.ppermute(field, 'rows', route)  5.91 us
    unnamed x14, local copies, waits for them, and re-layouts  4.37 us
  transfers between devices with their start and end apart: 20, of which 1 were waited for; matrix products, arithmetic and copies ran while one was open for 2% of the time, Pallas kernels for 13%

profile of v3, /device:TPU:25, one launch (start us, length us, event | category | flops | bytes accessed | tf_op | source)
XLA Modules:
  0.0 103.3 jit_solution(2604830620679476607)
XLA Ops:
  0.0 1.1 %bitcast_select_fusion = bf16[2,256,256]{2,1,0:T(8,128)(2,1)S(1)} fusion(bf16[3,2,256,256]{3,2,1,0:T(8,128)(2,1)} %param.5, pred[]{:T(512)S(6)} %eq.4, bf16[1,2,256,256]{3,2,1,0:T(8,128)(2,1)} %param.6), kind=kLoop, calls=%fused_computation.8 | loop fusion | flops 131072 | bytes 786433 | tf_op jit(solution)/shard_map/jit(_where)/select_n | solution.py:177
  1.1 0.0 copy-start.2
  1.1 0.0 copy-start.4
  1.1 1.7 %collective-permute-start = (bf16[2,256,256]{2,1,0:T(8,128)(2,1)S(1)}, bf16[2,256,256]{2,1,0:T(8,128)(2,1)S(1)}, u32[]{:S(2)}, u32[]{:S(2)}) collective-permute-start(bf16[2,256,256]{2,1,0:T(8,128)(2,1)S(1)} %bitcast_select_fusion), channel_id=1, source_target_pairs={{0,1},{1,0},{2,3},{3,2},{4,5},{5,4},{6,7},{7,6},{8,9},{9,8},{10,11... | collective-permute-start | bytes 786440 | tf_op jit(solution)/shard_map/ppermute | solution.py:151
  2.8 8.9 %collective-permute-start.1 = (bf16[2,256,256]{2,1,0:T(8,128)(2,1)S(1)}, bf16[2,256,256]{2,1,0:T(8,128)(2,1)S(1)}, u32[]{:S(2)}, u32[]{:S(2)}) collective-permute-start(bf16[2,256,256]{2,1,0:T(8,128)(2,1)S(1)} %bitcast_select_fusion), channel_id=1, source_target_pairs={{1,2},{2,1},{3,4},{4,3},{5,6},{6,5},{7,8},{8,7},{9,10},{10,9},{11,... | collective-permute-start | bytes 786440 | tf_op jit(solution)/shard_map/ppermute | solution.py:151
  11.8 1.1 %select_bitcast_fusion.2 = bf16[2,256,256]{2,1,0:T(8,128)(2,1)S(1)} fusion(bf16[3,2,256,256]{3,2,1,0:T(8,128)(2,1)} %param.5, pred[]{:T(512)S(6)} %eq.4), kind=kLoop, calls=%fused_computation.11 | loop fusion | flops 131072 | bytes 786433 | tf_op jit(solution)/shard_map/jit(_where)/select_n | solution.py:179
  12.8 0.1 collective-permute-start.5
  12.9 3.3 %collective-permute-start.6 = (bf16[2,256,256]{2,1,0:T(8,128)(2,1)S(1)}, bf16[2,256,256]{2,1,0:T(8,128)(2,1)S(1)}, u32[]{:S(2)}, u32[]{:S(2)}) collective-permute-start(bf16[2,256,256]{2,1,0:T(8,128)(2,1)S(1)} %select_bitcast_fusion.2), channel_id=1, source_target_pairs={{1,2},{2,1},{3,4},{4,3},{5,6},{6,5},{7,8},{8,7},{9,10},{10,9},{11,... | collective-permute-start | bytes 786440 | tf_op jit(solution)/shard_map/ppermute | solution.py:151
  16.3 0.0 collective-permute-done.first.x1a
  16.3 1.9 %collective-permute-start.2 = (bf16[2,256,256]{2,1,0:T(8,128)(2,1)S(1)}, bf16[2,256,256]{2,1,0:T(8,128)(2,1)S(1)}, u32[]{:S(2)}, u32[]{:S(2)}) collective-permute-start(bf16[2,256,256]{2,1,0:T(8,128)(2,1)S(1)} %collective-permute-done.first.x1a), channel_id=1, source_target_pairs={{0,128},{128,0},{1,129},{129,1},{2,130},{130,2},{3,131},{131,3},{4... | collective-permute-start | bytes 786440 | tf_op jit(solution)/shard_map/ppermute | solution.py:166
  18.2 0.0 collective-permute-done.1.second.x1b
  18.2 1.1 %collective-permute-start.3 = (bf16[2,256,256]{2,1,0:T(8,128)(2,1)S(1)}, bf16[2,256,256]{2,1,0:T(8,128)(2,1)S(1)}, u32[]{:S(2)}, u32[]{:S(2)}) collective-permute-start(bf16[2,256,256]{2,1,0:T(8,128)(2,1)S(1)} %collective-permute-done.1.second.x1b), channel_id=1, source_target_pairs={{0,128},{128,0},{1,129},{129,1},{2,130},{130,2},{3,131},{131,3},{4... | collective-permute-start | bytes 786440 | tf_op jit(solution)/shard_map/ppermute | solution.py:166
  19.3 0.1 pad_add_fusion.flags
  19.4 2.3 %copy-done = bf16[1,3,3,512,512]{4,3,2,1,0:T(8,128)(2,1)S(1)} copy-done((bf16[1,3,3,512,512]{4,3,2,1,0:T(8,128)(2,1)S(1)}, bf16[1,3,3,512,512]{4,3,2,1,0:T(8,128)(2,1)}, u32[]{:S(2)}) %copy-start) | copy-done | bytes 4718616
  21.7 0.9 copy-done.3
  22.7 0.5 shard_map.55
  23.2 0.0 collective-permute-done.2.x0a
  23.2 0.0 collective-permute-done.3.x0b
  23.2 0.0 copy-done.2
  23.2 0.0 copy-done.4
  23.3 1.1 %copy-done.1 = bf16[1,3,3,512,256]{4,3,2,1,0:T(8,128)(2,1)S(1)} copy-done((bf16[1,3,3,512,256]{4,3,2,1,0:T(8,128)(2,1)S(1)}, bf16[1,3,3,512,256]{4,3,2,1,0:T(8,128)(2,1)}, u32[]{:S(2)}) %copy-start.1) | copy-done | bytes 2359320
  24.3 0.6 shard_map.56.own
  24.9 0.1 collective-permute-start.4
  25.0 10.8 %all-gather = bf16[4,256,256]{2,1,0:T(8,128)(2,1)S(1)} all-gather(bf16[2,256,256]{2,1,0:T(8,128)(2,1)S(1)} %shard_map.56.own), channel_id=2, replica_groups={{0,128},{127,255},{1,2},{3,4},{5,6},{7,8},{9,10},{11,12},{13,14},{15,16..., dimensions={0}, use_global_device_ids=true | all-gather | bytes 786432 | tf_op jit(solution)/shard_map/all_gather | solution.py:159
  35.8 5.8 %collective-permute-start.7 = (bf16[2,256,256]{2,1,0:T(8,128)(2,1)S(1)}, bf16[2,256,256]{2,1,0:T(8,128)(2,1)S(1)}, u32[]{:S(2)}, u32[]{:S(2)}) collective-permute-start(bf16[2,256,256]{2,1,0:T(8,128)(2,1)S(1)} %shard_map.56.own), channel_id=1, source_target_pairs={{0,128},{128,0},{1,129},{129,1},{2,130},{130,2},{3,131},{131,3},{4... | collective-permute-start | bytes 786440 | tf_op jit(solution)/shard_map/ppermute | solution.py:166
  41.7 0.1 collective-permute-start.9
  41.8 0.0 collective-permute-done.4.first
  41.8 0.5 collective-permute-start.8
  42.3 0.0 collective-permute-done.5.x0a
  42.3 0.1 collective-permute-start.11
  42.4 0.0 collective-permute-done.6.x0b
  42.4 0.4 collective-permute-start.12
  42.8 2.7 %shard_map.57 = (f32[1024,256]{1,0:T(8,128)S(1)}, f32[512,256]{1,0:T(8,128)S(1)}) custom-call(s32[2]{0:T(128)S(1)} %pad_add_fusion.flags, bf16[2,256,256]{2,1,0:T(8,128)(2,1)S(1)} %shard_map.56.own, bf16[2,256,256]{2,1,0:T(8,128)(2,1)S(1)} %collective-permute-done.4.first, bf16[2,256,256]{2,1,0:T(8,128)(2,1)S(1)} %fusion.2.second, ...), custom_call_target="tpu_custom_call" | custom-call | flops 2415919104 | bytes 1048576 | tf_op jit(solution)/shard_map/pallas_call | solution.py:118
  45.6 0.0 collective-permute-done.9.x1b
  45.6 0.0 collective-permute-done.7.x1
  45.6 0.0 collective-permute-done.8.x1a
  45.6 4.9 %shard_map.58.own = bf16[2,256,256]{2,1,0:T(8,128)(2,1)S(1)} custom-call(s32[2]{0:T(128)S(1)} %pad_add_fusion.flags, bf16[2,256,256]{2,1,0:T(8,128)(2,1)S(1)} %shard_map.56.own, bf16[2,256,256]{2,1,0:T(8,128)(2,1)S(1)} %collective-permute-done.4.first, bf16[2,256,256]{2,1,0:T(8,128)(2,1)S(1)} %fusion.2.second, f32[1024,256]{1,0:T(8,128)S(1)} %get-tuple-element.15.pre_r, ...), custom_call_target="tpu_custom_call" | custom-call | flops 2415919104 | bytes 1048576 | tf_op jit(solution)/shard_map/pallas_call | solution.py:131
  50.5 0.1 collective-permute-start.10
  50.6 13.2 %all-gather.1 = bf16[4,256,256]{2,1,0:T(8,128)(2,1)S(1)} all-gather(bf16[2,256,256]{2,1,0:T(8,128)(2,1)S(1)} %shard_map.58.own), channel_id=3, replica_groups={{0,128},{127,255},{1,2},{3,4},{5,6},{7,8},{9,10},{11,12},{13,14},{15,16..., dimensions={0}, use_global_device_ids=true | all-gather | bytes 786432 | tf_op jit(solution)/shard_map/all_gather | solution.py:159
  63.8 0.7 collective-permute-start.13
  64.5 0.1 collective-permute-start.15
  64.6 0.0 collective-permute-done.10.first
  64.6 0.5 collective-permute-start.14
  65.1 0.1 pad.2.clone
  65.2 2.5 %shard_map.59 = (f32[1024,256]{1,0:T(8,128)S(1)}, f32[512,256]{1,0:T(8,128)S(1)}) custom-call(s32[2]{0:T(128)S(1)} %pad_add_fusion.flags, bf16[2,256,256]{2,1,0:T(8,128)(2,1)S(1)} %shard_map.58.own, bf16[2,256,256]{2,1,0:T(8,128)(2,1)S(1)} %collective-permute-done.10.first, bf16[2,256,256]{2,1,0:T(8,128)(2,1)S(1)} %fusion.1.second, ...), custom_call_target="tpu_custom_call" | custom-call | flops 2415919104 | bytes 1048576 | tf_op jit(solution)/shard_map/pallas_call | solution.py:118
  67.7 0.0 collective-permute-done.11.x0a
  67.8 0.0 collective-permute-done.12.x0b
  67.8 0.0 collective-permute-done.15.x1b
  67.8 0.0 collective-permute-done.13.x1
  67.8 0.0 collective-permute-done.14.x1a
  67.8 5.1 %shard_map.60.own = bf16[2,256,256]{2,1,0:T(8,128)(2,1)S(1)} custom-call(s32[2]{0:T(128)S(1)} %pad_add_fusion.flags, bf16[2,256,256]{2,1,0:T(8,128)(2,1)S(1)} %shard_map.58.own, bf16[2,256,256]{2,1,0:T(8,128)(2,1)S(1)} %collective-permute-done.10.first, bf16[2,256,256]{2,1,0:T(8,128)(2,1)S(1)} %fusion.1.second, f32[1024,256]{1,0:T(8,128)S(1)} %get-tuple-element.17.pre_r, ...), custom_call_target="tpu_custom_call" | custom-call | flops 2415919104 | bytes 1048576 | tf_op jit(solution)/shard_map/pallas_call | solution.py:131
  72.9 12.8 %all-gather.2 = bf16[4,256,256]{2,1,0:T(8,128)(2,1)S(1)} all-gather(bf16[2,256,256]{2,1,0:T(8,128)(2,1)S(1)} %shard_map.60.own), channel_id=4, replica_groups={{0,128},{127,255},{1,2},{3,4},{5,6},{7,8},{9,10},{11,12},{13,14},{15,16..., dimensions={0}, use_global_device_ids=true | all-gather | bytes 786432 | tf_op jit(solution)/shard_map/all_gather | solution.py:159
  85.7 0.0 collective-permute-start.16
  85.7 0.9 collective-permute-start.17
  86.6 0.1 collective-permute-start.19
  86.8 5.9 %collective-permute-done.16.first = bf16[2,256,256]{2,1,0:T(8,128)(2,1)S(1)} collective-permute-done((bf16[2,256,256]{2,1,0:T(8,128)(2,1)S(1)}, bf16[2,256,256]{2,1,0:T(8,128)(2,1)S(1)}, u32[]{:S(2)}, u32[]{:S(2)}) %collective-permute-start.16) | collective-permute-done | bytes 262176 | tf_op jit(solution)/shard_map/ppermute | solution.py:151
  92.6 1.8 %collective-permute-start.18 = (bf16[2,256,256]{2,1,0:T(8,128)(2,1)S(1)}, bf16[2,256,256]{2,1,0:T(8,128)(2,1)S(1)}, u32[]{:S(2)}, u32[]{:S(2)}) collective-permute-start(bf16[2,256,256]{2,1,0:T(8,128)(2,1)S(1)} %collective-permute-done.16.first), channel_id=1, source_target_pairs={{0,128},{128,0},{1,129},{129,1},{2,130},{130,2},{3,131},{131,3},{4... | collective-permute-start | bytes 786440 | tf_op jit(solution)/shard_map/ppermute | solution.py:166
  94.4 1.0 maximum_bitcast_fusion
  95.4 2.6 %shard_map.61 = (f32[1024,256]{1,0:T(8,128)S(1)}, f32[512,256]{1,0:T(8,128)S(1)}) custom-call(s32[2]{0:T(128)S(1)} %pad_add_fusion.flags, bf16[2,256,256]{2,1,0:T(8,128)(2,1)S(1)} %shard_map.60.own, bf16[2,256,256]{2,1,0:T(8,128)(2,1)S(1)} %collective-permute-done.16.first, bf16[2,256,256]{2,1,0:T(8,128)(2,1)S(1)} %fusion.second, ...), custom_call_target="tpu_custom_call" | custom-call | flops 2415919104 | bytes 1048576 | tf_op jit(solution)/shard_map/pallas_call | solution.py:118
  98.0 0.0 collective-permute-done.19.x1b
  98.0 0.0 collective-permute-done.17.x1
  98.0 0.0 collective-permute-done.18.x1a
  98.0 4.5 %shard_map.62 = bf16[2,256,256]{2,1,0:T(8,128)(2,1)S(1)} custom-call(s32[2]{0:T(128)S(1)} %pad_add_fusion.flags, bf16[2,256,256]{2,1,0:T(8,128)(2,1)S(1)} %shard_map.60.own, bf16[2,256,256]{2,1,0:T(8,128)(2,1)S(1)} %collective-permute-done.16.first, bf16[2,256,256]{2,1,0:T(8,128)(2,1)S(1)} %fusion.second, f32[1024,256]{1,0:T(8,128)S(1)} %get-tuple-element.19.pre_r, ...), custom_call_target="tpu_custom_call" | custom-call | flops 2415919104 | bytes 1048576 | tf_op jit(solution)/shard_map/pallas_call | solution.py:131
  102.5 0.7 bitcast_dynamic-update-slice_fusion
  (12 shorter events, 0.1 us)
Async XLA Ops:
  1.1 22.2 %copy-start.2 = (bf16[3,2,256,256]{3,2,1,0:T(8,128)(2,1)S(1)}, bf16[3,2,256,256]{3,2,1,0:T(8,128)(2,1)}, u32[]{:S(2)}) copy-start(bf16[3,2,256,256]{3,2,1,0:T(8,128)(2,1)} %param.5) | copy-start | bytes 2359300
  1.1 22.2 %copy-start.4 = (f32[1,768]{1,0:T(1,128)S(1)}, f32[1,768]{1,0:T(1,128)}, u32[]{:S(2)}) copy-start(f32[1,768]{1,0:T(1,128)} %bias.7) | copy-start | bytes 9220
  1.1 15.2 %collective-permute-start = (bf16[2,256,256]{2,1,0:T(8,128)(2,1)S(1)}, bf16[2,256,256]{2,1,0:T(8,128)(2,1)S(1)}, u32[]{:S(2)}, u32[]{:S(2)}) collective-permute-start(bf16[2,256,256]{2,1,0:T(8,128)(2,1)S(1)} %bitcast_select_fusion), channel_id=1, source_target_pairs={{0,1},{1,0},{2,3},{3,2},{4,5},{5,4},{6,7},{7,6},{8,9},{9,8},{10,11... | collective-permute-start | bytes 786440 | tf_op jit(solution)/shard_map/ppermute | solution.py:151
  2.8 15.4 %collective-permute-start.1 = (bf16[2,256,256]{2,1,0:T(8,128)(2,1)S(1)}, bf16[2,256,256]{2,1,0:T(8,128)(2,1)S(1)}, u32[]{:S(2)}, u32[]{:S(2)}) collective-permute-start(bf16[2,256,256]{2,1,0:T(8,128)(2,1)S(1)} %bitcast_select_fusion), channel_id=1, source_target_pairs={{1,2},{2,1},{3,4},{4,3},{5,6},{6,5},{7,8},{8,7},{9,10},{10,9},{11,... | collective-permute-start | bytes 786440 | tf_op jit(solution)/shard_map/ppermute | solution.py:151
  12.8 29.5 %collective-permute-start.5 = (bf16[2,256,256]{2,1,0:T(8,128)(2,1)S(1)}, bf16[2,256,256]{2,1,0:T(8,128)(2,1)S(1)}, u32[]{:S(2)}, u32[]{:S(2)}) collective-permute-start(bf16[2,256,256]{2,1,0:T(8,128)(2,1)S(1)} %select_bitcast_fusion.2), channel_id=1, source_target_pairs={{0,1},{1,0},{2,3},{3,2},{4,5},{5,4},{6,7},{7,6},{8,9},{9,8},{10,11... | collective-permute-start | bytes 786440 | tf_op jit(solution)/shard_map/ppermute | solution.py:151
  12.9 29.5 %collective-permute-start.6 = (bf16[2,256,256]{2,1,0:T(8,128)(2,1)S(1)}, bf16[2,256,256]{2,1,0:T(8,128)(2,1)S(1)}, u32[]{:S(2)}, u32[]{:S(2)}) collective-permute-start(bf16[2,256,256]{2,1,0:T(8,128)(2,1)S(1)} %select_bitcast_fusion.2), channel_id=1, source_target_pairs={{1,2},{2,1},{3,4},{4,3},{5,6},{6,5},{7,8},{8,7},{9,10},{10,9},{11,... | collective-permute-start | bytes 786440 | tf_op jit(solution)/shard_map/ppermute | solution.py:151
  16.3 6.9 %collective-permute-start.2 = (bf16[2,256,256]{2,1,0:T(8,128)(2,1)S(1)}, bf16[2,256,256]{2,1,0:T(8,128)(2,1)S(1)}, u32[]{:S(2)}, u32[]{:S(2)}) collective-permute-start(bf16[2,256,256]{2,1,0:T(8,128)(2,1)S(1)} %collective-permute-done.first.x1a), channel_id=1, source_target_pairs={{0,128},{128,0},{1,129},{129,1},{2,130},{130,2},{3,131},{131,3},{4... | collective-permute-start | bytes 786440 | tf_op jit(solution)/shard_map/ppermute | solution.py:166
  18.2 5.1 %collective-permute-start.3 = (bf16[2,256,256]{2,1,0:T(8,128)(2,1)S(1)}, bf16[2,256,256]{2,1,0:T(8,128)(2,1)S(1)}, u32[]{:S(2)}, u32[]{:S(2)}) collective-permute-start(bf16[2,256,256]{2,1,0:T(8,128)(2,1)S(1)} %collective-permute-done.1.second.x1b), channel_id=1, source_target_pairs={{0,128},{128,0},{1,129},{129,1},{2,130},{130,2},{3,131},{131,3},{4... | collective-permute-start | bytes 786440 | tf_op jit(solution)/shard_map/ppermute | solution.py:166
  19.4 2.3 %copy-start = (bf16[1,3,3,512,512]{4,3,2,1,0:T(8,128)(2,1)S(1)}, bf16[1,3,3,512,512]{4,3,2,1,0:T(8,128)(2,1)}, u32[]{:S(2)}) copy-start(bf16[1,3,3,512,512]{4,3,2,1,0:T(8,128)(2,1)} %param.7) | copy-start | bytes 14155780
  21.7 0.9 copy-start.3
  22.7 1.7 %copy-start.1 = (bf16[1,3,3,512,256]{4,3,2,1,0:T(8,128)(2,1)S(1)}, bf16[1,3,3,512,256]{4,3,2,1,0:T(8,128)(2,1)}, u32[]{:S(2)}) copy-start(bf16[1,3,3,512,256]{4,3,2,1,0:T(8,128)(2,1)} %param.8) | copy-start | bytes 7077892
  22.7 20.1 %slice-start = ((s8[4718592]{0:T(1024)(128)(4,1)}), s8[4194304]{0:T(1024)(128)(4,1)S(1)}, s32[]{:S(2)}) async-start(s8[4718592]{0:T(1024)(128)(4,1)} %bitcast.22), calls=%async_computation | async-start | bytes 8388608
  24.3 18.5 %slice-start.1 = ((s8[4718592]{0:T(1024)(128)(4,1)}), s8[524288]{0:T(1024)(128)(4,1)S(1)}, s32[]{:S(2)}) async-start(s8[4718592]{0:T(1024)(128)(4,1)} %bitcast.22), calls=%async_computation.1 | async-start | bytes 1048576
  24.9 16.9 %collective-permute-start.4 = (bf16[2,256,256]{2,1,0:T(8,128)(2,1)S(1)}, bf16[2,256,256]{2,1,0:T(8,128)(2,1)S(1)}, u32[]{:S(2)}, u32[]{:S(2)}) collective-permute-start(bf16[2,256,256]{2,1,0:T(8,128)(2,1)S(1)} %shard_map.56.own), channel_id=1, source_target_pairs={{0,1},{1,0},{2,3},{3,2},{4,5},{5,4},{6,7},{7,6},{8,9},{9,8},{10,11... | collective-permute-start | bytes 786440 | tf_op jit(solution)/shard_map/ppermute | solution.py:151
  35.8 9.7 %collective-permute-start.7 = (bf16[2,256,256]{2,1,0:T(8,128)(2,1)S(1)}, bf16[2,256,256]{2,1,0:T(8,128)(2,1)S(1)}, u32[]{:S(2)}, u32[]{:S(2)}) collective-permute-start(bf16[2,256,256]{2,1,0:T(8,128)(2,1)S(1)} %shard_map.56.own), channel_id=1, source_target_pairs={{0,128},{128,0},{1,129},{129,1},{2,130},{130,2},{3,131},{131,3},{4... | collective-permute-start | bytes 786440 | tf_op jit(solution)/shard_map/ppermute | solution.py:166
  41.7 3.9 %collective-permute-start.9 = (bf16[2,256,256]{2,1,0:T(8,128)(2,1)S(1)}, bf16[2,256,256]{2,1,0:T(8,128)(2,1)S(1)}, u32[]{:S(2)}, u32[]{:S(2)}) collective-permute-start(bf16[2,256,256]{2,1,0:T(8,128)(2,1)S(1)} %fusion.2.second), channel_id=1, source_target_pairs={{0,128},{128,0},{1,129},{129,1},{2,130},{130,2},{3,131},{131,3},{4... | collective-permute-start | bytes 786440 | tf_op jit(solution)/shard_map/ppermute | solution.py:166
  41.8 3.8 %collective-permute-start.8 = (bf16[2,256,256]{2,1,0:T(8,128)(2,1)S(1)}, bf16[2,256,256]{2,1,0:T(8,128)(2,1)S(1)}, u32[]{:S(2)}, u32[]{:S(2)}) collective-permute-start(bf16[2,256,256]{2,1,0:T(8,128)(2,1)S(1)} %collective-permute-done.4.first), channel_id=1, source_target_pairs={{0,128},{128,0},{1,129},{129,1},{2,130},{130,2},{3,131},{131,3},{4... | collective-permute-start | bytes 786440 | tf_op jit(solution)/shard_map/ppermute | solution.py:166
  42.3 25.5 %collective-permute-start.11 = (bf16[2,256,256]{2,1,0:T(8,128)(2,1)S(1)}, bf16[2,256,256]{2,1,0:T(8,128)(2,1)S(1)}, u32[]{:S(2)}, u32[]{:S(2)}) collective-permute-start(bf16[2,256,256]{2,1,0:T(8,128)(2,1)S(1)} %collective-permute-done.5.x0a), channel_id=1, source_target_pairs={{0,128},{128,0},{1,129},{129,1},{2,130},{130,2},{3,131},{131,3},{4... | collective-permute-start | bytes 786440 | tf_op jit(solution)/shard_map/ppermute | solution.py:166
  42.4 25.4 %collective-permute-start.12 = (bf16[2,256,256]{2,1,0:T(8,128)(2,1)S(1)}, bf16[2,256,256]{2,1,0:T(8,128)(2,1)S(1)}, u32[]{:S(2)}, u32[]{:S(2)}) collective-permute-start(bf16[2,256,256]{2,1,0:T(8,128)(2,1)S(1)} %collective-permute-done.6.x0b), channel_id=1, source_target_pairs={{0,128},{128,0},{1,129},{129,1},{2,130},{130,2},{3,131},{131,3},{4... | collective-permute-start | bytes 786440 | tf_op jit(solution)/shard_map/ppermute | solution.py:166
  50.5 14.1 %collective-permute-start.10 = (bf16[2,256,256]{2,1,0:T(8,128)(2,1)S(1)}, bf16[2,256,256]{2,1,0:T(8,128)(2,1)S(1)}, u32[]{:S(2)}, u32[]{:S(2)}) collective-permute-start(bf16[2,256,256]{2,1,0:T(8,128)(2,1)S(1)} %shard_map.58.own), channel_id=1, source_target_pairs={{0,1},{1,0},{2,3},{3,2},{4,5},{5,4},{6,7},{7,6},{8,9},{9,8},{10,11... | collective-permute-start | bytes 786440 | tf_op jit(solution)/shard_map/ppermute | solution.py:151
  63.8 4.0 %collective-permute-start.13 = (bf16[2,256,256]{2,1,0:T(8,128)(2,1)S(1)}, bf16[2,256,256]{2,1,0:T(8,128)(2,1)S(1)}, u32[]{:S(2)}, u32[]{:S(2)}) collective-permute-start(bf16[2,256,256]{2,1,0:T(8,128)(2,1)S(1)} %shard_map.58.own), channel_id=1, source_target_pairs={{0,128},{128,0},{1,129},{129,1},{2,130},{130,2},{3,131},{131,3},{4... | collective-permute-start | bytes 786440 | tf_op jit(solution)/shard_map/ppermute | solution.py:166
  64.5 3.3 %collective-permute-start.15 = (bf16[2,256,256]{2,1,0:T(8,128)(2,1)S(1)}, bf16[2,256,256]{2,1,0:T(8,128)(2,1)S(1)}, u32[]{:S(2)}, u32[]{:S(2)}) collective-permute-start(bf16[2,256,256]{2,1,0:T(8,128)(2,1)S(1)} %fusion.1.second), channel_id=1, source_target_pairs={{0,128},{128,0},{1,129},{129,1},{2,130},{130,2},{3,131},{131,3},{4... | collective-permute-start | bytes 786440 | tf_op jit(solution)/shard_map/ppermute | solution.py:166
  64.6 3.2 %collective-permute-start.14 = (bf16[2,256,256]{2,1,0:T(8,128)(2,1)S(1)}, bf16[2,256,256]{2,1,0:T(8,128)(2,1)S(1)}, u32[]{:S(2)}, u32[]{:S(2)}) collective-permute-start(bf16[2,256,256]{2,1,0:T(8,128)(2,1)S(1)} %collective-permute-done.10.first), channel_id=1, source_target_pairs={{0,128},{128,0},{1,129},{129,1},{2,130},{130,2},{3,131},{131,3},{4... | collective-permute-start | bytes 786440 | tf_op jit(solution)/shard_map/ppermute | solution.py:166
  85.7 7.0 %collective-permute-start.16 = (bf16[2,256,256]{2,1,0:T(8,128)(2,1)S(1)}, bf16[2,256,256]{2,1,0:T(8,128)(2,1)S(1)}, u32[]{:S(2)}, u32[]{:S(2)}) collective-permute-start(bf16[2,256,256]{2,1,0:T(8,128)(2,1)S(1)} %shard_map.60.own), channel_id=1, source_target_pairs={{0,1},{1,0},{2,3},{3,2},{4,5},{5,4},{6,7},{7,6},{8,9},{9,8},{10,11... | collective-permute-start | bytes 786440 | tf_op jit(solution)/shard_map/ppermute | solution.py:151
  85.7 12.3 %collective-permute-start.17 = (bf16[2,256,256]{2,1,0:T(8,128)(2,1)S(1)}, bf16[2,256,256]{2,1,0:T(8,128)(2,1)S(1)}, u32[]{:S(2)}, u32[]{:S(2)}) collective-permute-start(bf16[2,256,256]{2,1,0:T(8,128)(2,1)S(1)} %shard_map.60.own), channel_id=1, source_target_pairs={{0,128},{128,0},{1,129},{129,1},{2,130},{130,2},{3,131},{131,3},{4... | collective-permute-start | bytes 786440 | tf_op jit(solution)/shard_map/ppermute | solution.py:166
  86.6 11.4 %collective-permute-start.19 = (bf16[2,256,256]{2,1,0:T(8,128)(2,1)S(1)}, bf16[2,256,256]{2,1,0:T(8,128)(2,1)S(1)}, u32[]{:S(2)}, u32[]{:S(2)}) collective-permute-start(bf16[2,256,256]{2,1,0:T(8,128)(2,1)S(1)} %fusion.second), channel_id=1, source_target_pairs={{0,128},{128,0},{1,129},{129,1},{2,130},{130,2},{3,131},{131,3},{4... | collective-permute-start | bytes 786440 | tf_op jit(solution)/shard_map/ppermute | solution.py:166
  92.6 5.4 %collective-permute-start.18 = (bf16[2,256,256]{2,1,0:T(8,128)(2,1)S(1)}, bf16[2,256,256]{2,1,0:T(8,128)(2,1)S(1)}, u32[]{:S(2)}, u32[]{:S(2)}) collective-permute-start(bf16[2,256,256]{2,1,0:T(8,128)(2,1)S(1)} %collective-permute-done.16.first), channel_id=1, source_target_pairs={{0,128},{128,0},{1,129},{129,1},{2,130},{130,2},{3,131},{131,3},{4... | collective-permute-start | bytes 786440 | tf_op jit(solution)/shard_map/ppermute | solution.py:166

commit v4 on v3

v4 whole, which is shorter than its diff:
```python
import functools

import jax
import jax.numpy as jnp
from jax import lax
from jax.experimental import pallas as pl
from jax.experimental.pallas import tpu as pltpu
from jax.sharding import PartitionSpec as P

VMEM_BYTES = 16 * 1024 * 1024


def widen(target, row, value):
    cols, channels = value.shape
    wide = value.astype(jnp.float32)
    position = lax.broadcasted_iota(jnp.int32, (cols, channels), 0)
    left = jnp.where(position == 0, 0.0, pltpu.roll(wide, 1, 0))
    right = jnp.where(position == cols - 1, 0.0, pltpu.roll(wide, cols - 1, 0))
    target[row, :, 0:channels] = left.astype(jnp.bfloat16)
    target[row, :, channels : 2 * channels] = value
    target[row, :, 2 * channels : 3 * channels] = right.astype(jnp.bfloat16)


def halo_row(first, second, odd, row):
    one, other = first[row % 2], second[row % 2]
    return jnp.where(odd == (row < 2), one, other)


def fill(target, own, first, second, odd, base=0):
    for row in range(2):
        widen(target, row, halo_row(first, second, odd, row))
        widen(target, row + 2, own[base + row])
        widen(target, row + 4, halo_row(first, second, odd, row + 2))


def taps(source, start, rows):
    _, cols, width = source.shape
    return jnp.concatenate(
        [source[start + tap : start + tap + rows].reshape(rows * cols, width) for tap in range(3)],
        -1,
    )


def columns(weight, lo, channels, out_lo, out_hi):
    return weight[:, :, lo : lo + channels, out_lo:out_hi].reshape(9 * channels, out_hi - out_lo)


def product(left, right):
    return jnp.dot(left, right, preferred_element_type=jnp.float32)


def active(lag, layer):
    return layer == 0 if lag == 0 else layer == 1 if lag == 3 else layer >= 0


def is_odd():
    return lax.rem(lax.axis_index("rows"), 2) == 1


def early_kernel(lag, own, first, second, wg, pre_r, pre_u, wide, *streamed):
    cols, channels = own.shape[1:]

    @pl.when(active(lag, lax.axis_index("layer")))
    def _():
        lo = channels
        weight = wg
        if streamed:
            weight, ready = streamed
            copy = pltpu.make_async_copy(wg.at[:, :, channels : 2 * channels], weight, ready)
            copy.start()
            lo = 0
        fill(wide, own, first, second, is_odd())
        if streamed:
            copy.wait()
        inner = product(taps(wide, 1, 2), columns(weight, lo, channels, 0, 2 * channels))
        edges = jnp.concatenate([taps(wide, 0, 1), taps(wide, 3, 1)], 0)
        outer = product(edges, columns(weight, lo, channels, channels, 2 * channels))
        pre_u[...] = inner[:, 0:channels]
        pre_r[cols : 3 * cols] = inner[:, channels : 2 * channels]
        pre_r[0:cols] = outer[0:cols]
        pre_r[3 * cols : 4 * cols] = outer[cols : 2 * cols]


def late_body(lag, own, first, second, pre, x0, x1, wg, wc, bias, wide, wide_r, store):
    cols, channels = own.shape[1:]
    layer, odd = lax.axis_index("layer"), is_odd()
    if lag < 3:
        @pl.when(layer == 0)
        def _():
            fill(wide, *x0, odd, 2 * lag)

    if lag > 0:
        @pl.when(layer == 1)
        def _():
            fill(wide, *x1, odd)

    of_reset = product(taps(wide, 0, 4), columns(wg, 0, channels, channels, 2 * channels))
    for row in range(4):
        part = slice(row * cols, (row + 1) * cols)
        held = own[row - 1] if 0 < row < 3 else halo_row(first, second, odd, 1 if row == 0 else 2)
        gate = jax.nn.sigmoid(
            pre[0][part] + of_reset[part] + bias[:, channels : 2 * channels]
        )
        widen(wide_r, row, (gate * held.astype(jnp.float32)).astype(jnp.bfloat16))
    weight = jnp.concatenate(
        [columns(wg, 0, channels, 0, channels), columns(wc, 0, channels, 0, channels)], -1
    )
    inner = product(taps(wide, 1, 2), weight)
    sum_u = pre[1][...] + inner[:, 0:channels]
    sum_c = inner[:, channels : 2 * channels] + product(
        taps(wide_r, 0, 2), columns(wc, channels, channels, 0, channels)
    )
    for row in range(2):
        part = slice(row * cols, (row + 1) * cols)
        held = own[row].astype(jnp.float32)
        update = jax.nn.sigmoid(sum_u[part] + bias[:, 0:channels])
        candidate = jnp.tanh(sum_c[part] + bias[:, 2 * channels : 3 * channels])
        store(row, ((1.0 - update) * held + update * candidate).astype(jnp.bfloat16))


def late_kernel(lag, *refs):
    own, first, second, pre_r, pre_u = refs[0:5]
    x0, x1 = refs[5:8], refs[8:11]
    wg, wc, bias, out, wide, wide_r = refs[11:17]

    def store(row, value):
        out[row] = value

    @pl.when(active(lag, lax.axis_index("layer")))
    def _():
        late_body(
            lag, own, first, second, (pre_r, pre_u), x0, x1, wg, wc, bias, wide, wide_r, store
        )

    if lag == 0:
        @pl.when(lax.axis_index("layer") == 1)
        def _():
            out[...] = own[...]


def last_kernel(*refs):
    own, first, second, pre_r, pre_u = refs[0:5]
    x1 = refs[5:8]
    wg, wc, bias, state0, state1, out, wide, wide_r, result, sent = refs[8:18]
    layer = lax.axis_index("layer")

    @pl.when(layer == 0)
    def _():
        copies = [
            pltpu.make_async_copy(state, out.at[frame], sent.at[frame])
            for frame, state in enumerate((state0, state1, own))
        ]
        for copy in copies:
            copy.start()
        for copy in copies:
            copy.wait()

    @pl.when(layer == 1)
    def _():
        copies = [
            pltpu.make_async_copy(state, out.at[frame], sent.at[frame])
            for frame, state in enumerate((state1, own))
        ]
        for copy in copies:
            copy.start()

        def store(row, value):
            result[row] = value
            copy = pltpu.make_async_copy(result.at[row], out.at[2, row], sent.at[2 + row])
            copy.start()
            copies.append(copy)

        late_body(
            3, own, first, second, (pre_r, pre_u), None, x1, wg, wc, bias, wide, wide_r, store
        )
        for copy in copies:
            copy.wait()


HELD = pl.BlockSpec(memory_space=pltpu.VMEM)
ANYWHERE = pl.BlockSpec(memory_space=pl.ANY)
OUTSIDE = pl.BlockSpec(memory_space=pltpu.HBM)


def cost(units, cols, channels):
    return pl.CostEstimate(
        flops=2 * units * cols * channels * 9 * channels, bytes_accessed=1 << 20, transcendentals=0
    )


def wide_rows(rows, cols, channels):
    return pltpu.VMEM((rows, cols, 3 * channels), jnp.bfloat16)


def early(lag, state, wg):
    _, cols, channels = state[0].shape
    pre = lambda n: jax.ShapeDtypeStruct((n * cols, channels), jnp.float32)
    scratch = [wide_rows(6, cols, channels)]
    if lag == 0:
        scratch += [
            pltpu.VMEM((3, 3, channels, 2 * channels), jnp.bfloat16), pltpu.SemaphoreType.DMA
        ]
    if lag == 0:
        wg = pltpu.with_memory_space_constraint(wg, pltpu.HBM)
    return pl.pallas_call(
        functools.partial(early_kernel, lag),
        out_shape=[pre(4), pre(2)],
        in_specs=[HELD] * 3 + [OUTSIDE if lag == 0 else HELD],
        out_specs=[HELD] * 2,
        scratch_shapes=scratch,
        compiler_params=pltpu.CompilerParams(vmem_limit_bytes=VMEM_BYTES),
        cost_estimate=cost(6, cols, channels),
    )(*state, wg)


def late(lag, state, pre, x0, x1, wg, wc, bias):
    _, cols, channels = state[0].shape
    return pl.pallas_call(
        functools.partial(late_kernel, lag),
        out_shape=jax.ShapeDtypeStruct((2, cols, channels), jnp.bfloat16),
        in_specs=[HELD] * 14,
        out_specs=HELD,
        scratch_shapes=[wide_rows(6, cols, channels), wide_rows(4, cols, channels)],
        compiler_params=pltpu.CompilerParams(vmem_limit_bytes=VMEM_BYTES),
        cost_estimate=cost(10, cols, channels),
    )(*state, *pre, *x0, *x1, wg, wc, bias)


def last(state, pre, x1, wg, wc, bias, earlier):
    _, cols, channels = state[0].shape
    return pl.pallas_call(
        last_kernel,
        out_shape=jax.ShapeDtypeStruct((3, 2, cols, channels), jnp.bfloat16),
        in_specs=[HELD] * 13,
        out_specs=ANYWHERE,
        scratch_shapes=[
            wide_rows(6, cols, channels),
            wide_rows(4, cols, channels),
            pltpu.VMEM((2, cols, channels), jnp.bfloat16),
            pltpu.SemaphoreType.DMA((4,)),
        ],
        compiler_params=pltpu.CompilerParams(vmem_limit_bytes=VMEM_BYTES),
        cost_estimate=cost(10, cols, channels),
    )(*state, *pre, *x1, wg, wc, bias, *earlier)


def pair_swap(field, start):
    count = lax.axis_size("rows")
    route = []
    for low in range(start, count - 1, 2):
        route += [(low, low + 1), (low + 1, low)]
    return lax.ppermute(field, "rows", route)


def gathered_swap(field, strip):
    count = lax.axis_size("rows")
    groups = [[0, count], [count - 1, 2 * count - 1]]
    for layer in range(2):
        groups += [[layer * count + low, layer * count + low + 1] for low in range(1, count - 1, 2)]
    both = lax.all_gather(field, ("layer", "rows"), axis_index_groups=groups)
    inner = jnp.logical_and(strip > 0, strip < count - 1)
    partner = jnp.where(lax.rem(strip, 2) == 1, both[1], both[0])
    return jnp.where(inner, partner, jnp.zeros_like(partner))


def across(field):
    return lax.ppermute(field, "layer", [(0, 1), (1, 0)])


def shards(frames, initial_state, w_gates, w_cand, biases):
    layer = lax.axis_index("layer")
    strip = lax.axis_index("rows")
    wg, wc = w_gates[0], w_cand[0]
    hidden = initial_state[0]
    rows = frames.reshape((6,) + hidden.shape[1:])

    field = jnp.where(layer == 0, hidden, frames[0])
    first, second = pair_swap(field, 0), pair_swap(field, 1)
    later_field = jnp.where(layer == 0, frames[1], frames[2])
    late_first, late_second = pair_swap(later_field, 0), pair_swap(later_field, 1)
    halos = [
        (across(first), across(second)),
        (late_first, late_second),
        (across(late_first), across(late_second)),
    ]
    below = (field, first, second)
    pre = early(0, below, wg)
    pre = lax.optimization_barrier((*pre, late_first, late_second))[0:2]
    hidden = late(0, (hidden, first, second), pre, (rows, *halos[0]), below, wg, wc, biases)
    states = [hidden]
    for step in range(1, 4):
        first = pair_swap(hidden, 0)
        own_below = across(hidden)
        second = gathered_swap(hidden, strip)
        below = (own_below, across(first), across(second))
        state = (hidden, first, second)
        pre = early(step, state, wg)
        if step == 3:
            return last(state, pre, below, wg, wc, biases, states[0:2])[None]
        hidden = late(step, state, pre, (rows, *halos[step]), below, wg, wc, biases)
        states.append(hidden)


def solution(mesh):
    placed = (
        P(None, "rows", None, None),
        P("layer", "rows", None, None),
        P("layer", None, None, None, None),
        P("layer", None, None, None, None),
        P("layer", None),
    )
    return jax.shard_map(
        shards,
        mesh=mesh,
        in_specs=placed,
        out_specs=P("layer", None, "rows", None, None),
        check_vma=False,
    )
```

time: 104 us -> 96.5 us (0.928)
  local copies, waits for them, and re-layouts: 5.17 us -> 1.12 us
  blocking collectives: 36.8 us -> 35.6 us
  waiting for transfers between devices: 5.95 us -> 4.9 us
    pallas_call x0 -> x1, Pallas kernels: none -> 4.86 us  [last(): pl.pallas_call(last_kernel, out_shape=jax.ShapeDtypeStruct((3, 2, cols, c...]
    pallas_call x4 -> x3, Pallas kernels: 15.1 us -> 10.9 us  [late(): pl.pallas_call(functools.partial(late_kernel, lag), out_shape=jax.ShapeDt...]
    unnamed x14, local copies, waits for them, and re-layouts: 4.37 us -> 1.12 us
    all_gather x3, blocking collectives: 36.8 us -> 35.6 us  [gathered_swap(): both = lax.all_gather(field, ('layer', 'rows'), axis_index_groups=groups)]
    ppermute x7, waiting for transfers between devices: 5.91 us -> 4.86 us  [pair_swap(): return lax.ppermute(field, 'rows', route)]
  transfers between devices with their start and end apart: 20 -> 20, of which waited for: 1 -> 1; matrix products, arithmetic and copies ran while one was open for 2% -> 2% of each run, Pallas kernels for 13% -> 14%
where the time goes in v4:
time: 96.5 us; the launch traced here: 96.2 us
  blocking collectives  35.6 us (37%)
  starting transfers between devices  27.7 us (29%)
  Pallas kernels  23.3 us (24%)
  waiting for transfers between devices  4.9 us (5%)
  other arithmetic  3.08 us (3%)
  local copies, waits for them, and re-layouts  1.12 us (1%)
    all_gather x3, blocking collectives, gathered_swap(): both = lax.all_gather(field, ('layer', 'rows'), axis_index_groups=groups)  35.6 us
    ppermute x7, starting transfers between devices, pair_swap(): return lax.ppermute(field, 'rows', route)  14.3 us
    ppermute x13, starting transfers between devices, across(): return lax.ppermute(field, 'layer', [(0, 1), (1, 0)])  13.5 us
    pallas_call x3, Pallas kernels, late(): pl.pallas_call(functools.partial(late_kernel, lag), out_shape=jax.ShapeDt...  10.9 us
    pallas_call x4, Pallas kernels, early(): pl.pallas_call(functools.partial(early_kernel, lag), out_shape=[pre(4), p...  7.53 us
    ppermute x7, waiting for transfers between devices, pair_swap(): return lax.ppermute(field, 'rows', route)  4.86 us
    pallas_call x1, Pallas kernels, last(): pl.pallas_call(last_kernel, out_shape=jax.ShapeDtypeStruct((3, 2, cols, c...  4.86 us
  transfers between devices with their start and end apart: 20, of which 1 were waited for; matrix products, arithmetic and copies ran while one was open for 2% of the time, Pallas kernels for 14%

profile of v4, /device:TPU:25, one launch (start us, length us, event | category | flops | bytes accessed | tf_op | source)
XLA Modules:
  0.0 96.2 jit_solution(7409445901835690679)
XLA Ops:
  0.0 0.0 copy-start.2
  0.0 0.0 copy-start.1
  0.0 1.2 %bitcast_select_fusion.own.refs_8_ = bf16[2,256,256]{2,1,0:T(8,128)(2,1)S(1)} fusion(bf16[3,2,256,256]{3,2,1,0:T(8,128)(2,1)} %param.5, pred[]{:T(512)S(6)} %eq.4, bf16[1,2,256,256]{3,2,1,0:T(8,128)(2,1)} %param.6), kind=kLoop, calls=%fused_computation.6 | loop fusion | flops 131072 | bytes 786433 | tf_op jit(solution)/shard_map/jit(_where)/select_n | solution.py:277
  1.2 0.0 copy-start.4
  1.2 1.7 %collective-permute-start = (bf16[2,256,256]{2,1,0:T(8,128)(2,1)S(1)}, bf16[2,256,256]{2,1,0:T(8,128)(2,1)S(1)}, u32[]{:S(2)}, u32[]{:S(2)}) collective-permute-start(bf16[2,256,256]{2,1,0:T(8,128)(2,1)S(1)} %bitcast_select_fusion.own.refs_8_), channel_id=1, source_target_pairs={{0,1},{1,0},{2,3},{3,2},{4,5},{5,4},{6,7},{7,6},{8,9},{9,8},{10,11... | collective-permute-start | bytes 786440 | tf_op jit(solution)/shard_map/ppermute | solution.py:252
  3.0 8.9 %collective-permute-start.1 = (bf16[2,256,256]{2,1,0:T(8,128)(2,1)S(1)}, bf16[2,256,256]{2,1,0:T(8,128)(2,1)}, u32[]{:S(2)}, u32[]{:S(2)}) collective-permute-start(bf16[2,256,256]{2,1,0:T(8,128)(2,1)S(1)} %bitcast_select_fusion.own.refs_8_), channel_id=1, source_target_pairs={{1,2},{2,1},{3,4},{4,3},{5,6},{6,5},{7,8},{8,7},{9,10},{10,9},{11,... | collective-permute-start | bytes 786440 | tf_op jit(solution)/shard_map/ppermute | solution.py:252
  11.9 1.8 %select_bitcast_fusion = bf16[2,256,256]{2,1,0:T(8,128)(2,1)} fusion(bf16[3,2,256,256]{3,2,1,0:T(8,128)(2,1)} %param.5, pred[]{:T(512)S(6)} %eq.4), kind=kLoop, calls=%fused_computation.7 | loop fusion | flops 131072 | bytes 786433 | tf_op jit(solution)/shard_map/jit(_where)/select_n | solution.py:279
  13.7 0.0 collective-permute-start.2
  13.7 3.4 %collective-permute-start.3 = (bf16[2,256,256]{2,1,0:T(8,128)(2,1)}, bf16[2,256,256]{2,1,0:T(8,128)(2,1)}, u32[]{:S(2)}, u32[]{:S(2)}) collective-permute-start(bf16[2,256,256]{2,1,0:T(8,128)(2,1)} %select_bitcast_fusion), channel_id=1, source_target_pairs={{1,2},{2,1},{3,4},{4,3},{5,6},{6,5},{7,8},{8,7},{9,10},{10,9},{11,... | collective-permute-start | bytes 786440 | tf_op jit(solution)/shard_map/ppermute | solution.py:252
  17.0 0.0 collective-permute-done.first.refs_1_.refs_9_
  17.1 0.0 copy-done.4
  17.1 1.9 %collective-permute-start.4 = (bf16[2,256,256]{2,1,0:T(8,128)(2,1)S(1)}, bf16[2,256,256]{2,1,0:T(8,128)(2,1)}, u32[]{:S(2)}, u32[]{:S(2)}) collective-permute-start(bf16[2,256,256]{2,1,0:T(8,128)(2,1)S(1)} %collective-permute-done.first.refs_1_.refs_9_), channel_id=1, source_target_pairs={{0,128},{128,0},{1,129},{129,1},{2,130},{130,2},{3,131},{131,3},{4... | collective-permute-start | bytes 786440 | tf_op jit(solution)/shard_map/ppermute | solution.py:267
  18.9 0.0 collective-permute-done.1.second.refs_2_.refs_10_
  18.9 0.3 collective-permute-start.5
  19.3 0.0 copy-start
  19.3 1.1 %copy-done.5 = bf16[2,256,256]{2,1,0:T(8,128)(2,1)S(1)} copy-done((bf16[2,256,256]{2,1,0:T(8,128)(2,1)S(1)}, bf16[2,256,256]{2,1,0:T(8,128)(2,1)}, u32[]{:S(2)}) %copy-start.5) | copy-done | bytes 262168
  20.4 1.4 %shard_map.55 = (f32[1024,256]{1,0:T(8,128)S(1)}, f32[512,256]{1,0:T(8,128)S(1)}) custom-call(bf16[2,256,256]{2,1,0:T(8,128)(2,1)S(1)} %copy-done.5, bf16[2,256,256]{2,1,0:T(8,128)(2,1)S(1)} %collective-permute-done.first.refs_1_.refs_9_, bf16[2,256,256]{2,1,0:T(8,128)(2,1)} %collective-permute-done.1.second.refs_2_.refs_10_, bf16[3,3,512,512]{3,2,1,0:T(8,128)(2,1)} %bitcast.10), custom_call_target="tpu_custom_call" | custom-call | flops 1811939328 | bytes 1048576 | tf_op jit(solution)/shard_map/pallas_call | solution.py:205
  21.8 0.0 collective-permute-done.2.refs_6_
  21.8 4.8 %collective-permute-done.3.refs_7_ = bf16[2,256,256]{2,1,0:T(8,128)(2,1)} collective-permute-done((bf16[2,256,256]{2,1,0:T(8,128)(2,1)}, bf16[2,256,256]{2,1,0:T(8,128)(2,1)}, u32[]{:S(2)}, u32[]{:S(2)}) %collective-permute-start.3) | collective-permute-done | bytes 262176 | tf_op jit(solution)/shard_map/ppermute | solution.py:252
  26.7 0.0 collective-permute-done.4.refs_6_
  26.7 0.0 collective-permute-done.5.refs_7_
  26.7 0.0 copy-done.2
  26.7 0.0 copy-done.1
  26.7 0.0 copy-done
  26.7 0.0 copy-done.3
  26.7 0.0 copy-done.6
  26.7 1.2 %shard_map.56.own.refs_0_.refs_11_ = bf16[2,256,256]{2,1,0:T(8,128)(2,1)S(1)} custom-call(bf16[2,256,256]{2,1,0:T(8,128)(2,1)S(1)} %bitcast.25, bf16[2,256,256]{2,1,0:T(8,128)(2,1)S(1)} %collective-permute-done.first.refs_1_.refs_9_, bf16[2,256,256]{2,1,0:T(8,128)(2,1)} %collective-permute-done.1.second.refs_2_.refs_10_, ...), custom_call_target="tpu_custom_call" | custom-call | flops 3019898880 | bytes 1048576 | tf_op jit(solution)/shard_map/pallas_call | solution.py:218
  27.9 0.1 collective-permute-start.6
  28.0 10.1 %all-gather = bf16[4,256,256]{2,1,0:T(8,128)(2,1)S(1)} all-gather(bf16[2,256,256]{2,1,0:T(8,128)(2,1)S(1)} %shard_map.56.own.refs_0_.refs_11_), channel_id=2, replica_groups={{0,128},{127,255},{1,2},{3,4},{5,6},{7,8},{9,10},{11,12},{13,14},{15,16..., dimensions={0}, use_global_device_ids=true | all-gather | bytes 786432 | tf_op jit(solution)/shard_map/all_gather | solution.py:260
  38.2 7.2 %collective-permute-start.7 = (bf16[2,256,256]{2,1,0:T(8,128)(2,1)S(1)}, bf16[2,256,256]{2,1,0:T(8,128)(2,1)S(1)}, u32[]{:S(2)}, u32[]{:S(2)}) collective-permute-start(bf16[2,256,256]{2,1,0:T(8,128)(2,1)S(1)} %shard_map.56.own.refs_0_.refs_11_), channel_id=1, source_target_pairs={{0,128},{128,0},{1,129},{129,1},{2,130},{130,2},{3,131},{131,3},{4... | collective-permute-start | bytes 786440 | tf_op jit(solution)/shard_map/ppermute | solution.py:267
  45.4 0.1 collective-permute-start.9
  45.5 0.0 collective-permute-done.6.first.refs_1_
  45.5 0.5 collective-permute-start.8
  46.0 0.1 collective-permute-start.11
  46.1 0.4 collective-permute-start.12
  46.5 2.0 %shard_map.57 = (f32[1024,256]{1,0:T(8,128)S(1)}, f32[512,256]{1,0:T(8,128)S(1)}) custom-call(bf16[2,256,256]{2,1,0:T(8,128)(2,1)S(1)} %shard_map.56.own.refs_0_.refs_11_, bf16[2,256,256]{2,1,0:T(8,128)(2,1)S(1)} %collective-permute-done.6.first.refs_1_, bf16[2,256,256]{2,1,0:T(8,128)(2,1)S(1)} %fusion.2.second.refs_2_, bf16[3,3,512,512]{3,2,1,0:T(8,128)(2,1)S(1)} %bitcast.12), custom_call_target="tpu_custom_call" | custom-call | flops 1811939328 | bytes 1048576 | tf_op jit(solution)/shard_map/pallas_call | solution.py:205
  48.5 0.0 collective-permute-done.9.refs_10_
  48.5 0.0 collective-permute-done.7.refs_8_
  48.5 0.0 collective-permute-done.8.refs_9_
  48.6 5.5 %shard_map.58.own.refs_0_.refs_12_ = bf16[2,256,256]{2,1,0:T(8,128)(2,1)S(1)} custom-call(bf16[2,256,256]{2,1,0:T(8,128)(2,1)S(1)} %shard_map.56.own.refs_0_.refs_11_, bf16[2,256,256]{2,1,0:T(8,128)(2,1)S(1)} %collective-permute-done.6.first.refs_1_, bf16[2,256,256]{2,1,0:T(8,128)(2,1)S(1)} %fusion.2.second.refs_2_, ...), custom_call_target="tpu_custom_call" | custom-call | flops 3019898880 | bytes 1048576 | tf_op jit(solution)/shard_map/pallas_call | solution.py:218
  54.0 0.1 collective-permute-start.10
  54.1 12.8 %all-gather.1 = bf16[4,256,256]{2,1,0:T(8,128)(2,1)S(1)} all-gather(bf16[2,256,256]{2,1,0:T(8,128)(2,1)S(1)} %shard_map.58.own.refs_0_.refs_12_), channel_id=3, replica_groups={{0,128},{127,255},{1,2},{3,4},{5,6},{7,8},{9,10},{11,12},{13,14},{15,16..., dimensions={0}, use_global_device_ids=true | all-gather | bytes 786432 | tf_op jit(solution)/shard_map/all_gather | solution.py:260
  66.9 0.9 collective-permute-start.13
  67.8 0.1 collective-permute-start.15
  67.9 0.0 collective-permute-done.10.first.refs_1_
  67.9 0.5 collective-permute-start.14
  68.4 2.0 %shard_map.59 = (f32[1024,256]{1,0:T(8,128)S(1)}, f32[512,256]{1,0:T(8,128)S(1)}) custom-call(bf16[2,256,256]{2,1,0:T(8,128)(2,1)S(1)} %shard_map.58.own.refs_0_.refs_12_, bf16[2,256,256]{2,1,0:T(8,128)(2,1)S(1)} %collective-permute-done.10.first.refs_1_, bf16[2,256,256]{2,1,0:T(8,128)(2,1)S(1)} %fusion.1.second.refs_2_, bf16[3,3,512,512]{3,2,1,0:T(8,128)(2,1)S(1)} %bitcast.14), custom_call_target="tpu_custom_call" | custom-call | flops 1811939328 | bytes 1048576 | tf_op jit(solution)/shard_map/pallas_call | solution.py:205
  70.4 0.0 collective-permute-done.11.refs_6_
  70.5 0.0 collective-permute-done.12.refs_7_
  70.5 0.0 collective-permute-done.15.refs_10_
  70.5 0.0 collective-permute-done.13.refs_8_
  70.5 0.0 collective-permute-done.14.refs_9_
  70.5 4.3 %shard_map.60.own.refs_0_ = bf16[2,256,256]{2,1,0:T(8,128)(2,1)S(1)} custom-call(bf16[2,256,256]{2,1,0:T(8,128)(2,1)S(1)} %shard_map.58.own.refs_0_.refs_12_, bf16[2,256,256]{2,1,0:T(8,128)(2,1)S(1)} %collective-permute-done.10.first.refs_1_, bf16[2,256,256]{2,1,0:T(8,128)(2,1)S(1)} %fusion.1.second.refs_2_, f32[1024,256]{1,0:T(8,128)S(1)} %get-tuple-element.21.refs_3_, ...), custom_call_target="tpu_custom_call" | custom-call | flops 3019898880 | bytes 1048576 | tf_op jit(solution)/shard_map/pallas_call | solution.py:218
  74.8 0.1 collective-permute-start.16
  74.9 12.7 %all-gather.2 = bf16[4,256,256]{2,1,0:T(8,128)(2,1)S(1)} all-gather(bf16[2,256,256]{2,1,0:T(8,128)(2,1)S(1)} %shard_map.60.own.refs_0_), channel_id=4, replica_groups={{0,128},{127,255},{1,2},{3,4},{5,6},{7,8},{9,10},{11,12},{13,14},{15,16..., dimensions={0}, use_global_device_ids=true | all-gather | bytes 786432 | tf_op jit(solution)/shard_map/all_gather | solution.py:260
  87.5 1.0 collective-permute-start.17
  88.5 0.1 collective-permute-start.19
  88.6 0.0 collective-permute-done.16.first.refs_1_
  88.6 0.5 collective-permute-start.18
  89.1 2.0 %shard_map.61 = (f32[1024,256]{1,0:T(8,128)S(1)}, f32[512,256]{1,0:T(8,128)S(1)}) custom-call(bf16[2,256,256]{2,1,0:T(8,128)(2,1)S(1)} %shard_map.60.own.refs_0_, bf16[2,256,256]{2,1,0:T(8,128)(2,1)S(1)} %collective-permute-done.16.first.refs_1_, bf16[2,256,256]{2,1,0:T(8,128)(2,1)S(1)} %fusion.second.refs_2_, bf16[3,3,512,512]{3,2,1,0:T(8,128)(2,1)S(1)} %bitcast.16), custom_call_target="tpu_custom_call" | custom-call | flops 1811939328 | bytes 1048576 | tf_op jit(solution)/shard_map/pallas_call | solution.py:205
  91.1 0.0 collective-permute-done.19.refs_7_
  91.2 0.0 collective-permute-done.17.refs_5_
  91.2 0.0 collective-permute-done.18.refs_6_
  91.2 4.9 %shard_map.62 = bf16[3,2,256,256]{3,2,1,0:T(8,128)(2,1)} custom-call(bf16[2,256,256]{2,1,0:T(8,128)(2,1)S(1)} %shard_map.60.own.refs_0_, bf16[2,256,256]{2,1,0:T(8,128)(2,1)S(1)} %collective-permute-done.16.first.refs_1_, bf16[2,256,256]{2,1,0:T(8,128)(2,1)S(1)} %fusion.second.refs_2_, f32[1024,256]{1,0:T(8,128)S(1)} %get-tuple-element.23.refs_3_, ...), custom_call_target="tpu_custom_call" | custom-call | flops 3019898880 | bytes 1048576 | tf_op jit(solution)/shard_map/pallas_call | solution.py:231
  (6 shorter events, 0.1 us)
Async XLA Ops:
  0.0 26.7 %copy-start.2 = (bf16[3,2,256,256]{3,2,1,0:T(8,128)(2,1)S(1)}, bf16[3,2,256,256]{3,2,1,0:T(8,128)(2,1)}, u32[]{:S(2)}) copy-start(bf16[3,2,256,256]{3,2,1,0:T(8,128)(2,1)} %param.5) | copy-start | bytes 2359300
  0.0 26.7 %copy-start.1 = (bf16[1,3,3,512,256]{4,3,2,1,0:T(8,128)(2,1)S(1)}, bf16[1,3,3,512,256]{4,3,2,1,0:T(8,128)(2,1)}, u32[]{:S(2)}) copy-start(bf16[1,3,3,512,256]{4,3,2,1,0:T(8,128)(2,1)} %param.8) | copy-start | bytes 7077892
  1.2 15.8 %copy-start.4 = (bf16[2,256,256]{2,1,0:T(8,128)(2,1)}, bf16[2,256,256]{2,1,0:T(8,128)(2,1)S(1)}, u32[]{:S(2)}) copy-start(bf16[2,256,256]{2,1,0:T(8,128)(2,1)S(1)} %bitcast_select_fusion.own.refs_8_) | copy-start | bytes 786436
  1.2 15.8 %collective-permute-start = (bf16[2,256,256]{2,1,0:T(8,128)(2,1)S(1)}, bf16[2,256,256]{2,1,0:T(8,128)(2,1)S(1)}, u32[]{:S(2)}, u32[]{:S(2)}) collective-permute-start(bf16[2,256,256]{2,1,0:T(8,128)(2,1)S(1)} %bitcast_select_fusion.own.refs_8_), channel_id=1, source_target_pairs={{0,1},{1,0},{2,3},{3,2},{4,5},{5,4},{6,7},{7,6},{8,9},{9,8},{10,11... | collective-permute-start | bytes 786440 | tf_op jit(solution)/shard_map/ppermute | solution.py:252
  3.0 16.0 %collective-permute-start.1 = (bf16[2,256,256]{2,1,0:T(8,128)(2,1)S(1)}, bf16[2,256,256]{2,1,0:T(8,128)(2,1)}, u32[]{:S(2)}, u32[]{:S(2)}) collective-permute-start(bf16[2,256,256]{2,1,0:T(8,128)(2,1)S(1)} %bitcast_select_fusion.own.refs_8_), channel_id=1, source_target_pairs={{1,2},{2,1},{3,4},{4,3},{5,6},{6,5},{7,8},{8,7},{9,10},{10,9},{11,... | collective-permute-start | bytes 786440 | tf_op jit(solution)/shard_map/ppermute | solution.py:252
  13.7 8.1 %collective-permute-start.2 = (bf16[2,256,256]{2,1,0:T(8,128)(2,1)}, bf16[2,256,256]{2,1,0:T(8,128)(2,1)}, u32[]{:S(2)}, u32[]{:S(2)}) collective-permute-start(bf16[2,256,256]{2,1,0:T(8,128)(2,1)} %select_bitcast_fusion), channel_id=1, source_target_pairs={{0,1},{1,0},{2,3},{3,2},{4,5},{5,4},{6,7},{7,6},{8,9},{9,8},{10,11... | collective-permute-start | bytes 786440 | tf_op jit(solution)/shard_map/ppermute | solution.py:252
  13.7 13.0 %collective-permute-start.3 = (bf16[2,256,256]{2,1,0:T(8,128)(2,1)}, bf16[2,256,256]{2,1,0:T(8,128)(2,1)}, u32[]{:S(2)}, u32[]{:S(2)}) collective-permute-start(bf16[2,256,256]{2,1,0:T(8,128)(2,1)} %select_bitcast_fusion), channel_id=1, source_target_pairs={{1,2},{2,1},{3,4},{4,3},{5,6},{6,5},{7,8},{8,7},{9,10},{10,9},{11,... | collective-permute-start | bytes 786440 | tf_op jit(solution)/shard_map/ppermute | solution.py:252
  17.1 9.6 %collective-permute-start.4 = (bf16[2,256,256]{2,1,0:T(8,128)(2,1)S(1)}, bf16[2,256,256]{2,1,0:T(8,128)(2,1)}, u32[]{:S(2)}, u32[]{:S(2)}) collective-permute-start(bf16[2,256,256]{2,1,0:T(8,128)(2,1)S(1)} %collective-permute-done.first.refs_1_.refs_9_), channel_id=1, source_target_pairs={{0,128},{128,0},{1,129},{129,1},{2,130},{130,2},{3,131},{131,3},{4... | collective-permute-start | bytes 786440 | tf_op jit(solution)/shard_map/ppermute | solution.py:267
  18.9 7.7 %collective-permute-start.5 = (bf16[2,256,256]{2,1,0:T(8,128)(2,1)}, bf16[2,256,256]{2,1,0:T(8,128)(2,1)}, u32[]{:S(2)}, u32[]{:S(2)}) collective-permute-start(bf16[2,256,256]{2,1,0:T(8,128)(2,1)} %collective-permute-done.1.second.refs_2_.refs_10_), channel_id=1, source_target_pairs={{0,128},{128,0},{1,129},{129,1},{2,130},{130,2},{3,131},{131,3},{4... | collective-permute-start | bytes 786440 | tf_op jit(solution)/shard_map/ppermute | solution.py:267
  19.3 7.4 %copy-start = (bf16[1,3,3,512,512]{4,3,2,1,0:T(8,128)(2,1)S(1)}, bf16[1,3,3,512,512]{4,3,2,1,0:T(8,128)(2,1)}, u32[]{:S(2)}) copy-start(bf16[1,3,3,512,512]{4,3,2,1,0:T(8,128)(2,1)} %param.7) | copy-start | bytes 14155780
  19.3 7.4 %copy-start.3 = (bf16[1,2,256,256]{3,2,1,0:T(8,128)(2,1)S(1)}, bf16[1,2,256,256]{3,2,1,0:T(8,128)(2,1)}, u32[]{:S(2)}) copy-start(bf16[1,2,256,256]{3,2,1,0:T(8,128)(2,1)} %param.6) | copy-start | bytes 786436
  19.3 1.1 %copy-start.5 = (bf16[2,256,256]{2,1,0:T(8,128)(2,1)S(1)}, bf16[2,256,256]{2,1,0:T(8,128)(2,1)}, u32[]{:S(2)}) copy-start(bf16[2,256,256]{2,1,0:T(8,128)(2,1)} %copy-done.4) | copy-start | bytes 786436
  20.4 6.4 %copy-start.6 = (f32[1,768]{1,0:T(1,128)S(1)}, f32[1,768]{1,0:T(1,128)}, u32[]{:S(2)}) copy-start(f32[1,768]{1,0:T(1,128)} %refs_10_.1) | copy-start | bytes 9220
  27.9 17.6 %collective-permute-start.6 = (bf16[2,256,256]{2,1,0:T(8,128)(2,1)S(1)}, bf16[2,256,256]{2,1,0:T(8,128)(2,1)S(1)}, u32[]{:S(2)}, u32[]{:S(2)}) collective-permute-start(bf16[2,256,256]{2,1,0:T(8,128)(2,1)S(1)} %shard_map.56.own.refs_0_.refs_11_), channel_id=1, source_target_pairs={{0,1},{1,0},{2,3},{3,2},{4,5},{5,4},{6,7},{7,6},{8,9},{9,8},{10,11... | collective-permute-start | bytes 786440 | tf_op jit(solution)/shard_map/ppermute | solution.py:252
  38.2 10.4 %collective-permute-start.7 = (bf16[2,256,256]{2,1,0:T(8,128)(2,1)S(1)}, bf16[2,256,256]{2,1,0:T(8,128)(2,1)S(1)}, u32[]{:S(2)}, u32[]{:S(2)}) collective-permute-start(bf16[2,256,256]{2,1,0:T(8,128)(2,1)S(1)} %shard_map.56.own.refs_0_.refs_11_), channel_id=1, source_target_pairs={{0,128},{128,0},{1,129},{129,1},{2,130},{130,2},{3,131},{131,3},{4... | collective-permute-start | bytes 786440 | tf_op jit(solution)/shard_map/ppermute | solution.py:267
  45.4 3.1 %collective-permute-start.9 = (bf16[2,256,256]{2,1,0:T(8,128)(2,1)S(1)}, bf16[2,256,256]{2,1,0:T(8,128)(2,1)S(1)}, u32[]{:S(2)}, u32[]{:S(2)}) collective-permute-start(bf16[2,256,256]{2,1,0:T(8,128)(2,1)S(1)} %fusion.2.second.refs_2_), channel_id=1, source_target_pairs={{0,128},{128,0},{1,129},{129,1},{2,130},{130,2},{3,131},{131,3},{4... | collective-permute-start | bytes 786440 | tf_op jit(solution)/shard_map/ppermute | solution.py:267
  45.5 3.1 %collective-permute-start.8 = (bf16[2,256,256]{2,1,0:T(8,128)(2,1)S(1)}, bf16[2,256,256]{2,1,0:T(8,128)(2,1)S(1)}, u32[]{:S(2)}, u32[]{:S(2)}) collective-permute-start(bf16[2,256,256]{2,1,0:T(8,128)(2,1)S(1)} %collective-permute-done.6.first.refs_1_), channel_id=1, source_target_pairs={{0,128},{128,0},{1,129},{129,1},{2,130},{130,2},{3,131},{131,3},{4... | collective-permute-start | bytes 786440 | tf_op jit(solution)/shard_map/ppermute | solution.py:267
  46.0 24.5 %collective-permute-start.11 = (bf16[2,256,256]{2,1,0:T(8,128)(2,1)}, bf16[2,256,256]{2,1,0:T(8,128)(2,1)S(1)}, u32[]{:S(2)}, u32[]{:S(2)}) collective-permute-start(bf16[2,256,256]{2,1,0:T(8,128)(2,1)} %collective-permute-done.2.refs_6_), channel_id=1, source_target_pairs={{0,128},{128,0},{1,129},{129,1},{2,130},{130,2},{3,131},{131,3},{4... | collective-permute-start | bytes 786440 | tf_op jit(solution)/shard_map/ppermute | solution.py:267
  46.1 24.4 %collective-permute-start.12 = (bf16[2,256,256]{2,1,0:T(8,128)(2,1)}, bf16[2,256,256]{2,1,0:T(8,128)(2,1)S(1)}, u32[]{:S(2)}, u32[]{:S(2)}) collective-permute-start(bf16[2,256,256]{2,1,0:T(8,128)(2,1)} %collective-permute-done.3.refs_7_), channel_id=1, source_target_pairs={{0,128},{128,0},{1,129},{129,1},{2,130},{130,2},{3,131},{131,3},{4... | collective-permute-start | bytes 786440 | tf_op jit(solution)/shard_map/ppermute | solution.py:267
  54.0 13.9 %collective-permute-start.10 = (bf16[2,256,256]{2,1,0:T(8,128)(2,1)S(1)}, bf16[2,256,256]{2,1,0:T(8,128)(2,1)S(1)}, u32[]{:S(2)}, u32[]{:S(2)}) collective-permute-start(bf16[2,256,256]{2,1,0:T(8,128)(2,1)S(1)} %shard_map.58.own.refs_0_.refs_12_), channel_id=1, source_target_pairs={{0,1},{1,0},{2,3},{3,2},{4,5},{5,4},{6,7},{7,6},{8,9},{9,8},{10,11... | collective-permute-start | bytes 786440 | tf_op jit(solution)/shard_map/ppermute | solution.py:252
  66.9 3.6 %collective-permute-start.13 = (bf16[2,256,256]{2,1,0:T(8,128)(2,1)S(1)}, bf16[2,256,256]{2,1,0:T(8,128)(2,1)S(1)}, u32[]{:S(2)}, u32[]{:S(2)}) collective-permute-start(bf16[2,256,256]{2,1,0:T(8,128)(2,1)S(1)} %shard_map.58.own.refs_0_.refs_12_), channel_id=1, source_target_pairs={{0,128},{128,0},{1,129},{129,1},{2,130},{130,2},{3,131},{131,3},{4... | collective-permute-start | bytes 786440 | tf_op jit(solution)/shard_map/ppermute | solution.py:267
  67.8 2.7 %collective-permute-start.15 = (bf16[2,256,256]{2,1,0:T(8,128)(2,1)S(1)}, bf16[2,256,256]{2,1,0:T(8,128)(2,1)S(1)}, u32[]{:S(2)}, u32[]{:S(2)}) collective-permute-start(bf16[2,256,256]{2,1,0:T(8,128)(2,1)S(1)} %fusion.1.second.refs_2_), channel_id=1, source_target_pairs={{0,128},{128,0},{1,129},{129,1},{2,130},{130,2},{3,131},{131,3},{4... | collective-permute-start | bytes 786440 | tf_op jit(solution)/shard_map/ppermute | solution.py:267
  67.9 2.6 %collective-permute-start.14 = (bf16[2,256,256]{2,1,0:T(8,128)(2,1)S(1)}, bf16[2,256,256]{2,1,0:T(8,128)(2,1)S(1)}, u32[]{:S(2)}, u32[]{:S(2)}) collective-permute-start(bf16[2,256,256]{2,1,0:T(8,128)(2,1)S(1)} %collective-permute-done.10.first.refs_1_), channel_id=1, source_target_pairs={{0,128},{128,0},{1,129},{129,1},{2,130},{130,2},{3,131},{131,3},{4... | collective-permute-start | bytes 786440 | tf_op jit(solution)/shard_map/ppermute | solution.py:267
  74.8 13.9 %collective-permute-start.16 = (bf16[2,256,256]{2,1,0:T(8,128)(2,1)S(1)}, bf16[2,256,256]{2,1,0:T(8,128)(2,1)S(1)}, u32[]{:S(2)}, u32[]{:S(2)}) collective-permute-start(bf16[2,256,256]{2,1,0:T(8,128)(2,1)S(1)} %shard_map.60.own.refs_0_), channel_id=1, source_target_pairs={{0,1},{1,0},{2,3},{3,2},{4,5},{5,4},{6,7},{7,6},{8,9},{9,8},{10,11... | collective-permute-start | bytes 786440 | tf_op jit(solution)/shard_map/ppermute | solution.py:252
  87.5 3.6 %collective-permute-start.17 = (bf16[2,256,256]{2,1,0:T(8,128)(2,1)S(1)}, bf16[2,256,256]{2,1,0:T(8,128)(2,1)S(1)}, u32[]{:S(2)}, u32[]{:S(2)}) collective-permute-start(bf16[2,256,256]{2,1,0:T(8,128)(2,1)S(1)} %shard_map.60.own.refs_0_), channel_id=1, source_target_pairs={{0,128},{128,0},{1,129},{129,1},{2,130},{130,2},{3,131},{131,3},{4... | collective-permute-start | bytes 786440 | tf_op jit(solution)/shard_map/ppermute | solution.py:267
  88.5 2.6 %collective-permute-start.19 = (bf16[2,256,256]{2,1,0:T(8,128)(2,1)S(1)}, bf16[2,256,256]{2,1,0:T(8,128)(2,1)S(1)}, u32[]{:S(2)}, u32[]{:S(2)}) collective-permute-start(bf16[2,256,256]{2,1,0:T(8,128)(2,1)S(1)} %fusion.second.refs_2_), channel_id=1, source_target_pairs={{0,128},{128,0},{1,129},{129,1},{2,130},{130,2},{3,131},{131,3},{4... | collective-permute-start | bytes 786440 | tf_op jit(solution)/shard_map/ppermute | solution.py:267
  88.6 2.5 %collective-permute-start.18 = (bf16[2,256,256]{2,1,0:T(8,128)(2,1)S(1)}, bf16[2,256,256]{2,1,0:T(8,128)(2,1)S(1)}, u32[]{:S(2)}, u32[]{:S(2)}) collective-permute-start(bf16[2,256,256]{2,1,0:T(8,128)(2,1)S(1)} %collective-permute-done.16.first.refs_1_), channel_id=1, source_target_pairs={{0,128},{128,0},{1,129},{129,1},{2,130},{130,2},{3,131},{131,3},{4... | collective-permute-start | bytes 786440 | tf_op jit(solution)/shard_map/ppermute | solution.py:267

commit v5 on v4

--- a/solution.py
+++ b/solution.py
@@ -8,6 +8,7 @@
 from jax.sharding import PartitionSpec as P
 
 VMEM_BYTES = 16 * 1024 * 1024
+SMALL_BYTES = 8 * 1024 * 1024
 
 
 def widen(target, row, value):
@@ -57,24 +58,42 @@
     return lax.rem(lax.axis_index("rows"), 2) == 1
 
 
-def early_kernel(lag, own, first, second, wg, pre_r, pre_u, wide, *streamed):
+def pick_kernel(initial, frames, out, ready):
+    layer = lax.axis_index("layer")
+    for wanted, source in enumerate((initial, frames.at[0:2])):
+        @pl.when(layer == wanted)
+        def _():
+            copy = pltpu.make_async_copy(source, out, ready)
+            copy.start()
+            copy.wait()
+
+
+def stage_kernel(frames, weight, out, state_weight, ready):
+    channels = weight.shape[2] // 2
+    load = pltpu.make_async_copy(
+        weight.at[:, :, channels : 2 * channels], state_weight, ready.at[0]
+    )
+    for wanted in range(2):
+        @pl.when(lax.axis_index("layer") == wanted)
+        def _():
+            copy = pltpu.make_async_copy(
+                frames.at[2 * wanted + 2 : 2 * wanted + 4], out, ready.at[1]
+            )
+            copy.start()
+            load.start()
+            copy.wait()
+            load.wait()
+
+
+def early_kernel(lag, own, first, second, wg, pre_r, pre_u, wide):
     cols, channels = own.shape[1:]
 
     @pl.when(active(lag, lax.axis_index("layer")))
     def _():
-        lo = channels
-        weight = wg
-        if streamed:
-            weight, ready = streamed
-            copy = pltpu.make_async_copy(wg.at[:, :, channels : 2 * channels], weight, ready)
-            copy.start()
-            lo = 0
         fill(wide, own, first, second, is_odd())
-        if streamed:
-            copy.wait()
-        inner = product(taps(wide, 1, 2), columns(weight, lo, channels, 0, 2 * channels))
+        inner = product(taps(wide, 1, 2), columns(wg, 0, channels, 0, 2 * channels))
         edges = jnp.concatenate([taps(wide, 0, 1), taps(wide, 3, 1)], 0)
-        outer = product(edges, columns(weight, lo, channels, channels, 2 * channels))
+        outer = product(edges, columns(wg, 0, channels, channels, 2 * channels))
         pre_u[...] = inner[:, 0:channels]
         pre_r[cols : 3 * cols] = inner[:, channels : 2 * channels]
         pre_r[0:cols] = outer[0:cols]
@@ -179,7 +198,6 @@
 
 HELD = pl.BlockSpec(memory_space=pltpu.VMEM)
 ANYWHERE = pl.BlockSpec(memory_space=pl.ANY)
-OUTSIDE = pl.BlockSpec(memory_space=pltpu.HBM)
 
 
 def cost(units, cols, channels):
@@ -192,22 +210,45 @@
     return pltpu.VMEM((rows, cols, 3 * channels), jnp.bfloat16)
 
 
+def outside(array):
+    return pltpu.with_memory_space_constraint(array, pltpu.HBM)
+
+
+def pick(initial, rows):
+    return pl.pallas_call(
+        pick_kernel,
+        out_shape=jax.ShapeDtypeStruct(initial.shape, initial.dtype),
+        in_specs=[ANYWHERE] * 2,
+        out_specs=HELD,
+        scratch_shapes=[pltpu.SemaphoreType.DMA],
+        compiler_params=pltpu.CompilerParams(vmem_limit_bytes=SMALL_BYTES),
+    )(outside(initial), outside(rows))
+
+
+def stage(rows, wg):
+    _, cols, channels = rows.shape
+    return pl.pallas_call(
+        stage_kernel,
+        out_shape=[
+            jax.ShapeDtypeStruct((2, cols, channels), rows.dtype),
+            jax.ShapeDtypeStruct((3, 3, channels, 2 * channels), wg.dtype),
+        ],
+        in_specs=[ANYWHERE] * 2,
+        out_specs=[HELD] * 2,
+        scratch_shapes=[pltpu.SemaphoreType.DMA((2,))],
+        compiler_params=pltpu.CompilerParams(vmem_limit_bytes=SMALL_BYTES),
+    )(outside(rows), outside(wg))
+
+
 def early(lag, state, wg):
     _, cols, channels = state[0].shape
     pre = lambda n: jax.ShapeDtypeStruct((n * cols, channels), jnp.float32)
-    scratch = [wide_rows(6, cols, channels)]
-    if lag == 0:
-        scratch += [
-            pltpu.VMEM((3, 3, channels, 2 * channels), jnp.bfloat16), pltpu.SemaphoreType.DMA
-        ]
-    if lag == 0:
-        wg = pltpu.with_memory_space_constraint(wg, pltpu.HBM)
     return pl.pallas_call(
         functools.partial(early_kernel, lag),
         out_shape=[pre(4), pre(2)],
-        in_specs=[HELD] * 3 + [OUTSIDE if lag == 0 else HELD],
+        in_specs=[HELD] * 4,
         out_specs=[HELD] * 2,
-        scratch_shapes=scratch,
+        scratch_shapes=[wide_rows(6, cols, channels)],
         compiler_params=pltpu.CompilerParams(vmem_limit_bytes=VMEM_BYTES),
         cost_estimate=cost(6, cols, channels),
     )(*state, wg)
@@ -252,14 +293,13 @@
     return lax.ppermute(field, "rows", route)
 
 
-def gathered_swap(field, strip):
+def gathered_swap(field, odd, inner):
     count = lax.axis_size("rows")
     groups = [[0, count], [count - 1, 2 * count - 1]]
     for layer in range(2):
         groups += [[layer * count + low, layer * count + low + 1] for low in range(1, count - 1, 2)]
     both = lax.all_gather(field, ("layer", "rows"), axis_index_groups=groups)
-    inner = jnp.logical_and(strip > 0, strip < count - 1)
-    partner = jnp.where(lax.rem(strip, 2) == 1, both[1], both[0])
+    partner = jnp.where(odd, both[1], both[0])
     return jnp.where(inner, partner, jnp.zeros_like(partner))
 
 
@@ -268,15 +308,17 @@
 
 
 def shards(frames, initial_state, w_gates, w_cand, biases):
-    layer = lax.axis_index("layer")
     strip = lax.axis_index("rows")
     wg, wc = w_gates[0], w_cand[0]
     hidden = initial_state[0]
     rows = frames.reshape((6,) + hidden.shape[1:])
 
-    field = jnp.where(layer == 0, hidden, frames[0])
+    odd = lax.rem(strip, 2) == 1
+    inner = jnp.logical_and(strip > 0, strip < lax.axis_size("rows") - 1)
+    field = pick(hidden, rows)
+    field, odd, inner = lax.optimization_barrier((field, odd, inner))
     first, second = pair_swap(field, 0), pair_swap(field, 1)
-    later_field = jnp.where(layer == 0, frames[1], frames[2])
+    later_field, wg_state = stage(rows, wg)
     late_first, late_second = pair_swap(later_field, 0), pair_swap(later_field, 1)
     halos = [
         (across(first), across(second)),
@@ -284,17 +326,17 @@
         (across(late_first), across(late_second)),
     ]
     below = (field, first, second)
-    pre = early(0, below, wg)
+    pre = early(0, below, wg_state)
     pre = lax.optimization_barrier((*pre, late_first, late_second))[0:2]
     hidden = late(0, (hidden, first, second), pre, (rows, *halos[0]), below, wg, wc, biases)
     states = [hidden]
     for step in range(1, 4):
         first = pair_swap(hidden, 0)
         own_below = across(hidden)
-        second = gathered_swap(hidden, strip)
+        second = gathered_swap(hidden, odd, inner)
         below = (own_below, across(first), across(second))
         state = (hidden, first, second)
-        pre = early(step, state, wg)
+        pre = early(step, state, wg_state)
         if step == 3:
             return last(state, pre, below, wg, wc, biases, states[0:2])[None]
         hidden = late(step, state, pre, (rows, *halos[step]), below, wg, wc, biases)

time: 96.5 us -> 94.2 us (0.976)
  other arithmetic: 3.08 us -> 0.09 us
  waiting for transfers between devices: 4.9 us -> 7.34 us
  local copies, waits for them, and re-layouts: 1.12 us -> 0.03 us
    select_n x2 -> x0, other arithmetic: 2.99 us -> none  [the longest x1 1.78 us: shards(): later_field = jnp.where(layer == 0, frames[1], frames[2])]
    pallas_call x0 -> x2, Pallas kernels: none -> 2.94 us  [the longest x1 1.93 us: stage(): pl.pallas_call(stage_kernel, out_shape=[jax.ShapeDtypeStruct((2, cols, ch...]
    ppermute x7, waiting for transfers between devices: 4.86 us -> 7.31 us  [pair_swap(): return lax.ppermute(field, 'rows', route)]
    pallas_call x3, Pallas kernels: 10.9 us -> 8.91 us  [late(): pl.pallas_call(functools.partial(late_kernel, lag), out_shape=jax.ShapeDt...]
    pallas_call x4, Pallas kernels: 7.53 us -> 6.14 us  [early(): pl.pallas_call(functools.partial(early_kernel, lag), out_shape=[pre(4), p...]
    unnamed x14 -> x12, local copies, waits for them, and re-layouts: 1.12 us -> 0.03 us
  transfers between devices with their start and end apart: 20 -> 20, of which waited for: 1 -> 2; matrix products, arithmetic and copies ran while one was open for 2% -> 0% of each run, Pallas kernels for 14% -> 14%
where the time goes in v5:
time: 94.2 us; the launch traced here: 94 us
  blocking collectives  35.7 us (38%)
  starting transfers between devices  27.5 us (29%)
  Pallas kernels  22.9 us (24%)
  waiting for transfers between devices  7.34 us (8%)
    all_gather x3, blocking collectives, gathered_swap(): both = lax.all_gather(field, ('layer', 'rows'), axis_index_groups=groups)  35.7 us
    ppermute x7, starting transfers between devices, pair_swap(): return lax.ppermute(field, 'rows', route)  14.4 us
    ppermute x13, starting transfers between devices, across(): return lax.ppermute(field, 'layer', [(0, 1), (1, 0)])  13.1 us
    pallas_call x3, Pallas kernels, late(): pl.pallas_call(functools.partial(late_kernel, lag), out_shape=jax.ShapeDt...  8.91 us
    ppermute x7, waiting for transfers between devices, pair_swap(): return lax.ppermute(field, 'rows', route)  7.31 us
    pallas_call x4, Pallas kernels, early(): pl.pallas_call(functools.partial(early_kernel, lag), out_shape=[pre(4), p...  6.14 us
    pallas_call x1, Pallas kernels, last(): pl.pallas_call(last_kernel, out_shape=jax.ShapeDtypeStruct((3, 2, cols, c...  4.86 us
    pallas_call x1, Pallas kernels, stage(): pl.pallas_call(stage_kernel, out_shape=[jax.ShapeDtypeStruct((2, cols, ch...  1.93 us
  transfers between devices with their start and end apart: 20, of which 2 were waited for; matrix products, arithmetic and copies ran while one was open for 0% of the time, Pallas kernels for 14%

profile of v5, /device:TPU:25, one launch (start us, length us, event | category | flops | bytes accessed | tf_op | source)
XLA Modules:
  0.0 94.0 jit_solution(10419631863543087904)
XLA Ops:
  0.0 0.0 slice-start
  0.0 1.0 %shard_map.55.own.refs_8_ = bf16[2,256,256]{2,1,0:T(8,128)(2,1)S(1)} custom-call(bf16[2,256,256]{2,1,0:T(8,128)(2,1)} %bitcast.21, bf16[6,256,256]{2,1,0:T(8,128)(2,1)} %bitcast.16), custom_call_target="tpu_custom_call" | custom-call | tf_op jit(solution)/shard_map/pallas_call | solution.py:218
  1.0 1.7 %collective-permute-start = (bf16[2,256,256]{2,1,0:T(8,128)(2,1)S(1)}, bf16[2,256,256]{2,1,0:T(8,128)(2,1)S(1)}, u32[]{:S(2)}, u32[]{:S(2)}) collective-permute-start(bf16[2,256,256]{2,1,0:T(8,128)(2,1)S(1)} %shard_map.55.own.refs_8_), channel_id=1, source_target_pairs={{0,1},{1,0},{2,3},{3,2},{4,5},{5,4},{6,7},{7,6},{8,9},{9,8},{10,11... | collective-permute-start | bytes 786440 | tf_op jit(solution)/shard_map/ppermute | solution.py:293
  2.8 8.9 %collective-permute-start.1 = (bf16[2,256,256]{2,1,0:T(8,128)(2,1)S(1)}, bf16[2,256,256]{2,1,0:T(8,128)(2,1)S(1)}, u32[]{:S(2)}, u32[]{:S(2)}) collective-permute-start(bf16[2,256,256]{2,1,0:T(8,128)(2,1)S(1)} %shard_map.55.own.refs_8_), channel_id=1, source_target_pairs={{1,2},{2,1},{3,4},{4,3},{5,6},{6,5},{7,8},{8,7},{9,10},{10,9},{11,... | collective-permute-start | bytes 786440 | tf_op jit(solution)/shard_map/ppermute | solution.py:293
  11.7 0.0 slice-start.1
  11.7 1.9 %shard_map.56 = (bf16[2,256,256]{2,1,0:T(8,128)(2,1)S(1)}, bf16[3,3,256,512]{3,2,1,0:T(8,128)(2,1)S(1)}) custom-call(bf16[6,256,256]{2,1,0:T(8,128)(2,1)} %bitcast.17, bf16[3,3,512,512]{3,2,1,0:T(8,128)(2,1)} %bitcast.5), custom_call_target="tpu_custom_call" | custom-call | tf_op jit(solution)/shard_map/pallas_call | solution.py:230
  13.7 0.1 collective-permute-start.2
  13.8 3.3 %collective-permute-start.3 = (bf16[2,256,256]{2,1,0:T(8,128)(2,1)S(1)}, bf16[2,256,256]{2,1,0:T(8,128)(2,1)S(1)}, u32[]{:S(2)}, u32[]{:S(2)}) collective-permute-start(bf16[2,256,256]{2,1,0:T(8,128)(2,1)S(1)} %get-tuple-element.24), channel_id=1, source_target_pairs={{1,2},{2,1},{3,4},{4,3},{5,6},{6,5},{7,8},{8,7},{9,10},{10,9},{11,... | collective-permute-start | bytes 786440 | tf_op jit(solution)/shard_map/ppermute | solution.py:293
  17.1 0.0 collective-permute-done.first.refs_1_.refs_9_
  17.1 1.9 %collective-permute-start.4 = (bf16[2,256,256]{2,1,0:T(8,128)(2,1)S(1)}, bf16[2,256,256]{2,1,0:T(8,128)(2,1)S(1)}, u32[]{:S(2)}, u32[]{:S(2)}) collective-permute-start(bf16[2,256,256]{2,1,0:T(8,128)(2,1)S(1)} %collective-permute-done.first.refs_1_.refs_9_), channel_id=1, source_target_pairs={{0,128},{128,0},{1,129},{129,1},{2,130},{130,2},{3,131},{131,3},{4... | collective-permute-start | bytes 786440 | tf_op jit(solution)/shard_map/ppermute | solution.py:307
  19.0 0.0 collective-permute-done.1.second.refs_2_.refs_10_
  19.0 0.1 collective-permute-start.5
  19.1 0.0 copy-start
  19.1 0.0 copy-start.1
  19.1 0.0 copy-start.2
  19.1 0.0 copy-start.3
  19.1 1.2 %collective-permute-done.2.refs_6_ = bf16[2,256,256]{2,1,0:T(8,128)(2,1)S(1)} collective-permute-done((bf16[2,256,256]{2,1,0:T(8,128)(2,1)S(1)}, bf16[2,256,256]{2,1,0:T(8,128)(2,1)S(1)}, u32[]{:S(2)}, u32[]{:S(2)}) %collective-permute-start.2) | collective-permute-done | bytes 262176 | tf_op jit(solution)/shard_map/ppermute | solution.py:293
  20.3 6.1 %collective-permute-done.3.refs_7_ = bf16[2,256,256]{2,1,0:T(8,128)(2,1)S(1)} collective-permute-done((bf16[2,256,256]{2,1,0:T(8,128)(2,1)S(1)}, bf16[2,256,256]{2,1,0:T(8,128)(2,1)S(1)}, u32[]{:S(2)}, u32[]{:S(2)}) %collective-permute-start.3) | collective-permute-done | bytes 262176 | tf_op jit(solution)/shard_map/ppermute | solution.py:293
  26.4 0.0 collective-permute-done.4.refs_6_
  26.4 0.0 collective-permute-done.5.refs_7_
  26.4 0.0 slice-done
  26.4 0.0 slice-done.1
  26.5 0.0 copy-done
  26.5 0.0 copy-done.1
  26.5 0.0 copy-done.2
  26.5 0.0 copy-done.3
  26.5 0.1 collective-permute-start.6
  26.6 10.1 %all-gather = bf16[4,256,256]{2,1,0:T(8,128)(2,1)S(1)} all-gather(bf16[2,256,256]{2,1,0:T(8,128)(2,1)S(1)} %shard_map.58.own.refs_0_.refs_11_), channel_id=2, replica_groups={{0,128},{127,255},{1,2},{3,4},{5,6},{7,8},{9,10},{11,12},{13,14},{15,16..., dimensions={0}, use_global_device_ids=true | all-gather | bytes 786432 | tf_op jit(solution)/shard_map/all_gather | solution.py:301
  36.8 7.2 %collective-permute-start.7 = (bf16[2,256,256]{2,1,0:T(8,128)(2,1)S(1)}, bf16[2,256,256]{2,1,0:T(8,128)(2,1)S(1)}, u32[]{:S(2)}, u32[]{:S(2)}) collective-permute-start(bf16[2,256,256]{2,1,0:T(8,128)(2,1)S(1)} %shard_map.58.own.refs_0_.refs_11_), channel_id=1, source_target_pairs={{0,128},{128,0},{1,129},{129,1},{2,130},{130,2},{3,131},{131,3},{4... | collective-permute-start | bytes 786440 | tf_op jit(solution)/shard_map/ppermute | solution.py:307
  44.0 0.1 collective-permute-start.9
  44.1 0.0 collective-permute-done.6.first.refs_1_
  44.1 0.5 collective-permute-start.8
  44.6 0.1 collective-permute-start.11
  44.7 0.4 collective-permute-start.12
  45.1 2.0 %shard_map.59 = (f32[1024,256]{1,0:T(8,128)S(1)}, f32[512,256]{1,0:T(8,128)S(1)}) custom-call(bf16[2,256,256]{2,1,0:T(8,128)(2,1)S(1)} %shard_map.58.own.refs_0_.refs_11_, bf16[2,256,256]{2,1,0:T(8,128)(2,1)S(1)} %collective-permute-done.6.first.refs_1_, bf16[2,256,256]{2,1,0:T(8,128)(2,1)S(1)} %fusion.2.second.refs_2_, ...), custom_call_target="tpu_custom_call" | custom-call | flops 1811939328 | bytes 1048576 | tf_op jit(solution)/shard_map/pallas_call | solution.py:246
  47.1 0.0 collective-permute-done.7.refs_8_
  47.1 0.0 collective-permute-done.9.refs_10_
  47.1 0.0 collective-permute-done.8.refs_9_
  47.1 4.6 %shard_map.60.own.refs_0_.refs_12_ = bf16[2,256,256]{2,1,0:T(8,128)(2,1)S(1)} custom-call(bf16[2,256,256]{2,1,0:T(8,128)(2,1)S(1)} %shard_map.58.own.refs_0_.refs_11_, bf16[2,256,256]{2,1,0:T(8,128)(2,1)S(1)} %collective-permute-done.6.first.refs_1_, bf16[2,256,256]{2,1,0:T(8,128)(2,1)S(1)} %fusion.2.second.refs_2_, ...), custom_call_target="tpu_custom_call" | custom-call | flops 3019898880 | bytes 1048576 | tf_op jit(solution)/shard_map/pallas_call | solution.py:259
  51.8 0.1 collective-permute-start.10
  51.9 12.8 %all-gather.1 = bf16[4,256,256]{2,1,0:T(8,128)(2,1)S(1)} all-gather(bf16[2,256,256]{2,1,0:T(8,128)(2,1)S(1)} %shard_map.60.own.refs_0_.refs_12_), channel_id=3, replica_groups={{0,128},{127,255},{1,2},{3,4},{5,6},{7,8},{9,10},{11,12},{13,14},{15,16..., dimensions={0}, use_global_device_ids=true | all-gather | bytes 786432 | tf_op jit(solution)/shard_map/all_gather | solution.py:301
  64.7 0.9 collective-permute-start.13
  65.6 0.1 collective-permute-start.15
  65.7 0.0 collective-permute-done.10.first.refs_1_
  65.7 0.5 collective-permute-start.14
  66.2 2.0 %shard_map.61 = (f32[1024,256]{1,0:T(8,128)S(1)}, f32[512,256]{1,0:T(8,128)S(1)}) custom-call(bf16[2,256,256]{2,1,0:T(8,128)(2,1)S(1)} %shard_map.60.own.refs_0_.refs_12_, bf16[2,256,256]{2,1,0:T(8,128)(2,1)S(1)} %collective-permute-done.10.first.refs_1_, bf16[2,256,256]{2,1,0:T(8,128)(2,1)S(1)} %fusion.1.second.refs_2_, ...), custom_call_target="tpu_custom_call" | custom-call | flops 1811939328 | bytes 1048576 | tf_op jit(solution)/shard_map/pallas_call | solution.py:246
  68.2 0.0 collective-permute-done.11.refs_6_
  68.2 0.0 collective-permute-done.12.refs_7_
  68.2 0.0 collective-permute-done.13.refs_8_
  68.2 0.0 collective-permute-done.15.refs_10_
  68.2 0.0 collective-permute-done.14.refs_9_
  68.3 4.2 %shard_map.62.own.refs_0_ = bf16[2,256,256]{2,1,0:T(8,128)(2,1)S(1)} custom-call(bf16[2,256,256]{2,1,0:T(8,128)(2,1)S(1)} %shard_map.60.own.refs_0_.refs_12_, bf16[2,256,256]{2,1,0:T(8,128)(2,1)S(1)} %collective-permute-done.10.first.refs_1_, bf16[2,256,256]{2,1,0:T(8,128)(2,1)S(1)} %fusion.1.second.refs_2_, f32[1024,256]{1,0:T(8,128)S(1)} %get-tuple-element.31.refs_3_, ...), custom_call_target="tpu_custom_call" | custom-call | flops 3019898880 | bytes 1048576 | tf_op jit(solution)/shard_map/pallas_call | solution.py:259
  72.5 0.1 collective-permute-start.16
  72.6 12.8 %all-gather.2 = bf16[4,256,256]{2,1,0:T(8,128)(2,1)S(1)} all-gather(bf16[2,256,256]{2,1,0:T(8,128)(2,1)S(1)} %shard_map.62.own.refs_0_), channel_id=4, replica_groups={{0,128},{127,255},{1,2},{3,4},{5,6},{7,8},{9,10},{11,12},{13,14},{15,16..., dimensions={0}, use_global_device_ids=true | all-gather | bytes 786432 | tf_op jit(solution)/shard_map/all_gather | solution.py:301
  85.4 0.9 collective-permute-start.17
  86.3 0.1 collective-permute-start.19
  86.4 0.0 collective-permute-done.16.first.refs_1_
  86.4 0.5 collective-permute-start.18
  86.9 2.0 %shard_map.63 = (f32[1024,256]{1,0:T(8,128)S(1)}, f32[512,256]{1,0:T(8,128)S(1)}) custom-call(bf16[2,256,256]{2,1,0:T(8,128)(2,1)S(1)} %shard_map.62.own.refs_0_, bf16[2,256,256]{2,1,0:T(8,128)(2,1)S(1)} %collective-permute-done.16.first.refs_1_, bf16[2,256,256]{2,1,0:T(8,128)(2,1)S(1)} %fusion.second.refs_2_, bf16[3,3,256,512]{3,2,1,0:T(8,128)(2,1)S(1)} %get-tuple-element.21.wg), custom_call_target="tpu_custom_call" | custom-call | flops 1811939328 | bytes 1048576 | tf_op jit(solution)/shard_map/pallas_call | solution.py:246
  88.9 0.0 collective-permute-done.17.refs_5_
  88.9 0.0 collective-permute-done.19.refs_7_
  88.9 0.0 collective-permute-done.18.refs_6_
  89.0 4.9 %shard_map.64 = bf16[3,2,256,256]{3,2,1,0:T(8,128)(2,1)} custom-call(bf16[2,256,256]{2,1,0:T(8,128)(2,1)S(1)} %shard_map.62.own.refs_0_, bf16[2,256,256]{2,1,0:T(8,128)(2,1)S(1)} %collective-permute-done.16.first.refs_1_, bf16[2,256,256]{2,1,0:T(8,128)(2,1)S(1)} %fusion.second.refs_2_, f32[1024,256]{1,0:T(8,128)S(1)} %get-tuple-element.33.refs_3_, ...), custom_call_target="tpu_custom_call" | custom-call | flops 3019898880 | bytes 1048576 | tf_op jit(solution)/shard_map/pallas_call | solution.py:272
  (6 shorter events, 0.1 us)
Async XLA Ops:
  0.0 26.4 %slice-start = ((s8[4718592]{0:T(1024)(128)(4,1)}), s8[524288]{0:T(1024)(128)(4,1)S(1)}, s32[]{:S(2)}) async-start(s8[4718592]{0:T(1024)(128)(4,1)} %bitcast.6), calls=%async_computation | async-start | bytes 1048576
  1.0 16.1 %collective-permute-start = (bf16[2,256,256]{2,1,0:T(8,128)(2,1)S(1)}, bf16[2,256,256]{2,1,0:T(8,128)(2,1)S(1)}, u32[]{:S(2)}, u32[]{:S(2)}) collective-permute-start(bf16[2,256,256]{2,1,0:T(8,128)(2,1)S(1)} %shard_map.55.own.refs_8_), channel_id=1, source_target_pairs={{0,1},{1,0},{2,3},{3,2},{4,5},{5,4},{6,7},{7,6},{8,9},{9,8},{10,11... | collective-permute-start | bytes 786440 | tf_op jit(solution)/shard_map/ppermute | solution.py:293
  2.8 16.2 %collective-permute-start.1 = (bf16[2,256,256]{2,1,0:T(8,128)(2,1)S(1)}, bf16[2,256,256]{2,1,0:T(8,128)(2,1)S(1)}, u32[]{:S(2)}, u32[]{:S(2)}) collective-permute-start(bf16[2,256,256]{2,1,0:T(8,128)(2,1)S(1)} %shard_map.55.own.refs_8_), channel_id=1, source_target_pairs={{1,2},{2,1},{3,4},{4,3},{5,6},{6,5},{7,8},{8,7},{9,10},{10,9},{11,... | collective-permute-start | bytes 786440 | tf_op jit(solution)/shard_map/ppermute | solution.py:293
  11.7 14.7 %slice-start.1 = ((s8[4718592]{0:T(1024)(128)(4,1)}), s8[4194304]{0:T(1024)(128)(4,1)S(1)}, s32[]{:S(2)}) async-start(s8[4718592]{0:T(1024)(128)(4,1)} %bitcast.6), calls=%async_computation.1 | async-start | bytes 8388608
  13.7 6.7 %collective-permute-start.2 = (bf16[2,256,256]{2,1,0:T(8,128)(2,1)S(1)}, bf16[2,256,256]{2,1,0:T(8,128)(2,1)S(1)}, u32[]{:S(2)}, u32[]{:S(2)}) collective-permute-start(bf16[2,256,256]{2,1,0:T(8,128)(2,1)S(1)} %get-tuple-element.24), channel_id=1, source_target_pairs={{0,1},{1,0},{2,3},{3,2},{4,5},{5,4},{6,7},{7,6},{8,9},{9,8},{10,11... | collective-permute-start | bytes 786440 | tf_op jit(solution)/shard_map/ppermute | solution.py:293
  13.8 12.7 %collective-permute-start.3 = (bf16[2,256,256]{2,1,0:T(8,128)(2,1)S(1)}, bf16[2,256,256]{2,1,0:T(8,128)(2,1)S(1)}, u32[]{:S(2)}, u32[]{:S(2)}) collective-permute-start(bf16[2,256,256]{2,1,0:T(8,128)(2,1)S(1)} %get-tuple-element.24), channel_id=1, source_target_pairs={{1,2},{2,1},{3,4},{4,3},{5,6},{6,5},{7,8},{8,7},{9,10},{10,9},{11,... | collective-permute-start | bytes 786440 | tf_op jit(solution)/shard_map/ppermute | solution.py:293
  17.1 9.3 %collective-permute-start.4 = (bf16[2,256,256]{2,1,0:T(8,128)(2,1)S(1)}, bf16[2,256,256]{2,1,0:T(8,128)(2,1)S(1)}, u32[]{:S(2)}, u32[]{:S(2)}) collective-permute-start(bf16[2,256,256]{2,1,0:T(8,128)(2,1)S(1)} %collective-permute-done.first.refs_1_.refs_9_), channel_id=1, source_target_pairs={{0,128},{128,0},{1,129},{129,1},{2,130},{130,2},{3,131},{131,3},{4... | collective-permute-start | bytes 786440 | tf_op jit(solution)/shard_map/ppermute | solution.py:307
  19.0 7.4 %collective-permute-start.5 = (bf16[2,256,256]{2,1,0:T(8,128)(2,1)S(1)}, bf16[2,256,256]{2,1,0:T(8,128)(2,1)S(1)}, u32[]{:S(2)}, u32[]{:S(2)}) collective-permute-start(bf16[2,256,256]{2,1,0:T(8,128)(2,1)S(1)} %collective-permute-done.1.second.refs_2_.refs_10_), channel_id=1, source_target_pairs={{0,128},{128,0},{1,129},{129,1},{2,130},{130,2},{3,131},{131,3},{4... | collective-permute-start | bytes 786440 | tf_op jit(solution)/shard_map/ppermute | solution.py:307
  19.1 7.4 %copy-start = (bf16[1,3,3,512,256]{4,3,2,1,0:T(8,128)(2,1)S(1)}, bf16[1,3,3,512,256]{4,3,2,1,0:T(8,128)(2,1)}, u32[]{:S(2)}) copy-start(bf16[1,3,3,512,256]{4,3,2,1,0:T(8,128)(2,1)} %param.8) | copy-start | bytes 7077892
  19.1 7.4 %copy-start.1 = (bf16[3,2,256,256]{3,2,1,0:T(8,128)(2,1)S(1)}, bf16[3,2,256,256]{3,2,1,0:T(8,128)(2,1)}, u32[]{:S(2)}) copy-start(bf16[3,2,256,256]{3,2,1,0:T(8,128)(2,1)} %param.5) | copy-start | bytes 2359300
  19.1 7.4 %copy-start.2 = (bf16[1,2,256,256]{3,2,1,0:T(8,128)(2,1)S(1)}, bf16[1,2,256,256]{3,2,1,0:T(8,128)(2,1)}, u32[]{:S(2)}) copy-start(bf16[1,2,256,256]{3,2,1,0:T(8,128)(2,1)} %param.6) | copy-start | bytes 786436
  19.1 7.4 %copy-start.3 = (f32[1,768]{1,0:T(1,128)S(1)}, f32[1,768]{1,0:T(1,128)}, u32[]{:S(2)}) copy-start(f32[1,768]{1,0:T(1,128)} %refs_10_.1) | copy-start | bytes 9220
  26.5 17.5 %collective-permute-start.6 = (bf16[2,256,256]{2,1,0:T(8,128)(2,1)S(1)}, bf16[2,256,256]{2,1,0:T(8,128)(2,1)S(1)}, u32[]{:S(2)}, u32[]{:S(2)}) collective-permute-start(bf16[2,256,256]{2,1,0:T(8,128)(2,1)S(1)} %shard_map.58.own.refs_0_.refs_11_), channel_id=1, source_target_pairs={{0,1},{1,0},{2,3},{3,2},{4,5},{5,4},{6,7},{7,6},{8,9},{9,8},{10,11... | collective-permute-start | bytes 786440 | tf_op jit(solution)/shard_map/ppermute | solution.py:293
  36.8 10.4 %collective-permute-start.7 = (bf16[2,256,256]{2,1,0:T(8,128)(2,1)S(1)}, bf16[2,256,256]{2,1,0:T(8,128)(2,1)S(1)}, u32[]{:S(2)}, u32[]{:S(2)}) collective-permute-start(bf16[2,256,256]{2,1,0:T(8,128)(2,1)S(1)} %shard_map.58.own.refs_0_.refs_11_), channel_id=1, source_target_pairs={{0,128},{128,0},{1,129},{129,1},{2,130},{130,2},{3,131},{131,3},{4... | collective-permute-start | bytes 786440 | tf_op jit(solution)/shard_map/ppermute | solution.py:307
  44.0 3.2 %collective-permute-start.9 = (bf16[2,256,256]{2,1,0:T(8,128)(2,1)S(1)}, bf16[2,256,256]{2,1,0:T(8,128)(2,1)S(1)}, u32[]{:S(2)}, u32[]{:S(2)}) collective-permute-start(bf16[2,256,256]{2,1,0:T(8,128)(2,1)S(1)} %fusion.2.second.refs_2_), channel_id=1, source_target_pairs={{0,128},{128,0},{1,129},{129,1},{2,130},{130,2},{3,131},{131,3},{4... | collective-permute-start | bytes 786440 | tf_op jit(solution)/shard_map/ppermute | solution.py:307
  44.1 3.1 %collective-permute-start.8 = (bf16[2,256,256]{2,1,0:T(8,128)(2,1)S(1)}, bf16[2,256,256]{2,1,0:T(8,128)(2,1)S(1)}, u32[]{:S(2)}, u32[]{:S(2)}) collective-permute-start(bf16[2,256,256]{2,1,0:T(8,128)(2,1)S(1)} %collective-permute-done.6.first.refs_1_), channel_id=1, source_target_pairs={{0,128},{128,0},{1,129},{129,1},{2,130},{130,2},{3,131},{131,3},{4... | collective-permute-start | bytes 786440 | tf_op jit(solution)/shard_map/ppermute | solution.py:307
  44.6 23.7 %collective-permute-start.11 = (bf16[2,256,256]{2,1,0:T(8,128)(2,1)S(1)}, bf16[2,256,256]{2,1,0:T(8,128)(2,1)S(1)}, u32[]{:S(2)}, u32[]{:S(2)}) collective-permute-start(bf16[2,256,256]{2,1,0:T(8,128)(2,1)S(1)} %collective-permute-done.2.refs_6_), channel_id=1, source_target_pairs={{0,128},{128,0},{1,129},{129,1},{2,130},{130,2},{3,131},{131,3},{4... | collective-permute-start | bytes 786440 | tf_op jit(solution)/shard_map/ppermute | solution.py:307
  44.7 23.6 %collective-permute-start.12 = (bf16[2,256,256]{2,1,0:T(8,128)(2,1)S(1)}, bf16[2,256,256]{2,1,0:T(8,128)(2,1)S(1)}, u32[]{:S(2)}, u32[]{:S(2)}) collective-permute-start(bf16[2,256,256]{2,1,0:T(8,128)(2,1)S(1)} %collective-permute-done.3.refs_7_), channel_id=1, source_target_pairs={{0,128},{128,0},{1,129},{129,1},{2,130},{130,2},{3,131},{131,3},{4... | collective-permute-start | bytes 786440 | tf_op jit(solution)/shard_map/ppermute | solution.py:307
  51.8 13.9 %collective-permute-start.10 = (bf16[2,256,256]{2,1,0:T(8,128)(2,1)S(1)}, bf16[2,256,256]{2,1,0:T(8,128)(2,1)S(1)}, u32[]{:S(2)}, u32[]{:S(2)}) collective-permute-start(bf16[2,256,256]{2,1,0:T(8,128)(2,1)S(1)} %shard_map.60.own.refs_0_.refs_12_), channel_id=1, source_target_pairs={{0,1},{1,0},{2,3},{3,2},{4,5},{5,4},{6,7},{7,6},{8,9},{9,8},{10,11... | collective-permute-start | bytes 786440 | tf_op jit(solution)/shard_map/ppermute | solution.py:293
  64.7 3.6 %collective-permute-start.13 = (bf16[2,256,256]{2,1,0:T(8,128)(2,1)S(1)}, bf16[2,256,256]{2,1,0:T(8,128)(2,1)S(1)}, u32[]{:S(2)}, u32[]{:S(2)}) collective-permute-start(bf16[2,256,256]{2,1,0:T(8,128)(2,1)S(1)} %shard_map.60.own.refs_0_.refs_12_), channel_id=1, source_target_pairs={{0,128},{128,0},{1,129},{129,1},{2,130},{130,2},{3,131},{131,3},{4... | collective-permute-start | bytes 786440 | tf_op jit(solution)/shard_map/ppermute | solution.py:307
  65.6 2.7 %collective-permute-start.15 = (bf16[2,256,256]{2,1,0:T(8,128)(2,1)S(1)}, bf16[2,256,256]{2,1,0:T(8,128)(2,1)S(1)}, u32[]{:S(2)}, u32[]{:S(2)}) collective-permute-start(bf16[2,256,256]{2,1,0:T(8,128)(2,1)S(1)} %fusion.1.second.refs_2_), channel_id=1, source_target_pairs={{0,128},{128,0},{1,129},{129,1},{2,130},{130,2},{3,131},{131,3},{4... | collective-permute-start | bytes 786440 | tf_op jit(solution)/shard_map/ppermute | solution.py:307
  65.7 2.6 %collective-permute-start.14 = (bf16[2,256,256]{2,1,0:T(8,128)(2,1)S(1)}, bf16[2,256,256]{2,1,0:T(8,128)(2,1)S(1)}, u32[]{:S(2)}, u32[]{:S(2)}) collective-permute-start(bf16[2,256,256]{2,1,0:T(8,128)(2,1)S(1)} %collective-permute-done.10.first.refs_1_), channel_id=1, source_target_pairs={{0,128},{128,0},{1,129},{129,1},{2,130},{130,2},{3,131},{131,3},{4... | collective-permute-start | bytes 786440 | tf_op jit(solution)/shard_map/ppermute | solution.py:307
  72.5 13.9 %collective-permute-start.16 = (bf16[2,256,256]{2,1,0:T(8,128)(2,1)S(1)}, bf16[2,256,256]{2,1,0:T(8,128)(2,1)S(1)}, u32[]{:S(2)}, u32[]{:S(2)}) collective-permute-start(bf16[2,256,256]{2,1,0:T(8,128)(2,1)S(1)} %shard_map.62.own.refs_0_), channel_id=1, source_target_pairs={{0,1},{1,0},{2,3},{3,2},{4,5},{5,4},{6,7},{7,6},{8,9},{9,8},{10,11... | collective-permute-start | bytes 786440 | tf_op jit(solution)/shard_map/ppermute | solution.py:293
  85.4 3.5 %collective-permute-start.17 = (bf16[2,256,256]{2,1,0:T(8,128)(2,1)S(1)}, bf16[2,256,256]{2,1,0:T(8,128)(2,1)S(1)}, u32[]{:S(2)}, u32[]{:S(2)}) collective-permute-start(bf16[2,256,256]{2,1,0:T(8,128)(2,1)S(1)} %shard_map.62.own.refs_0_), channel_id=1, source_target_pairs={{0,128},{128,0},{1,129},{129,1},{2,130},{130,2},{3,131},{131,3},{4... | collective-permute-start | bytes 786440 | tf_op jit(solution)/shard_map/ppermute | solution.py:307
  86.3 2.7 %collective-permute-start.19 = (bf16[2,256,256]{2,1,0:T(8,128)(2,1)S(1)}, bf16[2,256,256]{2,1,0:T(8,128)(2,1)S(1)}, u32[]{:S(2)}, u32[]{:S(2)}) collective-permute-start(bf16[2,256,256]{2,1,0:T(8,128)(2,1)S(1)} %fusion.second.refs_2_), channel_id=1, source_target_pairs={{0,128},{128,0},{1,129},{129,1},{2,130},{130,2},{3,131},{131,3},{4... | collective-permute-start | bytes 786440 | tf_op jit(solution)/shard_map/ppermute | solution.py:307
  86.4 2.6 %collective-permute-start.18 = (bf16[2,256,256]{2,1,0:T(8,128)(2,1)S(1)}, bf16[2,256,256]{2,1,0:T(8,128)(2,1)S(1)}, u32[]{:S(2)}, u32[]{:S(2)}) collective-permute-start(bf16[2,256,256]{2,1,0:T(8,128)(2,1)S(1)} %collective-permute-done.16.first.refs_1_), channel_id=1, source_target_pairs={{0,128},{128,0},{1,129},{129,1},{2,130},{130,2},{3,131},{131,3},{4... | collective-permute-start | bytes 786440 | tf_op jit(solution)/shard_map/ppermute | solution.py:307

commit v6 on v5

--- a/solution.py
+++ b/solution.py
@@ -58,31 +58,27 @@
     return lax.rem(lax.axis_index("rows"), 2) == 1
 
 
-def pick_kernel(initial, frames, out, ready):
-    layer = lax.axis_index("layer")
-    for wanted, source in enumerate((initial, frames.at[0:2])):
-        @pl.when(layer == wanted)
-        def _():
-            copy = pltpu.make_async_copy(source, out, ready)
-            copy.start()
-            copy.wait()
-
-
-def stage_kernel(frames, weight, out, state_weight, ready):
-    channels = weight.shape[2] // 2
-    load = pltpu.make_async_copy(
-        weight.at[:, :, channels : 2 * channels], state_weight, ready.at[0]
-    )
-    for wanted in range(2):
+def pick_kernel(initial, frames, out, later, ready):
+    for wanted, sources in enumerate(
+        ((initial, frames.at[2:4]), (frames.at[0:2], frames.at[4:6]))
+    ):
         @pl.when(lax.axis_index("layer") == wanted)
         def _():
-            copy = pltpu.make_async_copy(
-                frames.at[2 * wanted + 2 : 2 * wanted + 4], out, ready.at[1]
-            )
-            copy.start()
-            load.start()
-            copy.wait()
-            load.wait()
+            copies = [
+                pltpu.make_async_copy(source, target, ready.at[i])
+                for i, (source, target) in enumerate(zip(sources, (out, later)))
+            ]
+            for copy in copies:
+                copy.start()
+            for copy in copies:
+                copy.wait()
+
+
+def stage_kernel(weight, state_weight, ready):
+    channels = weight.shape[2] // 2
+    load = pltpu.make_async_copy(weight.at[:, :, channels : 2 * channels], state_weight, ready)
+    load.start()
+    load.wait()
 
 
 def early_kernel(lag, own, first, second, wg, pre_r, pre_u, wide):
@@ -217,27 +213,24 @@
 def pick(initial, rows):
     return pl.pallas_call(
         pick_kernel,
-        out_shape=jax.ShapeDtypeStruct(initial.shape, initial.dtype),
-        in_specs=[ANYWHERE] * 2,
-        out_specs=HELD,
-        scratch_shapes=[pltpu.SemaphoreType.DMA],
-        compiler_params=pltpu.CompilerParams(vmem_limit_bytes=SMALL_BYTES),
-    )(outside(initial), outside(rows))
-
-
-def stage(rows, wg):
-    _, cols, channels = rows.shape
-    return pl.pallas_call(
-        stage_kernel,
-        out_shape=[
-            jax.ShapeDtypeStruct((2, cols, channels), rows.dtype),
-            jax.ShapeDtypeStruct((3, 3, channels, 2 * channels), wg.dtype),
-        ],
+        out_shape=[jax.ShapeDtypeStruct(initial.shape, initial.dtype)] * 2,
         in_specs=[ANYWHERE] * 2,
         out_specs=[HELD] * 2,
         scratch_shapes=[pltpu.SemaphoreType.DMA((2,))],
         compiler_params=pltpu.CompilerParams(vmem_limit_bytes=SMALL_BYTES),
-    )(outside(rows), outside(wg))
+    )(outside(initial), outside(rows))
+
+
+def stage(wg):
+    _, _, depth, width = wg.shape
+    return pl.pallas_call(
+        stage_kernel,
+        out_shape=jax.ShapeDtypeStruct((3, 3, depth // 2, width), wg.dtype),
+        in_specs=[ANYWHERE],
+        out_specs=HELD,
+        scratch_shapes=[pltpu.SemaphoreType.DMA],
+        compiler_params=pltpu.CompilerParams(vmem_limit_bytes=SMALL_BYTES),
+    )(outside(wg))
 
 
 def early(lag, state, wg):
@@ -293,14 +286,15 @@
     return lax.ppermute(field, "rows", route)
 
 
-def gathered_swap(field, odd, inner):
+def gathered_swap(field, odd, inner, beside):
     count = lax.axis_size("rows")
     groups = [[0, count], [count - 1, 2 * count - 1]]
     for layer in range(2):
         groups += [[layer * count + low, layer * count + low + 1] for low in range(1, count - 1, 2)]
     both = lax.all_gather(field, ("layer", "rows"), axis_index_groups=groups)
+    both, beside = lax.optimization_barrier((both, beside))
     partner = jnp.where(odd, both[1], both[0])
-    return jnp.where(inner, partner, jnp.zeros_like(partner))
+    return jnp.where(inner, partner, jnp.zeros_like(partner)), beside
 
 
 def across(field):
@@ -315,13 +309,14 @@
 
     odd = lax.rem(strip, 2) == 1
     inner = jnp.logical_and(strip > 0, strip < lax.axis_size("rows") - 1)
-    field = pick(hidden, rows)
+    field, later_field = pick(hidden, rows)
     field, odd, inner = lax.optimization_barrier((field, odd, inner))
     first, second = pair_swap(field, 0), pair_swap(field, 1)
-    later_field, wg_state = stage(rows, wg)
+    wg_state = stage(wg)
     late_first, late_second = pair_swap(later_field, 0), pair_swap(later_field, 1)
+    first_after, wg_state = lax.optimization_barrier((first, wg_state))
     halos = [
-        (across(first), across(second)),
+        (across(first_after), across(second)),
         (late_first, late_second),
         (across(late_first), across(late_second)),
     ]
@@ -333,7 +328,7 @@
     for step in range(1, 4):
         first = pair_swap(hidden, 0)
         own_below = across(hidden)
-        second = gathered_swap(hidden, odd, inner)
+        second, own_below = gathered_swap(hidden, odd, inner, own_below)
         below = (own_below, across(first), across(second))
         state = (hidden, first, second)
         pre = early(step, state, wg_state)

time: 94.2 us -> 94.2 us (level)
  waiting for transfers between devices: 7.34 us -> 4.86 us
  blocking collectives: 35.7 us -> 38.1 us
    ppermute x7, waiting for transfers between devices: 7.31 us -> 4.82 us  [pair_swap(): return lax.ppermute(field, 'rows', route)]
    all_gather x3, blocking collectives: 35.7 us -> 38.1 us  [gathered_swap(): both = lax.all_gather(field, ('layer', 'rows'), axis_index_groups=groups)]
  transfers between devices with their start and end apart: 20 -> 20, of which waited for: 2 -> 1; matrix products, arithmetic and copies ran while one was open for 0% -> 0% of each run, Pallas kernels for 14% -> 8%
where the time goes in v6:
time: 94.2 us; the launch traced here: 94 us
  blocking collectives  38.1 us (40%)
  starting transfers between devices  27.7 us (29%)
  Pallas kernels  22.8 us (24%)
  waiting for transfers between devices  4.86 us (5%)
    all_gather x3, blocking collectives, gathered_swap(): both = lax.all_gather(field, ('layer', 'rows'), axis_index_groups=groups)  38.1 us
    ppermute x7, starting transfers between devices, pair_swap(): return lax.ppermute(field, 'rows', route)  14.1 us
    ppermute x13, starting transfers between devices, across(): return lax.ppermute(field, 'layer', [(0, 1), (1, 0)])  13.6 us
    pallas_call x3, Pallas kernels, late(): pl.pallas_call(functools.partial(late_kernel, lag), out_shape=jax.ShapeDt...  8.96 us
    pallas_call x4, Pallas kernels, early(): pl.pallas_call(functools.partial(early_kernel, lag), out_shape=[pre(4), p...  6.09 us
    pallas_call x1, Pallas kernels, last(): pl.pallas_call(last_kernel, out_shape=jax.ShapeDtypeStruct((3, 2, cols, c...  4.89 us
    ppermute x7, waiting for transfers between devices, pair_swap(): return lax.ppermute(field, 'rows', route)  4.82 us
  transfers between devices with their start and end apart: 20, of which 1 were waited for; matrix products, arithmetic and copies ran while one was open for 0% of the time, Pallas kernels for 8%

profile of v6, /device:TPU:25, one launch (start us, length us, event | category | flops | bytes accessed | tf_op | source)
XLA Modules:
  0.0 94.0 jit_solution(5000968407986943076)
XLA Ops:
  0.0 1.0 %shard_map.55 = (bf16[2,256,256]{2,1,0:T(8,128)(2,1)S(1)}, bf16[2,256,256]{2,1,0:T(8,128)(2,1)S(1)}) custom-call(bf16[2,256,256]{2,1,0:T(8,128)(2,1)} %bitcast.29, bf16[6,256,256]{2,1,0:T(8,128)(2,1)} %bitcast.25), custom_call_target="tpu_custom_call" | custom-call | tf_op jit(solution)/shard_map/pallas_call | solution.py:214
  1.1 1.7 %collective-permute-start = (bf16[2,256,256]{2,1,0:T(8,128)(2,1)S(1)}, bf16[2,256,256]{2,1,0:T(8,128)(2,1)S(1)}, u32[]{:S(2)}, u32[]{:S(2)}) collective-permute-start(bf16[2,256,256]{2,1,0:T(8,128)(2,1)S(1)} %get-tuple-element.29.own.refs_8_), channel_id=1, source_target_pairs={{0,1},{1,0},{2,3},{3,2},{4,5},{5,4},{6,7},{7,6},{8,9},{9,8},{10,11... | collective-permute-start | bytes 786440 | tf_op jit(solution)/shard_map/ppermute | solution.py:286
  2.8 8.9 %collective-permute-start.1 = (bf16[2,256,256]{2,1,0:T(8,128)(2,1)S(1)}, bf16[2,256,256]{2,1,0:T(8,128)(2,1)S(1)}, u32[]{:S(2)}, u32[]{:S(2)}) collective-permute-start(bf16[2,256,256]{2,1,0:T(8,128)(2,1)S(1)} %get-tuple-element.29.own.refs_8_), channel_id=1, source_target_pairs={{1,2},{2,1},{3,4},{4,3},{5,6},{6,5},{7,8},{8,7},{9,10},{10,9},{11,... | collective-permute-start | bytes 786440 | tf_op jit(solution)/shard_map/ppermute | solution.py:286
  11.7 0.1 collective-permute-start.2
  11.8 3.3 %collective-permute-start.3 = (bf16[2,256,256]{2,1,0:T(8,128)(2,1)S(1)}, bf16[2,256,256]{2,1,0:T(8,128)(2,1)S(1)}, u32[]{:S(2)}, u32[]{:S(2)}) collective-permute-start(bf16[2,256,256]{2,1,0:T(8,128)(2,1)S(1)} %get-tuple-element.33), channel_id=1, source_target_pairs={{1,2},{2,1},{3,4},{4,3},{5,6},{6,5},{7,8},{8,7},{9,10},{10,9},{11,... | collective-permute-start | bytes 786440 | tf_op jit(solution)/shard_map/ppermute | solution.py:286
  15.2 0.0 slice-start
  15.2 0.0 slice-start.1
  15.2 1.8 %shard_map.56.wg = bf16[3,3,256,512]{3,2,1,0:T(8,128)(2,1)S(1)} custom-call(bf16[3,3,512,512]{3,2,1,0:T(8,128)(2,1)} %bitcast.14), custom_call_target="tpu_custom_call" | custom-call | tf_op jit(solution)/shard_map/pallas_call | solution.py:226
  17.0 0.0 copy-start
  17.0 0.0 copy-start.1
  17.1 0.0 copy-start.2
  17.1 0.0 copy-start.3
  17.1 0.0 collective-permute-done.first.refs_1_.refs_9_
  17.1 1.9 %collective-permute-start.4 = (bf16[2,256,256]{2,1,0:T(8,128)(2,1)S(1)}, bf16[2,256,256]{2,1,0:T(8,128)(2,1)S(1)}, u32[]{:S(2)}, u32[]{:S(2)}) collective-permute-start(bf16[2,256,256]{2,1,0:T(8,128)(2,1)S(1)} %collective-permute-done.first.refs_1_.refs_9_), channel_id=1, source_target_pairs={{0,128},{128,0},{1,129},{129,1},{2,130},{130,2},{3,131},{131,3},{4... | collective-permute-start | bytes 786440 | tf_op jit(solution)/shard_map/ppermute | solution.py:301
  19.0 0.0 collective-permute-done.1.second.refs_2_.refs_10_
  19.0 0.7 collective-permute-start.5
  19.7 0.0 collective-permute-done.2.refs_6_
  19.7 4.8 %collective-permute-done.3.refs_7_ = bf16[2,256,256]{2,1,0:T(8,128)(2,1)S(1)} collective-permute-done((bf16[2,256,256]{2,1,0:T(8,128)(2,1)S(1)}, bf16[2,256,256]{2,1,0:T(8,128)(2,1)S(1)}, u32[]{:S(2)}, u32[]{:S(2)}) %collective-permute-start.3) | collective-permute-done | bytes 262176 | tf_op jit(solution)/shard_map/ppermute | solution.py:286
  24.5 0.0 collective-permute-done.4.refs_6_
  24.5 0.0 collective-permute-done.5.refs_7_
  24.5 0.0 slice-done
  24.5 0.0 slice-done.1
  24.5 0.0 copy-done
  24.5 0.0 copy-done.1
  24.5 0.0 copy-done.2
  24.6 0.0 copy-done.3
  24.6 6.1 %collective-permute-start.7 = (bf16[2,256,256]{2,1,0:T(8,128)(2,1)S(1)}, bf16[2,256,256]{2,1,0:T(8,128)(2,1)S(1)}, u32[]{:S(2)}, u32[]{:S(2)}) collective-permute-start(bf16[2,256,256]{2,1,0:T(8,128)(2,1)S(1)} %shard_map.58.own.refs_0_.refs_11_), channel_id=1, source_target_pairs={{0,128},{128,0},{1,129},{129,1},{2,130},{130,2},{3,131},{131,3},{4... | collective-permute-start | bytes 786440 | tf_op jit(solution)/shard_map/ppermute | solution.py:301
  30.7 0.0 collective-permute-start.6
  30.7 12.7 %all-gather = bf16[4,256,256]{2,1,0:T(8,128)(2,1)S(1)} all-gather(bf16[2,256,256]{2,1,0:T(8,128)(2,1)S(1)} %shard_map.58.own.refs_0_.refs_11_), channel_id=2, replica_groups={{0,128},{127,255},{1,2},{3,4},{5,6},{7,8},{9,10},{11,12},{13,14},{15,16..., dimensions={0}, use_global_device_ids=true | all-gather | bytes 786432 | tf_op jit(solution)/shard_map/all_gather | solution.py:294
  43.4 0.0 collective-permute-done.7.refs_8_
  43.4 0.0 collective-permute-done.6.first.refs_1_
  43.4 1.0 %collective-permute-start.8 = (bf16[2,256,256]{2,1,0:T(8,128)(2,1)S(1)}, bf16[2,256,256]{2,1,0:T(8,128)(2,1)S(1)}, u32[]{:S(2)}, u32[]{:S(2)}) collective-permute-start(bf16[2,256,256]{2,1,0:T(8,128)(2,1)S(1)} %collective-permute-done.6.first.refs_1_), channel_id=1, source_target_pairs={{0,128},{128,0},{1,129},{129,1},{2,130},{130,2},{3,131},{131,3},{4... | collective-permute-start | bytes 786440 | tf_op jit(solution)/shard_map/ppermute | solution.py:301
  44.5 0.1 collective-permute-start.9
  44.6 2.0 %shard_map.59 = (f32[1024,256]{1,0:T(8,128)S(1)}, f32[512,256]{1,0:T(8,128)S(1)}) custom-call(bf16[2,256,256]{2,1,0:T(8,128)(2,1)S(1)} %shard_map.58.own.refs_0_.refs_11_, bf16[2,256,256]{2,1,0:T(8,128)(2,1)S(1)} %collective-permute-done.6.first.refs_1_, bf16[2,256,256]{2,1,0:T(8,128)(2,1)S(1)} %select_bitcast_fusion.2.second.refs_2_, ...), custom_call_target="tpu_custom_call" | custom-call | flops 1811939328 | bytes 1048576 | tf_op jit(solution)/shard_map/pallas_call | solution.py:239
  46.6 0.0 collective-permute-done.8.refs_9_
  46.6 0.0 collective-permute-done.9.refs_10_
  46.6 4.6 %shard_map.60.own.refs_0_.refs_12_ = bf16[2,256,256]{2,1,0:T(8,128)(2,1)S(1)} custom-call(bf16[2,256,256]{2,1,0:T(8,128)(2,1)S(1)} %shard_map.58.own.refs_0_.refs_11_, bf16[2,256,256]{2,1,0:T(8,128)(2,1)S(1)} %collective-permute-done.6.first.refs_1_, bf16[2,256,256]{2,1,0:T(8,128)(2,1)S(1)} %select_bitcast_fusion.2.second.refs_2_, ...), custom_call_target="tpu_custom_call" | custom-call | flops 3019898880 | bytes 1048576 | tf_op jit(solution)/shard_map/pallas_call | solution.py:252
  51.3 0.5 collective-permute-start.11
  51.8 0.1 collective-permute-start.12
  51.9 0.4 collective-permute-start.13
  52.3 0.0 collective-permute-start.10
  52.3 12.8 %all-gather.1 = bf16[4,256,256]{2,1,0:T(8,128)(2,1)S(1)} all-gather(bf16[2,256,256]{2,1,0:T(8,128)(2,1)S(1)} %shard_map.60.own.refs_0_.refs_12_), channel_id=3, replica_groups={{0,128},{127,255},{1,2},{3,4},{5,6},{7,8},{9,10},{11,12},{13,14},{15,16..., dimensions={0}, use_global_device_ids=true | all-gather | bytes 786432 | tf_op jit(solution)/shard_map/all_gather | solution.py:294
  65.1 0.0 collective-permute-done.11.refs_8_
  65.1 0.0 collective-permute-done.10.first.refs_1_
  65.1 1.0 %collective-permute-start.14 = (bf16[2,256,256]{2,1,0:T(8,128)(2,1)S(1)}, bf16[2,256,256]{2,1,0:T(8,128)(2,1)S(1)}, u32[]{:S(2)}, u32[]{:S(2)}) collective-permute-start(bf16[2,256,256]{2,1,0:T(8,128)(2,1)S(1)} %collective-permute-done.10.first.refs_1_), channel_id=1, source_target_pairs={{0,128},{128,0},{1,129},{129,1},{2,130},{130,2},{3,131},{131,3},{4... | collective-permute-start | bytes 786440 | tf_op jit(solution)/shard_map/ppermute | solution.py:301
  66.1 0.1 collective-permute-start.15
  66.2 2.0 %shard_map.61 = (f32[1024,256]{1,0:T(8,128)S(1)}, f32[512,256]{1,0:T(8,128)S(1)}) custom-call(bf16[2,256,256]{2,1,0:T(8,128)(2,1)S(1)} %shard_map.60.own.refs_0_.refs_12_, bf16[2,256,256]{2,1,0:T(8,128)(2,1)S(1)} %collective-permute-done.10.first.refs_1_, bf16[2,256,256]{2,1,0:T(8,128)(2,1)S(1)} %select_bitcast_fusion.1.second.refs_2_, ...), custom_call_target="tpu_custom_call" | custom-call | flops 1811939328 | bytes 1048576 | tf_op jit(solution)/shard_map/pallas_call | solution.py:239
  68.2 0.0 collective-permute-done.12.refs_6_
  68.2 0.0 collective-permute-done.13.refs_7_
  68.2 0.0 collective-permute-done.14.refs_9_
  68.2 0.0 collective-permute-done.15.refs_10_
  68.3 4.3 %shard_map.62.own.refs_0_ = bf16[2,256,256]{2,1,0:T(8,128)(2,1)S(1)} custom-call(bf16[2,256,256]{2,1,0:T(8,128)(2,1)S(1)} %shard_map.60.own.refs_0_.refs_12_, bf16[2,256,256]{2,1,0:T(8,128)(2,1)S(1)} %collective-permute-done.10.first.refs_1_, bf16[2,256,256]{2,1,0:T(8,128)(2,1)S(1)} %select_bitcast_fusion.1.second.refs_2_, ...), custom_call_target="tpu_custom_call" | custom-call | flops 3019898880 | bytes 1048576 | tf_op jit(solution)/shard_map/pallas_call | solution.py:252
  72.5 0.5 collective-permute-start.17
  73.0 0.0 collective-permute-start.16
  73.0 12.7 %all-gather.2 = bf16[4,256,256]{2,1,0:T(8,128)(2,1)S(1)} all-gather(bf16[2,256,256]{2,1,0:T(8,128)(2,1)S(1)} %shard_map.62.own.refs_0_), channel_id=4, replica_groups={{0,128},{127,255},{1,2},{3,4},{5,6},{7,8},{9,10},{11,12},{13,14},{15,16..., dimensions={0}, use_global_device_ids=true | all-gather | bytes 786432 | tf_op jit(solution)/shard_map/all_gather | solution.py:294
  85.7 0.0 collective-permute-done.17.refs_5_
  85.7 0.0 collective-permute-done.16.first.refs_1_
  85.7 1.0 %collective-permute-start.18 = (bf16[2,256,256]{2,1,0:T(8,128)(2,1)S(1)}, bf16[2,256,256]{2,1,0:T(8,128)(2,1)S(1)}, u32[]{:S(2)}, u32[]{:S(2)}) collective-permute-start(bf16[2,256,256]{2,1,0:T(8,128)(2,1)S(1)} %collective-permute-done.16.first.refs_1_), channel_id=1, source_target_pairs={{0,128},{128,0},{1,129},{129,1},{2,130},{130,2},{3,131},{131,3},{4... | collective-permute-start | bytes 786440 | tf_op jit(solution)/shard_map/ppermute | solution.py:301
  86.8 0.1 collective-permute-start.19
  86.9 2.0 %shard_map.63 = (f32[1024,256]{1,0:T(8,128)S(1)}, f32[512,256]{1,0:T(8,128)S(1)}) custom-call(bf16[2,256,256]{2,1,0:T(8,128)(2,1)S(1)} %shard_map.62.own.refs_0_, bf16[2,256,256]{2,1,0:T(8,128)(2,1)S(1)} %collective-permute-done.16.first.refs_1_, bf16[2,256,256]{2,1,0:T(8,128)(2,1)S(1)} %select_bitcast_fusion.second.refs_2_, ...), custom_call_target="tpu_custom_call" | custom-call | flops 1811939328 | bytes 1048576 | tf_op jit(solution)/shard_map/pallas_call | solution.py:239
  88.9 0.0 collective-permute-done.18.refs_6_
  88.9 0.0 collective-permute-done.19.refs_7_
  88.9 4.9 %shard_map.64 = bf16[3,2,256,256]{3,2,1,0:T(8,128)(2,1)} custom-call(bf16[2,256,256]{2,1,0:T(8,128)(2,1)S(1)} %shard_map.62.own.refs_0_, bf16[2,256,256]{2,1,0:T(8,128)(2,1)S(1)} %collective-permute-done.16.first.refs_1_, bf16[2,256,256]{2,1,0:T(8,128)(2,1)S(1)} %select_bitcast_fusion.second.refs_2_, f32[1024,256]{1,0:T(8,128)S(1)} %get-tuple-element.48.refs_3_, ...), custom_call_target="tpu_custom_call" | custom-call | flops 3019898880 | bytes 1048576 | tf_op jit(solution)/shard_map/pallas_call | solution.py:265
  (6 shorter events, 0.1 us)
Async XLA Ops:
  1.1 16.0 %collective-permute-start = (bf16[2,256,256]{2,1,0:T(8,128)(2,1)S(1)}, bf16[2,256,256]{2,1,0:T(8,128)(2,1)S(1)}, u32[]{:S(2)}, u32[]{:S(2)}) collective-permute-start(bf16[2,256,256]{2,1,0:T(8,128)(2,1)S(1)} %get-tuple-element.29.own.refs_8_), channel_id=1, source_target_pairs={{0,1},{1,0},{2,3},{3,2},{4,5},{5,4},{6,7},{7,6},{8,9},{9,8},{10,11... | collective-permute-start | bytes 786440 | tf_op jit(solution)/shard_map/ppermute | solution.py:286
  2.8 16.2 %collective-permute-start.1 = (bf16[2,256,256]{2,1,0:T(8,128)(2,1)S(1)}, bf16[2,256,256]{2,1,0:T(8,128)(2,1)S(1)}, u32[]{:S(2)}, u32[]{:S(2)}) collective-permute-start(bf16[2,256,256]{2,1,0:T(8,128)(2,1)S(1)} %get-tuple-element.29.own.refs_8_), channel_id=1, source_target_pairs={{1,2},{2,1},{3,4},{4,3},{5,6},{6,5},{7,8},{8,7},{9,10},{10,9},{11,... | collective-permute-start | bytes 786440 | tf_op jit(solution)/shard_map/ppermute | solution.py:286
  11.7 8.0 %collective-permute-start.2 = (bf16[2,256,256]{2,1,0:T(8,128)(2,1)S(1)}, bf16[2,256,256]{2,1,0:T(8,128)(2,1)S(1)}, u32[]{:S(2)}, u32[]{:S(2)}) collective-permute-start(bf16[2,256,256]{2,1,0:T(8,128)(2,1)S(1)} %get-tuple-element.33), channel_id=1, source_target_pairs={{0,1},{1,0},{2,3},{3,2},{4,5},{5,4},{6,7},{7,6},{8,9},{9,8},{10,11... | collective-permute-start | bytes 786440 | tf_op jit(solution)/shard_map/ppermute | solution.py:286
  11.8 12.7 %collective-permute-start.3 = (bf16[2,256,256]{2,1,0:T(8,128)(2,1)S(1)}, bf16[2,256,256]{2,1,0:T(8,128)(2,1)S(1)}, u32[]{:S(2)}, u32[]{:S(2)}) collective-permute-start(bf16[2,256,256]{2,1,0:T(8,128)(2,1)S(1)} %get-tuple-element.33), channel_id=1, source_target_pairs={{1,2},{2,1},{3,4},{4,3},{5,6},{6,5},{7,8},{8,7},{9,10},{10,9},{11,... | collective-permute-start | bytes 786440 | tf_op jit(solution)/shard_map/ppermute | solution.py:286
  15.2 9.3 %slice-start = ((s8[4718592]{0:T(1024)(128)(4,1)}), s8[4194304]{0:T(1024)(128)(4,1)S(1)}, s32[]{:S(2)}) async-start(s8[4718592]{0:T(1024)(128)(4,1)} %bitcast.15), calls=%async_computation | async-start | bytes 8388608
  15.2 9.3 %slice-start.1 = ((s8[4718592]{0:T(1024)(128)(4,1)}), s8[524288]{0:T(1024)(128)(4,1)S(1)}, s32[]{:S(2)}) async-start(s8[4718592]{0:T(1024)(128)(4,1)} %bitcast.15), calls=%async_computation.1 | async-start | bytes 1048576
  17.0 7.5 %copy-start = (bf16[1,3,3,512,256]{4,3,2,1,0:T(8,128)(2,1)S(1)}, bf16[1,3,3,512,256]{4,3,2,1,0:T(8,128)(2,1)}, u32[]{:S(2)}) copy-start(bf16[1,3,3,512,256]{4,3,2,1,0:T(8,128)(2,1)} %param.8) | copy-start | bytes 7077892
  17.0 7.5 %copy-start.1 = (bf16[3,2,256,256]{3,2,1,0:T(8,128)(2,1)S(1)}, bf16[3,2,256,256]{3,2,1,0:T(8,128)(2,1)}, u32[]{:S(2)}) copy-start(bf16[3,2,256,256]{3,2,1,0:T(8,128)(2,1)} %param.5) | copy-start | bytes 2359300
  17.1 7.5 %copy-start.2 = (bf16[1,2,256,256]{3,2,1,0:T(8,128)(2,1)S(1)}, bf16[1,2,256,256]{3,2,1,0:T(8,128)(2,1)}, u32[]{:S(2)}) copy-start(bf16[1,2,256,256]{3,2,1,0:T(8,128)(2,1)} %param.6) | copy-start | bytes 786436
  17.1 7.5 %copy-start.3 = (f32[1,768]{1,0:T(1,128)S(1)}, f32[1,768]{1,0:T(1,128)}, u32[]{:S(2)}) copy-start(f32[1,768]{1,0:T(1,128)} %refs_10_.1) | copy-start | bytes 9220
  17.1 7.4 %collective-permute-start.4 = (bf16[2,256,256]{2,1,0:T(8,128)(2,1)S(1)}, bf16[2,256,256]{2,1,0:T(8,128)(2,1)S(1)}, u32[]{:S(2)}, u32[]{:S(2)}) collective-permute-start(bf16[2,256,256]{2,1,0:T(8,128)(2,1)S(1)} %collective-permute-done.first.refs_1_.refs_9_), channel_id=1, source_target_pairs={{0,128},{128,0},{1,129},{129,1},{2,130},{130,2},{3,131},{131,3},{4... | collective-permute-start | bytes 786440 | tf_op jit(solution)/shard_map/ppermute | solution.py:301
  19.0 5.5 %collective-permute-start.5 = (bf16[2,256,256]{2,1,0:T(8,128)(2,1)S(1)}, bf16[2,256,256]{2,1,0:T(8,128)(2,1)S(1)}, u32[]{:S(2)}, u32[]{:S(2)}) collective-permute-start(bf16[2,256,256]{2,1,0:T(8,128)(2,1)S(1)} %collective-permute-done.1.second.refs_2_.refs_10_), channel_id=1, source_target_pairs={{0,128},{128,0},{1,129},{129,1},{2,130},{130,2},{3,131},{131,3},{4... | collective-permute-start | bytes 786440 | tf_op jit(solution)/shard_map/ppermute | solution.py:301
  24.6 18.8 %collective-permute-start.7 = (bf16[2,256,256]{2,1,0:T(8,128)(2,1)S(1)}, bf16[2,256,256]{2,1,0:T(8,128)(2,1)S(1)}, u32[]{:S(2)}, u32[]{:S(2)}) collective-permute-start(bf16[2,256,256]{2,1,0:T(8,128)(2,1)S(1)} %shard_map.58.own.refs_0_.refs_11_), channel_id=1, source_target_pairs={{0,128},{128,0},{1,129},{129,1},{2,130},{130,2},{3,131},{131,3},{4... | collective-permute-start | bytes 786440 | tf_op jit(solution)/shard_map/ppermute | solution.py:301
  30.7 12.7 %collective-permute-start.6 = (bf16[2,256,256]{2,1,0:T(8,128)(2,1)S(1)}, bf16[2,256,256]{2,1,0:T(8,128)(2,1)S(1)}, u32[]{:S(2)}, u32[]{:S(2)}) collective-permute-start(bf16[2,256,256]{2,1,0:T(8,128)(2,1)S(1)} %shard_map.58.own.refs_0_.refs_11_), channel_id=1, source_target_pairs={{0,1},{1,0},{2,3},{3,2},{4,5},{5,4},{6,7},{7,6},{8,9},{9,8},{10,11... | collective-permute-start | bytes 786440 | tf_op jit(solution)/shard_map/ppermute | solution.py:286
  43.4 3.2 %collective-permute-start.8 = (bf16[2,256,256]{2,1,0:T(8,128)(2,1)S(1)}, bf16[2,256,256]{2,1,0:T(8,128)(2,1)S(1)}, u32[]{:S(2)}, u32[]{:S(2)}) collective-permute-start(bf16[2,256,256]{2,1,0:T(8,128)(2,1)S(1)} %collective-permute-done.6.first.refs_1_), channel_id=1, source_target_pairs={{0,128},{128,0},{1,129},{129,1},{2,130},{130,2},{3,131},{131,3},{4... | collective-permute-start | bytes 786440 | tf_op jit(solution)/shard_map/ppermute | solution.py:301
  44.5 2.1 %collective-permute-start.9 = (bf16[2,256,256]{2,1,0:T(8,128)(2,1)S(1)}, bf16[2,256,256]{2,1,0:T(8,128)(2,1)S(1)}, u32[]{:S(2)}, u32[]{:S(2)}) collective-permute-start(bf16[2,256,256]{2,1,0:T(8,128)(2,1)S(1)} %select_bitcast_fusion.2.second.refs_2_), channel_id=1, source_target_pairs={{0,128},{128,0},{1,129},{129,1},{2,130},{130,2},{3,131},{131,3},{4... | collective-permute-start | bytes 786440 | tf_op jit(solution)/shard_map/ppermute | solution.py:301
  51.3 13.8 %collective-permute-start.11 = (bf16[2,256,256]{2,1,0:T(8,128)(2,1)S(1)}, bf16[2,256,256]{2,1,0:T(8,128)(2,1)S(1)}, u32[]{:S(2)}, u32[]{:S(2)}) collective-permute-start(bf16[2,256,256]{2,1,0:T(8,128)(2,1)S(1)} %shard_map.60.own.refs_0_.refs_12_), channel_id=1, source_target_pairs={{0,128},{128,0},{1,129},{129,1},{2,130},{130,2},{3,131},{131,3},{4... | collective-permute-start | bytes 786440 | tf_op jit(solution)/shard_map/ppermute | solution.py:301
  51.8 16.4 %collective-permute-start.12 = (bf16[2,256,256]{2,1,0:T(8,128)(2,1)S(1)}, bf16[2,256,256]{2,1,0:T(8,128)(2,1)S(1)}, u32[]{:S(2)}, u32[]{:S(2)}) collective-permute-start(bf16[2,256,256]{2,1,0:T(8,128)(2,1)S(1)} %collective-permute-done.2.refs_6_), channel_id=1, source_target_pairs={{0,128},{128,0},{1,129},{129,1},{2,130},{130,2},{3,131},{131,3},{4... | collective-permute-start | bytes 786440 | tf_op jit(solution)/shard_map/ppermute | solution.py:301
  51.9 16.3 %collective-permute-start.13 = (bf16[2,256,256]{2,1,0:T(8,128)(2,1)S(1)}, bf16[2,256,256]{2,1,0:T(8,128)(2,1)S(1)}, u32[]{:S(2)}, u32[]{:S(2)}) collective-permute-start(bf16[2,256,256]{2,1,0:T(8,128)(2,1)S(1)} %collective-permute-done.3.refs_7_), channel_id=1, source_target_pairs={{0,128},{128,0},{1,129},{129,1},{2,130},{130,2},{3,131},{131,3},{4... | collective-permute-start | bytes 786440 | tf_op jit(solution)/shard_map/ppermute | solution.py:301
  52.3 12.8 %collective-permute-start.10 = (bf16[2,256,256]{2,1,0:T(8,128)(2,1)S(1)}, bf16[2,256,256]{2,1,0:T(8,128)(2,1)S(1)}, u32[]{:S(2)}, u32[]{:S(2)}) collective-permute-start(bf16[2,256,256]{2,1,0:T(8,128)(2,1)S(1)} %shard_map.60.own.refs_0_.refs_12_), channel_id=1, source_target_pairs={{0,1},{1,0},{2,3},{3,2},{4,5},{5,4},{6,7},{7,6},{8,9},{9,8},{10,11... | collective-permute-start | bytes 786440 | tf_op jit(solution)/shard_map/ppermute | solution.py:286
  65.1 3.1 %collective-permute-start.14 = (bf16[2,256,256]{2,1,0:T(8,128)(2,1)S(1)}, bf16[2,256,256]{2,1,0:T(8,128)(2,1)S(1)}, u32[]{:S(2)}, u32[]{:S(2)}) collective-permute-start(bf16[2,256,256]{2,1,0:T(8,128)(2,1)S(1)} %collective-permute-done.10.first.refs_1_), channel_id=1, source_target_pairs={{0,128},{128,0},{1,129},{129,1},{2,130},{130,2},{3,131},{131,3},{4... | collective-permute-start | bytes 786440 | tf_op jit(solution)/shard_map/ppermute | solution.py:301
  66.1 2.2 %collective-permute-start.15 = (bf16[2,256,256]{2,1,0:T(8,128)(2,1)S(1)}, bf16[2,256,256]{2,1,0:T(8,128)(2,1)S(1)}, u32[]{:S(2)}, u32[]{:S(2)}) collective-permute-start(bf16[2,256,256]{2,1,0:T(8,128)(2,1)S(1)} %select_bitcast_fusion.1.second.refs_2_), channel_id=1, source_target_pairs={{0,128},{128,0},{1,129},{129,1},{2,130},{130,2},{3,131},{131,3},{4... | collective-permute-start | bytes 786440 | tf_op jit(solution)/shard_map/ppermute | solution.py:301
  72.5 13.1 %collective-permute-start.17 = (bf16[2,256,256]{2,1,0:T(8,128)(2,1)S(1)}, bf16[2,256,256]{2,1,0:T(8,128)(2,1)S(1)}, u32[]{:S(2)}, u32[]{:S(2)}) collective-permute-start(bf16[2,256,256]{2,1,0:T(8,128)(2,1)S(1)} %shard_map.62.own.refs_0_), channel_id=1, source_target_pairs={{0,128},{128,0},{1,129},{129,1},{2,130},{130,2},{3,131},{131,3},{4... | collective-permute-start | bytes 786440 | tf_op jit(solution)/shard_map/ppermute | solution.py:301
  73.0 12.7 %collective-permute-start.16 = (bf16[2,256,256]{2,1,0:T(8,128)(2,1)S(1)}, bf16[2,256,256]{2,1,0:T(8,128)(2,1)S(1)}, u32[]{:S(2)}, u32[]{:S(2)}) collective-permute-start(bf16[2,256,256]{2,1,0:T(8,128)(2,1)S(1)} %shard_map.62.own.refs_0_), channel_id=1, source_target_pairs={{0,1},{1,0},{2,3},{3,2},{4,5},{5,4},{6,7},{7,6},{8,9},{9,8},{10,11... | collective-permute-start | bytes 786440 | tf_op jit(solution)/shard_map/ppermute | solution.py:286
  85.7 3.2 %collective-permute-start.18 = (bf16[2,256,256]{2,1,0:T(8,128)(2,1)S(1)}, bf16[2,256,256]{2,1,0:T(8,128)(2,1)S(1)}, u32[]{:S(2)}, u32[]{:S(2)}) collective-permute-start(bf16[2,256,256]{2,1,0:T(8,128)(2,1)S(1)} %collective-permute-done.16.first.refs_1_), channel_id=1, source_target_pairs={{0,128},{128,0},{1,129},{129,1},{2,130},{130,2},{3,131},{131,3},{4... | collective-permute-start | bytes 786440 | tf_op jit(solution)/shard_map/ppermute | solution.py:301
  86.8 2.1 %collective-permute-start.19 = (bf16[2,256,256]{2,1,0:T(8,128)(2,1)S(1)}, bf16[2,256,256]{2,1,0:T(8,128)(2,1)S(1)}, u32[]{:S(2)}, u32[]{:S(2)}) collective-permute-start(bf16[2,256,256]{2,1,0:T(8,128)(2,1)S(1)} %select_bitcast_fusion.second.refs_2_), channel_id=1, source_target_pairs={{0,128},{128,0},{1,129},{129,1},{2,130},{130,2},{3,131},{131,3},{4... | collective-permute-start | bytes 786440 | tf_op jit(solution)/shard_map/ppermute | solution.py:301

commit v7 on v6

--- a/solution.py
+++ b/solution.py
@@ -27,11 +27,18 @@
     return jnp.where(odd == (row < 2), one, other)
 
 
-def fill(target, own, first, second, odd, base=0):
-    for row in range(2):
-        widen(target, row, halo_row(first, second, odd, row))
-        widen(target, row + 2, own[base + row])
-        widen(target, row + 4, halo_row(first, second, odd, row + 2))
+def spread(own, first, second, base=0):
+    odd = is_odd()
+    return (
+        [functools.partial(halo_row, first, second, odd, row) for row in range(2)]
+        + [functools.partial(lambda row: own[base + row], row) for row in range(2)]
+        + [functools.partial(halo_row, first, second, odd, row) for row in range(2, 4)]
+    )
+
+
+def fill(target, rows):
+    for row, value in enumerate(rows):
+        widen(target, row, value())
 
 
 def taps(source, start, rows):
@@ -50,8 +57,11 @@
     return jnp.dot(left, right, preferred_element_type=jnp.float32)
 
 
-def active(lag, layer):
-    return layer == 0 if lag == 0 else layer == 1 if lag == 3 else layer >= 0
+def where_active(lag, work):
+    if lag in (0, 3):
+        pl.when(lax.axis_index("layer") == (0 if lag == 0 else 1))(work)
+    else:
+        work()
 
 
 def is_odd():
@@ -84,9 +94,8 @@
 def early_kernel(lag, own, first, second, wg, pre_r, pre_u, wide):
     cols, channels = own.shape[1:]
 
-    @pl.when(active(lag, lax.axis_index("layer")))
-    def _():
-        fill(wide, own, first, second, is_odd())
+    def work():
+        fill(wide, spread(own, first, second))
         inner = product(taps(wide, 1, 2), columns(wg, 0, channels, 0, 2 * channels))
         edges = jnp.concatenate([taps(wide, 0, 1), taps(wide, 3, 1)], 0)
         outer = product(edges, columns(wg, 0, channels, channels, 2 * channels))
@@ -95,19 +104,20 @@
         pre_r[0:cols] = outer[0:cols]
         pre_r[3 * cols : 4 * cols] = outer[cols : 2 * cols]
 
+    where_active(lag, work)
+
 
 def late_body(lag, own, first, second, pre, x0, x1, wg, wc, bias, wide, wide_r, store):
     cols, channels = own.shape[1:]
-    layer, odd = lax.axis_index("layer"), is_odd()
-    if lag < 3:
-        @pl.when(layer == 0)
-        def _():
-            fill(wide, *x0, odd, 2 * lag)
-
-    if lag > 0:
-        @pl.when(layer == 1)
-        def _():
-            fill(wide, *x1, odd)
+    odd = is_odd()
+    if lag == 0:
+        fill(wide, spread(*x0))
+    elif lag == 3:
+        fill(wide, spread(*x1))
+    else:
+        lower = lax.axis_index("layer") == 0
+        for row, (one, other) in enumerate(zip(spread(*x0, 2 * lag), spread(*x1))):
+            widen(wide, row, jnp.where(lower, one(), other()))
 
     of_reset = product(taps(wide, 0, 4), columns(wg, 0, channels, channels, 2 * channels))
     for row in range(4):
@@ -141,12 +151,12 @@
     def store(row, value):
         out[row] = value
 
-    @pl.when(active(lag, lax.axis_index("layer")))
-    def _():
+    def work():
         late_body(
             lag, own, first, second, (pre_r, pre_u), x0, x1, wg, wc, bias, wide, wide_r, store
         )
 
+    where_active(lag, work)
     if lag == 0:
         @pl.when(lax.axis_index("layer") == 1)
         def _():
@@ -292,7 +302,8 @@
     for layer in range(2):
         groups += [[layer * count + low, layer * count + low + 1] for low in range(1, count - 1, 2)]
     both = lax.all_gather(field, ("layer", "rows"), axis_index_groups=groups)
-    both, beside = lax.optimization_barrier((both, beside))
+    if beside is not None:
+        both, beside = lax.optimization_barrier((both, beside))
     partner = jnp.where(odd, both[1], both[0])
     return jnp.where(inner, partner, jnp.zeros_like(partner)), beside
 
@@ -328,7 +339,8 @@
     for step in range(1, 4):
         first = pair_swap(hidden, 0)
         own_below = across(hidden)
-        second, own_below = gathered_swap(hidden, odd, inner, own_below)
+        second, waited = gathered_swap(hidden, odd, inner, own_below if step > 1 else None)
+        own_below = waited if step > 1 else own_below
         below = (own_below, across(first), across(second))
         state = (hidden, first, second)
         pre = early(step, state, wg_state)

time: 94.2 us -> 91 us (0.966)
  blocking collectives: 38.1 us -> 35.3 us
  Pallas kernels: 22.8 us -> 21.5 us
    all_gather x3, blocking collectives: 38.1 us -> 35.3 us  [gathered_swap(): both = lax.all_gather(field, ('layer', 'rows'), axis_index_groups=groups)]
    pallas_call x3, Pallas kernels: 8.96 us -> 7.9 us  [late(): pl.pallas_call(functools.partial(late_kernel, lag), out_shape=jax.ShapeDt...]
  transfers between devices with their start and end apart: 20 -> 20, of which waited for: 1 -> 1; matrix products, arithmetic and copies ran while one was open for 0% -> 0% of each run, Pallas kernels for 8% -> 9%
where the time goes in v7:
time: 91 us; the launch traced here: 90.8 us
  blocking collectives  35.3 us (39%)
  starting transfers between devices  28.5 us (31%)
  Pallas kernels  21.5 us (24%)
  waiting for transfers between devices  4.86 us (5%)
    all_gather x3, blocking collectives, gathered_swap(): both = lax.all_gather(field, ('layer', 'rows'), axis_index_groups=groups)  35.3 us
    ppermute x13, starting transfers between devices, across(): return lax.ppermute(field, 'layer', [(0, 1), (1, 0)])  14.3 us
    ppermute x7, starting transfers between devices, pair_swap(): return lax.ppermute(field, 'rows', route)  14.2 us
    pallas_call x3, Pallas kernels, late(): pl.pallas_call(functools.partial(late_kernel, lag), out_shape=jax.ShapeDt...  7.9 us
    pallas_call x4, Pallas kernels, early(): pl.pallas_call(functools.partial(early_kernel, lag), out_shape=[pre(4), p...  6.09 us
    ppermute x7, waiting for transfers between devices, pair_swap(): return lax.ppermute(field, 'rows', route)  4.82 us
    pallas_call x1, Pallas kernels, last(): pl.pallas_call(last_kernel, out_shape=jax.ShapeDtypeStruct((3, 2, cols, c...  4.63 us
    pallas_call x1, Pallas kernels, stage(): pl.pallas_call(stage_kernel, out_shape=jax.ShapeDtypeStruct((3, 3, depth...  1.83 us
  transfers between devices with their start and end apart: 20, of which 1 were waited for; matrix products, arithmetic and copies ran while one was open for 0% of the time, Pallas kernels for 9%

profile of v7, /device:TPU:25, one launch (start us, length us, event | category | flops | bytes accessed | tf_op | source)
XLA Modules:
  0.0 90.8 jit_solution(1492009438083098444)
XLA Ops:
  0.0 1.0 %shard_map.55 = (bf16[2,256,256]{2,1,0:T(8,128)(2,1)S(1)}, bf16[2,256,256]{2,1,0:T(8,128)(2,1)S(1)}) custom-call(bf16[2,256,256]{2,1,0:T(8,128)(2,1)} %bitcast.26, bf16[6,256,256]{2,1,0:T(8,128)(2,1)} %bitcast.22), custom_call_target="tpu_custom_call" | custom-call | tf_op jit(solution)/shard_map/pallas_call | solution.py:224
  1.1 1.7 %collective-permute-start = (bf16[2,256,256]{2,1,0:T(8,128)(2,1)S(1)}, bf16[2,256,256]{2,1,0:T(8,128)(2,1)S(1)}, u32[]{:S(2)}, u32[]{:S(2)}) collective-permute-start(bf16[2,256,256]{2,1,0:T(8,128)(2,1)S(1)} %get-tuple-element.27.own.refs_8_), channel_id=1, source_target_pairs={{0,1},{1,0},{2,3},{3,2},{4,5},{5,4},{6,7},{7,6},{8,9},{9,8},{10,11... | collective-permute-start | bytes 786440 | tf_op jit(solution)/shard_map/ppermute | solution.py:296
  2.8 8.9 %collective-permute-start.1 = (bf16[2,256,256]{2,1,0:T(8,128)(2,1)S(1)}, bf16[2,256,256]{2,1,0:T(8,128)(2,1)S(1)}, u32[]{:S(2)}, u32[]{:S(2)}) collective-permute-start(bf16[2,256,256]{2,1,0:T(8,128)(2,1)S(1)} %get-tuple-element.27.own.refs_8_), channel_id=1, source_target_pairs={{1,2},{2,1},{3,4},{4,3},{5,6},{6,5},{7,8},{8,7},{9,10},{10,9},{11,... | collective-permute-start | bytes 786440 | tf_op jit(solution)/shard_map/ppermute | solution.py:296
  11.7 0.1 collective-permute-start.2
  11.8 3.3 %collective-permute-start.3 = (bf16[2,256,256]{2,1,0:T(8,128)(2,1)S(1)}, bf16[2,256,256]{2,1,0:T(8,128)(2,1)S(1)}, u32[]{:S(2)}, u32[]{:S(2)}) collective-permute-start(bf16[2,256,256]{2,1,0:T(8,128)(2,1)S(1)} %get-tuple-element.31), channel_id=1, source_target_pairs={{1,2},{2,1},{3,4},{4,3},{5,6},{6,5},{7,8},{8,7},{9,10},{10,9},{11,... | collective-permute-start | bytes 786440 | tf_op jit(solution)/shard_map/ppermute | solution.py:296
  15.2 0.0 slice-start
  15.2 0.0 slice-start.1
  15.2 1.8 %shard_map.56.wg = bf16[3,3,256,512]{3,2,1,0:T(8,128)(2,1)S(1)} custom-call(bf16[3,3,512,512]{3,2,1,0:T(8,128)(2,1)} %bitcast.11), custom_call_target="tpu_custom_call" | custom-call | tf_op jit(solution)/shard_map/pallas_call | solution.py:236
  17.0 0.0 copy-start
  17.0 0.0 copy-start.1
  17.1 0.0 copy-start.2
  17.1 0.0 copy-start.3
  17.1 0.0 collective-permute-done.first.refs_1_.refs_9_
  17.1 1.9 %collective-permute-start.4 = (bf16[2,256,256]{2,1,0:T(8,128)(2,1)S(1)}, bf16[2,256,256]{2,1,0:T(8,128)(2,1)S(1)}, u32[]{:S(2)}, u32[]{:S(2)}) collective-permute-start(bf16[2,256,256]{2,1,0:T(8,128)(2,1)S(1)} %collective-permute-done.first.refs_1_.refs_9_), channel_id=1, source_target_pairs={{0,128},{128,0},{1,129},{129,1},{2,130},{130,2},{3,131},{131,3},{4... | collective-permute-start | bytes 786440 | tf_op jit(solution)/shard_map/ppermute | solution.py:312
  19.0 0.0 collective-permute-done.1.second.refs_2_.refs_10_
  19.0 0.7 collective-permute-start.5
  19.7 0.0 collective-permute-done.2.refs_6_
  19.7 4.8 %collective-permute-done.3.refs_7_ = bf16[2,256,256]{2,1,0:T(8,128)(2,1)S(1)} collective-permute-done((bf16[2,256,256]{2,1,0:T(8,128)(2,1)S(1)}, bf16[2,256,256]{2,1,0:T(8,128)(2,1)S(1)}, u32[]{:S(2)}, u32[]{:S(2)}) %collective-permute-start.3) | collective-permute-done | bytes 262176 | tf_op jit(solution)/shard_map/ppermute | solution.py:296
  24.5 0.0 collective-permute-done.4.refs_6_
  24.5 0.0 collective-permute-done.5.refs_7_
  24.5 0.0 slice-done
  24.5 0.0 slice-done.1
  24.5 0.0 copy-done
  24.5 0.0 copy-done.1
  24.5 0.0 copy-done.2
  24.6 0.0 copy-done.3
  24.6 0.1 collective-permute-start.6
  24.7 10.1 %all-gather = bf16[4,256,256]{2,1,0:T(8,128)(2,1)S(1)} all-gather(bf16[2,256,256]{2,1,0:T(8,128)(2,1)S(1)} %shard_map.58.own.refs_0_.refs_11_), channel_id=2, replica_groups={{0,128},{127,255},{1,2},{3,4},{5,6},{7,8},{9,10},{11,12},{13,14},{15,16..., dimensions={0}, use_global_device_ids=true | all-gather | bytes 786432 | tf_op jit(solution)/shard_map/all_gather | solution.py:304
  34.8 7.2 %collective-permute-start.7 = (bf16[2,256,256]{2,1,0:T(8,128)(2,1)S(1)}, bf16[2,256,256]{2,1,0:T(8,128)(2,1)S(1)}, u32[]{:S(2)}, u32[]{:S(2)}) collective-permute-start(bf16[2,256,256]{2,1,0:T(8,128)(2,1)S(1)} %shard_map.58.own.refs_0_.refs_11_), channel_id=1, source_target_pairs={{0,128},{128,0},{1,129},{129,1},{2,130},{130,2},{3,131},{131,3},{4... | collective-permute-start | bytes 786440 | tf_op jit(solution)/shard_map/ppermute | solution.py:312
  42.1 0.1 collective-permute-start.9
  42.2 0.0 collective-permute-done.6.first.refs_1_
  42.2 0.5 collective-permute-start.8
  42.7 2.0 %shard_map.59 = (f32[1024,256]{1,0:T(8,128)S(1)}, f32[512,256]{1,0:T(8,128)S(1)}) custom-call(bf16[2,256,256]{2,1,0:T(8,128)(2,1)S(1)} %shard_map.58.own.refs_0_.refs_11_, bf16[2,256,256]{2,1,0:T(8,128)(2,1)S(1)} %collective-permute-done.6.first.refs_1_, bf16[2,256,256]{2,1,0:T(8,128)(2,1)S(1)} %fusion.second.refs_2_, bf16[3,3,256,512]{3,2,1,0:T(8,128)(2,1)S(1)} %shard_map.56.wg), custom_call_target="tpu_custom_call" | custom-call | flops 1811939328 | bytes 1048576 | tf_op jit(solution)/shard_map/pallas_call | solution.py:249
  44.7 0.0 collective-permute-done.7.refs_8_
  44.7 0.0 collective-permute-done.9.refs_10_
  44.7 0.0 collective-permute-done.8.refs_9_
  44.7 3.9 %shard_map.60.own.refs_0_.refs_12_ = bf16[2,256,256]{2,1,0:T(8,128)(2,1)S(1)} custom-call(bf16[2,256,256]{2,1,0:T(8,128)(2,1)S(1)} %shard_map.58.own.refs_0_.refs_11_, bf16[2,256,256]{2,1,0:T(8,128)(2,1)S(1)} %collective-permute-done.6.first.refs_1_, bf16[2,256,256]{2,1,0:T(8,128)(2,1)S(1)} %fusion.second.refs_2_, ...), custom_call_target="tpu_custom_call" | custom-call | flops 3019898880 | bytes 1048576 | tf_op jit(solution)/shard_map/pallas_call | solution.py:262
  48.6 0.4 collective-permute-start.11
  49.0 0.2 collective-permute-start.12
  49.2 0.3 collective-permute-start.13
  49.5 0.0 collective-permute-start.10
  49.5 12.6 %all-gather.1 = bf16[4,256,256]{2,1,0:T(8,128)(2,1)S(1)} all-gather(bf16[2,256,256]{2,1,0:T(8,128)(2,1)S(1)} %shard_map.60.own.refs_0_.refs_12_), channel_id=3, replica_groups={{0,128},{127,255},{1,2},{3,4},{5,6},{7,8},{9,10},{11,12},{13,14},{15,16..., dimensions={0}, use_global_device_ids=true | all-gather | bytes 786432 | tf_op jit(solution)/shard_map/all_gather | solution.py:304
  62.1 0.0 collective-permute-done.11.refs_8_
  62.1 0.0 collective-permute-done.10.first.refs_1_
  62.2 1.1 %collective-permute-start.14 = (bf16[2,256,256]{2,1,0:T(8,128)(2,1)S(1)}, bf16[2,256,256]{2,1,0:T(8,128)(2,1)S(1)}, u32[]{:S(2)}, u32[]{:S(2)}) collective-permute-start(bf16[2,256,256]{2,1,0:T(8,128)(2,1)S(1)} %collective-permute-done.10.first.refs_1_), channel_id=1, source_target_pairs={{0,128},{128,0},{1,129},{129,1},{2,130},{130,2},{3,131},{131,3},{4... | collective-permute-start | bytes 786440 | tf_op jit(solution)/shard_map/ppermute | solution.py:312
  63.3 0.1 collective-permute-start.15
  63.4 2.0 %shard_map.61 = (f32[1024,256]{1,0:T(8,128)S(1)}, f32[512,256]{1,0:T(8,128)S(1)}) custom-call(bf16[2,256,256]{2,1,0:T(8,128)(2,1)S(1)} %shard_map.60.own.refs_0_.refs_12_, bf16[2,256,256]{2,1,0:T(8,128)(2,1)S(1)} %collective-permute-done.10.first.refs_1_, bf16[2,256,256]{2,1,0:T(8,128)(2,1)S(1)} %select_bitcast_fusion.1.second.refs_2_, ...), custom_call_target="tpu_custom_call" | custom-call | flops 1811939328 | bytes 1048576 | tf_op jit(solution)/shard_map/pallas_call | solution.py:249
  65.4 0.0 collective-permute-done.12.refs_6_
  65.4 0.0 collective-permute-done.13.refs_7_
  65.4 0.0 collective-permute-done.14.refs_9_
  65.4 0.0 collective-permute-done.15.refs_10_
  65.5 3.9 %shard_map.62.own.refs_0_ = bf16[2,256,256]{2,1,0:T(8,128)(2,1)S(1)} custom-call(bf16[2,256,256]{2,1,0:T(8,128)(2,1)S(1)} %shard_map.60.own.refs_0_.refs_12_, bf16[2,256,256]{2,1,0:T(8,128)(2,1)S(1)} %collective-permute-done.10.first.refs_1_, bf16[2,256,256]{2,1,0:T(8,128)(2,1)S(1)} %select_bitcast_fusion.1.second.refs_2_, ...), custom_call_target="tpu_custom_call" | custom-call | flops 3019898880 | bytes 1048576 | tf_op jit(solution)/shard_map/pallas_call | solution.py:262
  69.4 0.7 collective-permute-start.17
  70.1 0.0 collective-permute-start.16
  70.1 12.7 %all-gather.2 = bf16[4,256,256]{2,1,0:T(8,128)(2,1)S(1)} all-gather(bf16[2,256,256]{2,1,0:T(8,128)(2,1)S(1)} %shard_map.62.own.refs_0_), channel_id=4, replica_groups={{0,128},{127,255},{1,2},{3,4},{5,6},{7,8},{9,10},{11,12},{13,14},{15,16..., dimensions={0}, use_global_device_ids=true | all-gather | bytes 786432 | tf_op jit(solution)/shard_map/all_gather | solution.py:304
  82.8 0.0 collective-permute-done.17.refs_5_
  82.8 0.0 collective-permute-done.16.first.refs_1_
  82.8 1.0 %collective-permute-start.18 = (bf16[2,256,256]{2,1,0:T(8,128)(2,1)S(1)}, bf16[2,256,256]{2,1,0:T(8,128)(2,1)S(1)}, u32[]{:S(2)}, u32[]{:S(2)}) collective-permute-start(bf16[2,256,256]{2,1,0:T(8,128)(2,1)S(1)} %collective-permute-done.16.first.refs_1_), channel_id=1, source_target_pairs={{0,128},{128,0},{1,129},{129,1},{2,130},{130,2},{3,131},{131,3},{4... | collective-permute-start | bytes 786440 | tf_op jit(solution)/shard_map/ppermute | solution.py:312
  83.9 0.1 collective-permute-start.19
  84.0 2.0 %shard_map.63 = (f32[1024,256]{1,0:T(8,128)S(1)}, f32[512,256]{1,0:T(8,128)S(1)}) custom-call(bf16[2,256,256]{2,1,0:T(8,128)(2,1)S(1)} %shard_map.62.own.refs_0_, bf16[2,256,256]{2,1,0:T(8,128)(2,1)S(1)} %collective-permute-done.16.first.refs_1_, bf16[2,256,256]{2,1,0:T(8,128)(2,1)S(1)} %select_bitcast_fusion.second.refs_2_, ...), custom_call_target="tpu_custom_call" | custom-call | flops 1811939328 | bytes 1048576 | tf_op jit(solution)/shard_map/pallas_call | solution.py:249
  86.0 0.0 collective-permute-done.18.refs_6_
  86.0 0.0 collective-permute-done.19.refs_7_
  86.0 4.6 %shard_map.64 = bf16[3,2,256,256]{3,2,1,0:T(8,128)(2,1)} custom-call(bf16[2,256,256]{2,1,0:T(8,128)(2,1)S(1)} %shard_map.62.own.refs_0_, bf16[2,256,256]{2,1,0:T(8,128)(2,1)S(1)} %collective-permute-done.16.first.refs_1_, bf16[2,256,256]{2,1,0:T(8,128)(2,1)S(1)} %select_bitcast_fusion.second.refs_2_, f32[1024,256]{1,0:T(8,128)S(1)} %get-tuple-element.44.refs_3_, ...), custom_call_target="tpu_custom_call" | custom-call | flops 3019898880 | bytes 1048576 | tf_op jit(solution)/shard_map/pallas_call | solution.py:275
  (6 shorter events, 0.1 us)
Async XLA Ops:
  1.1 16.0 %collective-permute-start = (bf16[2,256,256]{2,1,0:T(8,128)(2,1)S(1)}, bf16[2,256,256]{2,1,0:T(8,128)(2,1)S(1)}, u32[]{:S(2)}, u32[]{:S(2)}) collective-permute-start(bf16[2,256,256]{2,1,0:T(8,128)(2,1)S(1)} %get-tuple-element.27.own.refs_8_), channel_id=1, source_target_pairs={{0,1},{1,0},{2,3},{3,2},{4,5},{5,4},{6,7},{7,6},{8,9},{9,8},{10,11... | collective-permute-start | bytes 786440 | tf_op jit(solution)/shard_map/ppermute | solution.py:296
  2.8 16.2 %collective-permute-start.1 = (bf16[2,256,256]{2,1,0:T(8,128)(2,1)S(1)}, bf16[2,256,256]{2,1,0:T(8,128)(2,1)S(1)}, u32[]{:S(2)}, u32[]{:S(2)}) collective-permute-start(bf16[2,256,256]{2,1,0:T(8,128)(2,1)S(1)} %get-tuple-element.27.own.refs_8_), channel_id=1, source_target_pairs={{1,2},{2,1},{3,4},{4,3},{5,6},{6,5},{7,8},{8,7},{9,10},{10,9},{11,... | collective-permute-start | bytes 786440 | tf_op jit(solution)/shard_map/ppermute | solution.py:296
  11.7 8.0 %collective-permute-start.2 = (bf16[2,256,256]{2,1,0:T(8,128)(2,1)S(1)}, bf16[2,256,256]{2,1,0:T(8,128)(2,1)S(1)}, u32[]{:S(2)}, u32[]{:S(2)}) collective-permute-start(bf16[2,256,256]{2,1,0:T(8,128)(2,1)S(1)} %get-tuple-element.31), channel_id=1, source_target_pairs={{0,1},{1,0},{2,3},{3,2},{4,5},{5,4},{6,7},{7,6},{8,9},{9,8},{10,11... | collective-permute-start | bytes 786440 | tf_op jit(solution)/shard_map/ppermute | solution.py:296
  11.8 12.7 %collective-permute-start.3 = (bf16[2,256,256]{2,1,0:T(8,128)(2,1)S(1)}, bf16[2,256,256]{2,1,0:T(8,128)(2,1)S(1)}, u32[]{:S(2)}, u32[]{:S(2)}) collective-permute-start(bf16[2,256,256]{2,1,0:T(8,128)(2,1)S(1)} %get-tuple-element.31), channel_id=1, source_target_pairs={{1,2},{2,1},{3,4},{4,3},{5,6},{6,5},{7,8},{8,7},{9,10},{10,9},{11,... | collective-permute-start | bytes 786440 | tf_op jit(solution)/shard_map/ppermute | solution.py:296
  15.2 9.3 %slice-start = ((s8[4718592]{0:T(1024)(128)(4,1)}), s8[4194304]{0:T(1024)(128)(4,1)S(1)}, s32[]{:S(2)}) async-start(s8[4718592]{0:T(1024)(128)(4,1)} %bitcast.12), calls=%async_computation | async-start | bytes 8388608
  15.2 9.3 %slice-start.1 = ((s8[4718592]{0:T(1024)(128)(4,1)}), s8[524288]{0:T(1024)(128)(4,1)S(1)}, s32[]{:S(2)}) async-start(s8[4718592]{0:T(1024)(128)(4,1)} %bitcast.12), calls=%async_computation.1 | async-start | bytes 1048576
  17.0 7.5 %copy-start = (bf16[1,3,3,512,256]{4,3,2,1,0:T(8,128)(2,1)S(1)}, bf16[1,3,3,512,256]{4,3,2,1,0:T(8,128)(2,1)}, u32[]{:S(2)}) copy-start(bf16[1,3,3,512,256]{4,3,2,1,0:T(8,128)(2,1)} %param.8) | copy-start | bytes 7077892
  17.0 7.5 %copy-start.1 = (bf16[3,2,256,256]{3,2,1,0:T(8,128)(2,1)S(1)}, bf16[3,2,256,256]{3,2,1,0:T(8,128)(2,1)}, u32[]{:S(2)}) copy-start(bf16[3,2,256,256]{3,2,1,0:T(8,128)(2,1)} %param.5) | copy-start | bytes 2359300
  17.1 7.5 %copy-start.2 = (bf16[1,2,256,256]{3,2,1,0:T(8,128)(2,1)S(1)}, bf16[1,2,256,256]{3,2,1,0:T(8,128)(2,1)}, u32[]{:S(2)}) copy-start(bf16[1,2,256,256]{3,2,1,0:T(8,128)(2,1)} %param.6) | copy-start | bytes 786436
  17.1 7.5 %copy-start.3 = (f32[1,768]{1,0:T(1,128)S(1)}, f32[1,768]{1,0:T(1,128)}, u32[]{:S(2)}) copy-start(f32[1,768]{1,0:T(1,128)} %refs_10_.1) | copy-start | bytes 9220
  17.1 7.4 %collective-permute-start.4 = (bf16[2,256,256]{2,1,0:T(8,128)(2,1)S(1)}, bf16[2,256,256]{2,1,0:T(8,128)(2,1)S(1)}, u32[]{:S(2)}, u32[]{:S(2)}) collective-permute-start(bf16[2,256,256]{2,1,0:T(8,128)(2,1)S(1)} %collective-permute-done.first.refs_1_.refs_9_), channel_id=1, source_target_pairs={{0,128},{128,0},{1,129},{129,1},{2,130},{130,2},{3,131},{131,3},{4... | collective-permute-start | bytes 786440 | tf_op jit(solution)/shard_map/ppermute | solution.py:312
  19.0 5.5 %collective-permute-start.5 = (bf16[2,256,256]{2,1,0:T(8,128)(2,1)S(1)}, bf16[2,256,256]{2,1,0:T(8,128)(2,1)S(1)}, u32[]{:S(2)}, u32[]{:S(2)}) collective-permute-start(bf16[2,256,256]{2,1,0:T(8,128)(2,1)S(1)} %collective-permute-done.1.second.refs_2_.refs_10_), channel_id=1, source_target_pairs={{0,128},{128,0},{1,129},{129,1},{2,130},{130,2},{3,131},{131,3},{4... | collective-permute-start | bytes 786440 | tf_op jit(solution)/shard_map/ppermute | solution.py:312
  24.6 17.5 %collective-permute-start.6 = (bf16[2,256,256]{2,1,0:T(8,128)(2,1)S(1)}, bf16[2,256,256]{2,1,0:T(8,128)(2,1)S(1)}, u32[]{:S(2)}, u32[]{:S(2)}) collective-permute-start(bf16[2,256,256]{2,1,0:T(8,128)(2,1)S(1)} %shard_map.58.own.refs_0_.refs_11_), channel_id=1, source_target_pairs={{0,1},{1,0},{2,3},{3,2},{4,5},{5,4},{6,7},{7,6},{8,9},{9,8},{10,11... | collective-permute-start | bytes 786440 | tf_op jit(solution)/shard_map/ppermute | solution.py:296
  34.8 9.8 %collective-permute-start.7 = (bf16[2,256,256]{2,1,0:T(8,128)(2,1)S(1)}, bf16[2,256,256]{2,1,0:T(8,128)(2,1)S(1)}, u32[]{:S(2)}, u32[]{:S(2)}) collective-permute-start(bf16[2,256,256]{2,1,0:T(8,128)(2,1)S(1)} %shard_map.58.own.refs_0_.refs_11_), channel_id=1, source_target_pairs={{0,128},{128,0},{1,129},{129,1},{2,130},{130,2},{3,131},{131,3},{4... | collective-permute-start | bytes 786440 | tf_op jit(solution)/shard_map/ppermute | solution.py:312
  42.1 2.6 %collective-permute-start.9 = (bf16[2,256,256]{2,1,0:T(8,128)(2,1)S(1)}, bf16[2,256,256]{2,1,0:T(8,128)(2,1)S(1)}, u32[]{:S(2)}, u32[]{:S(2)}) collective-permute-start(bf16[2,256,256]{2,1,0:T(8,128)(2,1)S(1)} %fusion.second.refs_2_), channel_id=1, source_target_pairs={{0,128},{128,0},{1,129},{129,1},{2,130},{130,2},{3,131},{131,3},{4... | collective-permute-start | bytes 786440 | tf_op jit(solution)/shard_map/ppermute | solution.py:312
  42.2 2.5 %collective-permute-start.8 = (bf16[2,256,256]{2,1,0:T(8,128)(2,1)S(1)}, bf16[2,256,256]{2,1,0:T(8,128)(2,1)S(1)}, u32[]{:S(2)}, u32[]{:S(2)}) collective-permute-start(bf16[2,256,256]{2,1,0:T(8,128)(2,1)S(1)} %collective-permute-done.6.first.refs_1_), channel_id=1, source_target_pairs={{0,128},{128,0},{1,129},{129,1},{2,130},{130,2},{3,131},{131,3},{4... | collective-permute-start | bytes 786440 | tf_op jit(solution)/shard_map/ppermute | solution.py:312
  48.6 13.5 %collective-permute-start.11 = (bf16[2,256,256]{2,1,0:T(8,128)(2,1)S(1)}, bf16[2,256,256]{2,1,0:T(8,128)(2,1)S(1)}, u32[]{:S(2)}, u32[]{:S(2)}) collective-permute-start(bf16[2,256,256]{2,1,0:T(8,128)(2,1)S(1)} %shard_map.60.own.refs_0_.refs_12_), channel_id=1, source_target_pairs={{0,128},{128,0},{1,129},{129,1},{2,130},{130,2},{3,131},{131,3},{4... | collective-permute-start | bytes 786440 | tf_op jit(solution)/shard_map/ppermute | solution.py:312
  49.0 16.4 %collective-permute-start.12 = (bf16[2,256,256]{2,1,0:T(8,128)(2,1)S(1)}, bf16[2,256,256]{2,1,0:T(8,128)(2,1)S(1)}, u32[]{:S(2)}, u32[]{:S(2)}) collective-permute-start(bf16[2,256,256]{2,1,0:T(8,128)(2,1)S(1)} %collective-permute-done.2.refs_6_), channel_id=1, source_target_pairs={{0,128},{128,0},{1,129},{129,1},{2,130},{130,2},{3,131},{131,3},{4... | collective-permute-start | bytes 786440 | tf_op jit(solution)/shard_map/ppermute | solution.py:312
  49.2 16.2 %collective-permute-start.13 = (bf16[2,256,256]{2,1,0:T(8,128)(2,1)S(1)}, bf16[2,256,256]{2,1,0:T(8,128)(2,1)S(1)}, u32[]{:S(2)}, u32[]{:S(2)}) collective-permute-start(bf16[2,256,256]{2,1,0:T(8,128)(2,1)S(1)} %collective-permute-done.3.refs_7_), channel_id=1, source_target_pairs={{0,128},{128,0},{1,129},{129,1},{2,130},{130,2},{3,131},{131,3},{4... | collective-permute-start | bytes 786440 | tf_op jit(solution)/shard_map/ppermute | solution.py:312
  49.5 12.6 %collective-permute-start.10 = (bf16[2,256,256]{2,1,0:T(8,128)(2,1)S(1)}, bf16[2,256,256]{2,1,0:T(8,128)(2,1)S(1)}, u32[]{:S(2)}, u32[]{:S(2)}) collective-permute-start(bf16[2,256,256]{2,1,0:T(8,128)(2,1)S(1)} %shard_map.60.own.refs_0_.refs_12_), channel_id=1, source_target_pairs={{0,1},{1,0},{2,3},{3,2},{4,5},{5,4},{6,7},{7,6},{8,9},{9,8},{10,11... | collective-permute-start | bytes 786440 | tf_op jit(solution)/shard_map/ppermute | solution.py:296
  62.2 3.3 %collective-permute-start.14 = (bf16[2,256,256]{2,1,0:T(8,128)(2,1)S(1)}, bf16[2,256,256]{2,1,0:T(8,128)(2,1)S(1)}, u32[]{:S(2)}, u32[]{:S(2)}) collective-permute-start(bf16[2,256,256]{2,1,0:T(8,128)(2,1)S(1)} %collective-permute-done.10.first.refs_1_), channel_id=1, source_target_pairs={{0,128},{128,0},{1,129},{129,1},{2,130},{130,2},{3,131},{131,3},{4... | collective-permute-start | bytes 786440 | tf_op jit(solution)/shard_map/ppermute | solution.py:312
  63.3 2.2 %collective-permute-start.15 = (bf16[2,256,256]{2,1,0:T(8,128)(2,1)S(1)}, bf16[2,256,256]{2,1,0:T(8,128)(2,1)S(1)}, u32[]{:S(2)}, u32[]{:S(2)}) collective-permute-start(bf16[2,256,256]{2,1,0:T(8,128)(2,1)S(1)} %select_bitcast_fusion.1.second.refs_2_), channel_id=1, source_target_pairs={{0,128},{128,0},{1,129},{129,1},{2,130},{130,2},{3,131},{131,3},{4... | collective-permute-start | bytes 786440 | tf_op jit(solution)/shard_map/ppermute | solution.py:312
  69.4 13.4 %collective-permute-start.17 = (bf16[2,256,256]{2,1,0:T(8,128)(2,1)S(1)}, bf16[2,256,256]{2,1,0:T(8,128)(2,1)S(1)}, u32[]{:S(2)}, u32[]{:S(2)}) collective-permute-start(bf16[2,256,256]{2,1,0:T(8,128)(2,1)S(1)} %shard_map.62.own.refs_0_), channel_id=1, source_target_pairs={{0,128},{128,0},{1,129},{129,1},{2,130},{130,2},{3,131},{131,3},{4... | collective-permute-start | bytes 786440 | tf_op jit(solution)/shard_map/ppermute | solution.py:312
  70.1 12.7 %collective-permute-start.16 = (bf16[2,256,256]{2,1,0:T(8,128)(2,1)S(1)}, bf16[2,256,256]{2,1,0:T(8,128)(2,1)S(1)}, u32[]{:S(2)}, u32[]{:S(2)}) collective-permute-start(bf16[2,256,256]{2,1,0:T(8,128)(2,1)S(1)} %shard_map.62.own.refs_0_), channel_id=1, source_target_pairs={{0,1},{1,0},{2,3},{3,2},{4,5},{5,4},{6,7},{7,6},{8,9},{9,8},{10,11... | collective-permute-start | bytes 786440 | tf_op jit(solution)/shard_map/ppermute | solution.py:296
  82.8 3.2 %collective-permute-start.18 = (bf16[2,256,256]{2,1,0:T(8,128)(2,1)S(1)}, bf16[2,256,256]{2,1,0:T(8,128)(2,1)S(1)}, u32[]{:S(2)}, u32[]{:S(2)}) collective-permute-start(bf16[2,256,256]{2,1,0:T(8,128)(2,1)S(1)} %collective-permute-done.16.first.refs_1_), channel_id=1, source_target_pairs={{0,128},{128,0},{1,129},{129,1},{2,130},{130,2},{3,131},{131,3},{4... | collective-permute-start | bytes 786440 | tf_op jit(solution)/shard_map/ppermute | solution.py:312
  83.9 2.1 %collective-permute-start.19 = (bf16[2,256,256]{2,1,0:T(8,128)(2,1)S(1)}, bf16[2,256,256]{2,1,0:T(8,128)(2,1)S(1)}, u32[]{:S(2)}, u32[]{:S(2)}) collective-permute-start(bf16[2,256,256]{2,1,0:T(8,128)(2,1)S(1)} %select_bitcast_fusion.second.refs_2_), channel_id=1, source_target_pairs={{0,128},{128,0},{1,129},{129,1},{2,130},{130,2},{3,131},{131,3},{4... | collective-permute-start | bytes 786440 | tf_op jit(solution)/shard_map/ppermute | solution.py:312

commit v8 on v7

--- a/solution.py
+++ b/solution.py
@@ -322,18 +322,20 @@
     inner = jnp.logical_and(strip > 0, strip < lax.axis_size("rows") - 1)
     field, later_field = pick(hidden, rows)
     field, odd, inner = lax.optimization_barrier((field, odd, inner))
-    first, second = pair_swap(field, 0), pair_swap(field, 1)
+    second = pair_swap(field, 1)
+    first = pair_swap(field, 0)
     wg_state = stage(wg)
-    late_first, late_second = pair_swap(later_field, 0), pair_swap(later_field, 1)
-    first_after, wg_state = lax.optimization_barrier((first, wg_state))
+    late_second = pair_swap(later_field, 1)
+    late_first = pair_swap(later_field, 0)
+    second_after, wg_state = lax.optimization_barrier((second, wg_state))
     halos = [
-        (across(first_after), across(second)),
+        (across(first), across(second_after)),
         (late_first, late_second),
         (across(late_first), across(late_second)),
     ]
     below = (field, first, second)
     pre = early(0, below, wg_state)
-    pre = lax.optimization_barrier((*pre, late_first, late_second))[0:2]
+    pre = lax.optimization_barrier((*pre, late_second, late_first))[0:2]
     hidden = late(0, (hidden, first, second), pre, (rows, *halos[0]), below, wg, wc, biases)
     states = [hidden]
     for step in range(1, 4):

time: 91 us -> 90.2 us (level)
  transfers between devices with their start and end apart: 20 -> 20, of which waited for: 1 -> 3; matrix products, arithmetic and copies ran while one was open for 0% -> 0% of each run, Pallas kernels for 9% -> 9%
where the time goes in v8:
time: 90.2 us; the launch traced here: 90 us
  blocking collectives  35.3 us (39%)
  starting transfers between devices  28.3 us (31%)
  Pallas kernels  21.5 us (24%)
  waiting for transfers between devices  4.33 us (5%)
    all_gather x3, blocking collectives, gathered_swap(): both = lax.all_gather(field, ('layer', 'rows'), axis_index_groups=groups)  35.3 us
    ppermute x13, starting transfers between devices, across(): return lax.ppermute(field, 'layer', [(0, 1), (1, 0)])  14.8 us
    ppermute x7, starting transfers between devices, pair_swap(): return lax.ppermute(field, 'rows', route)  13.5 us
    pallas_call x3, Pallas kernels, late(): pl.pallas_call(functools.partial(late_kernel, lag), out_shape=jax.ShapeDt...  7.88 us
    pallas_call x4, Pallas kernels, early(): pl.pallas_call(functools.partial(early_kernel, lag), out_shape=[pre(4), p...  6.09 us
    pallas_call x1, Pallas kernels, last(): pl.pallas_call(last_kernel, out_shape=jax.ShapeDtypeStruct((3, 2, cols, c...  4.63 us
    ppermute x7, waiting for transfers between devices, pair_swap(): return lax.ppermute(field, 'rows', route)  4.29 us
    pallas_call x1, Pallas kernels, stage(): pl.pallas_call(stage_kernel, out_shape=jax.ShapeDtypeStruct((3, 3, depth...  1.83 us
  transfers between devices with their start and end apart: 20, of which 3 were waited for; matrix products, arithmetic and copies ran while one was open for 0% of the time, Pallas kernels for 9%

profile of v8, /device:TPU:25, one launch (start us, length us, event | category | flops | bytes accessed | tf_op | source)
XLA Modules:
  0.0 90.0 jit_solution(5774412555563271898)
XLA Ops:
  0.0 1.0 %shard_map.55 = (bf16[2,256,256]{2,1,0:T(8,128)(2,1)S(1)}, bf16[2,256,256]{2,1,0:T(8,128)(2,1)S(1)}) custom-call(bf16[2,256,256]{2,1,0:T(8,128)(2,1)} %bitcast.26, bf16[6,256,256]{2,1,0:T(8,128)(2,1)} %bitcast.22), custom_call_target="tpu_custom_call" | custom-call | tf_op jit(solution)/shard_map/pallas_call | solution.py:224
  1.1 9.9 %collective-permute-start.1 = (bf16[2,256,256]{2,1,0:T(8,128)(2,1)S(1)}, bf16[2,256,256]{2,1,0:T(8,128)(2,1)S(1)}, u32[]{:S(2)}, u32[]{:S(2)}) collective-permute-start(bf16[2,256,256]{2,1,0:T(8,128)(2,1)S(1)} %get-tuple-element.27.own.refs_8_), channel_id=1, source_target_pairs={{1,2},{2,1},{3,4},{4,3},{5,6},{6,5},{7,8},{8,7},{9,10},{10,9},{11,... | collective-permute-start | bytes 786440 | tf_op jit(solution)/shard_map/ppermute | solution.py:296
  10.9 0.1 collective-permute-start
  11.0 3.3 %collective-permute-start.2 = (bf16[2,256,256]{2,1,0:T(8,128)(2,1)S(1)}, bf16[2,256,256]{2,1,0:T(8,128)(2,1)S(1)}, u32[]{:S(2)}, u32[]{:S(2)}) collective-permute-start(bf16[2,256,256]{2,1,0:T(8,128)(2,1)S(1)} %get-tuple-element.31), channel_id=1, source_target_pairs={{1,2},{2,1},{3,4},{4,3},{5,6},{6,5},{7,8},{8,7},{9,10},{10,9},{11,... | collective-permute-start | bytes 786440 | tf_op jit(solution)/shard_map/ppermute | solution.py:296
  14.4 0.1 collective-permute-start.3
  14.5 0.0 slice-start
  14.5 0.0 slice-start.1
  14.5 1.8 %shard_map.56.wg = bf16[3,3,256,512]{3,2,1,0:T(8,128)(2,1)S(1)} custom-call(bf16[3,3,512,512]{3,2,1,0:T(8,128)(2,1)} %bitcast.11), custom_call_target="tpu_custom_call" | custom-call | tf_op jit(solution)/shard_map/pallas_call | solution.py:236
  16.3 0.0 copy-start
  16.3 0.0 copy-start.1
  16.4 0.0 copy-start.2
  16.4 0.0 copy-start.3
  16.4 0.6 collective-permute-done.1.second.refs_2_.refs_10_
  16.9 0.9 %collective-permute-done.first.refs_1_.refs_9_ = bf16[2,256,256]{2,1,0:T(8,128)(2,1)S(1)} collective-permute-done((bf16[2,256,256]{2,1,0:T(8,128)(2,1)S(1)}, bf16[2,256,256]{2,1,0:T(8,128)(2,1)S(1)}, u32[]{:S(2)}, u32[]{:S(2)}) %collective-permute-start) | collective-permute-done | bytes 262176 | tf_op jit(solution)/shard_map/ppermute | solution.py:296
  17.9 3.3 %collective-permute-start.4 = (bf16[2,256,256]{2,1,0:T(8,128)(2,1)S(1)}, bf16[2,256,256]{2,1,0:T(8,128)(2,1)S(1)}, u32[]{:S(2)}, u32[]{:S(2)}) collective-permute-start(bf16[2,256,256]{2,1,0:T(8,128)(2,1)S(1)} %collective-permute-done.first.refs_1_.refs_9_), channel_id=1, source_target_pairs={{0,128},{128,0},{1,129},{129,1},{2,130},{130,2},{3,131},{131,3},{4... | collective-permute-start | bytes 786440 | tf_op jit(solution)/shard_map/ppermute | solution.py:312
  21.2 0.0 collective-permute-start.5
  21.2 2.8 %collective-permute-done.2.refs_7_ = bf16[2,256,256]{2,1,0:T(8,128)(2,1)S(1)} collective-permute-done((bf16[2,256,256]{2,1,0:T(8,128)(2,1)S(1)}, bf16[2,256,256]{2,1,0:T(8,128)(2,1)S(1)}, u32[]{:S(2)}, u32[]{:S(2)}) %collective-permute-start.2) | collective-permute-done | bytes 262176 | tf_op jit(solution)/shard_map/ppermute | solution.py:296
  24.0 0.0 collective-permute-done.3.refs_6_
  24.0 0.0 collective-permute-done.4.refs_6_
  24.0 0.0 collective-permute-done.5.refs_7_
  24.0 0.0 slice-done
  24.0 0.0 slice-done.1
  24.0 0.0 copy-done
  24.0 0.0 copy-done.1
  24.0 0.0 copy-done.2
  24.1 0.0 copy-done.3
  24.1 0.1 collective-permute-start.6
  24.2 10.1 %all-gather = bf16[4,256,256]{2,1,0:T(8,128)(2,1)S(1)} all-gather(bf16[2,256,256]{2,1,0:T(8,128)(2,1)S(1)} %shard_map.58.own.refs_0_.refs_11_), channel_id=2, replica_groups={{0,128},{127,255},{1,2},{3,4},{5,6},{7,8},{9,10},{11,12},{13,14},{15,16..., dimensions={0}, use_global_device_ids=true | all-gather | bytes 786432 | tf_op jit(solution)/shard_map/all_gather | solution.py:304
  34.3 6.9 %collective-permute-start.7 = (bf16[2,256,256]{2,1,0:T(8,128)(2,1)S(1)}, bf16[2,256,256]{2,1,0:T(8,128)(2,1)S(1)}, u32[]{:S(2)}, u32[]{:S(2)}) collective-permute-start(bf16[2,256,256]{2,1,0:T(8,128)(2,1)S(1)} %shard_map.58.own.refs_0_.refs_11_), channel_id=1, source_target_pairs={{0,128},{128,0},{1,129},{129,1},{2,130},{130,2},{3,131},{131,3},{4... | collective-permute-start | bytes 786440 | tf_op jit(solution)/shard_map/ppermute | solution.py:312
  41.3 0.1 collective-permute-start.9
  41.4 0.0 collective-permute-done.6.first.refs_1_
  41.4 0.5 collective-permute-start.8
  41.9 2.0 %shard_map.59 = (f32[1024,256]{1,0:T(8,128)S(1)}, f32[512,256]{1,0:T(8,128)S(1)}) custom-call(bf16[2,256,256]{2,1,0:T(8,128)(2,1)S(1)} %shard_map.58.own.refs_0_.refs_11_, bf16[2,256,256]{2,1,0:T(8,128)(2,1)S(1)} %collective-permute-done.6.first.refs_1_, bf16[2,256,256]{2,1,0:T(8,128)(2,1)S(1)} %fusion.second.refs_2_, bf16[3,3,256,512]{3,2,1,0:T(8,128)(2,1)S(1)} %shard_map.56.wg), custom_call_target="tpu_custom_call" | custom-call | flops 1811939328 | bytes 1048576 | tf_op jit(solution)/shard_map/pallas_call | solution.py:249
  43.9 0.0 collective-permute-done.7.refs_8_
  43.9 0.0 collective-permute-done.9.refs_10_
  43.9 0.0 collective-permute-done.8.refs_9_
  43.9 3.9 %shard_map.60.own.refs_0_.refs_12_ = bf16[2,256,256]{2,1,0:T(8,128)(2,1)S(1)} custom-call(bf16[2,256,256]{2,1,0:T(8,128)(2,1)S(1)} %shard_map.58.own.refs_0_.refs_11_, bf16[2,256,256]{2,1,0:T(8,128)(2,1)S(1)} %collective-permute-done.6.first.refs_1_, bf16[2,256,256]{2,1,0:T(8,128)(2,1)S(1)} %fusion.second.refs_2_, ...), custom_call_target="tpu_custom_call" | custom-call | flops 3019898880 | bytes 1048576 | tf_op jit(solution)/shard_map/pallas_call | solution.py:262
  47.8 0.4 collective-permute-start.11
  48.2 0.2 collective-permute-start.12
  48.4 0.3 collective-permute-start.13
  48.7 0.0 collective-permute-start.10
  48.7 12.6 %all-gather.1 = bf16[4,256,256]{2,1,0:T(8,128)(2,1)S(1)} all-gather(bf16[2,256,256]{2,1,0:T(8,128)(2,1)S(1)} %shard_map.60.own.refs_0_.refs_12_), channel_id=3, replica_groups={{0,128},{127,255},{1,2},{3,4},{5,6},{7,8},{9,10},{11,12},{13,14},{15,16..., dimensions={0}, use_global_device_ids=true | all-gather | bytes 786432 | tf_op jit(solution)/shard_map/all_gather | solution.py:304
  61.3 0.0 collective-permute-done.11.refs_8_
  61.3 0.0 collective-permute-done.10.first.refs_1_
  61.4 1.1 %collective-permute-start.14 = (bf16[2,256,256]{2,1,0:T(8,128)(2,1)S(1)}, bf16[2,256,256]{2,1,0:T(8,128)(2,1)S(1)}, u32[]{:S(2)}, u32[]{:S(2)}) collective-permute-start(bf16[2,256,256]{2,1,0:T(8,128)(2,1)S(1)} %collective-permute-done.10.first.refs_1_), channel_id=1, source_target_pairs={{0,128},{128,0},{1,129},{129,1},{2,130},{130,2},{3,131},{131,3},{4... | collective-permute-start | bytes 786440 | tf_op jit(solution)/shard_map/ppermute | solution.py:312
  62.5 0.1 collective-permute-start.15
  62.6 2.0 %shard_map.61 = (f32[1024,256]{1,0:T(8,128)S(1)}, f32[512,256]{1,0:T(8,128)S(1)}) custom-call(bf16[2,256,256]{2,1,0:T(8,128)(2,1)S(1)} %shard_map.60.own.refs_0_.refs_12_, bf16[2,256,256]{2,1,0:T(8,128)(2,1)S(1)} %collective-permute-done.10.first.refs_1_, bf16[2,256,256]{2,1,0:T(8,128)(2,1)S(1)} %select_bitcast_fusion.1.second.refs_2_, ...), custom_call_target="tpu_custom_call" | custom-call | flops 1811939328 | bytes 1048576 | tf_op jit(solution)/shard_map/pallas_call | solution.py:249
  64.6 0.0 collective-permute-done.12.refs_6_
  64.6 0.0 collective-permute-done.13.refs_7_
  64.6 0.0 collective-permute-done.14.refs_9_
  64.6 0.0 collective-permute-done.15.refs_10_
  64.6 3.9 %shard_map.62.own.refs_0_ = bf16[2,256,256]{2,1,0:T(8,128)(2,1)S(1)} custom-call(bf16[2,256,256]{2,1,0:T(8,128)(2,1)S(1)} %shard_map.60.own.refs_0_.refs_12_, bf16[2,256,256]{2,1,0:T(8,128)(2,1)S(1)} %collective-permute-done.10.first.refs_1_, bf16[2,256,256]{2,1,0:T(8,128)(2,1)S(1)} %select_bitcast_fusion.1.second.refs_2_, ...), custom_call_target="tpu_custom_call" | custom-call | flops 3019898880 | bytes 1048576 | tf_op jit(solution)/shard_map/pallas_call | solution.py:262
  68.6 0.7 collective-permute-start.17
  69.3 0.0 collective-permute-start.16
  69.3 12.7 %all-gather.2 = bf16[4,256,256]{2,1,0:T(8,128)(2,1)S(1)} all-gather(bf16[2,256,256]{2,1,0:T(8,128)(2,1)S(1)} %shard_map.62.own.refs_0_), channel_id=4, replica_groups={{0,128},{127,255},{1,2},{3,4},{5,6},{7,8},{9,10},{11,12},{13,14},{15,16..., dimensions={0}, use_global_device_ids=true | all-gather | bytes 786432 | tf_op jit(solution)/shard_map/all_gather | solution.py:304
  82.0 0.0 collective-permute-done.17.refs_5_
  82.0 0.0 collective-permute-done.16.first.refs_1_
  82.0 1.0 %collective-permute-start.18 = (bf16[2,256,256]{2,1,0:T(8,128)(2,1)S(1)}, bf16[2,256,256]{2,1,0:T(8,128)(2,1)S(1)}, u32[]{:S(2)}, u32[]{:S(2)}) collective-permute-start(bf16[2,256,256]{2,1,0:T(8,128)(2,1)S(1)} %collective-permute-done.16.first.refs_1_), channel_id=1, source_target_pairs={{0,128},{128,0},{1,129},{129,1},{2,130},{130,2},{3,131},{131,3},{4... | collective-permute-start | bytes 786440 | tf_op jit(solution)/shard_map/ppermute | solution.py:312
  83.1 0.1 collective-permute-start.19
  83.2 2.0 %shard_map.63 = (f32[1024,256]{1,0:T(8,128)S(1)}, f32[512,256]{1,0:T(8,128)S(1)}) custom-call(bf16[2,256,256]{2,1,0:T(8,128)(2,1)S(1)} %shard_map.62.own.refs_0_, bf16[2,256,256]{2,1,0:T(8,128)(2,1)S(1)} %collective-permute-done.16.first.refs_1_, bf16[2,256,256]{2,1,0:T(8,128)(2,1)S(1)} %select_bitcast_fusion.second.refs_2_, ...), custom_call_target="tpu_custom_call" | custom-call | flops 1811939328 | bytes 1048576 | tf_op jit(solution)/shard_map/pallas_call | solution.py:249
  85.2 0.0 collective-permute-done.18.refs_6_
  85.2 0.0 collective-permute-done.19.refs_7_
  85.2 4.6 %shard_map.64 = bf16[3,2,256,256]{3,2,1,0:T(8,128)(2,1)} custom-call(bf16[2,256,256]{2,1,0:T(8,128)(2,1)S(1)} %shard_map.62.own.refs_0_, bf16[2,256,256]{2,1,0:T(8,128)(2,1)S(1)} %collective-permute-done.16.first.refs_1_, bf16[2,256,256]{2,1,0:T(8,128)(2,1)S(1)} %select_bitcast_fusion.second.refs_2_, f32[1024,256]{1,0:T(8,128)S(1)} %get-tuple-element.44.refs_3_, ...), custom_call_target="tpu_custom_call" | custom-call | flops 3019898880 | bytes 1048576 | tf_op jit(solution)/shard_map/pallas_call | solution.py:275
  (6 shorter events, 0.1 us)
Async XLA Ops:
  1.1 15.9 %collective-permute-start.1 = (bf16[2,256,256]{2,1,0:T(8,128)(2,1)S(1)}, bf16[2,256,256]{2,1,0:T(8,128)(2,1)S(1)}, u32[]{:S(2)}, u32[]{:S(2)}) collective-permute-start(bf16[2,256,256]{2,1,0:T(8,128)(2,1)S(1)} %get-tuple-element.27.own.refs_8_), channel_id=1, source_target_pairs={{1,2},{2,1},{3,4},{4,3},{5,6},{6,5},{7,8},{8,7},{9,10},{10,9},{11,... | collective-permute-start | bytes 786440 | tf_op jit(solution)/shard_map/ppermute | solution.py:296
  10.9 6.9 %collective-permute-start = (bf16[2,256,256]{2,1,0:T(8,128)(2,1)S(1)}, bf16[2,256,256]{2,1,0:T(8,128)(2,1)S(1)}, u32[]{:S(2)}, u32[]{:S(2)}) collective-permute-start(bf16[2,256,256]{2,1,0:T(8,128)(2,1)S(1)} %get-tuple-element.27.own.refs_8_), channel_id=1, source_target_pairs={{0,1},{1,0},{2,3},{3,2},{4,5},{5,4},{6,7},{7,6},{8,9},{9,8},{10,11... | collective-permute-start | bytes 786440 | tf_op jit(solution)/shard_map/ppermute | solution.py:296
  11.0 13.0 %collective-permute-start.2 = (bf16[2,256,256]{2,1,0:T(8,128)(2,1)S(1)}, bf16[2,256,256]{2,1,0:T(8,128)(2,1)S(1)}, u32[]{:S(2)}, u32[]{:S(2)}) collective-permute-start(bf16[2,256,256]{2,1,0:T(8,128)(2,1)S(1)} %get-tuple-element.31), channel_id=1, source_target_pairs={{1,2},{2,1},{3,4},{4,3},{5,6},{6,5},{7,8},{8,7},{9,10},{10,9},{11,... | collective-permute-start | bytes 786440 | tf_op jit(solution)/shard_map/ppermute | solution.py:296
  14.4 9.6 %collective-permute-start.3 = (bf16[2,256,256]{2,1,0:T(8,128)(2,1)S(1)}, bf16[2,256,256]{2,1,0:T(8,128)(2,1)S(1)}, u32[]{:S(2)}, u32[]{:S(2)}) collective-permute-start(bf16[2,256,256]{2,1,0:T(8,128)(2,1)S(1)} %get-tuple-element.31), channel_id=1, source_target_pairs={{0,1},{1,0},{2,3},{3,2},{4,5},{5,4},{6,7},{7,6},{8,9},{9,8},{10,11... | collective-permute-start | bytes 786440 | tf_op jit(solution)/shard_map/ppermute | solution.py:296
  14.5 9.5 %slice-start = ((s8[4718592]{0:T(1024)(128)(4,1)}), s8[4194304]{0:T(1024)(128)(4,1)S(1)}, s32[]{:S(2)}) async-start(s8[4718592]{0:T(1024)(128)(4,1)} %bitcast.12), calls=%async_computation | async-start | bytes 8388608
  14.5 9.5 %slice-start.1 = ((s8[4718592]{0:T(1024)(128)(4,1)}), s8[524288]{0:T(1024)(128)(4,1)S(1)}, s32[]{:S(2)}) async-start(s8[4718592]{0:T(1024)(128)(4,1)} %bitcast.12), calls=%async_computation.1 | async-start | bytes 1048576
  16.3 7.7 %copy-start = (bf16[1,3,3,512,256]{4,3,2,1,0:T(8,128)(2,1)S(1)}, bf16[1,3,3,512,256]{4,3,2,1,0:T(8,128)(2,1)}, u32[]{:S(2)}) copy-start(bf16[1,3,3,512,256]{4,3,2,1,0:T(8,128)(2,1)} %param.8) | copy-start | bytes 7077892
  16.3 7.7 %copy-start.1 = (bf16[3,2,256,256]{3,2,1,0:T(8,128)(2,1)S(1)}, bf16[3,2,256,256]{3,2,1,0:T(8,128)(2,1)}, u32[]{:S(2)}) copy-start(bf16[3,2,256,256]{3,2,1,0:T(8,128)(2,1)} %param.5) | copy-start | bytes 2359300
  16.4 7.7 %copy-start.2 = (bf16[1,2,256,256]{3,2,1,0:T(8,128)(2,1)S(1)}, bf16[1,2,256,256]{3,2,1,0:T(8,128)(2,1)}, u32[]{:S(2)}) copy-start(bf16[1,2,256,256]{3,2,1,0:T(8,128)(2,1)} %param.6) | copy-start | bytes 786436
  16.4 7.7 %copy-start.3 = (f32[1,768]{1,0:T(1,128)S(1)}, f32[1,768]{1,0:T(1,128)}, u32[]{:S(2)}) copy-start(f32[1,768]{1,0:T(1,128)} %refs_10_.1) | copy-start | bytes 9220
  17.9 6.1 %collective-permute-start.4 = (bf16[2,256,256]{2,1,0:T(8,128)(2,1)S(1)}, bf16[2,256,256]{2,1,0:T(8,128)(2,1)S(1)}, u32[]{:S(2)}, u32[]{:S(2)}) collective-permute-start(bf16[2,256,256]{2,1,0:T(8,128)(2,1)S(1)} %collective-permute-done.first.refs_1_.refs_9_), channel_id=1, source_target_pairs={{0,128},{128,0},{1,129},{129,1},{2,130},{130,2},{3,131},{131,3},{4... | collective-permute-start | bytes 786440 | tf_op jit(solution)/shard_map/ppermute | solution.py:312
  21.2 2.8 %collective-permute-start.5 = (bf16[2,256,256]{2,1,0:T(8,128)(2,1)S(1)}, bf16[2,256,256]{2,1,0:T(8,128)(2,1)S(1)}, u32[]{:S(2)}, u32[]{:S(2)}) collective-permute-start(bf16[2,256,256]{2,1,0:T(8,128)(2,1)S(1)} %collective-permute-done.1.second.refs_2_.refs_10_), channel_id=1, source_target_pairs={{0,128},{128,0},{1,129},{129,1},{2,130},{130,2},{3,131},{131,3},{4... | collective-permute-start | bytes 786440 | tf_op jit(solution)/shard_map/ppermute | solution.py:312
  24.1 17.2 %collective-permute-start.6 = (bf16[2,256,256]{2,1,0:T(8,128)(2,1)S(1)}, bf16[2,256,256]{2,1,0:T(8,128)(2,1)S(1)}, u32[]{:S(2)}, u32[]{:S(2)}) collective-permute-start(bf16[2,256,256]{2,1,0:T(8,128)(2,1)S(1)} %shard_map.58.own.refs_0_.refs_11_), channel_id=1, source_target_pairs={{0,1},{1,0},{2,3},{3,2},{4,5},{5,4},{6,7},{7,6},{8,9},{9,8},{10,11... | collective-permute-start | bytes 786440 | tf_op jit(solution)/shard_map/ppermute | solution.py:296
  34.3 9.6 %collective-permute-start.7 = (bf16[2,256,256]{2,1,0:T(8,128)(2,1)S(1)}, bf16[2,256,256]{2,1,0:T(8,128)(2,1)S(1)}, u32[]{:S(2)}, u32[]{:S(2)}) collective-permute-start(bf16[2,256,256]{2,1,0:T(8,128)(2,1)S(1)} %shard_map.58.own.refs_0_.refs_11_), channel_id=1, source_target_pairs={{0,128},{128,0},{1,129},{129,1},{2,130},{130,2},{3,131},{131,3},{4... | collective-permute-start | bytes 786440 | tf_op jit(solution)/shard_map/ppermute | solution.py:312
  41.3 2.6 %collective-permute-start.9 = (bf16[2,256,256]{2,1,0:T(8,128)(2,1)S(1)}, bf16[2,256,256]{2,1,0:T(8,128)(2,1)S(1)}, u32[]{:S(2)}, u32[]{:S(2)}) collective-permute-start(bf16[2,256,256]{2,1,0:T(8,128)(2,1)S(1)} %fusion.second.refs_2_), channel_id=1, source_target_pairs={{0,128},{128,0},{1,129},{129,1},{2,130},{130,2},{3,131},{131,3},{4... | collective-permute-start | bytes 786440 | tf_op jit(solution)/shard_map/ppermute | solution.py:312
  41.4 2.5 %collective-permute-start.8 = (bf16[2,256,256]{2,1,0:T(8,128)(2,1)S(1)}, bf16[2,256,256]{2,1,0:T(8,128)(2,1)S(1)}, u32[]{:S(2)}, u32[]{:S(2)}) collective-permute-start(bf16[2,256,256]{2,1,0:T(8,128)(2,1)S(1)} %collective-permute-done.6.first.refs_1_), channel_id=1, source_target_pairs={{0,128},{128,0},{1,129},{129,1},{2,130},{130,2},{3,131},{131,3},{4... | collective-permute-start | bytes 786440 | tf_op jit(solution)/shard_map/ppermute | solution.py:312
  47.8 13.5 %collective-permute-start.11 = (bf16[2,256,256]{2,1,0:T(8,128)(2,1)S(1)}, bf16[2,256,256]{2,1,0:T(8,128)(2,1)S(1)}, u32[]{:S(2)}, u32[]{:S(2)}) collective-permute-start(bf16[2,256,256]{2,1,0:T(8,128)(2,1)S(1)} %shard_map.60.own.refs_0_.refs_12_), channel_id=1, source_target_pairs={{0,128},{128,0},{1,129},{129,1},{2,130},{130,2},{3,131},{131,3},{4... | collective-permute-start | bytes 786440 | tf_op jit(solution)/shard_map/ppermute | solution.py:312
  48.2 16.4 %collective-permute-start.12 = (bf16[2,256,256]{2,1,0:T(8,128)(2,1)S(1)}, bf16[2,256,256]{2,1,0:T(8,128)(2,1)S(1)}, u32[]{:S(2)}, u32[]{:S(2)}) collective-permute-start(bf16[2,256,256]{2,1,0:T(8,128)(2,1)S(1)} %collective-permute-done.3.refs_6_), channel_id=1, source_target_pairs={{0,128},{128,0},{1,129},{129,1},{2,130},{130,2},{3,131},{131,3},{4... | collective-permute-start | bytes 786440 | tf_op jit(solution)/shard_map/ppermute | solution.py:312
  48.4 16.2 %collective-permute-start.13 = (bf16[2,256,256]{2,1,0:T(8,128)(2,1)S(1)}, bf16[2,256,256]{2,1,0:T(8,128)(2,1)S(1)}, u32[]{:S(2)}, u32[]{:S(2)}) collective-permute-start(bf16[2,256,256]{2,1,0:T(8,128)(2,1)S(1)} %collective-permute-done.2.refs_7_), channel_id=1, source_target_pairs={{0,128},{128,0},{1,129},{129,1},{2,130},{130,2},{3,131},{131,3},{4... | collective-permute-start | bytes 786440 | tf_op jit(solution)/shard_map/ppermute | solution.py:312
  48.7 12.6 %collective-permute-start.10 = (bf16[2,256,256]{2,1,0:T(8,128)(2,1)S(1)}, bf16[2,256,256]{2,1,0:T(8,128)(2,1)S(1)}, u32[]{:S(2)}, u32[]{:S(2)}) collective-permute-start(bf16[2,256,256]{2,1,0:T(8,128)(2,1)S(1)} %shard_map.60.own.refs_0_.refs_12_), channel_id=1, source_target_pairs={{0,1},{1,0},{2,3},{3,2},{4,5},{5,4},{6,7},{7,6},{8,9},{9,8},{10,11... | collective-permute-start | bytes 786440 | tf_op jit(solution)/shard_map/ppermute | solution.py:296
  61.4 3.3 %collective-permute-start.14 = (bf16[2,256,256]{2,1,0:T(8,128)(2,1)S(1)}, bf16[2,256,256]{2,1,0:T(8,128)(2,1)S(1)}, u32[]{:S(2)}, u32[]{:S(2)}) collective-permute-start(bf16[2,256,256]{2,1,0:T(8,128)(2,1)S(1)} %collective-permute-done.10.first.refs_1_), channel_id=1, source_target_pairs={{0,128},{128,0},{1,129},{129,1},{2,130},{130,2},{3,131},{131,3},{4... | collective-permute-start | bytes 786440 | tf_op jit(solution)/shard_map/ppermute | solution.py:312
  62.5 2.2 %collective-permute-start.15 = (bf16[2,256,256]{2,1,0:T(8,128)(2,1)S(1)}, bf16[2,256,256]{2,1,0:T(8,128)(2,1)S(1)}, u32[]{:S(2)}, u32[]{:S(2)}) collective-permute-start(bf16[2,256,256]{2,1,0:T(8,128)(2,1)S(1)} %select_bitcast_fusion.1.second.refs_2_), channel_id=1, source_target_pairs={{0,128},{128,0},{1,129},{129,1},{2,130},{130,2},{3,131},{131,3},{4... | collective-permute-start | bytes 786440 | tf_op jit(solution)/shard_map/ppermute | solution.py:312
  68.6 13.4 %collective-permute-start.17 = (bf16[2,256,256]{2,1,0:T(8,128)(2,1)S(1)}, bf16[2,256,256]{2,1,0:T(8,128)(2,1)S(1)}, u32[]{:S(2)}, u32[]{:S(2)}) collective-permute-start(bf16[2,256,256]{2,1,0:T(8,128)(2,1)S(1)} %shard_map.62.own.refs_0_), channel_id=1, source_target_pairs={{0,128},{128,0},{1,129},{129,1},{2,130},{130,2},{3,131},{131,3},{4... | collective-permute-start | bytes 786440 | tf_op jit(solution)/shard_map/ppermute | solution.py:312
  69.3 12.7 %collective-permute-start.16 = (bf16[2,256,256]{2,1,0:T(8,128)(2,1)S(1)}, bf16[2,256,256]{2,1,0:T(8,128)(2,1)S(1)}, u32[]{:S(2)}, u32[]{:S(2)}) collective-permute-start(bf16[2,256,256]{2,1,0:T(8,128)(2,1)S(1)} %shard_map.62.own.refs_0_), channel_id=1, source_target_pairs={{0,1},{1,0},{2,3},{3,2},{4,5},{5,4},{6,7},{7,6},{8,9},{9,8},{10,11... | collective-permute-start | bytes 786440 | tf_op jit(solution)/shard_map/ppermute | solution.py:296
  82.0 3.2 %collective-permute-start.18 = (bf16[2,256,256]{2,1,0:T(8,128)(2,1)S(1)}, bf16[2,256,256]{2,1,0:T(8,128)(2,1)S(1)}, u32[]{:S(2)}, u32[]{:S(2)}) collective-permute-start(bf16[2,256,256]{2,1,0:T(8,128)(2,1)S(1)} %collective-permute-done.16.first.refs_1_), channel_id=1, source_target_pairs={{0,128},{128,0},{1,129},{129,1},{2,130},{130,2},{3,131},{131,3},{4... | collective-permute-start | bytes 786440 | tf_op jit(solution)/shard_map/ppermute | solution.py:312
  83.1 2.1 %collective-permute-start.19 = (bf16[2,256,256]{2,1,0:T(8,128)(2,1)S(1)}, bf16[2,256,256]{2,1,0:T(8,128)(2,1)S(1)}, u32[]{:S(2)}, u32[]{:S(2)}) collective-permute-start(bf16[2,256,256]{2,1,0:T(8,128)(2,1)S(1)} %select_bitcast_fusion.second.refs_2_), channel_id=1, source_target_pairs={{0,128},{128,0},{1,129},{129,1},{2,130},{130,2},{3,131},{131,3},{4... | collective-permute-start | bytes 786440 | tf_op jit(solution)/shard_map/ppermute | solution.py:312

commit v9 on v8

--- a/solution.py
+++ b/solution.py
@@ -302,10 +302,10 @@
     for layer in range(2):
         groups += [[layer * count + low, layer * count + low + 1] for low in range(1, count - 1, 2)]
     both = lax.all_gather(field, ("layer", "rows"), axis_index_groups=groups)
-    if beside is not None:
-        both, beside = lax.optimization_barrier((both, beside))
+    if beside:
+        both, *beside = lax.optimization_barrier((both, *beside))
     partner = jnp.where(odd, both[1], both[0])
-    return jnp.where(inner, partner, jnp.zeros_like(partner)), beside
+    return jnp.where(inner, partner, jnp.zeros_like(partner)), *beside
 
 
 def across(field):
@@ -341,8 +341,9 @@
     for step in range(1, 4):
         first = pair_swap(hidden, 0)
         own_below = across(hidden)
-        second, waited = gathered_swap(hidden, odd, inner, own_below if step > 1 else None)
-        own_below = waited if step > 1 else own_below
+        beside = (first, own_below) if step > 1 else ()
+        second, *beside = gathered_swap(hidden, odd, inner, beside)
+        first, own_below = beside or (first, own_below)
         below = (own_below, across(first), across(second))
         state = (hidden, first, second)
         pre = early(step, state, wg_state)

time: 90.2 us -> 90.4 us (level)
  no operation moved by 1% of the time
where the time goes in v9:
time: 90.4 us; the launch traced here: 90.2 us
  blocking collectives  35.4 us (39%)
  starting transfers between devices  28.4 us (31%)
  Pallas kernels  21.5 us (24%)
  waiting for transfers between devices  4.33 us (5%)
    all_gather x3, blocking collectives, gathered_swap(): both = lax.all_gather(field, ('layer', 'rows'), axis_index_groups=groups)  35.4 us
    ppermute x13, starting transfers between devices, across(): return lax.ppermute(field, 'layer', [(0, 1), (1, 0)])  14.5 us
    ppermute x7, starting transfers between devices, pair_swap(): return lax.ppermute(field, 'rows', route)  13.9 us
    pallas_call x3, Pallas kernels, late(): pl.pallas_call(functools.partial(late_kernel, lag), out_shape=jax.ShapeDt...  7.89 us
    pallas_call x4, Pallas kernels, early(): pl.pallas_call(functools.partial(early_kernel, lag), out_shape=[pre(4), p...  6.1 us
    pallas_call x1, Pallas kernels, last(): pl.pallas_call(last_kernel, out_shape=jax.ShapeDtypeStruct((3, 2, cols, c...  4.62 us
    ppermute x7, waiting for transfers between devices, pair_swap(): return lax.ppermute(field, 'rows', route)  4.29 us
    pallas_call x1, Pallas kernels, stage(): pl.pallas_call(stage_kernel, out_shape=jax.ShapeDtypeStruct((3, 3, depth...  1.83 us
  transfers between devices with their start and end apart: 20, of which 3 were waited for; matrix products, arithmetic and copies ran while one was open for 0% of the time, Pallas kernels for 9%

profile of v9, /device:TPU:25, one launch (start us, length us, event | category | flops | bytes accessed | tf_op | source)
XLA Modules:
  0.0 90.2 jit_solution(15405558477819961393)
XLA Ops:
  0.0 1.0 %shard_map.55 = (bf16[2,256,256]{2,1,0:T(8,128)(2,1)S(1)}, bf16[2,256,256]{2,1,0:T(8,128)(2,1)S(1)}) custom-call(bf16[2,256,256]{2,1,0:T(8,128)(2,1)} %bitcast.26, bf16[6,256,256]{2,1,0:T(8,128)(2,1)} %bitcast.22), custom_call_target="tpu_custom_call" | custom-call | tf_op jit(solution)/shard_map/pallas_call | solution.py:224
  1.1 9.9 %collective-permute-start.1 = (bf16[2,256,256]{2,1,0:T(8,128)(2,1)S(1)}, bf16[2,256,256]{2,1,0:T(8,128)(2,1)S(1)}, u32[]{:S(2)}, u32[]{:S(2)}) collective-permute-start(bf16[2,256,256]{2,1,0:T(8,128)(2,1)S(1)} %get-tuple-element.29.own.refs_8_), channel_id=1, source_target_pairs={{1,2},{2,1},{3,4},{4,3},{5,6},{6,5},{7,8},{8,7},{9,10},{10,9},{11,... | collective-permute-start | bytes 786440 | tf_op jit(solution)/shard_map/ppermute | solution.py:296
  10.9 0.1 collective-permute-start
  11.0 3.3 %collective-permute-start.2 = (bf16[2,256,256]{2,1,0:T(8,128)(2,1)S(1)}, bf16[2,256,256]{2,1,0:T(8,128)(2,1)S(1)}, u32[]{:S(2)}, u32[]{:S(2)}) collective-permute-start(bf16[2,256,256]{2,1,0:T(8,128)(2,1)S(1)} %get-tuple-element.33), channel_id=1, source_target_pairs={{1,2},{2,1},{3,4},{4,3},{5,6},{6,5},{7,8},{8,7},{9,10},{10,9},{11,... | collective-permute-start | bytes 786440 | tf_op jit(solution)/shard_map/ppermute | solution.py:296
  14.4 0.1 collective-permute-start.3
  14.5 0.0 slice-start
  14.5 0.0 slice-start.1
  14.5 1.8 %shard_map.56.wg = bf16[3,3,256,512]{3,2,1,0:T(8,128)(2,1)S(1)} custom-call(bf16[3,3,512,512]{3,2,1,0:T(8,128)(2,1)} %bitcast.11), custom_call_target="tpu_custom_call" | custom-call | tf_op jit(solution)/shard_map/pallas_call | solution.py:236
  16.3 0.0 copy-start
  16.3 0.0 copy-start.1
  16.4 0.0 copy-start.2
  16.4 0.0 copy-start.3
  16.4 0.6 collective-permute-done.1.second.refs_2_.refs_10_
  16.9 0.9 %collective-permute-done.first.refs_1_.refs_9_ = bf16[2,256,256]{2,1,0:T(8,128)(2,1)S(1)} collective-permute-done((bf16[2,256,256]{2,1,0:T(8,128)(2,1)S(1)}, bf16[2,256,256]{2,1,0:T(8,128)(2,1)S(1)}, u32[]{:S(2)}, u32[]{:S(2)}) %collective-permute-start) | collective-permute-done | bytes 262176 | tf_op jit(solution)/shard_map/ppermute | solution.py:296
  17.9 3.3 %collective-permute-start.4 = (bf16[2,256,256]{2,1,0:T(8,128)(2,1)S(1)}, bf16[2,256,256]{2,1,0:T(8,128)(2,1)S(1)}, u32[]{:S(2)}, u32[]{:S(2)}) collective-permute-start(bf16[2,256,256]{2,1,0:T(8,128)(2,1)S(1)} %collective-permute-done.first.refs_1_.refs_9_), channel_id=1, source_target_pairs={{0,128},{128,0},{1,129},{129,1},{2,130},{130,2},{3,131},{131,3},{4... | collective-permute-start | bytes 786440 | tf_op jit(solution)/shard_map/ppermute | solution.py:312
  21.2 0.0 collective-permute-start.5
  21.2 2.8 %collective-permute-done.2.refs_7_ = bf16[2,256,256]{2,1,0:T(8,128)(2,1)S(1)} collective-permute-done((bf16[2,256,256]{2,1,0:T(8,128)(2,1)S(1)}, bf16[2,256,256]{2,1,0:T(8,128)(2,1)S(1)}, u32[]{:S(2)}, u32[]{:S(2)}) %collective-permute-start.2) | collective-permute-done | bytes 262176 | tf_op jit(solution)/shard_map/ppermute | solution.py:296
  24.0 0.0 collective-permute-done.3.refs_6_
  24.0 0.0 collective-permute-done.4.refs_6_
  24.0 0.0 collective-permute-done.5.refs_7_
  24.0 0.0 slice-done
  24.0 0.0 slice-done.1
  24.0 0.0 copy-done
  24.0 0.0 copy-done.1
  24.0 0.0 copy-done.2
  24.1 0.0 copy-done.3
  24.1 0.1 collective-permute-start.6
  24.2 10.1 %all-gather = bf16[4,256,256]{2,1,0:T(8,128)(2,1)S(1)} all-gather(bf16[2,256,256]{2,1,0:T(8,128)(2,1)S(1)} %shard_map.58.own.refs_0_.refs_11_), channel_id=2, replica_groups={{0,128},{127,255},{1,2},{3,4},{5,6},{7,8},{9,10},{11,12},{13,14},{15,16..., dimensions={0}, use_global_device_ids=true | all-gather | bytes 786432 | tf_op jit(solution)/shard_map/all_gather | solution.py:304
  34.3 6.9 %collective-permute-start.7 = (bf16[2,256,256]{2,1,0:T(8,128)(2,1)S(1)}, bf16[2,256,256]{2,1,0:T(8,128)(2,1)S(1)}, u32[]{:S(2)}, u32[]{:S(2)}) collective-permute-start(bf16[2,256,256]{2,1,0:T(8,128)(2,1)S(1)} %shard_map.58.own.refs_0_.refs_11_), channel_id=1, source_target_pairs={{0,128},{128,0},{1,129},{129,1},{2,130},{130,2},{3,131},{131,3},{4... | collective-permute-start | bytes 786440 | tf_op jit(solution)/shard_map/ppermute | solution.py:312
  41.3 0.1 collective-permute-start.9
  41.4 0.0 collective-permute-done.6.first.refs_1_
  41.4 0.5 collective-permute-start.8
  41.9 2.0 %shard_map.59 = (f32[1024,256]{1,0:T(8,128)S(1)}, f32[512,256]{1,0:T(8,128)S(1)}) custom-call(bf16[2,256,256]{2,1,0:T(8,128)(2,1)S(1)} %shard_map.58.own.refs_0_.refs_11_, bf16[2,256,256]{2,1,0:T(8,128)(2,1)S(1)} %collective-permute-done.6.first.refs_1_, bf16[2,256,256]{2,1,0:T(8,128)(2,1)S(1)} %fusion.second.refs_2_, bf16[3,3,256,512]{3,2,1,0:T(8,128)(2,1)S(1)} %shard_map.56.wg), custom_call_target="tpu_custom_call" | custom-call | flops 1811939328 | bytes 1048576 | tf_op jit(solution)/shard_map/pallas_call | solution.py:249
  43.9 0.0 collective-permute-done.7.refs_8_
  43.9 0.0 collective-permute-done.9.refs_10_
  43.9 0.0 collective-permute-done.8.refs_9_
  43.9 3.9 %shard_map.60.own.refs_0_.refs_12_ = bf16[2,256,256]{2,1,0:T(8,128)(2,1)S(1)} custom-call(bf16[2,256,256]{2,1,0:T(8,128)(2,1)S(1)} %shard_map.58.own.refs_0_.refs_11_, bf16[2,256,256]{2,1,0:T(8,128)(2,1)S(1)} %collective-permute-done.6.first.refs_1_, bf16[2,256,256]{2,1,0:T(8,128)(2,1)S(1)} %fusion.second.refs_2_, ...), custom_call_target="tpu_custom_call" | custom-call | flops 3019898880 | bytes 1048576 | tf_op jit(solution)/shard_map/pallas_call | solution.py:262
  47.8 0.1 collective-permute-start.10
  47.9 0.4 collective-permute-start.11
  48.3 0.2 collective-permute-start.12
  48.5 0.3 collective-permute-start.13
  48.8 12.6 %all-gather.1 = bf16[4,256,256]{2,1,0:T(8,128)(2,1)S(1)} all-gather(bf16[2,256,256]{2,1,0:T(8,128)(2,1)S(1)} %shard_map.60.own.refs_0_.refs_12_), channel_id=3, replica_groups={{0,128},{127,255},{1,2},{3,4},{5,6},{7,8},{9,10},{11,12},{13,14},{15,16..., dimensions={0}, use_global_device_ids=true | all-gather | bytes 786432 | tf_op jit(solution)/shard_map/all_gather | solution.py:304
  61.4 0.0 collective-permute-done.10.first.refs_1_
  61.4 0.0 collective-permute-done.11.refs_8_
  61.4 1.1 %collective-permute-start.14 = (bf16[2,256,256]{2,1,0:T(8,128)(2,1)S(1)}, bf16[2,256,256]{2,1,0:T(8,128)(2,1)S(1)}, u32[]{:S(2)}, u32[]{:S(2)}) collective-permute-start(bf16[2,256,256]{2,1,0:T(8,128)(2,1)S(1)} %collective-permute-done.10.first.refs_1_), channel_id=1, source_target_pairs={{0,128},{128,0},{1,129},{129,1},{2,130},{130,2},{3,131},{131,3},{4... | collective-permute-start | bytes 786440 | tf_op jit(solution)/shard_map/ppermute | solution.py:312
  62.6 0.1 collective-permute-start.15
  62.7 2.0 %shard_map.61 = (f32[1024,256]{1,0:T(8,128)S(1)}, f32[512,256]{1,0:T(8,128)S(1)}) custom-call(bf16[2,256,256]{2,1,0:T(8,128)(2,1)S(1)} %shard_map.60.own.refs_0_.refs_12_, bf16[2,256,256]{2,1,0:T(8,128)(2,1)S(1)} %collective-permute-done.10.first.refs_1_, bf16[2,256,256]{2,1,0:T(8,128)(2,1)S(1)} %select_bitcast_fusion.1.second.refs_2_, ...), custom_call_target="tpu_custom_call" | custom-call | flops 1811939328 | bytes 1048576 | tf_op jit(solution)/shard_map/pallas_call | solution.py:249
  64.7 0.0 collective-permute-done.12.refs_6_
  64.7 0.0 collective-permute-done.13.refs_7_
  64.7 0.0 collective-permute-done.14.refs_9_
  64.7 0.0 collective-permute-done.15.refs_10_
  64.7 3.9 %shard_map.62.own.refs_0_ = bf16[2,256,256]{2,1,0:T(8,128)(2,1)S(1)} custom-call(bf16[2,256,256]{2,1,0:T(8,128)(2,1)S(1)} %shard_map.60.own.refs_0_.refs_12_, bf16[2,256,256]{2,1,0:T(8,128)(2,1)S(1)} %collective-permute-done.10.first.refs_1_, bf16[2,256,256]{2,1,0:T(8,128)(2,1)S(1)} %select_bitcast_fusion.1.second.refs_2_, ...), custom_call_target="tpu_custom_call" | custom-call | flops 3019898880 | bytes 1048576 | tf_op jit(solution)/shard_map/pallas_call | solution.py:262
  68.7 0.3 collective-permute-start.16
  69.0 0.5 collective-permute-start.17
  69.5 12.8 %all-gather.2 = bf16[4,256,256]{2,1,0:T(8,128)(2,1)S(1)} all-gather(bf16[2,256,256]{2,1,0:T(8,128)(2,1)S(1)} %shard_map.62.own.refs_0_), channel_id=4, replica_groups={{0,128},{127,255},{1,2},{3,4},{5,6},{7,8},{9,10},{11,12},{13,14},{15,16..., dimensions={0}, use_global_device_ids=true | all-gather | bytes 786432 | tf_op jit(solution)/shard_map/all_gather | solution.py:304
  82.3 0.0 collective-permute-done.16.first.refs_1_
  82.3 0.0 collective-permute-done.17.refs_5_
  82.3 1.0 %collective-permute-start.18 = (bf16[2,256,256]{2,1,0:T(8,128)(2,1)S(1)}, bf16[2,256,256]{2,1,0:T(8,128)(2,1)S(1)}, u32[]{:S(2)}, u32[]{:S(2)}) collective-permute-start(bf16[2,256,256]{2,1,0:T(8,128)(2,1)S(1)} %collective-permute-done.16.first.refs_1_), channel_id=1, source_target_pairs={{0,128},{128,0},{1,129},{129,1},{2,130},{130,2},{3,131},{131,3},{4... | collective-permute-start | bytes 786440 | tf_op jit(solution)/shard_map/ppermute | solution.py:312
  83.3 0.1 collective-permute-start.19
  83.4 2.0 %shard_map.63 = (f32[1024,256]{1,0:T(8,128)S(1)}, f32[512,256]{1,0:T(8,128)S(1)}) custom-call(bf16[2,256,256]{2,1,0:T(8,128)(2,1)S(1)} %shard_map.62.own.refs_0_, bf16[2,256,256]{2,1,0:T(8,128)(2,1)S(1)} %collective-permute-done.16.first.refs_1_, bf16[2,256,256]{2,1,0:T(8,128)(2,1)S(1)} %select_bitcast_fusion.second.refs_2_, ...), custom_call_target="tpu_custom_call" | custom-call | flops 1811939328 | bytes 1048576 | tf_op jit(solution)/shard_map/pallas_call | solution.py:249
  85.4 0.0 collective-permute-done.18.refs_6_
  85.4 0.0 collective-permute-done.19.refs_7_
  85.4 4.6 %shard_map.64 = bf16[3,2,256,256]{3,2,1,0:T(8,128)(2,1)} custom-call(bf16[2,256,256]{2,1,0:T(8,128)(2,1)S(1)} %shard_map.62.own.refs_0_, bf16[2,256,256]{2,1,0:T(8,128)(2,1)S(1)} %collective-permute-done.16.first.refs_1_, bf16[2,256,256]{2,1,0:T(8,128)(2,1)S(1)} %select_bitcast_fusion.second.refs_2_, f32[1024,256]{1,0:T(8,128)S(1)} %get-tuple-element.48.refs_3_, ...), custom_call_target="tpu_custom_call" | custom-call | flops 3019898880 | bytes 1048576 | tf_op jit(solution)/shard_map/pallas_call | solution.py:275
  (6 shorter events, 0.1 us)
Async XLA Ops:
  1.1 15.9 %collective-permute-start.1 = (bf16[2,256,256]{2,1,0:T(8,128)(2,1)S(1)}, bf16[2,256,256]{2,1,0:T(8,128)(2,1)S(1)}, u32[]{:S(2)}, u32[]{:S(2)}) collective-permute-start(bf16[2,256,256]{2,1,0:T(8,128)(2,1)S(1)} %get-tuple-element.29.own.refs_8_), channel_id=1, source_target_pairs={{1,2},{2,1},{3,4},{4,3},{5,6},{6,5},{7,8},{8,7},{9,10},{10,9},{11,... | collective-permute-start | bytes 786440 | tf_op jit(solution)/shard_map/ppermute | solution.py:296
  10.9 6.9 %collective-permute-start = (bf16[2,256,256]{2,1,0:T(8,128)(2,1)S(1)}, bf16[2,256,256]{2,1,0:T(8,128)(2,1)S(1)}, u32[]{:S(2)}, u32[]{:S(2)}) collective-permute-start(bf16[2,256,256]{2,1,0:T(8,128)(2,1)S(1)} %get-tuple-element.29.own.refs_8_), channel_id=1, source_target_pairs={{0,1},{1,0},{2,3},{3,2},{4,5},{5,4},{6,7},{7,6},{8,9},{9,8},{10,11... | collective-permute-start | bytes 786440 | tf_op jit(solution)/shard_map/ppermute | solution.py:296
  11.0 13.0 %collective-permute-start.2 = (bf16[2,256,256]{2,1,0:T(8,128)(2,1)S(1)}, bf16[2,256,256]{2,1,0:T(8,128)(2,1)S(1)}, u32[]{:S(2)}, u32[]{:S(2)}) collective-permute-start(bf16[2,256,256]{2,1,0:T(8,128)(2,1)S(1)} %get-tuple-element.33), channel_id=1, source_target_pairs={{1,2},{2,1},{3,4},{4,3},{5,6},{6,5},{7,8},{8,7},{9,10},{10,9},{11,... | collective-permute-start | bytes 786440 | tf_op jit(solution)/shard_map/ppermute | solution.py:296
  14.4 9.6 %collective-permute-start.3 = (bf16[2,256,256]{2,1,0:T(8,128)(2,1)S(1)}, bf16[2,256,256]{2,1,0:T(8,128)(2,1)S(1)}, u32[]{:S(2)}, u32[]{:S(2)}) collective-permute-start(bf16[2,256,256]{2,1,0:T(8,128)(2,1)S(1)} %get-tuple-element.33), channel_id=1, source_target_pairs={{0,1},{1,0},{2,3},{3,2},{4,5},{5,4},{6,7},{7,6},{8,9},{9,8},{10,11... | collective-permute-start | bytes 786440 | tf_op jit(solution)/shard_map/ppermute | solution.py:296
  14.5 9.5 %slice-start = ((s8[4718592]{0:T(1024)(128)(4,1)}), s8[4194304]{0:T(1024)(128)(4,1)S(1)}, s32[]{:S(2)}) async-start(s8[4718592]{0:T(1024)(128)(4,1)} %bitcast.12), calls=%async_computation | async-start | bytes 8388608
  14.5 9.5 %slice-start.1 = ((s8[4718592]{0:T(1024)(128)(4,1)}), s8[524288]{0:T(1024)(128)(4,1)S(1)}, s32[]{:S(2)}) async-start(s8[4718592]{0:T(1024)(128)(4,1)} %bitcast.12), calls=%async_computation.1 | async-start | bytes 1048576
  16.3 7.7 %copy-start = (bf16[1,3,3,512,256]{4,3,2,1,0:T(8,128)(2,1)S(1)}, bf16[1,3,3,512,256]{4,3,2,1,0:T(8,128)(2,1)}, u32[]{:S(2)}) copy-start(bf16[1,3,3,512,256]{4,3,2,1,0:T(8,128)(2,1)} %param.8) | copy-start | bytes 7077892
  16.3 7.7 %copy-start.1 = (bf16[3,2,256,256]{3,2,1,0:T(8,128)(2,1)S(1)}, bf16[3,2,256,256]{3,2,1,0:T(8,128)(2,1)}, u32[]{:S(2)}) copy-start(bf16[3,2,256,256]{3,2,1,0:T(8,128)(2,1)} %param.5) | copy-start | bytes 2359300
  16.4 7.7 %copy-start.2 = (bf16[1,2,256,256]{3,2,1,0:T(8,128)(2,1)S(1)}, bf16[1,2,256,256]{3,2,1,0:T(8,128)(2,1)}, u32[]{:S(2)}) copy-start(bf16[1,2,256,256]{3,2,1,0:T(8,128)(2,1)} %param.6) | copy-start | bytes 786436
  16.4 7.7 %copy-start.3 = (f32[1,768]{1,0:T(1,128)S(1)}, f32[1,768]{1,0:T(1,128)}, u32[]{:S(2)}) copy-start(f32[1,768]{1,0:T(1,128)} %refs_10_.1) | copy-start | bytes 9220
  17.9 6.1 %collective-permute-start.4 = (bf16[2,256,256]{2,1,0:T(8,128)(2,1)S(1)}, bf16[2,256,256]{2,1,0:T(8,128)(2,1)S(1)}, u32[]{:S(2)}, u32[]{:S(2)}) collective-permute-start(bf16[2,256,256]{2,1,0:T(8,128)(2,1)S(1)} %collective-permute-done.first.refs_1_.refs_9_), channel_id=1, source_target_pairs={{0,128},{128,0},{1,129},{129,1},{2,130},{130,2},{3,131},{131,3},{4... | collective-permute-start | bytes 786440 | tf_op jit(solution)/shard_map/ppermute | solution.py:312
  21.2 2.8 %collective-permute-start.5 = (bf16[2,256,256]{2,1,0:T(8,128)(2,1)S(1)}, bf16[2,256,256]{2,1,0:T(8,128)(2,1)S(1)}, u32[]{:S(2)}, u32[]{:S(2)}) collective-permute-start(bf16[2,256,256]{2,1,0:T(8,128)(2,1)S(1)} %collective-permute-done.1.second.refs_2_.refs_10_), channel_id=1, source_target_pairs={{0,128},{128,0},{1,129},{129,1},{2,130},{130,2},{3,131},{131,3},{4... | collective-permute-start | bytes 786440 | tf_op jit(solution)/shard_map/ppermute | solution.py:312
  24.1 17.2 %collective-permute-start.6 = (bf16[2,256,256]{2,1,0:T(8,128)(2,1)S(1)}, bf16[2,256,256]{2,1,0:T(8,128)(2,1)S(1)}, u32[]{:S(2)}, u32[]{:S(2)}) collective-permute-start(bf16[2,256,256]{2,1,0:T(8,128)(2,1)S(1)} %shard_map.58.own.refs_0_.refs_11_), channel_id=1, source_target_pairs={{0,1},{1,0},{2,3},{3,2},{4,5},{5,4},{6,7},{7,6},{8,9},{9,8},{10,11... | collective-permute-start | bytes 786440 | tf_op jit(solution)/shard_map/ppermute | solution.py:296
  34.3 9.6 %collective-permute-start.7 = (bf16[2,256,256]{2,1,0:T(8,128)(2,1)S(1)}, bf16[2,256,256]{2,1,0:T(8,128)(2,1)S(1)}, u32[]{:S(2)}, u32[]{:S(2)}) collective-permute-start(bf16[2,256,256]{2,1,0:T(8,128)(2,1)S(1)} %shard_map.58.own.refs_0_.refs_11_), channel_id=1, source_target_pairs={{0,128},{128,0},{1,129},{129,1},{2,130},{130,2},{3,131},{131,3},{4... | collective-permute-start | bytes 786440 | tf_op jit(solution)/shard_map/ppermute | solution.py:312
  41.3 2.6 %collective-permute-start.9 = (bf16[2,256,256]{2,1,0:T(8,128)(2,1)S(1)}, bf16[2,256,256]{2,1,0:T(8,128)(2,1)S(1)}, u32[]{:S(2)}, u32[]{:S(2)}) collective-permute-start(bf16[2,256,256]{2,1,0:T(8,128)(2,1)S(1)} %fusion.second.refs_2_), channel_id=1, source_target_pairs={{0,128},{128,0},{1,129},{129,1},{2,130},{130,2},{3,131},{131,3},{4... | collective-permute-start | bytes 786440 | tf_op jit(solution)/shard_map/ppermute | solution.py:312
  41.4 2.5 %collective-permute-start.8 = (bf16[2,256,256]{2,1,0:T(8,128)(2,1)S(1)}, bf16[2,256,256]{2,1,0:T(8,128)(2,1)S(1)}, u32[]{:S(2)}, u32[]{:S(2)}) collective-permute-start(bf16[2,256,256]{2,1,0:T(8,128)(2,1)S(1)} %collective-permute-done.6.first.refs_1_), channel_id=1, source_target_pairs={{0,128},{128,0},{1,129},{129,1},{2,130},{130,2},{3,131},{131,3},{4... | collective-permute-start | bytes 786440 | tf_op jit(solution)/shard_map/ppermute | solution.py:312
  47.8 13.6 %collective-permute-start.10 = (bf16[2,256,256]{2,1,0:T(8,128)(2,1)S(1)}, bf16[2,256,256]{2,1,0:T(8,128)(2,1)S(1)}, u32[]{:S(2)}, u32[]{:S(2)}) collective-permute-start(bf16[2,256,256]{2,1,0:T(8,128)(2,1)S(1)} %shard_map.60.own.refs_0_.refs_12_), channel_id=1, source_target_pairs={{0,1},{1,0},{2,3},{3,2},{4,5},{5,4},{6,7},{7,6},{8,9},{9,8},{10,11... | collective-permute-start | bytes 786440 | tf_op jit(solution)/shard_map/ppermute | solution.py:296
  47.9 13.5 %collective-permute-start.11 = (bf16[2,256,256]{2,1,0:T(8,128)(2,1)S(1)}, bf16[2,256,256]{2,1,0:T(8,128)(2,1)S(1)}, u32[]{:S(2)}, u32[]{:S(2)}) collective-permute-start(bf16[2,256,256]{2,1,0:T(8,128)(2,1)S(1)} %shard_map.60.own.refs_0_.refs_12_), channel_id=1, source_target_pairs={{0,128},{128,0},{1,129},{129,1},{2,130},{130,2},{3,131},{131,3},{4... | collective-permute-start | bytes 786440 | tf_op jit(solution)/shard_map/ppermute | solution.py:312
  48.3 16.4 %collective-permute-start.12 = (bf16[2,256,256]{2,1,0:T(8,128)(2,1)S(1)}, bf16[2,256,256]{2,1,0:T(8,128)(2,1)S(1)}, u32[]{:S(2)}, u32[]{:S(2)}) collective-permute-start(bf16[2,256,256]{2,1,0:T(8,128)(2,1)S(1)} %collective-permute-done.3.refs_6_), channel_id=1, source_target_pairs={{0,128},{128,0},{1,129},{129,1},{2,130},{130,2},{3,131},{131,3},{4... | collective-permute-start | bytes 786440 | tf_op jit(solution)/shard_map/ppermute | solution.py:312
  48.5 16.2 %collective-permute-start.13 = (bf16[2,256,256]{2,1,0:T(8,128)(2,1)S(1)}, bf16[2,256,256]{2,1,0:T(8,128)(2,1)S(1)}, u32[]{:S(2)}, u32[]{:S(2)}) collective-permute-start(bf16[2,256,256]{2,1,0:T(8,128)(2,1)S(1)} %collective-permute-done.2.refs_7_), channel_id=1, source_target_pairs={{0,128},{128,0},{1,129},{129,1},{2,130},{130,2},{3,131},{131,3},{4... | collective-permute-start | bytes 786440 | tf_op jit(solution)/shard_map/ppermute | solution.py:312
  61.4 3.3 %collective-permute-start.14 = (bf16[2,256,256]{2,1,0:T(8,128)(2,1)S(1)}, bf16[2,256,256]{2,1,0:T(8,128)(2,1)S(1)}, u32[]{:S(2)}, u32[]{:S(2)}) collective-permute-start(bf16[2,256,256]{2,1,0:T(8,128)(2,1)S(1)} %collective-permute-done.10.first.refs_1_), channel_id=1, source_target_pairs={{0,128},{128,0},{1,129},{129,1},{2,130},{130,2},{3,131},{131,3},{4... | collective-permute-start | bytes 786440 | tf_op jit(solution)/shard_map/ppermute | solution.py:312
  62.6 2.2 %collective-permute-start.15 = (bf16[2,256,256]{2,1,0:T(8,128)(2,1)S(1)}, bf16[2,256,256]{2,1,0:T(8,128)(2,1)S(1)}, u32[]{:S(2)}, u32[]{:S(2)}) collective-permute-start(bf16[2,256,256]{2,1,0:T(8,128)(2,1)S(1)} %select_bitcast_fusion.1.second.refs_2_), channel_id=1, source_target_pairs={{0,128},{128,0},{1,129},{129,1},{2,130},{130,2},{3,131},{131,3},{4... | collective-permute-start | bytes 786440 | tf_op jit(solution)/shard_map/ppermute | solution.py:312
  68.7 13.6 %collective-permute-start.16 = (bf16[2,256,256]{2,1,0:T(8,128)(2,1)S(1)}, bf16[2,256,256]{2,1,0:T(8,128)(2,1)S(1)}, u32[]{:S(2)}, u32[]{:S(2)}) collective-permute-start(bf16[2,256,256]{2,1,0:T(8,128)(2,1)S(1)} %shard_map.62.own.refs_0_), channel_id=1, source_target_pairs={{0,1},{1,0},{2,3},{3,2},{4,5},{5,4},{6,7},{7,6},{8,9},{9,8},{10,11... | collective-permute-start | bytes 786440 | tf_op jit(solution)/shard_map/ppermute | solution.py:296
  69.0 13.3 %collective-permute-start.17 = (bf16[2,256,256]{2,1,0:T(8,128)(2,1)S(1)}, bf16[2,256,256]{2,1,0:T(8,128)(2,1)S(1)}, u32[]{:S(2)}, u32[]{:S(2)}) collective-permute-start(bf16[2,256,256]{2,1,0:T(8,128)(2,1)S(1)} %shard_map.62.own.refs_0_), channel_id=1, source_target_pairs={{0,128},{128,0},{1,129},{129,1},{2,130},{130,2},{3,131},{131,3},{4... | collective-permute-start | bytes 786440 | tf_op jit(solution)/shard_map/ppermute | solution.py:312
  82.3 3.1 %collective-permute-start.18 = (bf16[2,256,256]{2,1,0:T(8,128)(2,1)S(1)}, bf16[2,256,256]{2,1,0:T(8,128)(2,1)S(1)}, u32[]{:S(2)}, u32[]{:S(2)}) collective-permute-start(bf16[2,256,256]{2,1,0:T(8,128)(2,1)S(1)} %collective-permute-done.16.first.refs_1_), channel_id=1, source_target_pairs={{0,128},{128,0},{1,129},{129,1},{2,130},{130,2},{3,131},{131,3},{4... | collective-permute-start | bytes 786440 | tf_op jit(solution)/shard_map/ppermute | solution.py:312
  83.3 2.1 %collective-permute-start.19 = (bf16[2,256,256]{2,1,0:T(8,128)(2,1)S(1)}, bf16[2,256,256]{2,1,0:T(8,128)(2,1)S(1)}, u32[]{:S(2)}, u32[]{:S(2)}) collective-permute-start(bf16[2,256,256]{2,1,0:T(8,128)(2,1)S(1)} %select_bitcast_fusion.second.refs_2_), channel_id=1, source_target_pairs={{0,128},{128,0},{1,129},{129,1},{2,130},{130,2},{3,131},{131,3},{4... | collective-permute-start | bytes 786440 | tf_op jit(solution)/shard_map/ppermute | solution.py:312

commit v10 on v8

--- a/solution.py
+++ b/solution.py
@@ -68,12 +68,21 @@
     return lax.rem(lax.axis_index("rows"), 2) == 1
 
 
-def pick_kernel(initial, frames, out, later, ready):
+def state_load(weight, state_weight, ready):
+    channels = weight.shape[2] // 2
+    return pltpu.make_async_copy(weight.at[:, :, channels : 2 * channels], state_weight, ready)
+
+
+def pick_kernel(initial, frames, weight, out, later, state_weight, ready):
     for wanted, sources in enumerate(
         ((initial, frames.at[2:4]), (frames.at[0:2], frames.at[4:6]))
     ):
         @pl.when(lax.axis_index("layer") == wanted)
         def _():
+            if wanted == 1:
+                load = state_load(weight, state_weight, ready.at[2])
+                load.start()
+                load.wait()
             copies = [
                 pltpu.make_async_copy(source, target, ready.at[i])
                 for i, (source, target) in enumerate(zip(sources, (out, later)))
@@ -84,11 +93,12 @@
                 copy.wait()
 
 
-def stage_kernel(weight, state_weight, ready):
-    channels = weight.shape[2] // 2
-    load = pltpu.make_async_copy(weight.at[:, :, channels : 2 * channels], state_weight, ready)
-    load.start()
-    load.wait()
+def stage_kernel(weight, given, state_weight, ready):
+    @pl.when(lax.axis_index("layer") == 0)
+    def _():
+        load = state_load(weight, state_weight, ready)
+        load.start()
+        load.wait()
 
 
 def early_kernel(lag, own, first, second, wg, pre_r, pre_u, wide):
@@ -220,27 +230,29 @@
     return pltpu.with_memory_space_constraint(array, pltpu.HBM)
 
 
-def pick(initial, rows):
+def pick(initial, rows, wg):
+    _, _, depth, width = wg.shape
     return pl.pallas_call(
         pick_kernel,
-        out_shape=[jax.ShapeDtypeStruct(initial.shape, initial.dtype)] * 2,
-        in_specs=[ANYWHERE] * 2,
-        out_specs=[HELD] * 2,
-        scratch_shapes=[pltpu.SemaphoreType.DMA((2,))],
+        out_shape=[jax.ShapeDtypeStruct(initial.shape, initial.dtype)] * 2
+        + [jax.ShapeDtypeStruct((3, 3, depth // 2, width), wg.dtype)],
+        in_specs=[ANYWHERE] * 3,
+        out_specs=[HELD] * 3,
+        scratch_shapes=[pltpu.SemaphoreType.DMA((3,))],
         compiler_params=pltpu.CompilerParams(vmem_limit_bytes=SMALL_BYTES),
-    )(outside(initial), outside(rows))
-
-
-def stage(wg):
-    _, _, depth, width = wg.shape
+    )(outside(initial), outside(rows), outside(wg))
+
+
+def stage(wg, given):
     return pl.pallas_call(
         stage_kernel,
-        out_shape=jax.ShapeDtypeStruct((3, 3, depth // 2, width), wg.dtype),
-        in_specs=[ANYWHERE],
+        out_shape=jax.ShapeDtypeStruct(given.shape, given.dtype),
+        in_specs=[ANYWHERE, HELD],
         out_specs=HELD,
         scratch_shapes=[pltpu.SemaphoreType.DMA],
+        input_output_aliases={1: 0},
         compiler_params=pltpu.CompilerParams(vmem_limit_bytes=SMALL_BYTES),
-    )(outside(wg))
+    )(outside(wg), given)
 
 
 def early(lag, state, wg):
@@ -320,11 +332,11 @@
 
     odd = lax.rem(strip, 2) == 1
     inner = jnp.logical_and(strip > 0, strip < lax.axis_size("rows") - 1)
-    field, later_field = pick(hidden, rows)
+    field, later_field, wg_state = pick(hidden, rows, wg)
     field, odd, inner = lax.optimization_barrier((field, odd, inner))
     second = pair_swap(field, 1)
     first = pair_swap(field, 0)
-    wg_state = stage(wg)
+    wg_state = stage(wg, wg_state)
     late_second = pair_swap(later_field, 1)
     late_first = pair_swap(later_field, 0)
     second_after, wg_state = lax.optimization_barrier((second, wg_state))

time: 90.2 us -> 91.4 us (1.013)
  waiting for transfers between devices: 4.33 us -> 9.92 us
  starting transfers between devices: 28.3 us -> 24 us
    ppermute x7, waiting for transfers between devices: 4.29 us -> 9.89 us  [pair_swap(): return lax.ppermute(field, 'rows', route)]
    ppermute x13, starting transfers between devices: 14.8 us -> 10.5 us  [across(): return lax.ppermute(field, 'layer', [(0, 1), (1, 0)])]
    pallas_call x1, Pallas kernels: 1.83 us -> 0.02 us  [stage(): pl.pallas_call(stage_kernel, out_shape=jax.ShapeDtypeStruct(given.shape,...]
    pallas_call x1, Pallas kernels: 1.04 us -> 2.72 us  [pick(): pl.pallas_call(pick_kernel, out_shape=[jax.ShapeDtypeStruct(initial.shape...]
  transfers between devices with their start and end apart: 20 -> 20, of which waited for: 3 -> 3; matrix products, arithmetic and copies ran while one was open for 0% -> 0% of each run, Pallas kernels for 9% -> 7%
where the time goes in v10:
time: 91.4 us; the launch traced here: 91.2 us
  blocking collectives  35.3 us (39%)
  starting transfers between devices  24 us (26%)
  Pallas kernels  21.4 us (23%)
  waiting for transfers between devices  9.92 us (11%)
    all_gather x3, blocking collectives, gathered_swap(): both = lax.all_gather(field, ('layer', 'rows'), axis_index_groups=groups)  35.3 us
    ppermute x7, starting transfers between devices, pair_swap(): return lax.ppermute(field, 'rows', route)  13.5 us
    ppermute x13, starting transfers between devices, across(): return lax.ppermute(field, 'layer', [(0, 1), (1, 0)])  10.5 us
    ppermute x7, waiting for transfers between devices, pair_swap(): return lax.ppermute(field, 'rows', route)  9.89 us
    pallas_call x3, Pallas kernels, late(): pl.pallas_call(functools.partial(late_kernel, lag), out_shape=jax.ShapeDt...  7.89 us
    pallas_call x4, Pallas kernels, early(): pl.pallas_call(functools.partial(early_kernel, lag), out_shape=[pre(4), p...  6.1 us
    pallas_call x1, Pallas kernels, last(): pl.pallas_call(last_kernel, out_shape=jax.ShapeDtypeStruct((3, 2, cols, c...  4.63 us
    pallas_call x1, Pallas kernels, pick(): pl.pallas_call(pick_kernel, out_shape=[jax.ShapeDtypeStruct(initial.shape...  2.72 us
  transfers between devices with their start and end apart: 20, of which 3 were waited for; matrix products, arithmetic and copies ran while one was open for 0% of the time, Pallas kernels for 7%

profile of v10, /device:TPU:25, one launch (start us, length us, event | category | flops | bytes accessed | tf_op | source)
XLA Modules:
  0.0 91.2 jit_solution(11011008767857500298)
XLA Ops:
  0.0 2.7 %shard_map.55 = (bf16[2,256,256]{2,1,0:T(8,128)(2,1)S(1)}, bf16[2,256,256]{2,1,0:T(8,128)(2,1)S(1)}, bf16[3,3,256,512]{3,2,1,0:T(8,128)(2,1)S(1)}) custom-call(bf16[2,256,256]{2,1,0:T(8,128)(2,1)} %bitcast.27, bf16[6,256,256]{2,1,0:T(8,128)(2,1)} %bitcast.23, bf16[3,3,512,512]{3,2,1,0:T(8,128)(2,1)} %bitcast.11), custom_call_target="tpu_custom_call" | custom-call | tf_op jit(solution)/shard_map/pallas_call | solution.py:235
  2.7 9.9 %collective-permute-start.1 = (bf16[2,256,256]{2,1,0:T(8,128)(2,1)S(1)}, bf16[2,256,256]{2,1,0:T(8,128)(2,1)S(1)}, u32[]{:S(2)}, u32[]{:S(2)}) collective-permute-start(bf16[2,256,256]{2,1,0:T(8,128)(2,1)S(1)} %get-tuple-element.28.own.refs_8_), channel_id=1, source_target_pairs={{1,2},{2,1},{3,4},{4,3},{5,6},{6,5},{7,8},{8,7},{9,10},{10,9},{11,... | collective-permute-start | bytes 786440 | tf_op jit(solution)/shard_map/ppermute | solution.py:308
  12.6 0.1 collective-permute-start
  12.7 3.3 %collective-permute-start.2 = (bf16[2,256,256]{2,1,0:T(8,128)(2,1)S(1)}, bf16[2,256,256]{2,1,0:T(8,128)(2,1)S(1)}, u32[]{:S(2)}, u32[]{:S(2)}) collective-permute-start(bf16[2,256,256]{2,1,0:T(8,128)(2,1)S(1)} %get-tuple-element.33), channel_id=1, source_target_pairs={{1,2},{2,1},{3,4},{4,3},{5,6},{6,5},{7,8},{8,7},{9,10},{10,9},{11,... | collective-permute-start | bytes 786440 | tf_op jit(solution)/shard_map/ppermute | solution.py:308
  16.0 0.1 collective-permute-start.3
  16.2 0.0 slice-start
  16.2 0.0 slice-start.1
  16.2 0.0 copy-start
  16.2 0.0 copy-start.1
  16.2 0.0 copy-start.2
  16.2 0.0 copy-start.3
  16.2 2.4 %collective-permute-done.1.second.refs_2_.refs_10_ = bf16[2,256,256]{2,1,0:T(8,128)(2,1)S(1)} collective-permute-done((bf16[2,256,256]{2,1,0:T(8,128)(2,1)S(1)}, bf16[2,256,256]{2,1,0:T(8,128)(2,1)S(1)}, u32[]{:S(2)}, u32[]{:S(2)}) %collective-permute-start.1) | collective-permute-done | bytes 262176 | tf_op jit(solution)/shard_map/ppermute | solution.py:308
  18.6 2.4 %collective-permute-done.first.refs_1_.refs_9_ = bf16[2,256,256]{2,1,0:T(8,128)(2,1)S(1)} collective-permute-done((bf16[2,256,256]{2,1,0:T(8,128)(2,1)S(1)}, bf16[2,256,256]{2,1,0:T(8,128)(2,1)S(1)}, u32[]{:S(2)}, u32[]{:S(2)}) %collective-permute-start) | collective-permute-done | bytes 262176 | tf_op jit(solution)/shard_map/ppermute | solution.py:308
  21.0 0.0 collective-permute-start.4
  21.0 0.5 collective-permute-start.5
  21.5 5.1 %collective-permute-done.2.refs_7_ = bf16[2,256,256]{2,1,0:T(8,128)(2,1)S(1)} collective-permute-done((bf16[2,256,256]{2,1,0:T(8,128)(2,1)S(1)}, bf16[2,256,256]{2,1,0:T(8,128)(2,1)S(1)}, u32[]{:S(2)}, u32[]{:S(2)}) %collective-permute-start.2) | collective-permute-done | bytes 262176 | tf_op jit(solution)/shard_map/ppermute | solution.py:308
  26.6 0.0 collective-permute-done.3.refs_6_
  26.6 0.0 collective-permute-done.4.refs_6_
  26.6 0.0 collective-permute-done.5.refs_7_
  26.6 0.0 slice-done
  26.7 0.0 slice-done.1
  26.7 0.0 copy-done
  26.7 0.0 copy-done.1
  26.7 0.0 copy-done.2
  26.7 0.0 copy-done.3
  26.8 0.1 collective-permute-start.6
  26.9 10.1 %all-gather = bf16[4,256,256]{2,1,0:T(8,128)(2,1)S(1)} all-gather(bf16[2,256,256]{2,1,0:T(8,128)(2,1)S(1)} %shard_map.58.own.refs_0_.refs_11_), channel_id=2, replica_groups={{0,128},{127,255},{1,2},{3,4},{5,6},{7,8},{9,10},{11,12},{13,14},{15,16..., dimensions={0}, use_global_device_ids=true | all-gather | bytes 786432 | tf_op jit(solution)/shard_map/all_gather | solution.py:316
  37.0 5.4 %collective-permute-start.7 = (bf16[2,256,256]{2,1,0:T(8,128)(2,1)S(1)}, bf16[2,256,256]{2,1,0:T(8,128)(2,1)S(1)}, u32[]{:S(2)}, u32[]{:S(2)}) collective-permute-start(bf16[2,256,256]{2,1,0:T(8,128)(2,1)S(1)} %shard_map.58.own.refs_0_.refs_11_), channel_id=1, source_target_pairs={{0,128},{128,0},{1,129},{129,1},{2,130},{130,2},{3,131},{131,3},{4... | collective-permute-start | bytes 786440 | tf_op jit(solution)/shard_map/ppermute | solution.py:324
  42.4 0.1 collective-permute-start.9
  42.5 0.0 collective-permute-done.6.first.refs_1_
  42.6 0.5 collective-permute-start.8
  43.0 2.0 %shard_map.59 = (f32[1024,256]{1,0:T(8,128)S(1)}, f32[512,256]{1,0:T(8,128)S(1)}) custom-call(bf16[2,256,256]{2,1,0:T(8,128)(2,1)S(1)} %shard_map.58.own.refs_0_.refs_11_, bf16[2,256,256]{2,1,0:T(8,128)(2,1)S(1)} %collective-permute-done.6.first.refs_1_, bf16[2,256,256]{2,1,0:T(8,128)(2,1)S(1)} %fusion.second.refs_2_, bf16[3,3,256,512]{3,2,1,0:T(8,128)(2,1)S(1)} %shard_map.56.wg), custom_call_target="tpu_custom_call" | custom-call | flops 1811939328 | bytes 1048576 | tf_op jit(solution)/shard_map/pallas_call | solution.py:261
  45.1 0.0 collective-permute-done.7.refs_8_
  45.1 0.0 collective-permute-done.9.refs_10_
  45.1 0.0 collective-permute-done.8.refs_9_
  45.1 3.9 %shard_map.60.own.refs_0_.refs_12_ = bf16[2,256,256]{2,1,0:T(8,128)(2,1)S(1)} custom-call(bf16[2,256,256]{2,1,0:T(8,128)(2,1)S(1)} %shard_map.58.own.refs_0_.refs_11_, bf16[2,256,256]{2,1,0:T(8,128)(2,1)S(1)} %collective-permute-done.6.first.refs_1_, bf16[2,256,256]{2,1,0:T(8,128)(2,1)S(1)} %fusion.second.refs_2_, ...), custom_call_target="tpu_custom_call" | custom-call | flops 3019898880 | bytes 1048576 | tf_op jit(solution)/shard_map/pallas_call | solution.py:274
  49.0 0.4 collective-permute-start.11
  49.4 0.2 collective-permute-start.12
  49.6 0.3 collective-permute-start.13
  49.9 0.0 collective-permute-start.10
  49.9 12.6 %all-gather.1 = bf16[4,256,256]{2,1,0:T(8,128)(2,1)S(1)} all-gather(bf16[2,256,256]{2,1,0:T(8,128)(2,1)S(1)} %shard_map.60.own.refs_0_.refs_12_), channel_id=3, replica_groups={{0,128},{127,255},{1,2},{3,4},{5,6},{7,8},{9,10},{11,12},{13,14},{15,16..., dimensions={0}, use_global_device_ids=true | all-gather | bytes 786432 | tf_op jit(solution)/shard_map/all_gather | solution.py:316
  62.5 0.0 collective-permute-done.11.refs_8_
  62.5 0.0 collective-permute-done.10.first.refs_1_
  62.5 1.1 %collective-permute-start.14 = (bf16[2,256,256]{2,1,0:T(8,128)(2,1)S(1)}, bf16[2,256,256]{2,1,0:T(8,128)(2,1)S(1)}, u32[]{:S(2)}, u32[]{:S(2)}) collective-permute-start(bf16[2,256,256]{2,1,0:T(8,128)(2,1)S(1)} %collective-permute-done.10.first.refs_1_), channel_id=1, source_target_pairs={{0,128},{128,0},{1,129},{129,1},{2,130},{130,2},{3,131},{131,3},{4... | collective-permute-start | bytes 786440 | tf_op jit(solution)/shard_map/ppermute | solution.py:324
  63.7 0.1 collective-permute-start.15
  63.8 2.0 %shard_map.61 = (f32[1024,256]{1,0:T(8,128)S(1)}, f32[512,256]{1,0:T(8,128)S(1)}) custom-call(bf16[2,256,256]{2,1,0:T(8,128)(2,1)S(1)} %shard_map.60.own.refs_0_.refs_12_, bf16[2,256,256]{2,1,0:T(8,128)(2,1)S(1)} %collective-permute-done.10.first.refs_1_, bf16[2,256,256]{2,1,0:T(8,128)(2,1)S(1)} %select_bitcast_fusion.1.second.refs_2_, ...), custom_call_target="tpu_custom_call" | custom-call | flops 1811939328 | bytes 1048576 | tf_op jit(solution)/shard_map/pallas_call | solution.py:261
  65.8 0.0 collective-permute-done.12.refs_6_
  65.8 0.0 collective-permute-done.13.refs_7_
  65.8 0.0 collective-permute-done.14.refs_9_
  65.8 0.0 collective-permute-done.15.refs_10_
  65.8 3.9 %shard_map.62.own.refs_0_ = bf16[2,256,256]{2,1,0:T(8,128)(2,1)S(1)} custom-call(bf16[2,256,256]{2,1,0:T(8,128)(2,1)S(1)} %shard_map.60.own.refs_0_.refs_12_, bf16[2,256,256]{2,1,0:T(8,128)(2,1)S(1)} %collective-permute-done.10.first.refs_1_, bf16[2,256,256]{2,1,0:T(8,128)(2,1)S(1)} %select_bitcast_fusion.1.second.refs_2_, ...), custom_call_target="tpu_custom_call" | custom-call | flops 3019898880 | bytes 1048576 | tf_op jit(solution)/shard_map/pallas_call | solution.py:274
  69.8 0.7 collective-permute-start.17
  70.5 0.0 collective-permute-start.16
  70.5 12.7 %all-gather.2 = bf16[4,256,256]{2,1,0:T(8,128)(2,1)S(1)} all-gather(bf16[2,256,256]{2,1,0:T(8,128)(2,1)S(1)} %shard_map.62.own.refs_0_), channel_id=4, replica_groups={{0,128},{127,255},{1,2},{3,4},{5,6},{7,8},{9,10},{11,12},{13,14},{15,16..., dimensions={0}, use_global_device_ids=true | all-gather | bytes 786432 | tf_op jit(solution)/shard_map/all_gather | solution.py:316
  83.2 0.0 collective-permute-done.17.refs_5_
  83.2 0.0 collective-permute-done.16.first.refs_1_
  83.2 1.0 %collective-permute-start.18 = (bf16[2,256,256]{2,1,0:T(8,128)(2,1)S(1)}, bf16[2,256,256]{2,1,0:T(8,128)(2,1)S(1)}, u32[]{:S(2)}, u32[]{:S(2)}) collective-permute-start(bf16[2,256,256]{2,1,0:T(8,128)(2,1)S(1)} %collective-permute-done.16.first.refs_1_), channel_id=1, source_target_pairs={{0,128},{128,0},{1,129},{129,1},{2,130},{130,2},{3,131},{131,3},{4... | collective-permute-start | bytes 786440 | tf_op jit(solution)/shard_map/ppermute | solution.py:324
  84.3 0.1 collective-permute-start.19
  84.4 2.0 %shard_map.63 = (f32[1024,256]{1,0:T(8,128)S(1)}, f32[512,256]{1,0:T(8,128)S(1)}) custom-call(bf16[2,256,256]{2,1,0:T(8,128)(2,1)S(1)} %shard_map.62.own.refs_0_, bf16[2,256,256]{2,1,0:T(8,128)(2,1)S(1)} %collective-permute-done.16.first.refs_1_, bf16[2,256,256]{2,1,0:T(8,128)(2,1)S(1)} %select_bitcast_fusion.second.refs_2_, ...), custom_call_target="tpu_custom_call" | custom-call | flops 1811939328 | bytes 1048576 | tf_op jit(solution)/shard_map/pallas_call | solution.py:261
  86.4 0.0 collective-permute-done.18.refs_6_
  86.4 0.0 collective-permute-done.19.refs_7_
  86.4 4.6 %shard_map.64 = bf16[3,2,256,256]{3,2,1,0:T(8,128)(2,1)} custom-call(bf16[2,256,256]{2,1,0:T(8,128)(2,1)S(1)} %shard_map.62.own.refs_0_, bf16[2,256,256]{2,1,0:T(8,128)(2,1)S(1)} %collective-permute-done.16.first.refs_1_, bf16[2,256,256]{2,1,0:T(8,128)(2,1)S(1)} %select_bitcast_fusion.second.refs_2_, f32[1024,256]{1,0:T(8,128)S(1)} %get-tuple-element.46.refs_3_, ...), custom_call_target="tpu_custom_call" | custom-call | flops 3019898880 | bytes 1048576 | tf_op jit(solution)/shard_map/pallas_call | solution.py:287
  (7 shorter events, 0.1 us)
Async XLA Ops:
  2.7 15.9 %collective-permute-start.1 = (bf16[2,256,256]{2,1,0:T(8,128)(2,1)S(1)}, bf16[2,256,256]{2,1,0:T(8,128)(2,1)S(1)}, u32[]{:S(2)}, u32[]{:S(2)}) collective-permute-start(bf16[2,256,256]{2,1,0:T(8,128)(2,1)S(1)} %get-tuple-element.28.own.refs_8_), channel_id=1, source_target_pairs={{1,2},{2,1},{3,4},{4,3},{5,6},{6,5},{7,8},{8,7},{9,10},{10,9},{11,... | collective-permute-start | bytes 786440 | tf_op jit(solution)/shard_map/ppermute | solution.py:308
  12.6 8.4 %collective-permute-start = (bf16[2,256,256]{2,1,0:T(8,128)(2,1)S(1)}, bf16[2,256,256]{2,1,0:T(8,128)(2,1)S(1)}, u32[]{:S(2)}, u32[]{:S(2)}) collective-permute-start(bf16[2,256,256]{2,1,0:T(8,128)(2,1)S(1)} %get-tuple-element.28.own.refs_8_), channel_id=1, source_target_pairs={{0,1},{1,0},{2,3},{3,2},{4,5},{5,4},{6,7},{7,6},{8,9},{9,8},{10,11... | collective-permute-start | bytes 786440 | tf_op jit(solution)/shard_map/ppermute | solution.py:308
  12.7 13.9 %collective-permute-start.2 = (bf16[2,256,256]{2,1,0:T(8,128)(2,1)S(1)}, bf16[2,256,256]{2,1,0:T(8,128)(2,1)S(1)}, u32[]{:S(2)}, u32[]{:S(2)}) collective-permute-start(bf16[2,256,256]{2,1,0:T(8,128)(2,1)S(1)} %get-tuple-element.33), channel_id=1, source_target_pairs={{1,2},{2,1},{3,4},{4,3},{5,6},{6,5},{7,8},{8,7},{9,10},{10,9},{11,... | collective-permute-start | bytes 786440 | tf_op jit(solution)/shard_map/ppermute | solution.py:308
  16.0 10.6 %collective-permute-start.3 = (bf16[2,256,256]{2,1,0:T(8,128)(2,1)S(1)}, bf16[2,256,256]{2,1,0:T(8,128)(2,1)S(1)}, u32[]{:S(2)}, u32[]{:S(2)}) collective-permute-start(bf16[2,256,256]{2,1,0:T(8,128)(2,1)S(1)} %get-tuple-element.33), channel_id=1, source_target_pairs={{0,1},{1,0},{2,3},{3,2},{4,5},{5,4},{6,7},{7,6},{8,9},{9,8},{10,11... | collective-permute-start | bytes 786440 | tf_op jit(solution)/shard_map/ppermute | solution.py:308
  16.2 10.5 %slice-start = ((s8[4718592]{0:T(1024)(128)(4,1)}), s8[4194304]{0:T(1024)(128)(4,1)S(1)}, s32[]{:S(2)}) async-start(s8[4718592]{0:T(1024)(128)(4,1)} %bitcast.13), calls=%async_computation | async-start | bytes 8388608
  16.2 10.5 %slice-start.1 = ((s8[4718592]{0:T(1024)(128)(4,1)}), s8[524288]{0:T(1024)(128)(4,1)S(1)}, s32[]{:S(2)}) async-start(s8[4718592]{0:T(1024)(128)(4,1)} %bitcast.13), calls=%async_computation.1 | async-start | bytes 1048576
  16.2 10.5 %copy-start = (bf16[1,3,3,512,256]{4,3,2,1,0:T(8,128)(2,1)S(1)}, bf16[1,3,3,512,256]{4,3,2,1,0:T(8,128)(2,1)}, u32[]{:S(2)}) copy-start(bf16[1,3,3,512,256]{4,3,2,1,0:T(8,128)(2,1)} %param.8) | copy-start | bytes 7077892
  16.2 10.5 %copy-start.1 = (bf16[3,2,256,256]{3,2,1,0:T(8,128)(2,1)S(1)}, bf16[3,2,256,256]{3,2,1,0:T(8,128)(2,1)}, u32[]{:S(2)}) copy-start(bf16[3,2,256,256]{3,2,1,0:T(8,128)(2,1)} %param.5) | copy-start | bytes 2359300
  16.2 10.5 %copy-start.2 = (bf16[1,2,256,256]{3,2,1,0:T(8,128)(2,1)S(1)}, bf16[1,2,256,256]{3,2,1,0:T(8,128)(2,1)}, u32[]{:S(2)}) copy-start(bf16[1,2,256,256]{3,2,1,0:T(8,128)(2,1)} %param.6) | copy-start | bytes 786436
  16.2 10.5 %copy-start.3 = (f32[1,768]{1,0:T(1,128)S(1)}, f32[1,768]{1,0:T(1,128)}, u32[]{:S(2)}) copy-start(f32[1,768]{1,0:T(1,128)} %refs_10_.1) | copy-start | bytes 9220
  21.0 5.6 %collective-permute-start.4 = (bf16[2,256,256]{2,1,0:T(8,128)(2,1)S(1)}, bf16[2,256,256]{2,1,0:T(8,128)(2,1)S(1)}, u32[]{:S(2)}, u32[]{:S(2)}) collective-permute-start(bf16[2,256,256]{2,1,0:T(8,128)(2,1)S(1)} %collective-permute-done.first.refs_1_.refs_9_), channel_id=1, source_target_pairs={{0,128},{128,0},{1,129},{129,1},{2,130},{130,2},{3,131},{131,3},{4... | collective-permute-start | bytes 786440 | tf_op jit(solution)/shard_map/ppermute | solution.py:324
  21.0 5.6 %collective-permute-start.5 = (bf16[2,256,256]{2,1,0:T(8,128)(2,1)S(1)}, bf16[2,256,256]{2,1,0:T(8,128)(2,1)S(1)}, u32[]{:S(2)}, u32[]{:S(2)}) collective-permute-start(bf16[2,256,256]{2,1,0:T(8,128)(2,1)S(1)} %collective-permute-done.1.second.refs_2_.refs_10_), channel_id=1, source_target_pairs={{0,128},{128,0},{1,129},{129,1},{2,130},{130,2},{3,131},{131,3},{4... | collective-permute-start | bytes 786440 | tf_op jit(solution)/shard_map/ppermute | solution.py:324
  26.8 15.8 %collective-permute-start.6 = (bf16[2,256,256]{2,1,0:T(8,128)(2,1)S(1)}, bf16[2,256,256]{2,1,0:T(8,128)(2,1)S(1)}, u32[]{:S(2)}, u32[]{:S(2)}) collective-permute-start(bf16[2,256,256]{2,1,0:T(8,128)(2,1)S(1)} %shard_map.58.own.refs_0_.refs_11_), channel_id=1, source_target_pairs={{0,1},{1,0},{2,3},{3,2},{4,5},{5,4},{6,7},{7,6},{8,9},{9,8},{10,11... | collective-permute-start | bytes 786440 | tf_op jit(solution)/shard_map/ppermute | solution.py:308
  37.0 8.1 %collective-permute-start.7 = (bf16[2,256,256]{2,1,0:T(8,128)(2,1)S(1)}, bf16[2,256,256]{2,1,0:T(8,128)(2,1)S(1)}, u32[]{:S(2)}, u32[]{:S(2)}) collective-permute-start(bf16[2,256,256]{2,1,0:T(8,128)(2,1)S(1)} %shard_map.58.own.refs_0_.refs_11_), channel_id=1, source_target_pairs={{0,128},{128,0},{1,129},{129,1},{2,130},{130,2},{3,131},{131,3},{4... | collective-permute-start | bytes 786440 | tf_op jit(solution)/shard_map/ppermute | solution.py:324
  42.4 2.6 %collective-permute-start.9 = (bf16[2,256,256]{2,1,0:T(8,128)(2,1)S(1)}, bf16[2,256,256]{2,1,0:T(8,128)(2,1)S(1)}, u32[]{:S(2)}, u32[]{:S(2)}) collective-permute-start(bf16[2,256,256]{2,1,0:T(8,128)(2,1)S(1)} %fusion.second.refs_2_), channel_id=1, source_target_pairs={{0,128},{128,0},{1,129},{129,1},{2,130},{130,2},{3,131},{131,3},{4... | collective-permute-start | bytes 786440 | tf_op jit(solution)/shard_map/ppermute | solution.py:324
  42.6 2.5 %collective-permute-start.8 = (bf16[2,256,256]{2,1,0:T(8,128)(2,1)S(1)}, bf16[2,256,256]{2,1,0:T(8,128)(2,1)S(1)}, u32[]{:S(2)}, u32[]{:S(2)}) collective-permute-start(bf16[2,256,256]{2,1,0:T(8,128)(2,1)S(1)} %collective-permute-done.6.first.refs_1_), channel_id=1, source_target_pairs={{0,128},{128,0},{1,129},{129,1},{2,130},{130,2},{3,131},{131,3},{4... | collective-permute-start | bytes 786440 | tf_op jit(solution)/shard_map/ppermute | solution.py:324
  49.0 13.5 %collective-permute-start.11 = (bf16[2,256,256]{2,1,0:T(8,128)(2,1)S(1)}, bf16[2,256,256]{2,1,0:T(8,128)(2,1)S(1)}, u32[]{:S(2)}, u32[]{:S(2)}) collective-permute-start(bf16[2,256,256]{2,1,0:T(8,128)(2,1)S(1)} %shard_map.60.own.refs_0_.refs_12_), channel_id=1, source_target_pairs={{0,128},{128,0},{1,129},{129,1},{2,130},{130,2},{3,131},{131,3},{4... | collective-permute-start | bytes 786440 | tf_op jit(solution)/shard_map/ppermute | solution.py:324
  49.4 16.4 %collective-permute-start.12 = (bf16[2,256,256]{2,1,0:T(8,128)(2,1)S(1)}, bf16[2,256,256]{2,1,0:T(8,128)(2,1)S(1)}, u32[]{:S(2)}, u32[]{:S(2)}) collective-permute-start(bf16[2,256,256]{2,1,0:T(8,128)(2,1)S(1)} %collective-permute-done.3.refs_6_), channel_id=1, source_target_pairs={{0,128},{128,0},{1,129},{129,1},{2,130},{130,2},{3,131},{131,3},{4... | collective-permute-start | bytes 786440 | tf_op jit(solution)/shard_map/ppermute | solution.py:324
  49.6 16.2 %collective-permute-start.13 = (bf16[2,256,256]{2,1,0:T(8,128)(2,1)S(1)}, bf16[2,256,256]{2,1,0:T(8,128)(2,1)S(1)}, u32[]{:S(2)}, u32[]{:S(2)}) collective-permute-start(bf16[2,256,256]{2,1,0:T(8,128)(2,1)S(1)} %collective-permute-done.2.refs_7_), channel_id=1, source_target_pairs={{0,128},{128,0},{1,129},{129,1},{2,130},{130,2},{3,131},{131,3},{4... | collective-permute-start | bytes 786440 | tf_op jit(solution)/shard_map/ppermute | solution.py:324
  49.9 12.6 %collective-permute-start.10 = (bf16[2,256,256]{2,1,0:T(8,128)(2,1)S(1)}, bf16[2,256,256]{2,1,0:T(8,128)(2,1)S(1)}, u32[]{:S(2)}, u32[]{:S(2)}) collective-permute-start(bf16[2,256,256]{2,1,0:T(8,128)(2,1)S(1)} %shard_map.60.own.refs_0_.refs_12_), channel_id=1, source_target_pairs={{0,1},{1,0},{2,3},{3,2},{4,5},{5,4},{6,7},{7,6},{8,9},{9,8},{10,11... | collective-permute-start | bytes 786440 | tf_op jit(solution)/shard_map/ppermute | solution.py:308
  62.5 3.3 %collective-permute-start.14 = (bf16[2,256,256]{2,1,0:T(8,128)(2,1)S(1)}, bf16[2,256,256]{2,1,0:T(8,128)(2,1)S(1)}, u32[]{:S(2)}, u32[]{:S(2)}) collective-permute-start(bf16[2,256,256]{2,1,0:T(8,128)(2,1)S(1)} %collective-permute-done.10.first.refs_1_), channel_id=1, source_target_pairs={{0,128},{128,0},{1,129},{129,1},{2,130},{130,2},{3,131},{131,3},{4... | collective-permute-start | bytes 786440 | tf_op jit(solution)/shard_map/ppermute | solution.py:324
  63.7 2.2 %collective-permute-start.15 = (bf16[2,256,256]{2,1,0:T(8,128)(2,1)S(1)}, bf16[2,256,256]{2,1,0:T(8,128)(2,1)S(1)}, u32[]{:S(2)}, u32[]{:S(2)}) collective-permute-start(bf16[2,256,256]{2,1,0:T(8,128)(2,1)S(1)} %select_bitcast_fusion.1.second.refs_2_), channel_id=1, source_target_pairs={{0,128},{128,0},{1,129},{129,1},{2,130},{130,2},{3,131},{131,3},{4... | collective-permute-start | bytes 786440 | tf_op jit(solution)/shard_map/ppermute | solution.py:324
  69.8 13.4 %collective-permute-start.17 = (bf16[2,256,256]{2,1,0:T(8,128)(2,1)S(1)}, bf16[2,256,256]{2,1,0:T(8,128)(2,1)S(1)}, u32[]{:S(2)}, u32[]{:S(2)}) collective-permute-start(bf16[2,256,256]{2,1,0:T(8,128)(2,1)S(1)} %shard_map.62.own.refs_0_), channel_id=1, source_target_pairs={{0,128},{128,0},{1,129},{129,1},{2,130},{130,2},{3,131},{131,3},{4... | collective-permute-start | bytes 786440 | tf_op jit(solution)/shard_map/ppermute | solution.py:324
  70.5 12.7 %collective-permute-start.16 = (bf16[2,256,256]{2,1,0:T(8,128)(2,1)S(1)}, bf16[2,256,256]{2,1,0:T(8,128)(2,1)S(1)}, u32[]{:S(2)}, u32[]{:S(2)}) collective-permute-start(bf16[2,256,256]{2,1,0:T(8,128)(2,1)S(1)} %shard_map.62.own.refs_0_), channel_id=1, source_target_pairs={{0,1},{1,0},{2,3},{3,2},{4,5},{5,4},{6,7},{7,6},{8,9},{9,8},{10,11... | collective-permute-start | bytes 786440 | tf_op jit(solution)/shard_map/ppermute | solution.py:308
  83.2 3.2 %collective-permute-start.18 = (bf16[2,256,256]{2,1,0:T(8,128)(2,1)S(1)}, bf16[2,256,256]{2,1,0:T(8,128)(2,1)S(1)}, u32[]{:S(2)}, u32[]{:S(2)}) collective-permute-start(bf16[2,256,256]{2,1,0:T(8,128)(2,1)S(1)} %collective-permute-done.16.first.refs_1_), channel_id=1, source_target_pairs={{0,128},{128,0},{1,129},{129,1},{2,130},{130,2},{3,131},{131,3},{4... | collective-permute-start | bytes 786440 | tf_op jit(solution)/shard_map/ppermute | solution.py:324
  84.3 2.1 %collective-permute-start.19 = (bf16[2,256,256]{2,1,0:T(8,128)(2,1)S(1)}, bf16[2,256,256]{2,1,0:T(8,128)(2,1)S(1)}, u32[]{:S(2)}, u32[]{:S(2)}) collective-permute-start(bf16[2,256,256]{2,1,0:T(8,128)(2,1)S(1)} %select_bitcast_fusion.second.refs_2_), channel_id=1, source_target_pairs={{0,128},{128,0},{1,129},{129,1},{2,130},{130,2},{3,131},{131,3},{4... | collective-permute-start | bytes 786440 | tf_op jit(solution)/shard_map/ppermute | solution.py:324

commit v11 on v8

--- a/solution.py
+++ b/solution.py
@@ -331,7 +331,6 @@
     halos = [
         (across(first), across(second_after)),
         (late_first, late_second),
-        (across(late_first), across(late_second)),
     ]
     below = (field, first, second)
     pre = early(0, below, wg_state)
@@ -346,6 +345,10 @@
         below = (own_below, across(first), across(second))
         state = (hidden, first, second)
         pre = early(step, state, wg_state)
+        if step == 1:
+            passed = lax.optimization_barrier((late_first, late_second, second))[0:2]
+            *pre, one, other = lax.optimization_barrier((*pre, *map(across, passed)))
+            halos.append((one, other))
         if step == 3:
             return last(state, pre, below, wg, wc, biases, states[0:2])[None]
         hidden = late(step, state, pre, (rows, *halos[step]), below, wg, wc, biases)

time: 90.2 us -> 91.5 us (1.014)
  transfers between devices with their start and end apart: 20 -> 20, of which waited for: 3 -> 4; matrix products, arithmetic and copies ran while one was open for 0% -> 0% of each run, Pallas kernels for 9% -> 9%
where the time goes in v11:
time: 91.5 us; the launch traced here: 91.3 us
  blocking collectives  35.2 us (38%)
  starting transfers between devices  28.9 us (32%)
  Pallas kernels  21.5 us (23%)
  waiting for transfers between devices  5.19 us (6%)
    all_gather x3, blocking collectives, gathered_swap(): both = lax.all_gather(field, ('layer', 'rows'), axis_index_groups=groups)  35.2 us
    ppermute x13, starting transfers between devices, across(): return lax.ppermute(field, 'layer', [(0, 1), (1, 0)])  15.4 us
    ppermute x7, starting transfers between devices, pair_swap(): return lax.ppermute(field, 'rows', route)  13.5 us
    pallas_call x3, Pallas kernels, late(): pl.pallas_call(functools.partial(late_kernel, lag), out_shape=jax.ShapeDt...  7.91 us
    pallas_call x4, Pallas kernels, early(): pl.pallas_call(functools.partial(early_kernel, lag), out_shape=[pre(4), p...  6.09 us
    ppermute x7, waiting for transfers between devices, pair_swap(): return lax.ppermute(field, 'rows', route)  5.15 us
    pallas_call x1, Pallas kernels, last(): pl.pallas_call(last_kernel, out_shape=jax.ShapeDtypeStruct((3, 2, cols, c...  4.63 us
  transfers between devices with their start and end apart: 20, of which 4 were waited for; matrix products, arithmetic and copies ran while one was open for 0% of the time, Pallas kernels for 9%

profile of v11, /device:TPU:25, one launch (start us, length us, event | category | flops | bytes accessed | tf_op | source)
XLA Modules:
  0.0 91.3 jit_solution(13075334482516528715)
XLA Ops:
  0.0 1.0 %shard_map.55 = (bf16[2,256,256]{2,1,0:T(8,128)(2,1)S(1)}, bf16[2,256,256]{2,1,0:T(8,128)(2,1)S(1)}) custom-call(bf16[2,256,256]{2,1,0:T(8,128)(2,1)} %bitcast.26, bf16[6,256,256]{2,1,0:T(8,128)(2,1)} %bitcast.22), custom_call_target="tpu_custom_call" | custom-call | tf_op jit(solution)/shard_map/pallas_call | solution.py:224
  1.1 9.9 %collective-permute-start.1 = (bf16[2,256,256]{2,1,0:T(8,128)(2,1)S(1)}, bf16[2,256,256]{2,1,0:T(8,128)(2,1)S(1)}, u32[]{:S(2)}, u32[]{:S(2)}) collective-permute-start(bf16[2,256,256]{2,1,0:T(8,128)(2,1)S(1)} %get-tuple-element.33.own.refs_8_), channel_id=1, source_target_pairs={{1,2},{2,1},{3,4},{4,3},{5,6},{6,5},{7,8},{8,7},{9,10},{10,9},{11,... | collective-permute-start | bytes 786440 | tf_op jit(solution)/shard_map/ppermute | solution.py:296
  10.9 0.1 collective-permute-start
  11.0 1.5 %collective-permute-start.3 = (bf16[2,256,256]{2,1,0:T(8,128)(2,1)S(1)}, bf16[2,256,256]{2,1,0:T(8,128)(2,1)S(1)}, u32[]{:S(2)}, u32[]{:S(2)}) collective-permute-start(bf16[2,256,256]{2,1,0:T(8,128)(2,1)S(1)} %get-tuple-element.37), channel_id=1, source_target_pairs={{0,1},{1,0},{2,3},{3,2},{4,5},{5,4},{6,7},{7,6},{8,9},{9,8},{10,11... | collective-permute-start | bytes 786440 | tf_op jit(solution)/shard_map/ppermute | solution.py:296
  12.5 2.0 %collective-permute-start.2 = (bf16[2,256,256]{2,1,0:T(8,128)(2,1)S(1)}, bf16[2,256,256]{2,1,0:T(8,128)(2,1)S(1)}, u32[]{:S(2)}, u32[]{:S(2)}) collective-permute-start(bf16[2,256,256]{2,1,0:T(8,128)(2,1)S(1)} %get-tuple-element.37), channel_id=1, source_target_pairs={{1,2},{2,1},{3,4},{4,3},{5,6},{6,5},{7,8},{8,7},{9,10},{10,9},{11,... | collective-permute-start | bytes 786440 | tf_op jit(solution)/shard_map/ppermute | solution.py:296
  14.5 0.0 slice-start
  14.5 0.0 slice-start.1
  14.5 1.8 %shard_map.56.wg = bf16[3,3,256,512]{3,2,1,0:T(8,128)(2,1)S(1)} custom-call(bf16[3,3,512,512]{3,2,1,0:T(8,128)(2,1)} %bitcast.11), custom_call_target="tpu_custom_call" | custom-call | tf_op jit(solution)/shard_map/pallas_call | solution.py:236
  16.3 0.0 copy-start
  16.3 0.0 copy-start.1
  16.3 0.0 copy-start.2
  16.4 0.0 copy-start.3
  16.4 0.6 collective-permute-done.1.second.refs_2_.refs_10_
  16.9 0.9 %collective-permute-done.first.refs_1_.refs_9_ = bf16[2,256,256]{2,1,0:T(8,128)(2,1)S(1)} collective-permute-done((bf16[2,256,256]{2,1,0:T(8,128)(2,1)S(1)}, bf16[2,256,256]{2,1,0:T(8,128)(2,1)S(1)}, u32[]{:S(2)}, u32[]{:S(2)}) %collective-permute-start) | collective-permute-done | bytes 262176 | tf_op jit(solution)/shard_map/ppermute | solution.py:296
  17.9 3.3 %collective-permute-start.4 = (bf16[2,256,256]{2,1,0:T(8,128)(2,1)S(1)}, bf16[2,256,256]{2,1,0:T(8,128)(2,1)S(1)}, u32[]{:S(2)}, u32[]{:S(2)}) collective-permute-start(bf16[2,256,256]{2,1,0:T(8,128)(2,1)S(1)} %collective-permute-done.first.refs_1_.refs_9_), channel_id=1, source_target_pairs={{0,128},{128,0},{1,129},{129,1},{2,130},{130,2},{3,131},{131,3},{4... | collective-permute-start | bytes 786440 | tf_op jit(solution)/shard_map/ppermute | solution.py:312
  21.2 0.0 collective-permute-start.5
  21.2 2.3 %collective-permute-done.3.refs_6_ = bf16[2,256,256]{2,1,0:T(8,128)(2,1)S(1)} collective-permute-done((bf16[2,256,256]{2,1,0:T(8,128)(2,1)S(1)}, bf16[2,256,256]{2,1,0:T(8,128)(2,1)S(1)}, u32[]{:S(2)}, u32[]{:S(2)}) %collective-permute-start.3) | collective-permute-done | bytes 262176 | tf_op jit(solution)/shard_map/ppermute | solution.py:296
  23.5 1.4 %collective-permute-done.2.refs_7_ = bf16[2,256,256]{2,1,0:T(8,128)(2,1)S(1)} collective-permute-done((bf16[2,256,256]{2,1,0:T(8,128)(2,1)S(1)}, bf16[2,256,256]{2,1,0:T(8,128)(2,1)S(1)}, u32[]{:S(2)}, u32[]{:S(2)}) %collective-permute-start.2) | collective-permute-done | bytes 262176 | tf_op jit(solution)/shard_map/ppermute | solution.py:296
  24.9 0.0 collective-permute-done.4.refs_6_
  24.9 0.0 collective-permute-done.5.refs_7_
  24.9 0.0 slice-done
  24.9 0.0 slice-done.1
  24.9 0.0 copy-done
  24.9 0.0 copy-done.1
  24.9 0.0 copy-done.2
  24.9 0.0 copy-done.3
  25.0 0.1 collective-permute-start.6
  25.1 10.1 %all-gather = bf16[4,256,256]{2,1,0:T(8,128)(2,1)S(1)} all-gather(bf16[2,256,256]{2,1,0:T(8,128)(2,1)S(1)} %shard_map.58.own.refs_0_.refs_11_), channel_id=2, replica_groups={{0,128},{127,255},{1,2},{3,4},{5,6},{7,8},{9,10},{11,12},{13,14},{15,16..., dimensions={0}, use_global_device_ids=true | all-gather | bytes 786432 | tf_op jit(solution)/shard_map/all_gather | solution.py:304
  35.2 7.6 %collective-permute-start.7 = (bf16[2,256,256]{2,1,0:T(8,128)(2,1)S(1)}, bf16[2,256,256]{2,1,0:T(8,128)(2,1)S(1)}, u32[]{:S(2)}, u32[]{:S(2)}) collective-permute-start(bf16[2,256,256]{2,1,0:T(8,128)(2,1)S(1)} %collective-permute-done.3.refs_6_), channel_id=1, source_target_pairs={{0,128},{128,0},{1,129},{129,1},{2,130},{130,2},{3,131},{131,3},{4... | collective-permute-start | bytes 786440 | tf_op jit(solution)/shard_map/ppermute | solution.py:312
  42.8 0.1 collective-permute-start.8
  42.9 0.4 collective-permute-start.9
  43.3 0.1 collective-permute-start.11
  43.4 0.0 collective-permute-done.6.first.refs_1_
  43.4 0.4 collective-permute-start.10
  43.8 2.0 %shard_map.59 = (f32[1024,256]{1,0:T(8,128)S(1)}, f32[512,256]{1,0:T(8,128)S(1)}) custom-call(bf16[2,256,256]{2,1,0:T(8,128)(2,1)S(1)} %shard_map.58.own.refs_0_.refs_11_, bf16[2,256,256]{2,1,0:T(8,128)(2,1)S(1)} %collective-permute-done.6.first.refs_1_, bf16[2,256,256]{2,1,0:T(8,128)(2,1)S(1)} %fusion.second.refs_2_, bf16[3,3,256,512]{3,2,1,0:T(8,128)(2,1)S(1)} %shard_map.56.wg), custom_call_target="tpu_custom_call" | custom-call | flops 1811939328 | bytes 1048576 | tf_op jit(solution)/shard_map/pallas_call | solution.py:249
  45.8 0.0 collective-permute-done.7.refs_6_
  45.9 0.0 collective-permute-done.8.refs_7_
  45.9 0.0 collective-permute-done.9.refs_8_
  45.9 0.0 collective-permute-done.11.refs_10_
  45.9 0.0 collective-permute-done.10.refs_9_
  45.9 3.9 %shard_map.60.own.refs_0_.refs_12_ = bf16[2,256,256]{2,1,0:T(8,128)(2,1)S(1)} custom-call(bf16[2,256,256]{2,1,0:T(8,128)(2,1)S(1)} %shard_map.58.own.refs_0_.refs_11_, bf16[2,256,256]{2,1,0:T(8,128)(2,1)S(1)} %collective-permute-done.6.first.refs_1_, bf16[2,256,256]{2,1,0:T(8,128)(2,1)S(1)} %fusion.second.refs_2_, ...), custom_call_target="tpu_custom_call" | custom-call | flops 3019898880 | bytes 1048576 | tf_op jit(solution)/shard_map/pallas_call | solution.py:262
  49.8 0.2 collective-permute-start.13
  50.0 0.0 collective-permute-start.12
  50.0 12.4 %all-gather.1 = bf16[4,256,256]{2,1,0:T(8,128)(2,1)S(1)} all-gather(bf16[2,256,256]{2,1,0:T(8,128)(2,1)S(1)} %shard_map.60.own.refs_0_.refs_12_), channel_id=3, replica_groups={{0,128},{127,255},{1,2},{3,4},{5,6},{7,8},{9,10},{11,12},{13,14},{15,16..., dimensions={0}, use_global_device_ids=true | all-gather | bytes 786432 | tf_op jit(solution)/shard_map/all_gather | solution.py:304
  62.4 0.0 collective-permute-done.13.refs_8_
  62.5 0.0 collective-permute-done.12.first.refs_1_
  62.5 1.3 %collective-permute-start.14 = (bf16[2,256,256]{2,1,0:T(8,128)(2,1)S(1)}, bf16[2,256,256]{2,1,0:T(8,128)(2,1)S(1)}, u32[]{:S(2)}, u32[]{:S(2)}) collective-permute-start(bf16[2,256,256]{2,1,0:T(8,128)(2,1)S(1)} %collective-permute-done.12.first.refs_1_), channel_id=1, source_target_pairs={{0,128},{128,0},{1,129},{129,1},{2,130},{130,2},{3,131},{131,3},{4... | collective-permute-start | bytes 786440 | tf_op jit(solution)/shard_map/ppermute | solution.py:312
  63.8 0.1 collective-permute-start.15
  63.9 2.0 %shard_map.61 = (f32[1024,256]{1,0:T(8,128)S(1)}, f32[512,256]{1,0:T(8,128)S(1)}) custom-call(bf16[2,256,256]{2,1,0:T(8,128)(2,1)S(1)} %shard_map.60.own.refs_0_.refs_12_, bf16[2,256,256]{2,1,0:T(8,128)(2,1)S(1)} %collective-permute-done.12.first.refs_1_, bf16[2,256,256]{2,1,0:T(8,128)(2,1)S(1)} %select_bitcast_fusion.1.second.refs_2_, ...), custom_call_target="tpu_custom_call" | custom-call | flops 1811939328 | bytes 1048576 | tf_op jit(solution)/shard_map/pallas_call | solution.py:249
  65.9 0.0 collective-permute-done.14.refs_9_
  65.9 0.0 collective-permute-done.15.refs_10_
  65.9 3.9 %shard_map.62.own.refs_0_ = bf16[2,256,256]{2,1,0:T(8,128)(2,1)S(1)} custom-call(bf16[2,256,256]{2,1,0:T(8,128)(2,1)S(1)} %shard_map.60.own.refs_0_.refs_12_, bf16[2,256,256]{2,1,0:T(8,128)(2,1)S(1)} %collective-permute-done.12.first.refs_1_, bf16[2,256,256]{2,1,0:T(8,128)(2,1)S(1)} %select_bitcast_fusion.1.second.refs_2_, ...), custom_call_target="tpu_custom_call" | custom-call | flops 3019898880 | bytes 1048576 | tf_op jit(solution)/shard_map/pallas_call | solution.py:262
  69.9 0.5 collective-permute-start.17
  70.4 0.0 collective-permute-start.16
  70.4 12.7 %all-gather.2 = bf16[4,256,256]{2,1,0:T(8,128)(2,1)S(1)} all-gather(bf16[2,256,256]{2,1,0:T(8,128)(2,1)S(1)} %shard_map.62.own.refs_0_), channel_id=4, replica_groups={{0,128},{127,255},{1,2},{3,4},{5,6},{7,8},{9,10},{11,12},{13,14},{15,16..., dimensions={0}, use_global_device_ids=true | all-gather | bytes 786432 | tf_op jit(solution)/shard_map/all_gather | solution.py:304
  83.0 0.0 collective-permute-done.17.refs_5_
  83.1 0.0 collective-permute-done.16.first.refs_1_
  83.1 1.3 %collective-permute-start.18 = (bf16[2,256,256]{2,1,0:T(8,128)(2,1)S(1)}, bf16[2,256,256]{2,1,0:T(8,128)(2,1)S(1)}, u32[]{:S(2)}, u32[]{:S(2)}) collective-permute-start(bf16[2,256,256]{2,1,0:T(8,128)(2,1)S(1)} %collective-permute-done.16.first.refs_1_), channel_id=1, source_target_pairs={{0,128},{128,0},{1,129},{129,1},{2,130},{130,2},{3,131},{131,3},{4... | collective-permute-start | bytes 786440 | tf_op jit(solution)/shard_map/ppermute | solution.py:312
  84.4 0.1 collective-permute-start.19
  84.5 2.0 %shard_map.63 = (f32[1024,256]{1,0:T(8,128)S(1)}, f32[512,256]{1,0:T(8,128)S(1)}) custom-call(bf16[2,256,256]{2,1,0:T(8,128)(2,1)S(1)} %shard_map.62.own.refs_0_, bf16[2,256,256]{2,1,0:T(8,128)(2,1)S(1)} %collective-permute-done.16.first.refs_1_, bf16[2,256,256]{2,1,0:T(8,128)(2,1)S(1)} %select_bitcast_fusion.second.refs_2_, ...), custom_call_target="tpu_custom_call" | custom-call | flops 1811939328 | bytes 1048576 | tf_op jit(solution)/shard_map/pallas_call | solution.py:249
  86.5 0.0 collective-permute-done.18.refs_6_
  86.5 0.0 collective-permute-done.19.refs_7_
  86.5 4.6 %shard_map.64 = bf16[3,2,256,256]{3,2,1,0:T(8,128)(2,1)} custom-call(bf16[2,256,256]{2,1,0:T(8,128)(2,1)S(1)} %shard_map.62.own.refs_0_, bf16[2,256,256]{2,1,0:T(8,128)(2,1)S(1)} %collective-permute-done.16.first.refs_1_, bf16[2,256,256]{2,1,0:T(8,128)(2,1)S(1)} %select_bitcast_fusion.second.refs_2_, f32[1024,256]{1,0:T(8,128)S(1)} %get-tuple-element.56.refs_3_, ...), custom_call_target="tpu_custom_call" | custom-call | flops 3019898880 | bytes 1048576 | tf_op jit(solution)/shard_map/pallas_call | solution.py:275
  (6 shorter events, 0.1 us)
Async XLA Ops:
  1.1 15.9 %collective-permute-start.1 = (bf16[2,256,256]{2,1,0:T(8,128)(2,1)S(1)}, bf16[2,256,256]{2,1,0:T(8,128)(2,1)S(1)}, u32[]{:S(2)}, u32[]{:S(2)}) collective-permute-start(bf16[2,256,256]{2,1,0:T(8,128)(2,1)S(1)} %get-tuple-element.33.own.refs_8_), channel_id=1, source_target_pairs={{1,2},{2,1},{3,4},{4,3},{5,6},{6,5},{7,8},{8,7},{9,10},{10,9},{11,... | collective-permute-start | bytes 786440 | tf_op jit(solution)/shard_map/ppermute | solution.py:296
  10.9 6.9 %collective-permute-start = (bf16[2,256,256]{2,1,0:T(8,128)(2,1)S(1)}, bf16[2,256,256]{2,1,0:T(8,128)(2,1)S(1)}, u32[]{:S(2)}, u32[]{:S(2)}) collective-permute-start(bf16[2,256,256]{2,1,0:T(8,128)(2,1)S(1)} %get-tuple-element.33.own.refs_8_), channel_id=1, source_target_pairs={{0,1},{1,0},{2,3},{3,2},{4,5},{5,4},{6,7},{7,6},{8,9},{9,8},{10,11... | collective-permute-start | bytes 786440 | tf_op jit(solution)/shard_map/ppermute | solution.py:296
  11.0 12.5 %collective-permute-start.3 = (bf16[2,256,256]{2,1,0:T(8,128)(2,1)S(1)}, bf16[2,256,256]{2,1,0:T(8,128)(2,1)S(1)}, u32[]{:S(2)}, u32[]{:S(2)}) collective-permute-start(bf16[2,256,256]{2,1,0:T(8,128)(2,1)S(1)} %get-tuple-element.37), channel_id=1, source_target_pairs={{0,1},{1,0},{2,3},{3,2},{4,5},{5,4},{6,7},{7,6},{8,9},{9,8},{10,11... | collective-permute-start | bytes 786440 | tf_op jit(solution)/shard_map/ppermute | solution.py:296
  12.5 12.4 %collective-permute-start.2 = (bf16[2,256,256]{2,1,0:T(8,128)(2,1)S(1)}, bf16[2,256,256]{2,1,0:T(8,128)(2,1)S(1)}, u32[]{:S(2)}, u32[]{:S(2)}) collective-permute-start(bf16[2,256,256]{2,1,0:T(8,128)(2,1)S(1)} %get-tuple-element.37), channel_id=1, source_target_pairs={{1,2},{2,1},{3,4},{4,3},{5,6},{6,5},{7,8},{8,7},{9,10},{10,9},{11,... | collective-permute-start | bytes 786440 | tf_op jit(solution)/shard_map/ppermute | solution.py:296
  14.5 10.4 %slice-start = ((s8[4718592]{0:T(1024)(128)(4,1)}), s8[4194304]{0:T(1024)(128)(4,1)S(1)}, s32[]{:S(2)}) async-start(s8[4718592]{0:T(1024)(128)(4,1)} %bitcast.12), calls=%async_computation | async-start | bytes 8388608
  14.5 10.4 %slice-start.1 = ((s8[4718592]{0:T(1024)(128)(4,1)}), s8[524288]{0:T(1024)(128)(4,1)S(1)}, s32[]{:S(2)}) async-start(s8[4718592]{0:T(1024)(128)(4,1)} %bitcast.12), calls=%async_computation.1 | async-start | bytes 1048576
  16.3 8.6 %copy-start = (bf16[1,3,3,512,256]{4,3,2,1,0:T(8,128)(2,1)S(1)}, bf16[1,3,3,512,256]{4,3,2,1,0:T(8,128)(2,1)}, u32[]{:S(2)}) copy-start(bf16[1,3,3,512,256]{4,3,2,1,0:T(8,128)(2,1)} %param.8) | copy-start | bytes 7077892
  16.3 8.6 %copy-start.1 = (bf16[3,2,256,256]{3,2,1,0:T(8,128)(2,1)S(1)}, bf16[3,2,256,256]{3,2,1,0:T(8,128)(2,1)}, u32[]{:S(2)}) copy-start(bf16[3,2,256,256]{3,2,1,0:T(8,128)(2,1)} %param.5) | copy-start | bytes 2359300
  16.3 8.6 %copy-start.2 = (bf16[1,2,256,256]{3,2,1,0:T(8,128)(2,1)S(1)}, bf16[1,2,256,256]{3,2,1,0:T(8,128)(2,1)}, u32[]{:S(2)}) copy-start(bf16[1,2,256,256]{3,2,1,0:T(8,128)(2,1)} %param.6) | copy-start | bytes 786436
  16.4 8.5 %copy-start.3 = (f32[1,768]{1,0:T(1,128)S(1)}, f32[1,768]{1,0:T(1,128)}, u32[]{:S(2)}) copy-start(f32[1,768]{1,0:T(1,128)} %refs_10_.1) | copy-start | bytes 9220
  17.9 7.0 %collective-permute-start.4 = (bf16[2,256,256]{2,1,0:T(8,128)(2,1)S(1)}, bf16[2,256,256]{2,1,0:T(8,128)(2,1)S(1)}, u32[]{:S(2)}, u32[]{:S(2)}) collective-permute-start(bf16[2,256,256]{2,1,0:T(8,128)(2,1)S(1)} %collective-permute-done.first.refs_1_.refs_9_), channel_id=1, source_target_pairs={{0,128},{128,0},{1,129},{129,1},{2,130},{130,2},{3,131},{131,3},{4... | collective-permute-start | bytes 786440 | tf_op jit(solution)/shard_map/ppermute | solution.py:312
  21.2 3.7 %collective-permute-start.5 = (bf16[2,256,256]{2,1,0:T(8,128)(2,1)S(1)}, bf16[2,256,256]{2,1,0:T(8,128)(2,1)S(1)}, u32[]{:S(2)}, u32[]{:S(2)}) collective-permute-start(bf16[2,256,256]{2,1,0:T(8,128)(2,1)S(1)} %collective-permute-done.1.second.refs_2_.refs_10_), channel_id=1, source_target_pairs={{0,128},{128,0},{1,129},{129,1},{2,130},{130,2},{3,131},{131,3},{4... | collective-permute-start | bytes 786440 | tf_op jit(solution)/shard_map/ppermute | solution.py:312
  25.0 18.4 %collective-permute-start.6 = (bf16[2,256,256]{2,1,0:T(8,128)(2,1)S(1)}, bf16[2,256,256]{2,1,0:T(8,128)(2,1)S(1)}, u32[]{:S(2)}, u32[]{:S(2)}) collective-permute-start(bf16[2,256,256]{2,1,0:T(8,128)(2,1)S(1)} %shard_map.58.own.refs_0_.refs_11_), channel_id=1, source_target_pairs={{0,1},{1,0},{2,3},{3,2},{4,5},{5,4},{6,7},{7,6},{8,9},{9,8},{10,11... | collective-permute-start | bytes 786440 | tf_op jit(solution)/shard_map/ppermute | solution.py:296
  35.2 10.6 %collective-permute-start.7 = (bf16[2,256,256]{2,1,0:T(8,128)(2,1)S(1)}, bf16[2,256,256]{2,1,0:T(8,128)(2,1)S(1)}, u32[]{:S(2)}, u32[]{:S(2)}) collective-permute-start(bf16[2,256,256]{2,1,0:T(8,128)(2,1)S(1)} %collective-permute-done.3.refs_6_), channel_id=1, source_target_pairs={{0,128},{128,0},{1,129},{129,1},{2,130},{130,2},{3,131},{131,3},{4... | collective-permute-start | bytes 786440 | tf_op jit(solution)/shard_map/ppermute | solution.py:312
  42.8 3.1 %collective-permute-start.8 = (bf16[2,256,256]{2,1,0:T(8,128)(2,1)S(1)}, bf16[2,256,256]{2,1,0:T(8,128)(2,1)S(1)}, u32[]{:S(2)}, u32[]{:S(2)}) collective-permute-start(bf16[2,256,256]{2,1,0:T(8,128)(2,1)S(1)} %collective-permute-done.2.refs_7_), channel_id=1, source_target_pairs={{0,128},{128,0},{1,129},{129,1},{2,130},{130,2},{3,131},{131,3},{4... | collective-permute-start | bytes 786440 | tf_op jit(solution)/shard_map/ppermute | solution.py:312
  42.9 3.0 %collective-permute-start.9 = (bf16[2,256,256]{2,1,0:T(8,128)(2,1)S(1)}, bf16[2,256,256]{2,1,0:T(8,128)(2,1)S(1)}, u32[]{:S(2)}, u32[]{:S(2)}) collective-permute-start(bf16[2,256,256]{2,1,0:T(8,128)(2,1)S(1)} %shard_map.58.own.refs_0_.refs_11_), channel_id=1, source_target_pairs={{0,128},{128,0},{1,129},{129,1},{2,130},{130,2},{3,131},{131,3},{4... | collective-permute-start | bytes 786440 | tf_op jit(solution)/shard_map/ppermute | solution.py:312
  43.3 2.6 %collective-permute-start.11 = (bf16[2,256,256]{2,1,0:T(8,128)(2,1)S(1)}, bf16[2,256,256]{2,1,0:T(8,128)(2,1)S(1)}, u32[]{:S(2)}, u32[]{:S(2)}) collective-permute-start(bf16[2,256,256]{2,1,0:T(8,128)(2,1)S(1)} %fusion.second.refs_2_), channel_id=1, source_target_pairs={{0,128},{128,0},{1,129},{129,1},{2,130},{130,2},{3,131},{131,3},{4... | collective-permute-start | bytes 786440 | tf_op jit(solution)/shard_map/ppermute | solution.py:312
  43.4 2.5 %collective-permute-start.10 = (bf16[2,256,256]{2,1,0:T(8,128)(2,1)S(1)}, bf16[2,256,256]{2,1,0:T(8,128)(2,1)S(1)}, u32[]{:S(2)}, u32[]{:S(2)}) collective-permute-start(bf16[2,256,256]{2,1,0:T(8,128)(2,1)S(1)} %collective-permute-done.6.first.refs_1_), channel_id=1, source_target_pairs={{0,128},{128,0},{1,129},{129,1},{2,130},{130,2},{3,131},{131,3},{4... | collective-permute-start | bytes 786440 | tf_op jit(solution)/shard_map/ppermute | solution.py:312
  49.8 12.6 %collective-permute-start.13 = (bf16[2,256,256]{2,1,0:T(8,128)(2,1)S(1)}, bf16[2,256,256]{2,1,0:T(8,128)(2,1)S(1)}, u32[]{:S(2)}, u32[]{:S(2)}) collective-permute-start(bf16[2,256,256]{2,1,0:T(8,128)(2,1)S(1)} %shard_map.60.own.refs_0_.refs_12_), channel_id=1, source_target_pairs={{0,128},{128,0},{1,129},{129,1},{2,130},{130,2},{3,131},{131,3},{4... | collective-permute-start | bytes 786440 | tf_op jit(solution)/shard_map/ppermute | solution.py:312
  50.0 12.5 %collective-permute-start.12 = (bf16[2,256,256]{2,1,0:T(8,128)(2,1)S(1)}, bf16[2,256,256]{2,1,0:T(8,128)(2,1)S(1)}, u32[]{:S(2)}, u32[]{:S(2)}) collective-permute-start(bf16[2,256,256]{2,1,0:T(8,128)(2,1)S(1)} %shard_map.60.own.refs_0_.refs_12_), channel_id=1, source_target_pairs={{0,1},{1,0},{2,3},{3,2},{4,5},{5,4},{6,7},{7,6},{8,9},{9,8},{10,11... | collective-permute-start | bytes 786440 | tf_op jit(solution)/shard_map/ppermute | solution.py:296
  62.5 3.4 %collective-permute-start.14 = (bf16[2,256,256]{2,1,0:T(8,128)(2,1)S(1)}, bf16[2,256,256]{2,1,0:T(8,128)(2,1)S(1)}, u32[]{:S(2)}, u32[]{:S(2)}) collective-permute-start(bf16[2,256,256]{2,1,0:T(8,128)(2,1)S(1)} %collective-permute-done.12.first.refs_1_), channel_id=1, source_target_pairs={{0,128},{128,0},{1,129},{129,1},{2,130},{130,2},{3,131},{131,3},{4... | collective-permute-start | bytes 786440 | tf_op jit(solution)/shard_map/ppermute | solution.py:312
  63.8 2.1 %collective-permute-start.15 = (bf16[2,256,256]{2,1,0:T(8,128)(2,1)S(1)}, bf16[2,256,256]{2,1,0:T(8,128)(2,1)S(1)}, u32[]{:S(2)}, u32[]{:S(2)}) collective-permute-start(bf16[2,256,256]{2,1,0:T(8,128)(2,1)S(1)} %select_bitcast_fusion.1.second.refs_2_), channel_id=1, source_target_pairs={{0,128},{128,0},{1,129},{129,1},{2,130},{130,2},{3,131},{131,3},{4... | collective-permute-start | bytes 786440 | tf_op jit(solution)/shard_map/ppermute | solution.py:312
  69.9 13.2 %collective-permute-start.17 = (bf16[2,256,256]{2,1,0:T(8,128)(2,1)S(1)}, bf16[2,256,256]{2,1,0:T(8,128)(2,1)S(1)}, u32[]{:S(2)}, u32[]{:S(2)}) collective-permute-start(bf16[2,256,256]{2,1,0:T(8,128)(2,1)S(1)} %shard_map.62.own.refs_0_), channel_id=1, source_target_pairs={{0,128},{128,0},{1,129},{129,1},{2,130},{130,2},{3,131},{131,3},{4... | collective-permute-start | bytes 786440 | tf_op jit(solution)/shard_map/ppermute | solution.py:312
  70.4 12.7 %collective-permute-start.16 = (bf16[2,256,256]{2,1,0:T(8,128)(2,1)S(1)}, bf16[2,256,256]{2,1,0:T(8,128)(2,1)S(1)}, u32[]{:S(2)}, u32[]{:S(2)}) collective-permute-start(bf16[2,256,256]{2,1,0:T(8,128)(2,1)S(1)} %shard_map.62.own.refs_0_), channel_id=1, source_target_pairs={{0,1},{1,0},{2,3},{3,2},{4,5},{5,4},{6,7},{7,6},{8,9},{9,8},{10,11... | collective-permute-start | bytes 786440 | tf_op jit(solution)/shard_map/ppermute | solution.py:296
  83.1 3.4 %collective-permute-start.18 = (bf16[2,256,256]{2,1,0:T(8,128)(2,1)S(1)}, bf16[2,256,256]{2,1,0:T(8,128)(2,1)S(1)}, u32[]{:S(2)}, u32[]{:S(2)}) collective-permute-start(bf16[2,256,256]{2,1,0:T(8,128)(2,1)S(1)} %collective-permute-done.16.first.refs_1_), channel_id=1, source_target_pairs={{0,128},{128,0},{1,129},{129,1},{2,130},{130,2},{3,131},{131,3},{4... | collective-permute-start | bytes 786440 | tf_op jit(solution)/shard_map/ppermute | solution.py:312
  84.4 2.1 %collective-permute-start.19 = (bf16[2,256,256]{2,1,0:T(8,128)(2,1)S(1)}, bf16[2,256,256]{2,1,0:T(8,128)(2,1)S(1)}, u32[]{:S(2)}, u32[]{:S(2)}) collective-permute-start(bf16[2,256,256]{2,1,0:T(8,128)(2,1)S(1)} %select_bitcast_fusion.second.refs_2_), channel_id=1, source_target_pairs={{0,128},{128,0},{1,129},{129,1},{2,130},{130,2},{3,131},{131,3},{4... | collective-permute-start | bytes 786440 | tf_op jit(solution)/shard_map/ppermute | solution.py:312
